TPU v7x, 32 devices: a whole 2x2x4 slice. The times are simulated.
32 devices in a mesh: grp: 2 (over x), seq: 4 (over y, core), sub: 4 (over z).
Axes of the slice: x: 2, y: 2, z: 4, core: 2. Of those that a mesh axis runs over, the one named last changes fastest.
Arguments:
- query_rows: bfloat16 [8, 512, 2048], P(('grp', 'sub'), 'seq'), parts along dimension 0, may hold values from -9 to 9
- key_rows: bfloat16 [8, 512, 256], P(('grp', 'sub'), 'seq'), parts along dimension 0, may hold values from -4 to 4
- value_rows: bfloat16 [8, 512, 256], P(('grp', 'sub'), 'seq'), parts along dimension 0, may hold values from -6 to 6
- residual_in: bfloat16 [8, 512, 2048], P(('grp', 'sub'), 'seq'), parts along dimension 0, may hold values from -6 to 6
- out_proj: bfloat16 [2048, 2048], P('seq'), may hold values from -0.5 to 0.5
- norm_gain: bfloat16 [2048], replicated, may hold values from 0.099609375 to 1.8984375
- expert_ids: int32 [8, 512, 8], P(('grp', 'sub'), 'seq'), parts along dimension 0, may hold values from 0 to 15, all different within a row; in each aligned block of 128 rows (0 to 127, 128 to 255, ..., all dimensions but the last counted through in order) at most 80 rows name the same one
- gate_weights: bfloat16 [8, 512, 8], P(('grp', 'sub'), 'seq'), parts along dimension 0, may hold values from 0.049804688 to 1
- expert_gate: bfloat16 [16, 2048, 768], P(('seq', 'sub')), may hold values from -0.125 to 0.125
- expert_up: bfloat16 [16, 2048, 768], P(('seq', 'sub')), may hold values from -0.125 to 0.125
- expert_down: bfloat16 [16, 768, 2048], P(('seq', 'sub')), may hold values from -0.21875 to 0.21875
Outputs:
- layer_out: bfloat16 [8, 512, 2048], P(('grp', 'sub'), 'seq'), parts along dimension 0
There are 2 independent parts, one for each index of `grp`. A program takes and returns all parts, laid end to end along the dimension named above; an argument that names none is the same for every part. Nothing has to cross between parts.
Inputs may be any that keep to these rules, and one draw needn't show every extreme that they name: `expert_ids`: A row names 8 different experts. In each aligned block of 128 rows (the rows of one device) no expert is named by more than 80 rows, a bound that some block reaches.
All inputs are finite; a program needn't handle non-finite values.
Results may differ from a plain program's by a relative error of at most 0.013.
Values may be sent and summed in bfloat16 or wider, within the bound.
No kernel may reach another device: no remote copies, remote signals or barrier semaphores. Data moves between devices by JAX's collectives and lax.ppermute only.
A program may use at most 128 MiB of HBM per device.

v0:
```python
import jax
import jax.numpy as jnp
from jax import lax
from jax.sharding import PartitionSpec as P

D = 2048
HD = 128
QH = 16
KVH = 2


def attend_head(queries, keys_one, values_one, block):
    length = queries.shape[0]
    scale = 1.0 / queries.shape[1] ** 0.5
    pieces = []
    for part_index in range(length // block):
        stop = (part_index + 1) * block
        rows_here = queries[part_index * block : stop]
        scores = (
            jnp.einsum("qd,kd->qk", rows_here, keys_one[:stop], preferred_element_type=jnp.float32)
            * scale
        )
        row_pos = part_index * block + jnp.arange(block, dtype=jnp.int32)
        col_pos = jnp.arange(stop, dtype=jnp.int32)
        scores = jnp.where(row_pos[:, None] >= col_pos[None, :], scores, -1e30)
        peak = jnp.max(scores, axis=1, keepdims=True)
        weights = jnp.exp(scores - peak)
        probs = (weights / jnp.sum(weights, axis=1, keepdims=True)).astype(jnp.bfloat16)
        pieces.append(
            jnp.dot(probs, values_one[:stop], preferred_element_type=jnp.float32).astype(
                jnp.bfloat16
            )
        )
    return jnp.concatenate(pieces, axis=0)


def rank_in_expert(flat_ids, experts):
    items = flat_ids.shape[0]
    width = 128
    n_parts = items // width
    onehot = (
        (flat_ids[:, None] == jnp.arange(experts, dtype=jnp.int32)[None, :])
        .astype(jnp.bfloat16)
        .reshape(n_parts, width, experts)
    )
    lower = (
        jnp.arange(width, dtype=jnp.int32)[:, None] > jnp.arange(width, dtype=jnp.int32)[None, :]
    ).astype(jnp.bfloat16)
    within = jnp.einsum("ij,bje->bie", lower, onehot, preferred_element_type=jnp.float32)
    part_counts = jnp.sum(onehot.astype(jnp.float32), axis=1)
    earlier = jnp.cumsum(part_counts, axis=0) - part_counts
    ranks = jnp.sum((within + earlier[:, None, :]) * onehot.astype(jnp.float32), axis=2)
    return ranks.reshape(items).astype(jnp.int32)


def per_device(
    query_rows,
    key_rows,
    value_rows,
    residual_in,
    out_proj,
    norm_gain,
    expert_ids,
    gate_weights,
    expert_gate,
    expert_up,
    expert_down,
):
    tokens = query_rows.shape[1]
    n_seq = lax.axis_size("seq")
    n_sub = lax.axis_size("sub")
    heads_here = QH // n_seq
    group = QH // KVH
    query_local = lax.all_to_all(query_rows, "seq", split_axis=2, concat_axis=1, tiled=True)
    key_full, value_full = (
        lax.all_gather(key_rows, "seq", axis=1, tiled=True),
        lax.all_gather(value_rows, "seq", axis=1, tiled=True),
    )
    first_head = lax.axis_index("seq") * heads_here
    key_list = []
    value_list = []
    for head in range(heads_here):
        kv_start = (first_head + head) // group * HD
        key_list.append(lax.dynamic_slice_in_dim(key_full[0], kv_start, HD, 1))
        value_list.append(lax.dynamic_slice_in_dim(value_full[0], kv_start, HD, 1))
    length = query_local.shape[1]
    block = min(length, max(512, length // 8))
    outputs = [
        attend_head(
            query_local[0, :, head * HD : (head + 1) * HD], key_list[head], value_list[head], block
        )
        for head in range(heads_here)
    ]
    head_block = jnp.concatenate(outputs, axis=1)[None]
    attended = lax.all_to_all(head_block, "seq", split_axis=1, concat_axis=2, tiled=True)[0]
    projected = jnp.dot(
        attended,
        lax.all_gather(out_proj, "seq", axis=0, tiled=True),
        preferred_element_type=jnp.float32,
    )
    hidden = (residual_in[0].astype(jnp.float32) + projected).astype(jnp.bfloat16)
    wide = hidden.astype(jnp.float32)
    normed = (
        wide
        * lax.rsqrt(jnp.mean(wide * wide, axis=1, keepdims=True) + 1e-06)
        * norm_gain.astype(jnp.float32)
    ).astype(jnp.bfloat16)
    topk = expert_ids.shape[2]
    experts = n_seq * n_sub
    cap = max(2, (5 * tokens * topk + 4 * experts - 1) // (4 * experts))
    flat_ids = expert_ids[0].reshape(-1)
    items = flat_ids.shape[0]
    ranks = rank_in_expert(flat_ids, experts)
    slot_of = flat_ids * cap + ranks
    slots_out = experts * cap
    item_of_slot = (
        jnp.full((slots_out,), items, jnp.int32).at[slot_of].set(jnp.arange(items, dtype=jnp.int32))
    )
    padded_rows = jnp.concatenate([normed, jnp.zeros((1, D), jnp.bfloat16)], axis=0)
    padded_gates = jnp.concatenate(
        [gate_weights[0].reshape(-1), jnp.zeros((1,), jnp.bfloat16)], axis=0
    )
    token_of_slot = jnp.where(item_of_slot < items, item_of_slot // topk, tokens)
    send_rows = padded_rows[token_of_slot].reshape(experts, cap, D)
    send_gates = padded_gates[item_of_slot].reshape(experts, cap)
    recv_rows, recv_gates = (
        lax.all_to_all(send_rows, ("seq", "sub"), split_axis=0, concat_axis=0, tiled=True),
        lax.all_to_all(send_gates, ("seq", "sub"), split_axis=0, concat_axis=0, tiled=True),
    )
    slots_in = experts * cap
    valid = recv_gates > 0
    counts = jnp.sum(valid.astype(jnp.int32), axis=1)
    offsets = jnp.cumsum(counts) - counts
    dest = jnp.where(
        valid, offsets[:, None] + jnp.arange(cap, dtype=jnp.int32)[None, :], slots_in
    ).reshape(-1)
    source_of = (
        jnp.full((slots_in + 1,), slots_in, jnp.int32)
        .at[dest]
        .set(jnp.arange(slots_in, dtype=jnp.int32))[:slots_in]
    )
    compact_rows = jnp.concatenate(
        [recv_rows.reshape(slots_in, D), jnp.zeros((1, D), jnp.bfloat16)], axis=0
    )[source_of]
    compact_gates = jnp.concatenate(
        [recv_gates.reshape(-1), jnp.zeros((1,), jnp.bfloat16)], axis=0
    )[source_of].astype(jnp.float32)
    filled = jnp.sum(counts)
    n_blocks = (filled + slots_in - 1) // slots_in
    w_gate = expert_gate[0]
    w_up = expert_up[0]
    w_down = expert_down[0]

    def expert_block(index, results):
        gate_proj = jnp.dot(compact_rows, w_gate, preferred_element_type=jnp.float32)
        up_proj = jnp.dot(compact_rows, w_up, preferred_element_type=jnp.float32)
        inner = (jax.nn.silu(gate_proj) * up_proj).astype(jnp.bfloat16)
        weighted = (
            jnp.dot(inner, w_down, preferred_element_type=jnp.float32) * compact_gates[:, None]
        )
        return weighted.astype(jnp.bfloat16)

    results = lax.fori_loop(0, n_blocks, expert_block, jnp.zeros((slots_in, D), jnp.bfloat16))
    returned = jnp.concatenate([results, jnp.zeros((1, D), jnp.bfloat16)], axis=0)[dest].reshape(
        experts, cap, D
    )
    back = lax.all_to_all(
        returned, ("seq", "sub"), split_axis=0, concat_axis=0, tiled=True
    ).reshape(slots_out, D)
    gathered = back[slot_of].reshape(tokens, topk, D).astype(jnp.float32)
    mixture = jnp.sum(gathered, axis=1)
    return (wide + mixture).astype(jnp.bfloat16)[None]


def solution(mesh):
    placed = (
        P(("grp", "sub"), "seq", None),
        P(("grp", "sub"), "seq", None),
        P(("grp", "sub"), "seq", None),
        P(("grp", "sub"), "seq", None),
        P("seq", None),
        P(),
        P(("grp", "sub"), "seq", None),
        P(("grp", "sub"), "seq", None),
        P(("seq", "sub"), None, None),
        P(("seq", "sub"), None, None),
        P(("seq", "sub"), None, None),
    )
    return jax.shard_map(
        per_device,
        mesh=mesh,
        in_specs=placed,
        out_specs=P(("grp", "sub"), "seq", None),
        check_vma=False,
    )
```

profile of v0, /device:TPU:0, one launch (start us, length us, event | category | flops | bytes accessed | tf_op | source)
XLA Modules:
  0.0 475.6 jit_solution(11727438130950992658)
XLA Ops:
  7.3 3.7 copy.33
  11.6 13.3 %reduce.9 = bf16[2048,128]{1,0:T(8,128)(2,1)} reduce(bf16[2048,1,128]{2,1,0:T(2,128)(2,1)} %bitcast.127, bf16[]{:T(256)} %broadcast.193), dimensions={1}, to_apply=%bitcast.95.reduce_sub_computation | reduce | bytes 1048578
  26.9 4.2 all-to-all-start
  32.1 18.6 %all_gather.9 = bf16[1,512,256]{2,1,0:T(8,128)(2,1)} all-gather(bf16[1,128,256]{2,1,0:T(8,128)(2,1)S(1)} %copy-done.6), channel_id=1, replica_groups=mesh['grp'=2,'seq'=4,'sub'=4] {'seq'}, dimensions={1}, use_global_device_ids=true | all-gather | bytes 327680 | tf_op jit(solution)/shard_map/all_gather | solution.py:76
  50.8 8.2 %all_gather.10 = bf16[1,512,256]{2,1,0:T(8,128)(2,1)S(1)} all-gather(bf16[1,128,256]{2,1,0:T(8,128)(2,1)S(1)} %copy-done.7), channel_id=1, replica_groups=mesh['grp'=2,'seq'=4,'sub'=4] {'seq'}, dimensions={1}, use_global_device_ids=true | all-gather | bytes 327680 | tf_op jit(solution)/shard_map/all_gather | solution.py:77
  58.9 3.5 reshape.277
  74.8 3.6 copy.35
  78.4 5.5 %reduce.10 = bf16[512,512]{1,0:T(8,128)(2,1)} reduce(bf16[512,1,512]{2,1,0:T(2,128)(2,1)} %bitcast.126, bf16[]{:T(256)} %broadcast.193), dimensions={1}, to_apply=%bitcast.97.reduce_sub_computation | reduce | bytes 1048578
  86.2 4.1 all-to-all-start.1
  90.4 4.3 scatter_custom_fusion
  94.8 8.0 %gather_fusion = bf16[1280]{0:T(1024)(128)(2,1)S(1)} fusion(bf16[1025]{0:T(1024)(128)(2,1)S(1)} %pad_maximum_fusion, s32[2048]{0:T(1024)S(1)} %get-tuple-element.173), kind=kCustom, calls=%fused_computation | custom fusion | bytes 10240 | tf_op jit(solution)/shard_map/gather | solution.py:125
  103.4 7.1 %all-to-all-start.2 = ((bf16[16,1,80]{2,1,0:T(2,128)(2,1)}), bf16[16,1,80]{2,1,0:T(2,128)(2,1)S(1)}, u32[]{:S(2)}, u32[]{:S(2)}) async-start(bf16[16,1,80]{2,1,0:T(2,128)(2,1)} %all_to_all.47), calls=%async_computation.2 | async-start | bytes 16384 | tf_op jit(solution)/shard_map/all_to_all | solution.py:128
  110.6 3.5 reshape.279
  118.3 4.9 %multiply_reduce_fusion = (f32[128]{0:T(128)S(1)}, f32[128,2048]{1,0:T(8,128)S(1)}) fusion(bf16[128,2048]{0,1:T(8,128)(2,1)} %bitcast.128, bf16[2048,2048]{1,0:T(8,128)(2,1)} %all-gather.2.cloned.1.call-done, bf16[1,128,2048]{2,1,0:T(8,128)(2,1)} %param.16), kind=kOutput, calls=%fused_computation.42 | convolution fusion | flops 1075314560 | bytes 10486272 | tf_op jit(solution)/shard_map/dot_general | solution.py:96
  125.3 11.9 %gather_fusion.2 = bf16[1280,2048]{1,0:T(8,128)(2,1)} fusion(bf16[129,2048]{1,0:T(8,128)(2,1)} %concatenate.21, s32[2048]{0:T(1024)S(1)} %get-tuple-element.172), kind=kCustom, calls=%fused_computation.2 | custom fusion | bytes 10490880 | tf_op jit(solution)/shard_map/gather | solution.py:124
  137.2 6.1 %all-to-all-start.3 = ((bf16[16,80,2048]{2,1,0:T(8,128)(2,1)}), bf16[16,80,2048]{2,1,0:T(8,128)(2,1)}, u32[]{:S(2)}, u32[]{:S(2)}) async-start(bf16[16,80,2048]{2,1,0:T(8,128)(2,1)} %bitcast.122), calls=%async_computation.3 | async-start | bytes 10485760 | tf_op jit(solution)/shard_map/all_to_all | solution.py:127
  145.7 5.5 %scatter_custom_fusion.1 = s32[1281]{0:T(1024)S(1)} fusion(s32[1280]{0:T(1024)S(1)} %fusion.47, s32[1280]{0:T(1024)S(1)} %iota.44, s32[]{:T(128)} %constant.125.clone.1), kind=kCustom, calls=%fused_computation.109 | custom fusion | bytes 5128 | tf_op jit(solution)/shard_map/scatter | solution.py:140
  151.2 8.0 %gather_fusion.1 = bf16[1280]{0:T(1024)(128)(2,1)S(1)} fusion(bf16[1281]{0:T(1024)(128)(2,1)S(1)} %pad_maximum_fusion.1, s32[2048]{0:T(1024)S(1)} %pad_clamp_fusion.2), kind=kCustom, calls=%fused_computation.1 | custom fusion | bytes 10240 | tf_op jit(solution)/shard_map/gather | solution.py:145
  159.2 101.1 %all-to-all-done.3 = bf16[16,80,2048]{2,1,0:T(8,128)(2,1)} async-done(((bf16[16,80,2048]{2,1,0:T(8,128)(2,1)}), bf16[16,80,2048]{2,1,0:T(8,128)(2,1)}, u32[]{:S(2)}, u32[]{:S(2)}) %all-to-all-start.3) | async-done | bytes 5242912 | tf_op jit(solution)/shard_map/all_to_all | solution.py:127
  260.3 5.7 %concatenate.22 = bf16[1281,2048]{1,0:T(8,128)(2,1)} pad(bf16[1280,2048]{1,0:T(8,128)(2,1)} %bitcast.28, bf16[]{:T(256)} %constant.121.clone.1), padding=0_1x0_0 | pad | bytes 10489858 | tf_op jit(solution)/shard_map/concatenate | solution.py:142
  265.9 14.0 %gather_fusion.3 = bf16[1280,2048]{1,0:T(8,128)(2,1)} fusion(bf16[1281,2048]{1,0:T(8,128)(2,1)} %concatenate.22, s32[2048]{0:T(1024)S(1)} %pad_clamp_fusion.2), kind=kCustom, calls=%fused_computation.3 | custom fusion | bytes 10490880 | tf_op jit(solution)/shard_map/gather | solution.py:142
  279.9 7.2 %fusion.4 = f32[1280,768]{1,0:T(8,128)S(1)} fusion(bf16[1280,2048]{1,0:T(8,128)(2,1)} %gather_fusion.3, bf16[1,2048,768]{2,1,0:T(8,128)(2,1)} %param.21), kind=kOutput, calls=%fused_computation.15 | convolution fusion | flops 4026531840 | bytes 12320768 | tf_op jit(solution)/shard_map/while/body/dot_general | solution.py:155
  287.2 4.8 %fusion = bf16[1280,768]{1,0:T(8,128)(2,1)S(1)} fusion(bf16[1280,2048]{1,0:T(8,128)(2,1)S(1)} %copy-done.4, f32[1280,768]{1,0:T(8,128)S(1)} %fusion.4, bf16[1,2048,768]{2,1,0:T(8,128)(2,1)S(1)} %copy-done.11), kind=kOutput, calls=%fused_computation.11 | convolution fusion | flops 4032430080 | bytes 14286848 | tf_op jit(solution)/shard_map/while/body/dot_general | solution.py:156
  292.0 6.9 %fusion.1 = f32[1280,2048]{1,0:T(8,128)} fusion(bf16[1280,768]{1,0:T(8,128)(2,1)S(1)} %fusion, bf16[1,768,2048]{2,1,0:T(8,128)(2,1)S(1)} %copy-done), kind=kOutput, calls=%fused_computation.12 | convolution fusion | flops 4026531840 | bytes 15597568 | tf_op jit(solution)/shard_map/while/body/dot_general | solution.py:159
  302.0 7.2 %while.14 = (s32[]{:T(128)}, bf16[1280,2048]{1,0:T(8,128)(2,1)}, s32[]{:T(128)}, f32[1280]{0:T(1024)S(1)}, f32[1280,2048]{1,0:T(8,128)}, /*index=5*/s32[]{:T(128)}) while((s32[]{:T(128)}, bf16[1280,2048]{1,0:T(8,128)(2,1)}, s32[]{:T(128)}, f32[1280]{0:T(1024)S(1)}, f32[1280,2048]{1,0:T(8,128)}, /*index=5*/s32[]{:T(128)}) %tuple.40), condition=%wide.region_18.19_spmd, body=%wide.region_17.18_spmd.sunk | while | flops 5242882 | bytes 15733829 | solution.py:163
  302.0 7.0 %multiply_convert_fusion.3 = bf16[1280,2048]{1,0:T(8,128)(2,1)} fusion(f32[1280,2048]{1,0:T(8,128)} %get-tuple-element.220, f32[1280]{0:T(1024)S(1)} %get-tuple-element.219), kind=kLoop, calls=%fused_computation.8.clone.1 | loop fusion | flops 5242880 | bytes 15733760 | tf_op jit(solution)/shard_map/while/body/convert_element_type | solution.py:161
  309.2 5.7 %concatenate.23 = bf16[1281,2048]{1,0:T(8,128)(2,1)} pad(bf16[1280,2048]{1,0:T(8,128)(2,1)} %get-tuple-element.147, bf16[]{:T(256)} %constant.121.clone.1), padding=0_1x0_0 | pad | bytes 10489858 | tf_op jit(solution)/shard_map/concatenate | solution.py:164
  314.8 14.0 %gather_fusion.4 = bf16[1280,2048]{1,0:T(8,128)(2,1)} fusion(bf16[1281,2048]{1,0:T(8,128)(2,1)} %concatenate.23, s32[2048]{0:T(1024)S(1)} %pad_clamp_fusion), kind=kCustom, calls=%fused_computation.4 | custom fusion | bytes 10490880 | tf_op jit(solution)/shard_map/gather | solution.py:164
  328.8 4.6 all-to-all-start.4
  333.4 116.8 %all-to-all-done.4 = bf16[16,80,2048]{2,1,0:T(8,128)(2,1)} async-done(((bf16[16,80,2048]{2,1,0:T(8,128)(2,1)}), bf16[16,80,2048]{2,1,0:T(8,128)(2,1)}, u32[]{:S(2)}, u32[]{:S(2)}) %all-to-all-start.4) | async-done | bytes 5242912 | tf_op jit(solution)/shard_map/all_to_all | solution.py:167
  450.2 12.2 %gather_fusion.5 = bf16[1024,2048]{1,0:T(8,128)(2,1)} fusion(bf16[1280,2048]{1,0:T(8,128)(2,1)} %bitcast.33, s32[1024]{0:T(1024)S(1)} %broadcast_clamp_fusion), kind=kCustom, calls=%fused_computation.5 | custom fusion | bytes 8392704 | tf_op jit(solution)/shard_map/gather | solution.py:170
  462.4 5.1 %convert_reduce_fusion = f32[128,2048]{1,0:T(8,128)S(1)} fusion(bf16[1024,2048]{1,0:T(8,128)(2,1)} %gather_fusion.5), kind=kLoop, calls=%fused_computation.9 | loop fusion | flops 3932160 | bytes 5242880 | tf_op jit(solution)/shard_map/reduce_sum | solution.py:171
  (93 shorter events, 31.4 us)
Async XLA Ops:
  6.5 285.5 %copy-start = (bf16[1,768,2048]{2,1,0:T(8,128)(2,1)S(1)}, bf16[1,768,2048]{2,1,0:T(8,128)(2,1)}, u32[]{:S(2)}) copy-start(bf16[1,768,2048]{2,1,0:T(8,128)(2,1)} %param.23) | copy-start | bytes 9437188
  6.5 24.6 %copy-start.10 = (bf16[1,128,8]{1,2,0:T(8,128)(2,1)S(1)}, bf16[1,128,8]{1,2,0:T(8,128)(2,1)}, u32[]{:S(2)}) copy-start(bf16[1,128,8]{1,2,0:T(8,128)(2,1)} %param.20) | copy-start | bytes 6148
  6.5 24.8 %copy-start.8 = (s32[1,128,8]{1,2,0:T(8,128)S(1)}, s32[1,128,8]{1,2,0:T(8,128)}, u32[]{:S(2)}) copy-start(s32[1,128,8]{1,2,0:T(8,128)} %param.19) | copy-start | bytes 12292
  6.5 25.6 %copy-start.6 = (bf16[1,128,256]{2,1,0:T(8,128)(2,1)S(1)}, bf16[1,128,256]{2,1,0:T(8,128)(2,1)}, u32[]{:S(2)}) copy-start(bf16[1,128,256]{2,1,0:T(8,128)(2,1)} %param.14) | copy-start | bytes 196612
  6.5 44.2 %copy-start.7 = (bf16[1,128,256]{2,1,0:T(8,128)(2,1)S(1)}, bf16[1,128,256]{2,1,0:T(8,128)(2,1)}, u32[]{:S(2)}) copy-start(bf16[1,128,256]{2,1,0:T(8,128)(2,1)} %param.15) | copy-start | bytes 196612
  6.5 111.7 %all-gather.2.cloned.1.call-start = ((), (), s32[]{:S(2)}) async-start(), calls=%async_computation.5 | async-start | bytes 10485760 | tf_op jit(solution)/shard_map/all_gather | solution.py:98
  26.9 32.0 %all-to-all-start = ((bf16[4,2,32768]{2,1,0:T(2,128)(2,1)}), bf16[4,2,32768]{2,1,0:T(2,128)(2,1)}, u32[]{:S(2)}, u32[]{:S(2)}) async-start(bf16[4,2,32768]{2,1,0:T(2,128)(2,1)} %reshape.276), calls=%async_computation | async-start | bytes 1048576 | tf_op jit(solution)/shard_map/all_to_all | solution.py:74
  66.6 4.5 copy-start.5
  73.6 16.8 %copy-start.9 = (bf16[2048]{0:T(1024)(128)(2,1)S(1)}, bf16[2048]{0:T(1024)(128)(2,1)}, u32[]{:S(2)}) copy-start(bf16[2048]{0:T(1024)(128)(2,1)} %param.18) | copy-start | bytes 12292
  86.2 17.2 %all-to-all-start.1 = ((bf16[4,2,32768]{2,1,0:T(2,128)(2,1)}), bf16[4,2,32768]{2,1,0:T(2,128)(2,1)}, u32[]{:S(2)}, u32[]{:S(2)}) async-start(bf16[4,2,32768]{2,1,0:T(2,128)(2,1)} %reshape.278), calls=%async_computation.1 | async-start | bytes 1048576 | tf_op jit(solution)/shard_map/all_to_all | solution.py:95
  103.4 33.8 %all-to-all-start.2 = ((bf16[16,1,80]{2,1,0:T(2,128)(2,1)}), bf16[16,1,80]{2,1,0:T(2,128)(2,1)S(1)}, u32[]{:S(2)}, u32[]{:S(2)}) async-start(bf16[16,1,80]{2,1,0:T(2,128)(2,1)} %all_to_all.47), calls=%async_computation.2 | async-start | bytes 16384 | tf_op jit(solution)/shard_map/all_to_all | solution.py:128
  123.2 1.0 copy-start.2
  137.2 123.1 %all-to-all-start.3 = ((bf16[16,80,2048]{2,1,0:T(8,128)(2,1)}), bf16[16,80,2048]{2,1,0:T(8,128)(2,1)}, u32[]{:S(2)}, u32[]{:S(2)}) async-start(bf16[16,80,2048]{2,1,0:T(8,128)(2,1)} %bitcast.122), calls=%async_computation.3 | async-start | bytes 10485760 | tf_op jit(solution)/shard_map/all_to_all | solution.py:127
  279.9 7.3 %copy-start.4 = (bf16[1280,2048]{1,0:T(8,128)(2,1)S(1)}, bf16[1280,2048]{1,0:T(8,128)(2,1)}, u32[]{:S(2)}) copy-start(bf16[1280,2048]{1,0:T(8,128)(2,1)} %gather_fusion.3) | copy-start | bytes 15728644
  279.9 7.3 %copy-start.11 = (bf16[1,2048,768]{2,1,0:T(8,128)(2,1)S(1)}, bf16[1,2048,768]{2,1,0:T(8,128)(2,1)}, u32[]{:S(2)}) copy-start(bf16[1,2048,768]{2,1,0:T(8,128)(2,1)} %param.22) | copy-start | bytes 9437188
  328.8 121.4 %all-to-all-start.4 = ((bf16[16,80,2048]{2,1,0:T(8,128)(2,1)}), bf16[16,80,2048]{2,1,0:T(8,128)(2,1)}, u32[]{:S(2)}, u32[]{:S(2)}) async-start(bf16[16,80,2048]{2,1,0:T(8,128)(2,1)} %bitcast.123), calls=%async_computation.4 | async-start | bytes 10485760 | tf_op jit(solution)/shard_map/all_to_all | solution.py:167
  450.2 18.3 %copy-start.1 = (bf16[1,768,2048]{2,1,0:T(8,128)(2,1)S(1)}, bf16[1,768,2048]{2,1,0:T(8,128)(2,1)}, u32[]{:S(2)}) copy-start(bf16[1,768,2048]{2,1,0:T(8,128)(2,1)} %param.23) | copy-start | bytes 9437188
  462.4 5.1 %copy-start.3 = (f32[128,2048]{1,0:T(8,128)S(1)}, f32[128,2048]{1,0:T(8,128)}, u32[]{:S(2)}) copy-start(f32[128,2048]{1,0:T(8,128)} %copy-done.2) | copy-start | bytes 3145732
Sparse Core Ops, SparseCore 0:
  8.9 69.4 all-gather.1
where the time goes:
time: 482 us; the launch traced here: 476 us
  waiting for transfers between devices  219 us (45%)
  local copies, waits for them, and re-layouts  123 us (26%)
  other arithmetic  35.1 us (7%)
  matrix products  30.6 us (6%)
  blocking collectives  26.8 us (6%)
  starting transfers between devices  26.3 us (5%)
  between operations  14.7 us (3%)
    all_to_all x1, waiting for transfers between devices, per_device(): lax.all_to_all(returned, ('seq', 'sub'), split_axis=0, concat_axis=0, til...  117 us
    all_to_all x1, waiting for transfers between devices, per_device(): lax.all_to_all(send_rows, ('seq', 'sub'), split_axis=0, concat_axis=0, ti...  101 us
    unnamed x34, local copies, waits for them, and re-layouts  21.1 us
    unnamed x2, other arithmetic  18.9 us
    all_gather x1, blocking collectives, per_device(): lax.all_gather(key_rows, 'seq', axis=1, tiled=True)  18.6 us
    gather x1, local copies, waits for them, and re-layouts, per_device(): jnp.concatenate([results, jnp.zeros((1, D), jnp.bfloat16)], axis=0)[dest]  14 us
    gather x1, local copies, waits for them, and re-layouts, per_device(): jnp.concatenate([recv_rows.reshape(slots_in, D), jnp.zeros((1, D), jnp.bf...  14 us
    gather x1, local copies, waits for them, and re-layouts, per_device(): gathered = back[slot_of].reshape(tokens, topk, D).astype(jnp.float32)  12.2 us
  transfers between devices with their start and end apart: 6, of which 2 were waited for; matrix products, arithmetic and copies ran while one was open for 21% of the time, Pallas kernels for 0%

commit v1 on v0

--- a/solution.py
+++ b/solution.py
@@ -1,6 +1,8 @@
 import jax
 import jax.numpy as jnp
 from jax import lax
+from jax.experimental import pallas as pl
+from jax.experimental.pallas import tpu as pltpu
 from jax.sharding import PartitionSpec as P
 
 D = 2048
@@ -51,6 +53,74 @@
     earlier = jnp.cumsum(part_counts, axis=0) - part_counts
     ranks = jnp.sum((within + earlier[:, None, :]) * onehot.astype(jnp.float32), axis=2)
     return ranks.reshape(items).astype(jnp.int32)
+
+
+def experts_kernel(gate_ref, row_ref, w_gate_ref, w_up_ref, w_down_ref, out_ref, packed, *, cap):
+    gates = gate_ref[0]
+    blocks, tokens = gates.shape
+    named = gates > 0
+    before = (
+        lax.broadcasted_iota(jnp.int32, (tokens, tokens), 0)
+        < lax.broadcasted_iota(jnp.int32, (tokens, tokens), 1)
+    ).astype(jnp.bfloat16)
+    rank = jnp.dot(named.astype(jnp.bfloat16), before, preferred_element_type=jnp.float32)
+    slot = jnp.where(named, rank.astype(jnp.int32), -1)
+    slots = lax.broadcasted_iota(jnp.int32, (cap, tokens), 0)
+    picks = []
+    weights = []
+    for block in range(blocks):
+        chosen = slots == slot[block : block + 1, :]
+        pick = chosen.astype(jnp.bfloat16)
+        picks.append(pick)
+        weights.append(
+            jnp.sum(jnp.where(chosen, gates[block : block + 1, :], 0.0), axis=1, keepdims=True)
+        )
+        packed[block * cap : (block + 1) * cap, :] = jnp.dot(
+            pick,
+            row_ref[block * tokens : (block + 1) * tokens, :],
+            preferred_element_type=jnp.float32,
+        ).astype(jnp.bfloat16)
+    rows = packed[...]
+    gate_proj = jnp.dot(rows, w_gate_ref[...], preferred_element_type=jnp.float32)
+    up_proj = jnp.dot(rows, w_up_ref[...], preferred_element_type=jnp.float32)
+    inner = (gate_proj / (1.0 + jnp.exp(-gate_proj)) * up_proj).astype(jnp.bfloat16)
+    result = jnp.dot(inner, w_down_ref[...], preferred_element_type=jnp.float32)
+    for block in range(blocks):
+        part = (result[block * cap : (block + 1) * cap] * weights[block]).astype(jnp.bfloat16)
+        out_ref[block * tokens : (block + 1) * tokens, :] = lax.dot_general(
+            picks[block],
+            part,
+            (((0,), (0,)), ((), ())),
+            preferred_element_type=jnp.float32,
+        ).astype(jnp.bfloat16)
+
+
+def experts_on_rows(gates, rows, w_gate, w_up, w_down, cap, blocks):
+    parts, tokens = gates.shape
+    width = rows.shape[1]
+    hidden_units = w_gate.shape[1]
+    steps = parts // blocks
+    fixed = lambda step: (0, 0)
+    return pl.pallas_call(
+        lambda *refs: experts_kernel(*refs, cap=cap),
+        grid=(steps,),
+        in_specs=[
+            pl.BlockSpec((1, blocks, tokens), lambda step: (step, 0, 0)),
+            pl.BlockSpec((blocks * tokens, width), lambda step: (step, 0)),
+            pl.BlockSpec((width, hidden_units), fixed),
+            pl.BlockSpec((width, hidden_units), fixed),
+            pl.BlockSpec((hidden_units, width), fixed),
+        ],
+        out_specs=pl.BlockSpec((blocks * tokens, width), lambda step: (step, 0)),
+        out_shape=jax.ShapeDtypeStruct(rows.shape, jnp.bfloat16),
+        scratch_shapes=[pltpu.VMEM((blocks * cap, width), jnp.bfloat16)],
+        compiler_params=pltpu.CompilerParams(vmem_limit_bytes=56 * 1024 * 1024),
+        cost_estimate=pl.CostEstimate(
+            flops=6 * parts * cap * width * hidden_units,
+            bytes_accessed=4 * rows.size + 6 * width * hidden_units,
+            transcendentals=parts * cap * hidden_units,
+        ),
+    )(gates.reshape(steps, blocks, tokens), rows, w_gate, w_up, w_down)
 
 
 def per_device(
@@ -108,6 +178,23 @@
     topk = expert_ids.shape[2]
     experts = n_seq * n_sub
     cap = max(2, (5 * tokens * topk + 4 * experts - 1) // (4 * experts))
+    if experts <= 2 * topk:
+        axes = ("seq", "sub")
+        table = jnp.sum(
+            jnp.where(
+                expert_ids[0][None] == jnp.arange(experts, dtype=jnp.int32)[:, None, None],
+                gate_weights[0].astype(jnp.float32)[None],
+                0.0,
+            ),
+            axis=2,
+        ).astype(jnp.bfloat16)
+        tables = lax.all_gather(table, axes, axis=0, tiled=False)
+        mine = lax.axis_index("seq") * n_sub + lax.axis_index("sub")
+        gates = lax.dynamic_index_in_dim(tables, mine, 1, keepdims=False).astype(jnp.float32)
+        rows = lax.all_gather(normed, axes, axis=0, tiled=True)
+        parts = experts_on_rows(gates, rows, expert_gate[0], expert_up[0], expert_down[0], cap, 4)
+        mixture = lax.psum_scatter(parts, axes, scatter_dimension=0, tiled=True)
+        return (wide + mixture.astype(jnp.float32)).astype(jnp.bfloat16)[None]
     flat_ids = expert_ids[0].reshape(-1)
     items = flat_ids.shape[0]
     ranks = rank_in_expert(flat_ids, experts)

time: 482 us -> 300 us (0.62); the launches traced: 476 us -> 300 us
  local copies, waits for them, and re-layouts: 123 us -> 7.55 us
  waiting for transfers between devices: 219 us -> 162 us
  blocking collectives: 26.8 us -> 59.5 us
  matrix products: 30.6 us -> 7.4 us
  Pallas kernels: 0 us -> 22.8 us
  starting transfers between devices: 26.3 us -> 7.79 us
  other arithmetic: 35.1 us -> 19.6 us
    all_to_all x3 -> x0, waiting for transfers between devices: 218 us -> none  [the longest x1 117 us: per_device(): lax.all_to_all(returned, ('seq', 'sub'), split_axis=0, concat_axis=0, til...]
    reduce_scatter x0 -> x1, waiting for transfers between devices: none -> 103 us  [per_device(): mixture = lax.psum_scatter(parts, axes, scatter_dimension=0, tiled=True)]
    gather x6 -> x0, local copies, waits for them, and re-layouts: 68.1 us -> none  [the longest x1 14 us: per_device(): jnp.concatenate([results, jnp.zeros((1, D), jnp.bfloat16)], axis=0)[dest]]
    all_gather x0 -> x1, waiting for transfers between devices: none -> 42.2 us  [per_device(): rows = lax.all_gather(normed, axes, axis=0, tiled=True)]
    all_gather x0 -> x1, blocking collectives: none -> 32.9 us  [per_device(): tables = lax.all_gather(table, axes, axis=0, tiled=False)]
    pallas_call x0 -> x1, Pallas kernels: none -> 22.8 us  [experts_on_rows(): pl.pallas_call(lambda *refs: experts_kernel(*refs, cap=cap), grid=(steps,...]
    dot_general x4 -> x0, matrix products: 19.1 us -> none  [the longest x1 7.24 us: expert_block(): jnp.dot(compact_rows, w_gate, preferred_element_type=jnp.float32)]
    all_to_all x3 -> x0, starting transfers between devices: 17.8 us -> none  [the longest x1 7.13 us: per_device(): lax.all_to_all(send_gates, ('seq', 'sub'), split_axis=0, concat_axis=0, t...]
  transfers between devices with their start and end apart: 6 -> 5, of which waited for: 2 -> 4; matrix products, arithmetic and copies ran while one was open for 21% -> 9% of each run, Pallas kernels for 0% -> 0%
where the time goes in v1:
time: 300 us
  waiting for transfers between devices  162 us (54%)
  blocking collectives  59.5 us (20%)
  Pallas kernels  22.8 us (8%)
  other arithmetic  19.6 us (7%)
  between operations  13.3 us (4%)
  starting transfers between devices  7.79 us (3%)
  local copies, waits for them, and re-layouts  7.55 us (3%)
  matrix products  7.4 us (2%)
    reduce_scatter x1, waiting for transfers between devices, per_device(): mixture = lax.psum_scatter(parts, axes, scatter_dimension=0, tiled=True)  103 us
    all_gather x1, waiting for transfers between devices, per_device(): rows = lax.all_gather(normed, axes, axis=0, tiled=True)  42.2 us
    all_gather x1, blocking collectives, per_device(): tables = lax.all_gather(table, axes, axis=0, tiled=False)  32.9 us
    pallas_call x1, Pallas kernels, experts_on_rows(): pl.pallas_call(lambda *refs: experts_kernel(*refs, cap=cap), grid=(steps,...  22.8 us
    all_gather x1, blocking collectives, per_device(): lax.all_gather(key_rows, 'seq', axis=1, tiled=True)  18.5 us
    unnamed x2, other arithmetic  15.2 us
    all_to_all x1, waiting for transfers between devices, per_device(): lax.all_to_all(head_block, 'seq', split_axis=1, concat_axis=2, tiled=True)  14.7 us
    all_gather x1, blocking collectives, per_device(): lax.all_gather(value_rows, 'seq', axis=1, tiled=True)  8.02 us
  transfers between devices with their start and end apart: 5, of which 4 were waited for; matrix products, arithmetic and copies ran while one was open for 9% of the time, Pallas kernels for 0%

profile of v1, /device:TPU:0, one launch (start us, length us, event | category | flops | bytes accessed | tf_op | source)
XLA Modules:
  0.0 300.0 jit_solution(6848261177519090218)
XLA Ops:
  6.5 0.7 all-gather.4.cloned.1.call-update
  7.3 2.4 copy.33
  9.6 0.5 broadcast.37
  10.1 11.4 %reduce = bf16[2048,128]{1,0:T(8,128)(2,1)S(1)} reduce(bf16[2048,1,128]{2,1,0:T(2,128)(2,1)S(1)} %bitcast.100, bf16[]{:T(256)} %broadcast.37), dimensions={1}, to_apply=%bitcast.76.reduce_sub_computation | reduce | bytes 1048578
  21.6 0.9 reshape.44
  22.5 4.2 %all-to-all-start = ((bf16[4,2,32768]{2,1,0:T(2,128)(2,1)}), bf16[4,2,32768]{2,1,0:T(2,128)(2,1)S(1)}, u32[]{:S(2)}, u32[]{:S(2)}) async-start(bf16[4,2,32768]{2,1,0:T(2,128)(2,1)} %reshape.44), calls=%async_computation | async-start | bytes 1048576 | tf_op jit(solution)/shard_map/all_to_all | solution.py:144
  26.7 18.5 %all_gather.16 = bf16[1,512,256]{2,1,0:T(8,128)(2,1)S(1)} all-gather(bf16[1,128,256]{2,1,0:T(8,128)(2,1)} %param.12), channel_id=1, replica_groups=mesh['grp'=2,'seq'=4,'sub'=4] {'seq'}, dimensions={1}, use_global_device_ids=true | all-gather | bytes 327680 | tf_op jit(solution)/shard_map/all_gather | solution.py:146
  45.3 8.0 %all_gather.17 = bf16[1,512,256]{2,1,0:T(8,128)(2,1)S(1)} all-gather(bf16[1,128,256]{2,1,0:T(8,128)(2,1)} %param.13), channel_id=1, replica_groups=mesh['grp'=2,'seq'=4,'sub'=4] {'seq'}, dimensions={1}, use_global_device_ids=true | all-gather | bytes 327680 | tf_op jit(solution)/shard_map/all_gather | solution.py:147
  53.3 0.5 reshape.45
  54.1 0.3 fusion.39
  54.6 0.3 fusion.40
  55.1 0.3 fusion.41
  55.6 0.3 fusion.42
  56.2 0.3 convolution_convert_fusion
  56.5 0.3 convolution_convert_fusion.1
  56.9 0.3 convolution_convert_fusion.2
  57.2 0.3 convolution_convert_fusion.3
  57.6 0.9 copy.35
  58.5 3.7 %reduce.1 = bf16[512,512]{1,0:T(8,128)(2,1)S(1)} reduce(bf16[512,1,512]{2,1,0:T(2,128)(2,1)S(1)} %bitcast.101, bf16[]{:T(256)} %broadcast.37), dimensions={1}, to_apply=%bitcast.78.reduce_sub_computation | reduce | bytes 1048578
  62.3 1.2 reshape.46
  63.5 3.5 %all-to-all-start.1 = ((bf16[4,2,32768]{2,1,0:T(2,128)(2,1)}), bf16[4,2,32768]{2,1,0:T(2,128)(2,1)S(1)}, u32[]{:S(2)}, u32[]{:S(2)}) async-start(bf16[4,2,32768]{2,1,0:T(2,128)(2,1)} %reshape.46), calls=%async_computation.1 | async-start | bytes 1048576 | tf_op jit(solution)/shard_map/all_to_all | solution.py:165
  67.0 14.7 %all-to-all-done.1 = bf16[4,2,32768]{2,1,0:T(2,128)(2,1)S(1)} async-done(((bf16[4,2,32768]{2,1,0:T(2,128)(2,1)}), bf16[4,2,32768]{2,1,0:T(2,128)(2,1)S(1)}, u32[]{:S(2)}, u32[]{:S(2)}) %all-to-all-start.1) | async-done | bytes 524320 | tf_op jit(solution)/shard_map/all_to_all | solution.py:165
  81.7 0.5 reshape.47
  82.6 1.4 all-gather.4.cloned.1.call-done
  84.0 4.8 %multiply_reduce_fusion = (f32[128]{0:T(128)S(1)}, f32[128,2048]{1,0:T(8,128)S(1)}) fusion(bf16[128,2048]{0,1:T(8,128)(2,1)S(1)} %bitcast.102, bf16[2048,2048]{1,0:T(8,128)(2,1)} %all-gather.4.cloned.1.call-done, bf16[1,128,2048]{2,1,0:T(8,128)(2,1)S(1)} %copy-done), kind=kOutput, calls=%fused_computation.21 | convolution fusion | flops 1075314560 | bytes 10486272 | tf_op jit(solution)/shard_map/dot_general | solution.py:166
  88.8 1.0 multiply_convert_fusion
  89.9 32.9 %all-gather = bf16[256,128]{1,0:T(8,128)(2,1)S(1)} all-gather(bf16[16,128]{1,0:T(8,128)(2,1)S(1)} %select_reduce_fusion), channel_id=2, replica_groups=mesh['grp'=2,'seq'=4,'sub'=4] {'seq','sub'}, dimensions={0}, use_global_device_ids=true | all-gather | bytes 69632 | tf_op jit(solution)/shard_map/all_gather | solution.py:191
  122.8 0.6 dynamic-slice_convert_fusion
  123.4 42.2 %all-gather.6.cloned.1.call-done.refs_1_ = bf16[2048,2048]{1,0:T(8,128)(2,1)} async-done(((bf16[128,2048]{1,0:T(8,128)(2,1)}), bf16[2048,2048]{1,0:T(8,128)(2,1)}) %all-gather.6.cloned.1.call-update) | async-done | bytes 8388624 | tf_op jit(solution)/shard_map/all_gather | solution.py:194
  165.7 22.8 %shard_map.109 = bf16[2048,2048]{1,0:T(8,128)(2,1)} custom-call(f32[4,4,128]{2,1,0:T(4,128)} %bitcast.110, bf16[2048,2048]{1,0:T(8,128)(2,1)} %all-gather.6.cloned.1.call-done.refs_1_, bf16[2048,768]{1,0:T(8,128)(2,1)} %bitcast.112, bf16[2048,768]{1,0:T(8,128)(2,1)} %bitcast.113, bf16[768,2048]{1,0:T(8,128)(2,1)} %bitcast.114), custom_call_target="tpu_custom_call" | custom-call | flops 12079595520 | bytes 26214400 | tf_op jit(solution)/shard_map/pallas_call | solution.py:104
  188.5 103.0 %reduce-scatter.2.cloned.1.call-done = bf16[128,2048]{1,0:T(8,128)(2,1)} async-done(((bf16[2048,2048]{1,0:T(8,128)(2,1)}), bf16[128,2048]{1,0:T(8,128)(2,1)}) %reduce-scatter.2.cloned.1.call-update) | async-done | bytes 524304 | tf_op jit(solution)/shard_map/reduce_scatter | solution.py:196
  291.5 1.9 fusion.14
  (27 shorter events, 1.7 us)
Async XLA Ops:
  6.5 77.4 %all-gather.4.cloned.1.call-start = ((), (), s32[]{:S(2)}) async-start(), calls=%async_computation.3 | async-start | bytes 10485760 | tf_op jit(solution)/shard_map/all_gather | solution.py:168
  22.5 30.8 %all-to-all-start = ((bf16[4,2,32768]{2,1,0:T(2,128)(2,1)}), bf16[4,2,32768]{2,1,0:T(2,128)(2,1)S(1)}, u32[]{:S(2)}, u32[]{:S(2)}) async-start(bf16[4,2,32768]{2,1,0:T(2,128)(2,1)} %reshape.44), calls=%async_computation | async-start | bytes 1048576 | tf_op jit(solution)/shard_map/all_to_all | solution.py:144
  56.9 10.1 %copy-start.1 = (bf16[2048]{0:T(1024)(128)(2,1)S(1)}, bf16[2048]{0:T(1024)(128)(2,1)}, u32[]{:S(2)}) copy-start(bf16[2048]{0:T(1024)(128)(2,1)} %param.16) | copy-start | bytes 12292
  57.2 26.8 %copy-start = (bf16[1,128,2048]{2,1,0:T(8,128)(2,1)S(1)}, bf16[1,128,2048]{2,1,0:T(8,128)(2,1)}, u32[]{:S(2)}) copy-start(bf16[1,128,2048]{2,1,0:T(8,128)(2,1)} %param.14) | copy-start | bytes 1572868
  63.5 18.2 %all-to-all-start.1 = ((bf16[4,2,32768]{2,1,0:T(2,128)(2,1)}), bf16[4,2,32768]{2,1,0:T(2,128)(2,1)S(1)}, u32[]{:S(2)}, u32[]{:S(2)}) async-start(bf16[4,2,32768]{2,1,0:T(2,128)(2,1)} %reshape.46), calls=%async_computation.1 | async-start | bytes 1048576 | tf_op jit(solution)/shard_map/all_to_all | solution.py:165
  66.9 98.7 %all-gather.6.cloned.1.call-start = ((), (), s32[]{:S(2)}) async-start(), calls=%async_computation.4 | async-start | bytes 8912896 | tf_op jit(solution)/shard_map/all_gather | solution.py:194
  84.0 5.8 %copy-start.3 = (bf16[1,128,8]{1,2,0:T(8,128)(2,1)S(1)}, bf16[1,128,8]{1,2,0:T(8,128)(2,1)}, u32[]{:S(2)}) copy-start(bf16[1,128,8]{1,2,0:T(8,128)(2,1)} %param.18) | copy-start | bytes 6148
  84.0 5.8 %copy-start.2 = (s32[1,128,8]{1,2,0:T(8,128)S(1)}, s32[1,128,8]{1,2,0:T(8,128)}, u32[]{:S(2)}) copy-start(s32[1,128,8]{1,2,0:T(8,128)} %param.17) | copy-start | bytes 12292
  89.8 201.7 %reduce-scatter.2.cloned.1.call-start = ((), (), s32[]{:S(2)}) async-start(), calls=%async_computation.5 | async-start | bytes 8912896 | tf_op jit(solution)/shard_map/reduce_scatter | solution.py:196
Sparse Core Ops, SparseCore 0:
  8.9 75.0 all-gather.3
  89.9 75.7 all-gather.5
  188.6 102.8 reduce-scatter.1

commit v2 on v0

--- a/solution.py
+++ b/solution.py
@@ -1,6 +1,10 @@
+import functools
+
 import jax
 import jax.numpy as jnp
 from jax import lax
+from jax.experimental import pallas as pl
+from jax.experimental.pallas import tpu as pltpu
 from jax.sharding import PartitionSpec as P
 
 D = 2048
@@ -51,6 +55,306 @@
     earlier = jnp.cumsum(part_counts, axis=0) - part_counts
     ranks = jnp.sum((within + earlier[:, None, :]) * onehot.astype(jnp.float32), axis=2)
     return ranks.reshape(items).astype(jnp.int32)
+
+
+def attend_kernel(place_ref, query_ref, *refs, scale):
+    kv_refs, (w_own_ref, w_other_ref, out_ref, keys, values, heads) = refs[:4], refs[4:]
+    rows = keys.shape[0] // 4
+    head_size = keys.shape[1]
+    core = place_ref[0]
+    query_start = pl.multiple_of(place_ref[1], head_size)
+    row_pos = place_ref[2] * rows + lax.broadcasted_iota(jnp.int32, (rows, 1), 0)
+    lane = lax.broadcasted_iota(jnp.int32, (1, rows), 1)
+    col_pos = jnp.concatenate([place_ref[3 + part] * rows + lane for part in range(4)], axis=1)
+    allowed = row_pos >= col_pos
+    for part, kv_ref in enumerate(kv_refs):
+        start = kv_ref.shape[1] - 2 * head_size
+        keys[part * rows : (part + 1) * rows, :] = kv_ref[:, start : start + head_size]
+        values[part * rows : (part + 1) * rows, :] = kv_ref[:, start + head_size :]
+    key_block = keys[...]
+    value_block = values[...]
+    for head in range(heads.shape[1] // head_size):
+        query = query_ref[:, pl.ds(query_start + head * head_size, head_size)]
+        scores = (
+            lax.dot_general(
+                query, key_block, (((1,), (1,)), ((), ())), preferred_element_type=jnp.float32
+            )
+            * scale
+        )
+        scores = jnp.where(allowed, scores, -1e30)
+        weights = jnp.exp(scores - jnp.max(scores, axis=1, keepdims=True))
+        probs = (weights / jnp.sum(weights, axis=1, keepdims=True)).astype(jnp.bfloat16)
+        heads[:, head * head_size : (head + 1) * head_size] = jnp.dot(
+            probs, value_block, preferred_element_type=jnp.float32
+        ).astype(jnp.bfloat16)
+    half = heads.shape[1] // 2
+    own = heads[:, pl.ds(pl.multiple_of(core * half, half), half)]
+    other = heads[:, pl.ds(pl.multiple_of((1 - core) * half, half), half)]
+    out_ref[...] = (
+        jnp.dot(own, w_own_ref[...], preferred_element_type=jnp.float32)
+        + jnp.dot(other, w_other_ref[...], preferred_element_type=jnp.float32)
+    ).astype(out_ref.dtype)
+
+
+def attend(place, queries, kv_parts, w_own, w_other, dtype):
+    tokens = queries.shape[0]
+    width = w_own.shape[1]
+    chip_width = 2 * w_own.shape[0]
+    return pl.pallas_call(
+        functools.partial(attend_kernel, scale=1.0 / HD**0.5),
+        in_specs=[pl.BlockSpec(memory_space=pltpu.SMEM)]
+        + [pl.BlockSpec(memory_space=pltpu.VMEM)] * 7,
+        out_specs=pl.BlockSpec(memory_space=pltpu.VMEM),
+        out_shape=jax.ShapeDtypeStruct((tokens, width), dtype),
+        scratch_shapes=[
+            pltpu.VMEM((4 * tokens, HD), jnp.bfloat16),
+            pltpu.VMEM((4 * tokens, HD), jnp.bfloat16),
+            pltpu.VMEM((tokens, chip_width), jnp.bfloat16),
+        ],
+        compiler_params=pltpu.CompilerParams(vmem_limit_bytes=32 * 1024 * 1024),
+        cost_estimate=pl.CostEstimate(
+            flops=16 * tokens * tokens * chip_width + 2 * tokens * chip_width * width,
+            bytes_accessed=4 * w_own.size + 4 * tokens * width,
+            transcendentals=4 * tokens * tokens * chip_width // HD,
+        ),
+    )(place, queries, *kv_parts, w_own, w_other)
+
+
+def norm_kernel(residual_ref, own_ref, other_ref, gain_ref, hidden_ref, normed_ref):
+    hidden = (
+        residual_ref[...].astype(jnp.float32) + own_ref[...] + other_ref[...].astype(jnp.float32)
+    ).astype(jnp.bfloat16)
+    hidden_ref[...] = hidden
+    wide = hidden.astype(jnp.float32)
+    normed_ref[...] = (
+        wide
+        * lax.rsqrt(jnp.mean(wide * wide, axis=1, keepdims=True) + 1e-06)
+        * gain_ref[...].astype(jnp.float32)
+    ).astype(jnp.bfloat16)
+
+
+def add_and_norm(residual, own, other, gain):
+    return pl.pallas_call(
+        norm_kernel,
+        in_specs=[pl.BlockSpec(memory_space=pltpu.VMEM)] * 4,
+        out_specs=[pl.BlockSpec(memory_space=pltpu.VMEM)] * 2,
+        out_shape=[jax.ShapeDtypeStruct(residual.shape, jnp.bfloat16)] * 2,
+        compiler_params=pltpu.CompilerParams(vmem_limit_bytes=32 * 1024 * 1024),
+    )(residual, own, other, gain)
+
+
+def experts_kernel(gate_ref, *refs, cap):
+    row_refs, refs = refs[:4], refs[4:]
+    w_gate_ref, w_up_ref, w_down_ref, own_ref, across_ref, other_ref, packed, total = refs
+    tokens = row_refs[0].shape[0]
+    step = pl.program_id(0)
+    gates = gate_ref[...]
+    named = gates > 0
+    before = (
+        lax.broadcasted_iota(jnp.int32, (tokens, tokens), 0)
+        < lax.broadcasted_iota(jnp.int32, (tokens, tokens), 1)
+    ).astype(jnp.bfloat16)
+    rank = jnp.dot(named.astype(jnp.bfloat16), before, preferred_element_type=jnp.float32)
+    slot = jnp.where(named, rank.astype(jnp.int32), -1)
+    slots = lax.broadcasted_iota(jnp.int32, (cap, tokens), 0)
+
+    def chosen_of(block):
+        return slots == slot[block : block + 1, :]
+
+    @pl.when(step == 0)
+    def _():
+        for block in range(4):
+            packed[block * cap : (block + 1) * cap, :] = jnp.dot(
+                chosen_of(block).astype(jnp.bfloat16),
+                row_refs[block][...],
+                preferred_element_type=jnp.float32,
+            ).astype(jnp.bfloat16)
+
+    rows = packed[...]
+    gate_proj = jnp.dot(rows, w_gate_ref[...], preferred_element_type=jnp.float32)
+    up_proj = jnp.dot(rows, w_up_ref[...], preferred_element_type=jnp.float32)
+    inner = (gate_proj / (1.0 + jnp.exp(-gate_proj)) * up_proj).astype(jnp.bfloat16)
+    result = jnp.dot(inner, w_down_ref[...], preferred_element_type=jnp.float32)
+
+    @pl.when(step == 0)
+    def _():
+        total[...] = result
+
+    @pl.when(step > 0)
+    def _():
+        total[...] += result
+
+    @pl.when(step == pl.num_programs(0) - 1)
+    def _():
+        targets = (
+            own_ref.at[...],
+            other_ref.at[0:tokens],
+            across_ref.at[...],
+            other_ref.at[tokens : 2 * tokens],
+        )
+        for block in range(4):
+            chosen = chosen_of(block)
+            weights = jnp.sum(
+                jnp.where(chosen, gates[block : block + 1, :], 0.0), axis=1, keepdims=True
+            )
+            part = (total[block * cap : (block + 1) * cap, :] * weights).astype(jnp.bfloat16)
+            targets[block][...] = lax.dot_general(
+                chosen.astype(jnp.bfloat16),
+                part,
+                (((0,), (0,)), ((), ())),
+                preferred_element_type=jnp.float32,
+            ).astype(jnp.bfloat16)
+
+
+def experts_on_rows(gates, row_blocks, w_gate, w_up, w_down, cap):
+    tokens, width = row_blocks[0].shape
+    hidden_units = w_gate.shape[1]
+    chunk = hidden_units // 3 if hidden_units % 384 == 0 else hidden_units
+    whole = pl.BlockSpec((tokens, width), lambda step: (0, 0))
+    return pl.pallas_call(
+        functools.partial(experts_kernel, cap=cap),
+        grid=(hidden_units // chunk,),
+        in_specs=[
+            pl.BlockSpec((4, tokens), lambda step: (0, 0)),
+            whole,
+            whole,
+            whole,
+            whole,
+            pl.BlockSpec((width, chunk), lambda step: (0, step)),
+            pl.BlockSpec((width, chunk), lambda step: (0, step)),
+            pl.BlockSpec((chunk, width), lambda step: (step, 0)),
+        ],
+        out_specs=[whole, whole, pl.BlockSpec((2 * tokens, width), lambda step: (0, 0))],
+        out_shape=[
+            jax.ShapeDtypeStruct((tokens, width), jnp.bfloat16),
+            jax.ShapeDtypeStruct((tokens, width), jnp.bfloat16),
+            jax.ShapeDtypeStruct((2 * tokens, width), jnp.bfloat16),
+        ],
+        scratch_shapes=[
+            pltpu.VMEM((4 * cap, width), jnp.bfloat16),
+            pltpu.VMEM((4 * cap, width), jnp.float32),
+        ],
+        compiler_params=pltpu.CompilerParams(vmem_limit_bytes=40 * 1024 * 1024),
+        cost_estimate=pl.CostEstimate(
+            flops=24 * cap * width * hidden_units,
+            bytes_accessed=16 * tokens * width + 6 * width * hidden_units,
+            transcendentals=4 * cap * hidden_units,
+        ),
+    )(gates, *row_blocks, w_gate, w_up, w_down)
+
+
+def gathered_plan(
+    query_rows,
+    key_rows,
+    value_rows,
+    residual_in,
+    out_proj,
+    norm_gain,
+    expert_ids,
+    gate_weights,
+    expert_gate,
+    expert_up,
+    expert_down,
+    cap,
+):
+    n_seq = lax.axis_size("seq")
+    n_sub = lax.axis_size("sub")
+    experts = n_seq * n_sub
+    place = lax.axis_index("seq")
+    core = place % 2
+    chip = place // 2
+    twin = [(index, index ^ 1) for index in range(n_seq)]
+    across = [(index, (index + 2) % n_seq) for index in range(n_seq)]
+    diagonal = [(index, (index ^ 1) ^ 2) for index in range(n_seq)]
+    order = [0] + list(range(1, n_sub, 2)) + list(reversed(range(2, n_sub, 2)))
+
+    def ring(steps):
+        return [(order[at], order[(at + steps) % n_sub]) for at in range(n_sub)]
+
+    queries = query_rows[0]
+    chip_width = queries.shape[1] // 2
+
+    def kv_of(head):
+        start = head * HD
+        return jnp.concatenate(
+            [
+                lax.dynamic_slice_in_dim(key_rows[0], start, HD, 1),
+                lax.dynamic_slice_in_dim(value_rows[0], start, HD, 1),
+            ],
+            axis=1,
+        )
+
+    kv_here = kv_of(chip)
+    kv_away = kv_of(1 - chip)
+    outgoing = jnp.concatenate(
+        [lax.dynamic_slice_in_dim(queries, (1 - chip) * chip_width, chip_width, 1), kv_away], axis=1
+    )
+    incoming = lax.ppermute(outgoing, "seq", across)
+    kv_twin = lax.ppermute(kv_here, "seq", twin)
+    kv_diagonal = lax.ppermute(kv_away, "seq", diagonal)
+    w_other = lax.ppermute(out_proj, "seq", twin)
+
+    table = jnp.sum(
+        jnp.where(
+            expert_ids[0][None] == jnp.arange(experts, dtype=jnp.int32)[:, None, None],
+            gate_weights[0].astype(jnp.float32)[None],
+            0.0,
+        ),
+        axis=2,
+    ).astype(jnp.bfloat16)
+    quad = jnp.stack(
+        [
+            table,
+            lax.ppermute(table, "seq", twin),
+            lax.ppermute(table, "seq", across),
+            lax.ppermute(table, "seq", diagonal),
+        ]
+    )
+    quads = [quad] + [lax.ppermute(quad, "sub", ring(steps)) for steps in range(1, n_sub)]
+    mine = place * n_sub + lax.axis_index("sub")
+    gates = lax.dynamic_index_in_dim(jnp.stack(quads), mine, 2, keepdims=False).astype(jnp.float32)
+
+    kv_parts = (kv_here, kv_twin, incoming, kv_diagonal)
+    columns = [place, place ^ 1, place ^ 2, place ^ 3]
+
+    def place_of(query_start, row_block):
+        return jnp.stack([core, query_start, row_block] + columns).astype(jnp.int32)
+
+    sent = attend(place_of(0 * place, place ^ 2), incoming, kv_parts, out_proj, w_other, jnp.bfloat16)
+    projected_across = lax.ppermute(sent, "seq", across)
+    projected = attend(
+        place_of(chip * chip_width, place), queries, kv_parts, out_proj, w_other, jnp.float32
+    )
+    hidden, normed = add_and_norm(residual_in[0], projected, projected_across, norm_gain[None])
+
+    rows = normed
+    sums = []
+    for step in range(n_sub):
+        rows_twin = lax.ppermute(rows, "seq", twin)
+        rows_across = lax.ppermute(rows, "seq", across)
+        rows_diagonal = lax.ppermute(rows_across, "seq", twin)
+        blocks = (rows, rows_twin, rows_across, rows_diagonal)
+        if step < n_sub - 1:
+            rows = lax.ppermute(rows, "sub", ring(1))
+        sums.append(
+            experts_on_rows(gates[step], blocks, expert_gate[0], expert_up[0], expert_down[0], cap)
+        )
+    tokens = queries.shape[0]
+    carried = None
+    for step in list(range(1, n_sub)) + [0]:
+        own, away, other = sums[step]
+        met = lax.ppermute(other, "seq", twin).astype(jnp.float32)
+        away = (away.astype(jnp.float32) + met[tokens:]).astype(jnp.bfloat16)
+        part = (
+            own.astype(jnp.float32)
+            + met[:tokens]
+            + lax.ppermute(away, "seq", across).astype(jnp.float32)
+        )
+        if carried is not None:
+            part = part + carried.astype(jnp.float32)
+        if step:
+            carried = lax.ppermute(part.astype(jnp.bfloat16), "sub", ring(1))
+    return (hidden.astype(jnp.float32) + part).astype(jnp.bfloat16)[None]
 
 
 def per_device(
@@ -69,6 +373,24 @@
     tokens = query_rows.shape[1]
     n_seq = lax.axis_size("seq")
     n_sub = lax.axis_size("sub")
+    experts = n_seq * n_sub
+    topk = expert_ids.shape[2]
+    cap = max(2, (5 * tokens * topk + 4 * experts - 1) // (4 * experts))
+    if n_seq == 2 * KVH and KVH == 2 and experts <= 2 * topk and cap % 16 == 0:
+        return gathered_plan(
+            query_rows,
+            key_rows,
+            value_rows,
+            residual_in,
+            out_proj,
+            norm_gain,
+            expert_ids,
+            gate_weights,
+            expert_gate,
+            expert_up,
+            expert_down,
+            cap,
+        )
     heads_here = QH // n_seq
     group = QH // KVH
     query_local = lax.all_to_all(query_rows, "seq", split_axis=2, concat_axis=1, tiled=True)
@@ -105,9 +427,6 @@
         * lax.rsqrt(jnp.mean(wide * wide, axis=1, keepdims=True) + 1e-06)
         * norm_gain.astype(jnp.float32)
     ).astype(jnp.bfloat16)
-    topk = expert_ids.shape[2]
-    experts = n_seq * n_sub
-    cap = max(2, (5 * tokens * topk + 4 * experts - 1) // (4 * experts))
     flat_ids = expert_ids[0].reshape(-1)
     items = flat_ids.shape[0]
     ranks = rank_in_expert(flat_ids, experts)

time: 482 us -> 188 us (0.39); the launches traced: 476 us -> 188 us
  waiting for transfers between devices: 219 us -> 97.4 us
  local copies, waits for them, and re-layouts: 123 us -> 14.9 us
  Pallas kernels: 0 us -> 39.4 us
  other arithmetic: 35.1 us -> 4.36 us
  matrix products: 30.6 us -> 0 us
  blocking collectives: 26.8 us -> 0 us
  between operations: 14.7 us -> 0.4 us
    all_to_all x5 -> x0, waiting for transfers between devices: 218 us -> none  [the longest x1 117 us: per_device(): lax.all_to_all(returned, ('seq', 'sub'), split_axis=0, concat_axis=0, til...]
    ppermute x0 -> x37, waiting for transfers between devices: none -> 97.4 us  [the longest x4 23.1 us: gathered_plan(): rows_across = lax.ppermute(rows, 'seq', across)]
    gather x6 -> x0, local copies, waits for them, and re-layouts: 68.1 us -> none  [the longest x1 14 us: per_device(): jnp.concatenate([results, jnp.zeros((1, D), jnp.bfloat16)], axis=0)[dest]]
    pallas_call x0 -> x7, Pallas kernels: none -> 39.4 us  [the longest x4 28.8 us: experts_on_rows(): pl.pallas_call(functools.partial(experts_kernel, cap=cap), grid=(hidden_u...]
    ppermute x0 -> x37, starting transfers between devices: none -> 31.1 us  [the longest x3 5.98 us: gathered_plan(): rows = lax.ppermute(rows, 'sub', ring(1))]
    dot_general x13 -> x0, matrix products: 30.6 us -> none  [the longest x1 7.24 us: expert_block(): jnp.dot(compact_rows, w_gate, preferred_element_type=jnp.float32)]
    all_gather x2 -> x0, blocking collectives: 26.8 us -> none  [the longest x1 18.6 us: per_device(): lax.all_gather(key_rows, 'seq', axis=1, tiled=True)]
    all_to_all x5 -> x0, starting transfers between devices: 26.2 us -> none  [the longest x1 7.13 us: per_device(): lax.all_to_all(send_gates, ('seq', 'sub'), split_axis=0, concat_axis=0, t...]
  transfers between devices with their start and end apart: 6 -> 37, of which waited for: 2 -> 18; matrix products, arithmetic and copies ran while one was open for 21% -> 3% of each run, Pallas kernels for 0% -> 18%
where the time goes in v2:
time: 188 us
  waiting for transfers between devices  97.4 us (52%)
  Pallas kernels  39.4 us (21%)
  starting transfers between devices  31.1 us (17%)
  local copies, waits for them, and re-layouts  14.9 us (8%)
  other arithmetic  4.36 us (2%)
    pallas_call x4, Pallas kernels, experts_on_rows(): pl.pallas_call(functools.partial(experts_kernel, cap=cap), grid=(hidden_u...  28.8 us
    ppermute x4, waiting for transfers between devices, gathered_plan(): rows_across = lax.ppermute(rows, 'seq', across)  23.1 us
    ppermute x4, waiting for transfers between devices, gathered_plan(): lax.ppermute(away, 'seq', across).astype(jnp.float32)  19 us
    ppermute x3, waiting for transfers between devices, gathered_plan(): rows = lax.ppermute(rows, 'sub', ring(1))  15.3 us
    ppermute x3, waiting for transfers between devices, gathered_plan(): carried = lax.ppermute(part.astype(jnp.bfloat16), 'sub', ring(1))  14.8 us
    unnamed x42, local copies, waits for them, and re-layouts  12.9 us
    pallas_call x2, Pallas kernels, attend(): pl.pallas_call(functools.partial(attend_kernel, scale=1.0 / HD ** 0.5), i...  9.17 us
    ppermute x1, waiting for transfers between devices, gathered_plan(): kv_diagonal = lax.ppermute(kv_away, 'seq', diagonal)  9.09 us
  transfers between devices with their start and end apart: 37, of which 18 were waited for; matrix products, arithmetic and copies ran while one was open for 3% of the time, Pallas kernels for 18%

profile of v2, /device:TPU:0, one launch (start us, length us, event | category | flops | bytes accessed | tf_op | source)
XLA Modules:
  0.0 187.7 jit_solution(9258204673135812803)
XLA Ops:
  2.3 2.6 %collective-permute-start.1 = (bf16[128,1280]{1,0:T(8,128)(2,1)S(1)}, bf16[128,1280]{1,0:T(8,128)(2,1)S(1)}, u32[]{:S(2)}, u32[]{:S(2)}) collective-permute-start(bf16[128,1280]{1,0:T(8,128)(2,1)S(1)} %pad_maximum_fusion), channel_id=1, source_target_pairs={{0,8},{4,12},{8,0},{12,4},{1,9},{5,13},{9,1},{13,5},{2,10},{6,14},... | collective-permute-start | bytes 983048 | tf_op jit(solution)/shard_map/ppermute | solution.py:292
  5.4 9.1 %collective-permute-done.2.refs_3_ = bf16[128,256]{1,0:T(8,128)(2,1)S(1)} collective-permute-done((bf16[128,256]{1,0:T(8,128)(2,1)S(1)}, bf16[128,256]{1,0:T(8,128)(2,1)S(1)}, u32[]{:S(2)}, u32[]{:S(2)}) %collective-permute-start.2) | collective-permute-done | bytes 65568 | tf_op jit(solution)/shard_map/ppermute | solution.py:294
  14.5 1.6 copy-done.4
  16.1 5.0 %shard_map.110 = bf16[128,2048]{1,0:T(8,128)(2,1)} custom-call(s32[7]{0:T(128)S(1)} %stack.66.place_ref, bf16[128,1280]{1,0:T(8,128)(2,1)S(1)} %collective-permute-done.1.refs_2_.query_ref, bf16[128,256]{1,0:T(8,128)(2,1)S(1)} %pad_maximum_fusion.1.refs_0_, bf16[128,256]{1,0:T(8,128)(2,1)S(1)} %collective-permute-done.refs_1_, ...), custom_call_target="tpu_custom_call" | custom-call | flops 805306368 | bytes 5242880 | tf_op jit(solution)/shard_map/pallas_call | solution.py:103
  21.1 1.6 collective-permute-start.4
  22.9 1.6 copy-done.5
  24.5 1.6 copy-done.7
  28.8 4.2 %shard_map.109.own_ref = f32[128,2048]{1,0:T(8,128)S(1)} custom-call(s32[7]{0:T(128)S(1)} %stack.65.place_ref, bf16[128,2048]{1,0:T(8,128)(2,1)S(1)} %bitcast.56, bf16[128,256]{1,0:T(8,128)(2,1)S(1)} %pad_maximum_fusion.1.refs_0_, bf16[128,256]{1,0:T(8,128)(2,1)S(1)} %copy-done.17, bf16[128,1280]{1,0:T(8,128)(2,1)S(1)} %collective-permute-done.1.refs_2_.query_ref, ...), custom_call_target="tpu_custom_call" | custom-call | flops 805306368 | bytes 5242880 | tf_op jit(solution)/shard_map/pallas_call | solution.py:103
  33.0 2.4 %collective-permute-done.4.other_ref = bf16[128,2048]{1,0:T(8,128)(2,1)} collective-permute-done((bf16[128,2048]{1,0:T(8,128)(2,1)}, bf16[128,2048]{1,0:T(8,128)(2,1)}, u32[]{:S(2)}, u32[]{:S(2)}) %collective-permute-start.4) | collective-permute-done | bytes 524320 | tf_op jit(solution)/shard_map/ppermute | solution.py:324
  38.5 1.7 collective-permute-start.16
  40.2 12.6 %collective-permute-done.16.refs_0_ = bf16[128,2048]{1,0:T(8,128)(2,1)} collective-permute-done((bf16[128,2048]{1,0:T(8,128)(2,1)S(1)}, bf16[128,2048]{1,0:T(8,128)(2,1)}, u32[]{:S(2)}, u32[]{:S(2)}) %collective-permute-start.16) | collective-permute-done | bytes 524320 | tf_op jit(solution)/shard_map/ppermute | solution.py:338
  53.5 1.5 collective-permute-start.30
  57.0 9.0 %collective-permute-done.6 = bf16[16,128]{1,0:T(8,128)(2,1)S(1)} collective-permute-done((bf16[16,128]{1,0:T(8,128)(2,1)S(1)}, bf16[16,128]{1,0:T(8,128)(2,1)S(1)}, u32[]{:S(2)}, u32[]{:S(2)}) %collective-permute-start.6) | collective-permute-done | bytes 4128 | tf_op jit(solution)/shard_map/ppermute | solution.py:309
  66.3 1.5 collective-permute-start.25
  67.9 3.5 %collective-permute-start.8 = (bf16[4,16,128]{2,0,1:T(4,128)(2,1)S(1)}, bf16[4,16,128]{2,0,1:T(4,128)(2,1)S(1)}, u32[]{:S(2)}, u32[]{:S(2)}) collective-permute-start(bf16[4,16,128]{2,0,1:T(4,128)(2,1)S(1)} %pad_maximum_fusion.3), channel_id=1, source_target_pairs={{0,1},{1,3},{3,2},{2,0},{4,5},{5,7},{7,6},{6,4},{8,9},{9,11},{11,1... | collective-permute-start | bytes 49160 | tf_op jit(solution)/shard_map/ppermute | solution.py:313
  73.9 3.1 %collective-permute-done.9 = bf16[4,16,128]{2,0,1:T(4,128)(2,1)S(1)} collective-permute-done((bf16[4,16,128]{2,0,1:T(4,128)(2,1)S(1)}, bf16[4,16,128]{2,0,1:T(4,128)(2,1)S(1)}, u32[]{:S(2)}, u32[]{:S(2)}) %collective-permute-start.9) | collective-permute-done | bytes 16416 | tf_op jit(solution)/shard_map/ppermute | solution.py:313
  77.1 3.6 %collective-permute-done.25.refs_2_ = bf16[128,2048]{1,0:T(8,128)(2,1)} collective-permute-done((bf16[128,2048]{1,0:T(8,128)(2,1)}, bf16[128,2048]{1,0:T(8,128)(2,1)}, u32[]{:S(2)}, u32[]{:S(2)}) %collective-permute-start.25) | collective-permute-done | bytes 524320 | tf_op jit(solution)/shard_map/ppermute | solution.py:334
  80.8 1.9 %copy-done.1 = bf16[1,2048,768]{2,1,0:T(8,128)(2,1)S(1)} copy-done((bf16[1,2048,768]{2,1,0:T(8,128)(2,1)S(1)}, bf16[1,2048,768]{2,1,0:T(8,128)(2,1)}, u32[]{:S(2)}) %copy-start.1) | copy-done | bytes 3145752
  82.7 1.9 %copy-done.3 = bf16[1,768,2048]{2,1,0:T(8,128)(2,1)S(1)} copy-done((bf16[1,768,2048]{2,1,0:T(8,128)(2,1)S(1)}, bf16[1,768,2048]{2,1,0:T(8,128)(2,1)}, u32[]{:S(2)}) %copy-start.3) | copy-done | bytes 3145752
  84.5 8.0 %shard_map.115 = (bf16[128,2048]{1,0:T(8,128)(2,1)S(1)}, bf16[128,2048]{1,0:T(8,128)(2,1)S(1)}, bf16[256,2048]{1,0:T(8,128)(2,1)S(1)}) custom-call(f32[4,128]{1,0:T(4,128)S(1)} %get-tuple-element.38.gate_ref, bf16[128,2048]{1,0:T(8,128)(2,1)} %collective-permute-done.16.refs_0_, bf16[128,2048]{1,0:T(8,128)(2,1)} %collective-permute-done.29.refs_1_, ...), custom_call_target="tpu_custom_call" | custom-call | flops 3019898880 | bytes 13631488 | tf_op jit(solution)/shard_map/pallas_call | solution.py:214
  93.1 3.5 %collective-permute-start.18 = (bf16[128,2048]{1,0:T(8,128)(2,1)}, bf16[128,2048]{1,0:T(8,128)(2,1)S(1)}, u32[]{:S(2)}, u32[]{:S(2)}) collective-permute-start(bf16[128,2048]{1,0:T(8,128)(2,1)} %collective-permute-done.17.refs_0_), channel_id=1, source_target_pairs={{0,1},{1,3},{3,2},{2,0},{4,5},{5,7},{7,6},{6,4},{8,9},{9,11},{11,1... | collective-permute-start | bytes 1572872 | tf_op jit(solution)/shard_map/ppermute | solution.py:338
  96.6 7.7 %shard_map.114 = (bf16[128,2048]{1,0:T(8,128)(2,1)S(1)}, bf16[128,2048]{1,0:T(8,128)(2,1)S(1)}, bf16[256,2048]{1,0:T(8,128)(2,1)S(1)}) custom-call(f32[4,128]{1,0:T(4,128)S(1)} %get-tuple-element.39.gate_ref, bf16[128,2048]{1,0:T(8,128)(2,1)} %collective-permute-done.17.refs_0_, bf16[128,2048]{1,0:T(8,128)(2,1)S(1)} %collective-permute-done.24.refs_1_, ...), custom_call_target="tpu_custom_call" | custom-call | flops 3019898880 | bytes 13631488 | tf_op jit(solution)/shard_map/pallas_call | solution.py:214
  104.4 1.5 collective-permute-start.12
  105.9 2.6 %collective-permute-done.18.refs_0_ = bf16[128,2048]{1,0:T(8,128)(2,1)S(1)} collective-permute-done((bf16[128,2048]{1,0:T(8,128)(2,1)}, bf16[128,2048]{1,0:T(8,128)(2,1)S(1)}, u32[]{:S(2)}, u32[]{:S(2)}) %collective-permute-start.18) | collective-permute-done | bytes 524320 | tf_op jit(solution)/shard_map/ppermute | solution.py:338
  111.0 8.2 %collective-permute-done.12.refs_2_ = bf16[128,2048]{1,0:T(8,128)(2,1)S(1)} collective-permute-done((bf16[128,2048]{1,0:T(8,128)(2,1)S(1)}, bf16[128,2048]{1,0:T(8,128)(2,1)S(1)}, u32[]{:S(2)}, u32[]{:S(2)}) %collective-permute-start.12) | collective-permute-done | bytes 524320 | tf_op jit(solution)/shard_map/ppermute | solution.py:334
  119.2 11.2 %collective-permute-done.20.refs_2_ = bf16[128,2048]{1,0:T(8,128)(2,1)S(1)} collective-permute-done((bf16[128,2048]{1,0:T(8,128)(2,1)S(1)}, bf16[128,2048]{1,0:T(8,128)(2,1)S(1)}, u32[]{:S(2)}, u32[]{:S(2)}) %collective-permute-start.20) | collective-permute-done | bytes 524320 | tf_op jit(solution)/shard_map/ppermute | solution.py:334
  132.1 9.1 %collective-permute-done.33 = bf16[128,2048]{1,0:T(8,128)(2,1)S(1)} collective-permute-done((bf16[128,2048]{1,0:T(8,128)(2,1)S(1)}, bf16[128,2048]{1,0:T(8,128)(2,1)S(1)}, u32[]{:S(2)}, u32[]{:S(2)}) %collective-permute-start.33) | collective-permute-done | bytes 524320 | tf_op jit(solution)/shard_map/ppermute | solution.py:351
  143.1 6.6 %shard_map.113 = (bf16[128,2048]{1,0:T(8,128)(2,1)S(1)}, bf16[128,2048]{1,0:T(8,128)(2,1)S(1)}, bf16[256,2048]{1,0:T(8,128)(2,1)S(1)}) custom-call(f32[4,128]{1,0:T(4,128)S(1)} %get-tuple-element.40.gate_ref, bf16[128,2048]{1,0:T(8,128)(2,1)S(1)} %collective-permute-done.18.refs_0_, bf16[128,2048]{1,0:T(8,128)(2,1)S(1)} %collective-permute-done.19.refs_1_, ...), custom_call_target="tpu_custom_call" | custom-call | flops 3019898880 | bytes 13631488 | tf_op jit(solution)/shard_map/pallas_call | solution.py:214
  149.8 6.6 %shard_map.112 = (bf16[128,2048]{1,0:T(8,128)(2,1)S(1)}, bf16[128,2048]{1,0:T(8,128)(2,1)S(1)}, bf16[256,2048]{1,0:T(8,128)(2,1)S(1)}) custom-call(f32[4,128]{1,0:T(4,128)S(1)} %get-tuple-element.37.gate_ref, bf16[128,2048]{1,0:T(8,128)(2,1)S(1)} %copy-done.12, bf16[128,2048]{1,0:T(8,128)(2,1)S(1)} %collective-permute-done.11.refs_1_, ...), custom_call_target="tpu_custom_call" | custom-call | flops 3019898880 | bytes 13631488 | tf_op jit(solution)/shard_map/pallas_call | solution.py:214
  160.8 11.4 %collective-permute-done.35 = bf16[128,2048]{1,0:T(8,128)(2,1)S(1)} collective-permute-done((bf16[128,2048]{1,0:T(8,128)(2,1)S(1)}, bf16[128,2048]{1,0:T(8,128)(2,1)S(1)}, u32[]{:S(2)}, u32[]{:S(2)}) %collective-permute-start.35) | collective-permute-done | bytes 524320 | tf_op jit(solution)/shard_map/ppermute | solution.py:356
  174.2 9.0 %collective-permute-done.15 = bf16[128,2048]{1,0:T(8,128)(2,1)S(1)} collective-permute-done((bf16[128,2048]{1,0:T(8,128)(2,1)S(1)}, bf16[128,2048]{1,0:T(8,128)(2,1)S(1)}, u32[]{:S(2)}, u32[]{:S(2)}) %collective-permute-start.15) | collective-permute-done | bytes 524320 | tf_op jit(solution)/shard_map/ppermute | solution.py:351
  183.1 3.3 %collective-permute-done.36 = bf16[128,2048]{1,0:T(8,128)(2,1)S(1)} collective-permute-done((bf16[128,2048]{1,0:T(8,128)(2,1)S(1)}, bf16[128,2048]{1,0:T(8,128)(2,1)S(1)}, u32[]{:S(2)}, u32[]{:S(2)}) %collective-permute-start.36) | collective-permute-done | bytes 524320 | tf_op jit(solution)/shard_map/ppermute | solution.py:356
  (121 shorter events, 28.7 us)
Async XLA Ops:
  0.0 14.5 %collective-permute-start.3 = (bf16[512,2048]{1,0:T(8,128)(2,1)}, bf16[512,2048]{1,0:T(8,128)(2,1)S(1)}, u32[]{:S(2)}, u32[]{:S(2)}) collective-permute-start(bf16[512,2048]{1,0:T(8,128)(2,1)} %refs_4_.3), channel_id=1, source_target_pairs={{0,4},{4,0},{8,12},{12,8},{1,5},{5,1},{9,13},{13,9},{2,6},{6,2},{1... | collective-permute-start | bytes 6291464 | tf_op jit(solution)/shard_map/ppermute | solution.py:295
  2.3 12.2 %collective-permute-start.1 = (bf16[128,1280]{1,0:T(8,128)(2,1)S(1)}, bf16[128,1280]{1,0:T(8,128)(2,1)S(1)}, u32[]{:S(2)}, u32[]{:S(2)}) collective-permute-start(bf16[128,1280]{1,0:T(8,128)(2,1)S(1)} %pad_maximum_fusion), channel_id=1, source_target_pairs={{0,8},{4,12},{8,0},{12,4},{1,9},{5,13},{9,1},{13,5},{2,10},{6,14},... | collective-permute-start | bytes 983048 | tf_op jit(solution)/shard_map/ppermute | solution.py:292
  4.9 9.6 %collective-permute-start.2 = (bf16[128,256]{1,0:T(8,128)(2,1)S(1)}, bf16[128,256]{1,0:T(8,128)(2,1)S(1)}, u32[]{:S(2)}, u32[]{:S(2)}) collective-permute-start(bf16[128,256]{1,0:T(8,128)(2,1)S(1)} %pad_maximum_fusion.2), channel_id=1, source_target_pairs={{0,12},{4,8},{8,4},{12,0},{1,13},{5,9},{9,5},{13,1},{2,14},{6,10},... | collective-permute-start | bytes 196616 | tf_op jit(solution)/shard_map/ppermute | solution.py:294
  5.1 9.4 %collective-permute-start = (bf16[128,256]{1,0:T(8,128)(2,1)S(1)}, bf16[128,256]{1,0:T(8,128)(2,1)S(1)}, u32[]{:S(2)}, u32[]{:S(2)}) collective-permute-start(bf16[128,256]{1,0:T(8,128)(2,1)S(1)} %pad_maximum_fusion.1.refs_0_), channel_id=1, source_target_pairs={{0,4},{4,0},{8,12},{12,8},{1,5},{5,1},{9,13},{13,9},{2,6},{6,2},{1... | collective-permute-start | bytes 196616 | tf_op jit(solution)/shard_map/ppermute | solution.py:293
  21.1 14.3 %collective-permute-start.4 = (bf16[128,2048]{1,0:T(8,128)(2,1)}, bf16[128,2048]{1,0:T(8,128)(2,1)}, u32[]{:S(2)}, u32[]{:S(2)}) collective-permute-start(bf16[128,2048]{1,0:T(8,128)(2,1)} %shard_map.110), channel_id=1, source_target_pairs={{0,8},{4,12},{8,0},{12,4},{1,9},{5,13},{9,1},{13,5},{2,10},{6,14},... | collective-permute-start | bytes 1572872 | tf_op jit(solution)/shard_map/ppermute | solution.py:324
  38.5 14.3 %collective-permute-start.16 = (bf16[128,2048]{1,0:T(8,128)(2,1)S(1)}, bf16[128,2048]{1,0:T(8,128)(2,1)}, u32[]{:S(2)}, u32[]{:S(2)}) collective-permute-start(bf16[128,2048]{1,0:T(8,128)(2,1)S(1)} %get-tuple-element.20.refs_0_), channel_id=1, source_target_pairs={{0,1},{1,3},{3,2},{2,0},{4,5},{5,7},{7,6},{6,4},{8,9},{9,11},{11,1... | collective-permute-start | bytes 1572872 | tf_op jit(solution)/shard_map/ppermute | solution.py:338
  52.8 13.6 %collective-permute-start.17 = (bf16[128,2048]{1,0:T(8,128)(2,1)}, bf16[128,2048]{1,0:T(8,128)(2,1)}, u32[]{:S(2)}, u32[]{:S(2)}) collective-permute-start(bf16[128,2048]{1,0:T(8,128)(2,1)} %collective-permute-done.16.refs_0_), channel_id=1, source_target_pairs={{0,1},{1,3},{3,2},{2,0},{4,5},{5,7},{7,6},{6,4},{8,9},{9,11},{11,1... | collective-permute-start | bytes 1572872 | tf_op jit(solution)/shard_map/ppermute | solution.py:338
  53.5 14.3 %collective-permute-start.30 = (bf16[128,2048]{1,0:T(8,128)(2,1)}, bf16[128,2048]{1,0:T(8,128)(2,1)}, u32[]{:S(2)}, u32[]{:S(2)}) collective-permute-start(bf16[128,2048]{1,0:T(8,128)(2,1)} %collective-permute-done.16.refs_0_), channel_id=1, source_target_pairs={{0,8},{4,12},{8,0},{12,4},{1,9},{5,13},{9,1},{13,5},{2,10},{6,14},... | collective-permute-start | bytes 1572872 | tf_op jit(solution)/shard_map/ppermute | solution.py:334
  55.1 10.9 %collective-permute-start.6 = (bf16[16,128]{1,0:T(8,128)(2,1)S(1)}, bf16[16,128]{1,0:T(8,128)(2,1)S(1)}, u32[]{:S(2)}, u32[]{:S(2)}) collective-permute-start(bf16[16,128]{1,0:T(8,128)(2,1)S(1)} %select_reduce_fusion), channel_id=1, source_target_pairs={{0,8},{4,12},{8,0},{12,4},{1,9},{5,13},{9,1},{13,5},{2,10},{6,14},... | collective-permute-start | bytes 12296 | tf_op jit(solution)/shard_map/ppermute | solution.py:309
  55.7 10.2 %collective-permute-start.7 = (bf16[16,128]{1,0:T(8,128)(2,1)S(1)}, bf16[16,128]{1,0:T(8,128)(2,1)S(1)}, u32[]{:S(2)}, u32[]{:S(2)}) collective-permute-start(bf16[16,128]{1,0:T(8,128)(2,1)S(1)} %select_reduce_fusion), channel_id=1, source_target_pairs={{0,12},{4,8},{8,4},{12,0},{1,13},{5,9},{9,5},{13,1},{2,14},{6,10},... | collective-permute-start | bytes 12296 | tf_op jit(solution)/shard_map/ppermute | solution.py:310
  66.0 14.7 %collective-permute-start.29 = (bf16[128,2048]{1,0:T(8,128)(2,1)}, bf16[128,2048]{1,0:T(8,128)(2,1)}, u32[]{:S(2)}, u32[]{:S(2)}) collective-permute-start(bf16[128,2048]{1,0:T(8,128)(2,1)} %collective-permute-done.16.refs_0_), channel_id=1, source_target_pairs={{0,4},{4,0},{8,12},{12,8},{1,5},{5,1},{9,13},{13,9},{2,6},{6,2},{1... | collective-permute-start | bytes 1572872 | tf_op jit(solution)/shard_map/ppermute | solution.py:333
  66.3 14.4 %collective-permute-start.25 = (bf16[128,2048]{1,0:T(8,128)(2,1)}, bf16[128,2048]{1,0:T(8,128)(2,1)}, u32[]{:S(2)}, u32[]{:S(2)}) collective-permute-start(bf16[128,2048]{1,0:T(8,128)(2,1)} %collective-permute-done.17.refs_0_), channel_id=1, source_target_pairs={{0,8},{4,12},{8,0},{12,4},{1,9},{5,13},{9,1},{13,5},{2,10},{6,14},... | collective-permute-start | bytes 1572872 | tf_op jit(solution)/shard_map/ppermute | solution.py:334
  67.8 12.9 %collective-permute-start.31 = (bf16[128,2048]{1,0:T(8,128)(2,1)}, bf16[128,2048]{1,0:T(8,128)(2,1)}, u32[]{:S(2)}, u32[]{:S(2)}) collective-permute-start(bf16[128,2048]{1,0:T(8,128)(2,1)} %collective-permute-done.30.refs_2_), channel_id=1, source_target_pairs={{0,4},{4,0},{8,12},{12,8},{1,5},{5,1},{9,13},{13,9},{2,6},{6,2},{1... | collective-permute-start | bytes 1572872 | tf_op jit(solution)/shard_map/ppermute | solution.py:335
  77.0 19.6 %collective-permute-start.24 = (bf16[128,2048]{1,0:T(8,128)(2,1)}, bf16[128,2048]{1,0:T(8,128)(2,1)S(1)}, u32[]{:S(2)}, u32[]{:S(2)}) collective-permute-start(bf16[128,2048]{1,0:T(8,128)(2,1)} %collective-permute-done.17.refs_0_), channel_id=1, source_target_pairs={{0,4},{4,0},{8,12},{12,8},{1,5},{5,1},{9,13},{13,9},{2,6},{6,2},{1... | collective-permute-start | bytes 1572872 | tf_op jit(solution)/shard_map/ppermute | solution.py:333
  80.7 15.9 %collective-permute-start.26 = (bf16[128,2048]{1,0:T(8,128)(2,1)}, bf16[128,2048]{1,0:T(8,128)(2,1)S(1)}, u32[]{:S(2)}, u32[]{:S(2)}) collective-permute-start(bf16[128,2048]{1,0:T(8,128)(2,1)} %collective-permute-done.25.refs_2_), channel_id=1, source_target_pairs={{0,4},{4,0},{8,12},{12,8},{1,5},{5,1},{9,13},{13,9},{2,6},{6,2},{1... | collective-permute-start | bytes 1572872 | tf_op jit(solution)/shard_map/ppermute | solution.py:335
  92.6 17.4 %collective-permute-start.32 = (bf16[256,2048]{1,0:T(8,128)(2,1)S(1)}, bf16[256,2048]{1,0:T(8,128)(2,1)S(1)}, u32[]{:S(2)}, u32[]{:S(2)}) collective-permute-start(bf16[256,2048]{1,0:T(8,128)(2,1)S(1)} %get-tuple-element.31), channel_id=1, source_target_pairs={{0,4},{4,0},{8,12},{12,8},{1,5},{5,1},{9,13},{13,9},{2,6},{6,2},{1... | collective-permute-start | bytes 3145736 | tf_op jit(solution)/shard_map/ppermute | solution.py:346
  93.1 15.4 %collective-permute-start.18 = (bf16[128,2048]{1,0:T(8,128)(2,1)}, bf16[128,2048]{1,0:T(8,128)(2,1)S(1)}, u32[]{:S(2)}, u32[]{:S(2)}) collective-permute-start(bf16[128,2048]{1,0:T(8,128)(2,1)} %collective-permute-done.17.refs_0_), channel_id=1, source_target_pairs={{0,1},{1,3},{3,2},{2,0},{4,5},{5,7},{7,6},{6,4},{8,9},{9,11},{11,1... | collective-permute-start | bytes 1572872 | tf_op jit(solution)/shard_map/ppermute | solution.py:338
  104.3 26.1 %collective-permute-start.27 = (bf16[256,2048]{1,0:T(8,128)(2,1)S(1)}, bf16[256,2048]{1,0:T(8,128)(2,1)S(1)}, u32[]{:S(2)}, u32[]{:S(2)}) collective-permute-start(bf16[256,2048]{1,0:T(8,128)(2,1)S(1)} %get-tuple-element.28), channel_id=1, source_target_pairs={{0,4},{4,0},{8,12},{12,8},{1,5},{5,1},{9,13},{13,9},{2,6},{6,2},{1... | collective-permute-start | bytes 3145736 | tf_op jit(solution)/shard_map/ppermute | solution.py:346
  104.4 14.8 %collective-permute-start.12 = (bf16[128,2048]{1,0:T(8,128)(2,1)S(1)}, bf16[128,2048]{1,0:T(8,128)(2,1)S(1)}, u32[]{:S(2)}, u32[]{:S(2)}) collective-permute-start(bf16[128,2048]{1,0:T(8,128)(2,1)S(1)} %copy-done.12), channel_id=1, source_target_pairs={{0,8},{4,12},{8,0},{12,4},{1,9},{5,13},{9,1},{13,5},{2,10},{6,14},... | collective-permute-start | bytes 1572872 | tf_op jit(solution)/shard_map/ppermute | solution.py:334
  108.5 21.9 %collective-permute-start.20 = (bf16[128,2048]{1,0:T(8,128)(2,1)S(1)}, bf16[128,2048]{1,0:T(8,128)(2,1)S(1)}, u32[]{:S(2)}, u32[]{:S(2)}) collective-permute-start(bf16[128,2048]{1,0:T(8,128)(2,1)S(1)} %collective-permute-done.18.refs_0_), channel_id=1, source_target_pairs={{0,8},{4,12},{8,0},{12,4},{1,9},{5,13},{9,1},{13,5},{2,10},{6,14},... | collective-permute-start | bytes 1572872 | tf_op jit(solution)/shard_map/ppermute | solution.py:334
  110.3 30.9 %collective-permute-start.33 = (bf16[128,2048]{1,0:T(8,128)(2,1)S(1)}, bf16[128,2048]{1,0:T(8,128)(2,1)S(1)}, u32[]{:S(2)}, u32[]{:S(2)}) collective-permute-start(bf16[128,2048]{1,0:T(8,128)(2,1)S(1)} %fusion), channel_id=1, source_target_pairs={{0,8},{4,12},{8,0},{12,4},{1,9},{5,13},{9,1},{13,5},{2,10},{6,14},... | collective-permute-start | bytes 1572872 | tf_op jit(solution)/shard_map/ppermute | solution.py:351
  111.0 38.8 %collective-permute-start.11 = (bf16[128,2048]{1,0:T(8,128)(2,1)S(1)}, bf16[128,2048]{1,0:T(8,128)(2,1)S(1)}, u32[]{:S(2)}, u32[]{:S(2)}) collective-permute-start(bf16[128,2048]{1,0:T(8,128)(2,1)S(1)} %copy-done.12), channel_id=1, source_target_pairs={{0,4},{4,0},{8,12},{12,8},{1,5},{5,1},{9,13},{13,9},{2,6},{6,2},{1... | collective-permute-start | bytes 1572872 | tf_op jit(solution)/shard_map/ppermute | solution.py:333
  119.2 30.6 %collective-permute-start.13 = (bf16[128,2048]{1,0:T(8,128)(2,1)S(1)}, bf16[128,2048]{1,0:T(8,128)(2,1)S(1)}, u32[]{:S(2)}, u32[]{:S(2)}) collective-permute-start(bf16[128,2048]{1,0:T(8,128)(2,1)S(1)} %collective-permute-done.12.refs_2_), channel_id=1, source_target_pairs={{0,4},{4,0},{8,12},{12,8},{1,5},{5,1},{9,13},{13,9},{2,6},{6,2},{1... | collective-permute-start | bytes 1572872 | tf_op jit(solution)/shard_map/ppermute | solution.py:335
  130.4 12.4 %collective-permute-start.19 = (bf16[128,2048]{1,0:T(8,128)(2,1)S(1)}, bf16[128,2048]{1,0:T(8,128)(2,1)S(1)}, u32[]{:S(2)}, u32[]{:S(2)}) collective-permute-start(bf16[128,2048]{1,0:T(8,128)(2,1)S(1)} %collective-permute-done.18.refs_0_), channel_id=1, source_target_pairs={{0,4},{4,0},{8,12},{12,8},{1,5},{5,1},{9,13},{13,9},{2,6},{6,2},{1... | collective-permute-start | bytes 1572872 | tf_op jit(solution)/shard_map/ppermute | solution.py:333
  130.4 12.7 %collective-permute-start.21 = (bf16[128,2048]{1,0:T(8,128)(2,1)S(1)}, bf16[128,2048]{1,0:T(8,128)(2,1)S(1)}, u32[]{:S(2)}, u32[]{:S(2)}) collective-permute-start(bf16[128,2048]{1,0:T(8,128)(2,1)S(1)} %collective-permute-done.20.refs_2_), channel_id=1, source_target_pairs={{0,4},{4,0},{8,12},{12,8},{1,5},{5,1},{9,13},{13,9},{2,6},{6,2},{1... | collective-permute-start | bytes 1572872 | tf_op jit(solution)/shard_map/ppermute | solution.py:335
  141.2 15.7 %collective-permute-start.28 = (bf16[128,2048]{1,0:T(8,128)(2,1)}, bf16[128,2048]{1,0:T(8,128)(2,1)S(1)}, u32[]{:S(2)}, u32[]{:S(2)}) collective-permute-start(bf16[128,2048]{1,0:T(8,128)(2,1)} %fusion.3), channel_id=1, source_target_pairs={{0,8},{4,12},{8,0},{12,4},{1,9},{5,13},{9,1},{13,5},{2,10},{6,14},... | collective-permute-start | bytes 1572872 | tf_op jit(solution)/shard_map/ppermute | solution.py:351
  142.9 14.1 %collective-permute-start.34 = (bf16[128,2048]{1,0:T(8,128)(2,1)S(1)}, bf16[128,2048]{1,0:T(8,128)(2,1)S(1)}, u32[]{:S(2)}, u32[]{:S(2)}) collective-permute-start(bf16[128,2048]{1,0:T(8,128)(2,1)S(1)} %fusion.2), channel_id=1, source_target_pairs={{0,1},{1,3},{3,2},{2,0},{4,5},{5,7},{7,6},{6,4},{8,9},{9,11},{11,1... | collective-permute-start | bytes 1572872 | tf_op jit(solution)/shard_map/ppermute | solution.py:356
  149.7 8.2 %collective-permute-start.22 = (bf16[256,2048]{1,0:T(8,128)(2,1)S(1)}, bf16[256,2048]{1,0:T(8,128)(2,1)S(1)}, u32[]{:S(2)}, u32[]{:S(2)}) collective-permute-start(bf16[256,2048]{1,0:T(8,128)(2,1)S(1)} %get-tuple-element.25), channel_id=1, source_target_pairs={{0,4},{4,0},{8,12},{12,8},{1,5},{5,1},{9,13},{13,9},{2,6},{6,2},{1... | collective-permute-start | bytes 3145736 | tf_op jit(solution)/shard_map/ppermute | solution.py:346
  157.3 14.8 %collective-permute-start.35 = (bf16[128,2048]{1,0:T(8,128)(2,1)S(1)}, bf16[128,2048]{1,0:T(8,128)(2,1)S(1)}, u32[]{:S(2)}, u32[]{:S(2)}) collective-permute-start(bf16[128,2048]{1,0:T(8,128)(2,1)S(1)} %fusion.6), channel_id=1, source_target_pairs={{0,1},{1,3},{3,2},{2,0},{4,5},{5,7},{7,6},{6,4},{8,9},{9,11},{11,1... | collective-permute-start | bytes 1572872 | tf_op jit(solution)/shard_map/ppermute | solution.py:356
  158.3 14.9 %collective-permute-start.23 = (bf16[128,2048]{1,0:T(8,128)(2,1)S(1)}, bf16[128,2048]{1,0:T(8,128)(2,1)S(1)}, u32[]{:S(2)}, u32[]{:S(2)}) collective-permute-start(bf16[128,2048]{1,0:T(8,128)(2,1)S(1)} %fusion.7), channel_id=1, source_target_pairs={{0,8},{4,12},{8,0},{12,4},{1,9},{5,13},{9,1},{13,5},{2,10},{6,14},... | collective-permute-start | bytes 1572872 | tf_op jit(solution)/shard_map/ppermute | solution.py:351
  159.6 23.6 %collective-permute-start.15 = (bf16[128,2048]{1,0:T(8,128)(2,1)S(1)}, bf16[128,2048]{1,0:T(8,128)(2,1)S(1)}, u32[]{:S(2)}, u32[]{:S(2)}) collective-permute-start(bf16[128,2048]{1,0:T(8,128)(2,1)S(1)} %fusion.11), channel_id=1, source_target_pairs={{0,8},{4,12},{8,0},{12,4},{1,9},{5,13},{9,1},{13,5},{2,10},{6,14},... | collective-permute-start | bytes 1572872 | tf_op jit(solution)/shard_map/ppermute | solution.py:351
  173.4 13.0 %collective-permute-start.36 = (bf16[128,2048]{1,0:T(8,128)(2,1)S(1)}, bf16[128,2048]{1,0:T(8,128)(2,1)S(1)}, u32[]{:S(2)}, u32[]{:S(2)}) collective-permute-start(bf16[128,2048]{1,0:T(8,128)(2,1)S(1)} %fusion.10), channel_id=1, source_target_pairs={{0,1},{1,3},{3,2},{2,0},{4,5},{5,7},{7,6},{6,4},{8,9},{9,11},{11,1... | collective-permute-start | bytes 1572872 | tf_op jit(solution)/shard_map/ppermute | solution.py:356
  (26 other events, 217.7 us)

commit v3 on v2

--- a/solution.py
+++ b/solution.py
@@ -58,7 +58,16 @@
 
 
 def attend_kernel(place_ref, query_ref, *refs, scale):
-    kv_refs, (w_own_ref, w_other_ref, out_ref, keys, values, heads) = refs[:4], refs[4:]
+    kv_refs, (w_own_ref, w_other_ref, out_ref, keys, values, heads, w_own, w_other, done) = (
+        refs[:4],
+        refs[4:],
+    )
+    fetches = [
+        pltpu.make_async_copy(w_own_ref, w_own, done.at[0]),
+        pltpu.make_async_copy(w_other_ref, w_other, done.at[1]),
+    ]
+    for fetch in fetches:
+        fetch.start()
     rows = keys.shape[0] // 4
     head_size = keys.shape[1]
     core = place_ref[0]
@@ -87,12 +96,14 @@
         heads[:, head * head_size : (head + 1) * head_size] = jnp.dot(
             probs, value_block, preferred_element_type=jnp.float32
         ).astype(jnp.bfloat16)
+    for fetch in fetches:
+        fetch.wait()
     half = heads.shape[1] // 2
     own = heads[:, pl.ds(pl.multiple_of(core * half, half), half)]
     other = heads[:, pl.ds(pl.multiple_of((1 - core) * half, half), half)]
     out_ref[...] = (
-        jnp.dot(own, w_own_ref[...], preferred_element_type=jnp.float32)
-        + jnp.dot(other, w_other_ref[...], preferred_element_type=jnp.float32)
+        jnp.dot(own, w_own[...], preferred_element_type=jnp.float32)
+        + jnp.dot(other, w_other[...], preferred_element_type=jnp.float32)
     ).astype(out_ref.dtype)
 
 
@@ -103,15 +114,19 @@
     return pl.pallas_call(
         functools.partial(attend_kernel, scale=1.0 / HD**0.5),
         in_specs=[pl.BlockSpec(memory_space=pltpu.SMEM)]
-        + [pl.BlockSpec(memory_space=pltpu.VMEM)] * 7,
+        + [pl.BlockSpec(memory_space=pltpu.VMEM)] * 5
+        + [pl.BlockSpec(memory_space=pl.ANY)] * 2,
         out_specs=pl.BlockSpec(memory_space=pltpu.VMEM),
         out_shape=jax.ShapeDtypeStruct((tokens, width), dtype),
         scratch_shapes=[
             pltpu.VMEM((4 * tokens, HD), jnp.bfloat16),
             pltpu.VMEM((4 * tokens, HD), jnp.bfloat16),
             pltpu.VMEM((tokens, chip_width), jnp.bfloat16),
+            pltpu.VMEM(w_own.shape, jnp.bfloat16),
+            pltpu.VMEM(w_other.shape, jnp.bfloat16),
+            pltpu.SemaphoreType.DMA((2,)),
         ],
-        compiler_params=pltpu.CompilerParams(vmem_limit_bytes=32 * 1024 * 1024),
+        compiler_params=pltpu.CompilerParams(vmem_limit_bytes=24 * 1024 * 1024),
         cost_estimate=pl.CostEstimate(
             flops=16 * tokens * tokens * chip_width + 2 * tokens * chip_width * width,
             bytes_accessed=4 * w_own.size + 4 * tokens * width,
@@ -143,11 +158,24 @@
     )(residual, own, other, gain)
 
 
-def experts_kernel(gate_ref, *refs, cap):
+def pass_kernel(*refs):
+    del refs
+
+
+def meet(*arrays):
+    return pl.pallas_call(
+        pass_kernel,
+        in_specs=[pl.BlockSpec(memory_space=pl.ANY)] * len(arrays),
+        out_specs=[pl.BlockSpec(memory_space=pl.ANY)] * len(arrays),
+        out_shape=[jax.ShapeDtypeStruct(array.shape, array.dtype) for array in arrays],
+        input_output_aliases={index: index for index in range(len(arrays))},
+    )(*arrays)
+
+
+def experts_kernel(gate_ref, *refs, cap, span):
     row_refs, refs = refs[:4], refs[4:]
-    w_gate_ref, w_up_ref, w_down_ref, own_ref, across_ref, other_ref, packed, total = refs
-    tokens = row_refs[0].shape[0]
-    step = pl.program_id(0)
+    w_gate_ref, w_up_ref, w_down_ref, own_ref, across_ref, other_ref, packed, inner = refs
+    tokens, width = row_refs[0].shape
     gates = gate_ref[...]
     named = gates > 0
     before = (
@@ -157,74 +185,52 @@
     rank = jnp.dot(named.astype(jnp.bfloat16), before, preferred_element_type=jnp.float32)
     slot = jnp.where(named, rank.astype(jnp.int32), -1)
     slots = lax.broadcasted_iota(jnp.int32, (cap, tokens), 0)
-
-    def chosen_of(block):
-        return slots == slot[block : block + 1, :]
-
-    @pl.when(step == 0)
-    def _():
+    picks, places, weights = [], [], []
+    for block in range(4):
+        chosen = slots == slot[block : block + 1, :]
+        pick = jnp.where(chosen, 1.0, 0.0)
+        picks.append(pick.astype(jnp.bfloat16))
+        places.append(jnp.transpose(pick).astype(jnp.bfloat16))
+        weights.append(
+            jnp.sum(jnp.where(chosen, gates[block : block + 1, :], 0.0), axis=1, keepdims=True)
+        )
+
+    for block in range(4):
+        packed[block * cap : (block + 1) * cap, :] = jnp.dot(
+            picks[block], row_refs[block][...], preferred_element_type=jnp.float32
+        ).astype(jnp.bfloat16)
+
+    @pl.loop(0, inner.shape[1] // span)
+    def _(index):
+        columns = pl.ds(pl.multiple_of(index * span, span), span)
+        gate_proj = jnp.dot(packed[...], w_gate_ref[:, columns], preferred_element_type=jnp.float32)
+        up_proj = jnp.dot(packed[...], w_up_ref[:, columns], preferred_element_type=jnp.float32)
+        inner[:, columns] = (gate_proj / (1.0 + jnp.exp(-gate_proj)) * up_proj).astype(jnp.bfloat16)
+
+    @pl.loop(0, width // span)
+    def _(index):
+        columns = pl.ds(pl.multiple_of(index * span, span), span)
+        result = jnp.dot(inner[...], w_down_ref[:, columns], preferred_element_type=jnp.float32)
+        targets = (
+            own_ref.at[:, columns],
+            other_ref.at[0:tokens, columns],
+            across_ref.at[:, columns],
+            other_ref.at[tokens : 2 * tokens, columns],
+        )
         for block in range(4):
-            packed[block * cap : (block + 1) * cap, :] = jnp.dot(
-                chosen_of(block).astype(jnp.bfloat16),
-                row_refs[block][...],
-                preferred_element_type=jnp.float32,
-            ).astype(jnp.bfloat16)
-
-    rows = packed[...]
-    gate_proj = jnp.dot(rows, w_gate_ref[...], preferred_element_type=jnp.float32)
-    up_proj = jnp.dot(rows, w_up_ref[...], preferred_element_type=jnp.float32)
-    inner = (gate_proj / (1.0 + jnp.exp(-gate_proj)) * up_proj).astype(jnp.bfloat16)
-    result = jnp.dot(inner, w_down_ref[...], preferred_element_type=jnp.float32)
-
-    @pl.when(step == 0)
-    def _():
-        total[...] = result
-
-    @pl.when(step > 0)
-    def _():
-        total[...] += result
-
-    @pl.when(step == pl.num_programs(0) - 1)
-    def _():
-        targets = (
-            own_ref.at[...],
-            other_ref.at[0:tokens],
-            across_ref.at[...],
-            other_ref.at[tokens : 2 * tokens],
-        )
-        for block in range(4):
-            chosen = chosen_of(block)
-            weights = jnp.sum(
-                jnp.where(chosen, gates[block : block + 1, :], 0.0), axis=1, keepdims=True
-            )
-            part = (total[block * cap : (block + 1) * cap, :] * weights).astype(jnp.bfloat16)
-            targets[block][...] = lax.dot_general(
-                chosen.astype(jnp.bfloat16),
-                part,
-                (((0,), (0,)), ((), ())),
-                preferred_element_type=jnp.float32,
+            part = (result[block * cap : (block + 1) * cap] * weights[block]).astype(jnp.bfloat16)
+            targets[block][...] = jnp.dot(
+                places[block], part, preferred_element_type=jnp.float32
             ).astype(jnp.bfloat16)
 
 
 def experts_on_rows(gates, row_blocks, w_gate, w_up, w_down, cap):
     tokens, width = row_blocks[0].shape
     hidden_units = w_gate.shape[1]
-    chunk = hidden_units // 3 if hidden_units % 384 == 0 else hidden_units
-    whole = pl.BlockSpec((tokens, width), lambda step: (0, 0))
     return pl.pallas_call(
-        functools.partial(experts_kernel, cap=cap),
-        grid=(hidden_units // chunk,),
-        in_specs=[
-            pl.BlockSpec((4, tokens), lambda step: (0, 0)),
-            whole,
-            whole,
-            whole,
-            whole,
-            pl.BlockSpec((width, chunk), lambda step: (0, step)),
-            pl.BlockSpec((width, chunk), lambda step: (0, step)),
-            pl.BlockSpec((chunk, width), lambda step: (step, 0)),
-        ],
-        out_specs=[whole, whole, pl.BlockSpec((2 * tokens, width), lambda step: (0, 0))],
+        functools.partial(experts_kernel, cap=cap, span=256),
+        in_specs=[pl.BlockSpec(memory_space=pltpu.VMEM)] * 8,
+        out_specs=[pl.BlockSpec(memory_space=pltpu.VMEM)] * 3,
         out_shape=[
             jax.ShapeDtypeStruct((tokens, width), jnp.bfloat16),
             jax.ShapeDtypeStruct((tokens, width), jnp.bfloat16),
@@ -232,9 +238,9 @@
         ],
         scratch_shapes=[
             pltpu.VMEM((4 * cap, width), jnp.bfloat16),
-            pltpu.VMEM((4 * cap, width), jnp.float32),
+            pltpu.VMEM((4 * cap, hidden_units), jnp.bfloat16),
         ],
-        compiler_params=pltpu.CompilerParams(vmem_limit_bytes=40 * 1024 * 1024),
+        compiler_params=pltpu.CompilerParams(vmem_limit_bytes=28 * 1024 * 1024),
         cost_estimate=pl.CostEstimate(
             flops=24 * cap * width * hidden_units,
             bytes_accessed=16 * tokens * width + 6 * width * hidden_units,
@@ -302,17 +308,14 @@
         ),
         axis=2,
     ).astype(jnp.bfloat16)
-    quad = jnp.stack(
-        [
-            table,
-            lax.ppermute(table, "seq", twin),
-            lax.ppermute(table, "seq", across),
-            lax.ppermute(table, "seq", diagonal),
-        ]
-    )
-    quads = [quad] + [lax.ppermute(quad, "sub", ring(steps)) for steps in range(1, n_sub)]
-    mine = place * n_sub + lax.axis_index("sub")
-    gates = lax.dynamic_index_in_dim(jnp.stack(quads), mine, 2, keepdims=False).astype(jnp.float32)
+    incoming, table_twin, table_across, table_diagonal = meet(
+        incoming,
+        lax.ppermute(table, "seq", twin),
+        lax.ppermute(table, "seq", across),
+        lax.ppermute(table, "seq", diagonal),
+    )
+    quad = jnp.stack([table, table_twin, table_across, table_diagonal])
+    quads = [lax.ppermute(quad, "sub", ring(steps)) for steps in range(1, n_sub)]
 
     kv_parts = (kv_here, kv_twin, incoming, kv_diagonal)
     columns = [place, place ^ 1, place ^ 2, place ^ 3]
@@ -325,36 +328,77 @@
     projected = attend(
         place_of(chip * chip_width, place), queries, kv_parts, out_proj, w_other, jnp.float32
     )
+    projected_across, *quads = meet(projected_across, *quads)
+    mine = place * n_sub + lax.axis_index("sub")
+    gates = lax.dynamic_index_in_dim(
+        jnp.stack([quad] + quads), mine, 2, keepdims=False
+    ).astype(jnp.float32)
     hidden, normed = add_and_norm(residual_in[0], projected, projected_across, norm_gain[None])
 
-    rows = normed
-    sums = []
-    for step in range(n_sub):
-        rows_twin = lax.ppermute(rows, "seq", twin)
-        rows_across = lax.ppermute(rows, "seq", across)
-        rows_diagonal = lax.ppermute(rows_across, "seq", twin)
-        blocks = (rows, rows_twin, rows_across, rows_diagonal)
-        if step < n_sub - 1:
-            rows = lax.ppermute(rows, "sub", ring(1))
-        sums.append(
-            experts_on_rows(gates[step], blocks, expert_gate[0], expert_up[0], expert_down[0], cap)
-        )
     tokens = queries.shape[0]
-    carried = None
-    for step in list(range(1, n_sub)) + [0]:
-        own, away, other = sums[step]
-        met = lax.ppermute(other, "seq", twin).astype(jnp.float32)
-        away = (away.astype(jnp.float32) + met[tokens:]).astype(jnp.bfloat16)
-        part = (
-            own.astype(jnp.float32)
-            + met[:tokens]
-            + lax.ppermute(away, "seq", across).astype(jnp.float32)
-        )
-        if carried is not None:
-            part = part + carried.astype(jnp.float32)
-        if step:
-            carried = lax.ppermute(part.astype(jnp.bfloat16), "sub", ring(1))
-    return (hidden.astype(jnp.float32) + part).astype(jnp.bfloat16)[None]
+    last = n_sub - 1
+    lag = max(n_sub, 4)
+    held = {("row", 0): normed}
+    halves = {}
+
+    def move_twin(array):
+        return lax.ppermute(array, "seq", twin)
+
+    def move_across(array):
+        return lax.ppermute(array, "seq", across)
+
+    def move_on(array):
+        return lax.ppermute(array, "sub", ring(1))
+
+    for turn in range(1, lag + n_sub + 1):
+        now = {}
+        if turn <= n_sub:
+            step = turn - 1
+            now["across", step] = move_across(held["row", step])
+            if step < last:
+                now["row", step + 1] = move_on(held["row", step])
+            held["twin", step] = move_twin(held["row", step])
+        if 2 <= turn <= n_sub + 1:
+            step = turn - 2
+            held["diagonal", step] = move_twin(held["across", step])
+        back = turn - lag
+        if 1 <= back <= n_sub:
+            step = back % n_sub
+            now["back", step] = move_across(held["away", step])
+        if 2 <= back:
+            step = back - 1
+            part = halves[step] + held["back", step].astype(jnp.float32)
+            if step > 1:
+                part = part + held["sum", step - 1].astype(jnp.float32)
+            now["sum", step] = move_on(part.astype(jnp.bfloat16))
+        step = turn - 2 if turn < lag + n_sub - 2 else 0
+        if turn == lag + n_sub - 2 or 1 <= step <= last:
+            own, away, other = experts_on_rows(
+                gates[step],
+                [held[name, step] for name in ("row", "twin", "across", "diagonal")],
+                expert_gate[0],
+                expert_up[0],
+                expert_down[0],
+                cap,
+            )
+            now["other", step] = other
+            held["own", step] = own
+            held["part", step] = away
+        step = turn - 3 if turn < lag + n_sub - 1 else 0
+        if turn == lag + n_sub - 1 or 1 <= step <= last:
+            met = move_twin(held["other", step]).astype(jnp.float32)
+            halves[step] = held["own", step].astype(jnp.float32) + met[:tokens]
+            now["away", step] = (held["part", step].astype(jnp.float32) + met[tokens:]).astype(
+                jnp.bfloat16
+            )
+        if turn < lag + n_sub:
+            met = meet(*now.values())
+            now = dict(zip(now.keys(), met))
+        held.update(now)
+    total = hidden.astype(jnp.float32) + halves[0] + held["back", 0].astype(jnp.float32)
+    if last:
+        total = total + held["sum", last].astype(jnp.float32)
+    return total.astype(jnp.bfloat16)[None]
 
 
 def per_device(

time: 188 us -> 199 us (1.059)
  waiting for transfers between devices: 97.4 us -> 64.2 us
  local copies, waits for them, and re-layouts: 14.9 us -> 44.9 us
  other arithmetic: 4.36 us -> 13.1 us
  Pallas kernels: 39.4 us -> 47.2 us
  starting transfers between devices: 31.1 us -> 27.5 us
    unnamed x42 -> x160, local copies, waits for them, and re-layouts: 12.9 us -> 38.7 us
    ppermute x26, waiting for transfers between devices: 72.6 us -> 55.5 us  [the longest x8 29.5 us: move_across(): return lax.ppermute(array, 'seq', across)]
    ppermute x1, waiting for transfers between devices: 9.09 us -> 0.01 us  [gathered_plan(): kv_diagonal = lax.ppermute(kv_away, 'seq', diagonal)]
    pallas_call x4 -> x13, Pallas kernels: 28.8 us -> 37.3 us  [the longest x4 37.3 us: experts_on_rows(): pl.pallas_call(functools.partial(experts_kernel, cap=cap, span=256), in_s...]
    convert_element_type x12, other arithmetic: 2.99 us -> 9.75 us  [the longest x3 5.15 us: gathered_plan(): now['sum', step] = move_on(part.astype(jnp.bfloat16))]
    ppermute x26, starting transfers between devices: 19.3 us -> 13.9 us  [the longest x8 7.58 us: move_across(): return lax.ppermute(array, 'seq', across)]
    ppermute x0 -> x3, local copies, waits for them, and re-layouts: none -> 3.96 us  [gathered_plan(): lax.ppermute(quad, 'sub', ring(steps))]
    ppermute x1, waiting for transfers between devices: 8.96 us -> 5 us  [gathered_plan(): lax.ppermute(table, 'seq', across)]
  transfers between devices with their start and end apart: 37 -> 37, of which waited for: 18 -> 16; matrix products, arithmetic and copies ran while one was open for 3% -> 8% of each run, Pallas kernels for 18% -> 21%
where the time goes in v3:
time: 199 us; the launch traced here: 198 us
  waiting for transfers between devices  64.2 us (32%)
  Pallas kernels  47.2 us (24%)
  local copies, waits for them, and re-layouts  44.9 us (23%)
  starting transfers between devices  27.5 us (14%)
  other arithmetic  13.1 us (7%)
    unnamed x160, local copies, waits for them, and re-layouts  38.7 us
    pallas_call x4, Pallas kernels, experts_on_rows(): pl.pallas_call(functools.partial(experts_kernel, cap=cap, span=256), in_s...  37.3 us
    ppermute x8, waiting for transfers between devices, move_across(): return lax.ppermute(array, 'seq', across)  29.5 us
    ppermute x6, waiting for transfers between devices, move_on(): return lax.ppermute(array, 'sub', ring(1))  19.5 us
    pallas_call x2, Pallas kernels, attend(): pl.pallas_call(functools.partial(attend_kernel, scale=1.0 / HD ** 0.5), i...  9.55 us
    ppermute x8, starting transfers between devices, move_across(): return lax.ppermute(array, 'seq', across)  7.58 us
    ppermute x12, waiting for transfers between devices, move_twin(): return lax.ppermute(array, 'seq', twin)  6.52 us
    ppermute x3, starting transfers between devices, gathered_plan(): lax.ppermute(quad, 'sub', ring(steps))  5.63 us
  transfers between devices with their start and end apart: 37, of which 16 were waited for; matrix products, arithmetic and copies ran while one was open for 8% of the time, Pallas kernels for 21%

profile of v3, /device:TPU:0, one launch (start us, length us, event | category | flops | bytes accessed | tf_op | source)
XLA Modules:
  0.0 197.7 jit_solution(15651797222595793957)
XLA Ops:
  2.6 2.9 %collective-permute-start.1 = (bf16[128,1280]{1,0:T(8,128)(2,1)S(1)}, bf16[128,1280]{1,0:T(8,128)(2,1)S(1)}, u32[]{:S(2)}, u32[]{:S(2)}) collective-permute-start(bf16[128,1280]{1,0:T(8,128)(2,1)S(1)} %pad_maximum_fusion), channel_id=1, source_target_pairs={{0,8},{4,12},{8,0},{12,4},{1,9},{5,13},{9,1},{13,5},{2,10},{6,14},... | collective-permute-start | bytes 983048 | tf_op jit(solution)/shard_map/ppermute | solution.py:298
  8.2 1.8 collective-permute-start.3
  10.0 5.0 %collective-permute-done.3.refs_2_ = bf16[16,128]{1,0:T(8,128)(2,1)S(1)} collective-permute-done((bf16[16,128]{1,0:T(8,128)(2,1)S(1)}, bf16[16,128]{1,0:T(8,128)(2,1)S(1)}, u32[]{:S(2)}, u32[]{:S(2)}) %collective-permute-start.3) | collective-permute-done | bytes 4128 | tf_op jit(solution)/shard_map/ppermute | solution.py:314
  15.7 2.3 %collective-permute-done.4.refs_3_ = bf16[16,128]{1,0:T(8,128)(2,1)S(1)} collective-permute-done((bf16[16,128]{1,0:T(8,128)(2,1)S(1)}, bf16[16,128]{1,0:T(8,128)(2,1)S(1)}, u32[]{:S(2)}, u32[]{:S(2)}) %collective-permute-start.4) | collective-permute-done | bytes 4128 | tf_op jit(solution)/shard_map/ppermute | solution.py:315
  23.3 5.2 %shard_map.111 = bf16[128,2048]{1,0:T(8,128)(2,1)} custom-call(s32[7]{0:T(128)S(1)} %stack.66.place_ref, bf16[128,1280]{1,0:T(8,128)(2,1)S(1)} %copy-done.11, bf16[128,256]{1,0:T(8,128)(2,1)S(1)} %pad_maximum_fusion.1.refs_0_, bf16[128,256]{1,0:T(8,128)(2,1)S(1)} %copy-done.43, bf16[128,1280]{1,0:T(8,128)(2,1)S(1)} %copy-done.11, ...), custom_call_target="tpu_custom_call" | custom-call | flops 805306368 | bytes 5242880 | tf_op jit(solution)/shard_map/pallas_call | solution.py:114
  28.5 1.8 collective-permute-start.7
  33.1 2.5 %collective-permute-start.9 = (bf16[4,16,128]{2,0,1:T(4,128)(2,1)}, bf16[4,16,128]{2,0,1:T(4,128)(2,1)}, u32[]{:S(2)}, u32[]{:S(2)}) collective-permute-start(bf16[4,16,128]{2,0,1:T(4,128)(2,1)} %pad_maximum_fusion.3), channel_id=1, source_target_pairs={{0,3},{1,2},{3,0},{2,1},{4,7},{5,6},{7,4},{6,5},{8,11},{9,10},{11,... | collective-permute-start | bytes 49160 | tf_op jit(solution)/shard_map/ppermute | solution.py:318
  43.3 4.4 %shard_map.110.own_ref = f32[128,2048]{1,0:T(8,128)S(1)} custom-call(s32[7]{0:T(128)S(1)} %stack.65.place_ref, bf16[128,2048]{1,0:T(8,128)(2,1)S(1)} %bitcast.62, bf16[128,256]{1,0:T(8,128)(2,1)S(1)} %pad_maximum_fusion.1.refs_0_, bf16[128,256]{1,0:T(8,128)(2,1)S(1)} %copy-done.44, bf16[128,1280]{1,0:T(8,128)(2,1)S(1)} %copy-done.12, ...), custom_call_target="tpu_custom_call" | custom-call | flops 805306368 | bytes 5242880 | tf_op jit(solution)/shard_map/pallas_call | solution.py:114
  55.7 10.2 %collective-permute-done.12.refs_0_ = bf16[128,2048]{1,0:T(8,128)(2,1)} collective-permute-done((bf16[128,2048]{1,0:T(8,128)(2,1)S(1)}, bf16[128,2048]{1,0:T(8,128)(2,1)}, u32[]{:S(2)}, u32[]{:S(2)}) %collective-permute-start.12) | collective-permute-done | bytes 524320 | tf_op jit(solution)/shard_map/ppermute | solution.py:348
  65.9 1.9 collective-permute-done.13.refs_1_
  68.9 10.1 %collective-permute-done.15.refs_0_ = bf16[128,2048]{1,0:T(8,128)(2,1)} collective-permute-done((bf16[128,2048]{1,0:T(8,128)(2,1)}, bf16[128,2048]{1,0:T(8,128)(2,1)}, u32[]{:S(2)}, u32[]{:S(2)}) %collective-permute-start.15) | collective-permute-done | bytes 524320 | tf_op jit(solution)/shard_map/ppermute | solution.py:348
  79.0 1.7 collective-permute-done.16.refs_1_
  83.0 1.9 copy-done.1
  84.9 1.9 copy-done.5
  86.8 9.6 %shard_map.117 = (bf16[128,2048]{1,0:T(8,128)(2,1)S(1)}, bf16[128,2048]{1,0:T(8,128)(2,1)S(1)}, bf16[256,2048]{1,0:T(8,128)(2,1)S(1)}) custom-call(f32[4,128]{1,0:T(4,128)S(1)} %get-tuple-element.96.gate_ref, bf16[128,2048]{1,0:T(8,128)(2,1)} %get-tuple-element.59.refs_0_, bf16[128,2048]{1,0:T(8,128)(2,1)} %collective-permute-done.19.refs_1_, ...), custom_call_target="tpu_custom_call" | custom-call | flops 3019898880 | bytes 13631488 | tf_op jit(solution)/shard_map/pallas_call | solution.py:230
  100.6 2.0 %collective-permute-done.22.refs_1_ = bf16[128,2048]{1,0:T(8,128)(2,1)S(1)} collective-permute-done((bf16[128,2048]{1,0:T(8,128)(2,1)}, bf16[128,2048]{1,0:T(8,128)(2,1)S(1)}, u32[]{:S(2)}, u32[]{:S(2)}) %collective-permute-start.22) | collective-permute-done | bytes 524320 | tf_op jit(solution)/shard_map/ppermute | solution.py:345
  103.4 1.9 copy-done.2
  105.2 1.9 copy-done.6
  107.1 9.3 %shard_map.119 = (bf16[128,2048]{1,0:T(8,128)(2,1)S(1)}, bf16[128,2048]{1,0:T(8,128)(2,1)S(1)}, bf16[256,2048]{1,0:T(8,128)(2,1)S(1)}) custom-call(f32[4,128]{1,0:T(4,128)S(1)} %get-tuple-element.95.gate_ref, bf16[128,2048]{1,0:T(8,128)(2,1)} %get-tuple-element.60.refs_0_, bf16[128,2048]{1,0:T(8,128)(2,1)S(1)} %collective-permute-done.22.refs_1_, ...), custom_call_target="tpu_custom_call" | custom-call | flops 3019898880 | bytes 13631488 | tf_op jit(solution)/shard_map/pallas_call | solution.py:230
  120.5 2.0 %collective-permute-done.26.refs_1_ = bf16[128,2048]{1,0:T(8,128)(2,1)S(1)} collective-permute-done((bf16[128,2048]{1,0:T(8,128)(2,1)}, bf16[128,2048]{1,0:T(8,128)(2,1)S(1)}, u32[]{:S(2)}, u32[]{:S(2)}) %collective-permute-start.26) | collective-permute-done | bytes 524320 | tf_op jit(solution)/shard_map/ppermute | solution.py:345
  123.3 1.9 copy-done.3
  125.1 1.9 copy-done.7
  127.0 9.3 %shard_map.121 = (bf16[128,2048]{1,0:T(8,128)(2,1)S(1)}, bf16[128,2048]{1,0:T(8,128)(2,1)S(1)}, bf16[256,2048]{1,0:T(8,128)(2,1)S(1)}) custom-call(f32[4,128]{1,0:T(4,128)S(1)} %get-tuple-element.94.gate_ref, bf16[128,2048]{1,0:T(8,128)(2,1)} %get-tuple-element.63.refs_0_, bf16[128,2048]{1,0:T(8,128)(2,1)S(1)} %collective-permute-done.26.refs_1_, ...), custom_call_target="tpu_custom_call" | custom-call | flops 3019898880 | bytes 13631488 | tf_op jit(solution)/shard_map/pallas_call | solution.py:230
  141.1 1.7 fusion.13
  142.9 2.2 %collective-permute-start.30 = (bf16[128,2048]{1,0:T(8,128)(2,1)S(1)}, bf16[128,2048]{1,0:T(8,128)(2,1)S(1)}, u32[]{:S(2)}, u32[]{:S(2)}) collective-permute-start(bf16[128,2048]{1,0:T(8,128)(2,1)S(1)} %fusion.13), channel_id=1, source_target_pairs={{0,1},{1,3},{3,2},{2,0},{4,5},{5,7},{7,6},{6,4},{8,9},{9,11},{11,1... | collective-permute-start | bytes 1572872 | tf_op jit(solution)/shard_map/ppermute | solution.py:351
  145.1 1.9 copy-done.4
  147.0 1.9 copy-done.8
  148.9 9.1 %shard_map.115 = (bf16[128,2048]{1,0:T(8,128)(2,1)S(1)}, bf16[128,2048]{1,0:T(8,128)(2,1)S(1)}, bf16[256,2048]{1,0:T(8,128)(2,1)S(1)}) custom-call(f32[4,128]{1,0:T(4,128)S(1)} %get-tuple-element.93.gate_ref, bf16[128,2048]{1,0:T(8,128)(2,1)S(1)} %copy-done.25, bf16[128,2048]{1,0:T(8,128)(2,1)S(1)} %collective-permute-done.11.refs_1_, ...), custom_call_target="tpu_custom_call" | custom-call | flops 3019898880 | bytes 13631488 | tf_op jit(solution)/shard_map/pallas_call | solution.py:230
  167.4 9.2 %collective-permute-done.33.refs_0_ = bf16[128,2048]{1,0:T(8,128)(2,1)S(1)} collective-permute-done((bf16[128,2048]{1,0:T(8,128)(2,1)}, bf16[128,2048]{1,0:T(8,128)(2,1)S(1)}, u32[]{:S(2)}, u32[]{:S(2)}) %collective-permute-start.33) | collective-permute-done | bytes 524320 | tf_op jit(solution)/shard_map/ppermute | solution.py:348
  176.6 2.9 %collective-permute-done.34.refs_1_ = bf16[128,2048]{1,0:T(8,128)(2,1)S(1)} collective-permute-done((bf16[128,2048]{1,0:T(8,128)(2,1)S(1)}, bf16[128,2048]{1,0:T(8,128)(2,1)S(1)}, u32[]{:S(2)}, u32[]{:S(2)}) %collective-permute-start.34) | collective-permute-done | bytes 524320 | tf_op jit(solution)/shard_map/ppermute | solution.py:351
  180.3 1.9 fusion.2
  183.5 13.0 %collective-permute-done.36 = bf16[128,2048]{1,0:T(8,128)(2,1)S(1)} collective-permute-done((bf16[128,2048]{1,0:T(8,128)(2,1)S(1)}, bf16[128,2048]{1,0:T(8,128)(2,1)S(1)}, u32[]{:S(2)}, u32[]{:S(2)}) %collective-permute-start.36) | collective-permute-done | bytes 524320 | tf_op jit(solution)/shard_map/ppermute | solution.py:351
  (254 shorter events, 59.9 us)
Async XLA Ops:
  0.0 20.6 %collective-permute-start.6 = (bf16[512,2048]{1,0:T(8,128)(2,1)}, bf16[512,2048]{1,0:T(8,128)(2,1)}, u32[]{:S(2)}, u32[]{:S(2)}) collective-permute-start(bf16[512,2048]{1,0:T(8,128)(2,1)} %refs_4_.3), channel_id=1, source_target_pairs={{0,4},{4,0},{8,12},{12,8},{1,5},{5,1},{9,13},{13,9},{2,6},{6,2},{1... | collective-permute-start | bytes 6291464 | tf_op jit(solution)/shard_map/ppermute | solution.py:301
  1.5 17.9 %collective-permute-start = (bf16[128,256]{1,0:T(8,128)(2,1)S(1)}, bf16[128,256]{1,0:T(8,128)(2,1)S(1)}, u32[]{:S(2)}, u32[]{:S(2)}) collective-permute-start(bf16[128,256]{1,0:T(8,128)(2,1)S(1)} %pad_maximum_fusion.1.refs_0_), channel_id=1, source_target_pairs={{0,4},{4,0},{8,12},{12,8},{1,5},{5,1},{9,13},{13,9},{2,6},{6,2},{1... | collective-permute-start | bytes 196616 | tf_op jit(solution)/shard_map/ppermute | solution.py:299
  2.6 15.4 %collective-permute-start.1 = (bf16[128,1280]{1,0:T(8,128)(2,1)S(1)}, bf16[128,1280]{1,0:T(8,128)(2,1)S(1)}, u32[]{:S(2)}, u32[]{:S(2)}) collective-permute-start(bf16[128,1280]{1,0:T(8,128)(2,1)S(1)} %pad_maximum_fusion), channel_id=1, source_target_pairs={{0,8},{4,12},{8,0},{12,4},{1,9},{5,13},{9,1},{13,5},{2,10},{6,14},... | collective-permute-start | bytes 983048 | tf_op jit(solution)/shard_map/ppermute | solution.py:298
  5.5 14.5 %collective-permute-start.5 = (bf16[128,256]{1,0:T(8,128)(2,1)S(1)}, bf16[128,256]{1,0:T(8,128)(2,1)S(1)}, u32[]{:S(2)}, u32[]{:S(2)}) collective-permute-start(bf16[128,256]{1,0:T(8,128)(2,1)S(1)} %pad_maximum_fusion.2), channel_id=1, source_target_pairs={{0,12},{4,8},{8,4},{12,0},{1,13},{5,9},{9,5},{13,1},{2,14},{6,10},... | collective-permute-start | bytes 196616 | tf_op jit(solution)/shard_map/ppermute | solution.py:300
  8.2 6.8 %collective-permute-start.3 = (bf16[16,128]{1,0:T(8,128)(2,1)S(1)}, bf16[16,128]{1,0:T(8,128)(2,1)S(1)}, u32[]{:S(2)}, u32[]{:S(2)}) collective-permute-start(bf16[16,128]{1,0:T(8,128)(2,1)S(1)} %select_reduce_fusion), channel_id=1, source_target_pairs={{0,8},{4,12},{8,0},{12,4},{1,9},{5,13},{9,1},{13,5},{2,10},{6,14},... | collective-permute-start | bytes 12296 | tf_op jit(solution)/shard_map/ppermute | solution.py:314
  28.5 20.2 %collective-permute-start.7 = (bf16[128,2048]{1,0:T(8,128)(2,1)}, bf16[128,2048]{1,0:T(8,128)(2,1)S(1)}, u32[]{:S(2)}, u32[]{:S(2)}) collective-permute-start(bf16[128,2048]{1,0:T(8,128)(2,1)} %shard_map.111), channel_id=1, source_target_pairs={{0,8},{4,12},{8,0},{12,4},{1,9},{5,13},{9,1},{13,5},{2,10},{6,14},... | collective-permute-start | bytes 1572872 | tf_op jit(solution)/shard_map/ppermute | solution.py:327
  31.5 5.7 %collective-permute-start.8 = (bf16[4,16,128]{2,0,1:T(4,128)(2,1)}, bf16[4,16,128]{2,0,1:T(4,128)(2,1)}, u32[]{:S(2)}, u32[]{:S(2)}) collective-permute-start(bf16[4,16,128]{2,0,1:T(4,128)(2,1)} %pad_maximum_fusion.3), channel_id=1, source_target_pairs={{0,1},{1,3},{3,2},{2,0},{4,5},{5,7},{7,6},{6,4},{8,9},{9,11},{11,1... | collective-permute-start | bytes 49160 | tf_op jit(solution)/shard_map/ppermute | solution.py:318
  33.1 5.9 %collective-permute-start.9 = (bf16[4,16,128]{2,0,1:T(4,128)(2,1)}, bf16[4,16,128]{2,0,1:T(4,128)(2,1)}, u32[]{:S(2)}, u32[]{:S(2)}) collective-permute-start(bf16[4,16,128]{2,0,1:T(4,128)(2,1)} %pad_maximum_fusion.3), channel_id=1, source_target_pairs={{0,3},{1,2},{3,0},{2,1},{4,7},{5,6},{7,4},{6,5},{8,11},{9,10},{11,... | collective-permute-start | bytes 49160 | tf_op jit(solution)/shard_map/ppermute | solution.py:318
  35.6 4.7 %collective-permute-start.10 = (bf16[4,16,128]{2,0,1:T(4,128)(2,1)}, bf16[4,16,128]{2,0,1:T(4,128)(2,1)}, u32[]{:S(2)}, u32[]{:S(2)}) collective-permute-start(bf16[4,16,128]{2,0,1:T(4,128)(2,1)} %pad_maximum_fusion.3), channel_id=1, source_target_pairs={{0,2},{1,0},{3,1},{2,3},{4,6},{5,4},{7,5},{6,7},{8,10},{9,8},{11,9... | collective-permute-start | bytes 49160 | tf_op jit(solution)/shard_map/ppermute | solution.py:318
  54.1 11.8 %collective-permute-start.12 = (bf16[128,2048]{1,0:T(8,128)(2,1)S(1)}, bf16[128,2048]{1,0:T(8,128)(2,1)}, u32[]{:S(2)}, u32[]{:S(2)}) collective-permute-start(bf16[128,2048]{1,0:T(8,128)(2,1)S(1)} %get-tuple-element.56.refs_0_), channel_id=1, source_target_pairs={{0,8},{4,12},{8,0},{12,4},{1,9},{5,13},{9,1},{13,5},{2,10},{6,14},... | collective-permute-start | bytes 1572872 | tf_op jit(solution)/shard_map/ppermute | solution.py:348
  54.9 12.9 %collective-permute-start.13 = (bf16[128,2048]{1,0:T(8,128)(2,1)S(1)}, bf16[128,2048]{1,0:T(8,128)(2,1)}, u32[]{:S(2)}, u32[]{:S(2)}) collective-permute-start(bf16[128,2048]{1,0:T(8,128)(2,1)S(1)} %get-tuple-element.56.refs_0_), channel_id=1, source_target_pairs={{0,1},{1,3},{3,2},{2,0},{4,5},{5,7},{7,6},{6,4},{8,9},{9,11},{11,1... | collective-permute-start | bytes 1572872 | tf_op jit(solution)/shard_map/ppermute | solution.py:351
  67.8 11.3 %collective-permute-start.15 = (bf16[128,2048]{1,0:T(8,128)(2,1)}, bf16[128,2048]{1,0:T(8,128)(2,1)}, u32[]{:S(2)}, u32[]{:S(2)}) collective-permute-start(bf16[128,2048]{1,0:T(8,128)(2,1)} %get-tuple-element.59.refs_0_), channel_id=1, source_target_pairs={{0,8},{4,12},{8,0},{12,4},{1,9},{5,13},{9,1},{13,5},{2,10},{6,14},... | collective-permute-start | bytes 1572872 | tf_op jit(solution)/shard_map/ppermute | solution.py:348
  68.9 11.8 %collective-permute-start.16 = (bf16[128,2048]{1,0:T(8,128)(2,1)}, bf16[128,2048]{1,0:T(8,128)(2,1)}, u32[]{:S(2)}, u32[]{:S(2)}) collective-permute-start(bf16[128,2048]{1,0:T(8,128)(2,1)} %get-tuple-element.59.refs_0_), channel_id=1, source_target_pairs={{0,1},{1,3},{3,2},{2,0},{4,5},{5,7},{7,6},{6,4},{8,9},{9,11},{11,1... | collective-permute-start | bytes 1572872 | tf_op jit(solution)/shard_map/ppermute | solution.py:351
  68.9 13.0 %collective-permute-start.19 = (bf16[128,2048]{1,0:T(8,128)(2,1)}, bf16[128,2048]{1,0:T(8,128)(2,1)}, u32[]{:S(2)}, u32[]{:S(2)}) collective-permute-start(bf16[128,2048]{1,0:T(8,128)(2,1)} %get-tuple-element.59.refs_0_), channel_id=1, source_target_pairs={{0,4},{4,0},{8,12},{12,8},{1,5},{5,1},{9,13},{13,9},{2,6},{6,2},{1... | collective-permute-start | bytes 1572872 | tf_op jit(solution)/shard_map/ppermute | solution.py:345
  80.9 18.1 %collective-permute-start.17 = (bf16[128,2048]{1,0:T(8,128)(2,1)}, bf16[128,2048]{1,0:T(8,128)(2,1)}, u32[]{:S(2)}, u32[]{:S(2)}) collective-permute-start(bf16[128,2048]{1,0:T(8,128)(2,1)} %get-tuple-element.60.refs_0_), channel_id=1, source_target_pairs={{0,8},{4,12},{8,0},{12,4},{1,9},{5,13},{9,1},{13,5},{2,10},{6,14},... | collective-permute-start | bytes 1572872 | tf_op jit(solution)/shard_map/ppermute | solution.py:348
  81.9 17.1 %collective-permute-start.18 = (bf16[128,2048]{1,0:T(8,128)(2,1)}, bf16[128,2048]{1,0:T(8,128)(2,1)}, u32[]{:S(2)}, u32[]{:S(2)}) collective-permute-start(bf16[128,2048]{1,0:T(8,128)(2,1)} %get-tuple-element.60.refs_0_), channel_id=1, source_target_pairs={{0,1},{1,3},{3,2},{2,0},{4,5},{5,7},{7,6},{6,4},{8,9},{9,11},{11,1... | collective-permute-start | bytes 1572872 | tf_op jit(solution)/shard_map/ppermute | solution.py:351
  99.0 17.5 %collective-permute-start.24 = (bf16[256,2048]{1,0:T(8,128)(2,1)}, bf16[256,2048]{1,0:T(8,128)(2,1)S(1)}, u32[]{:S(2)}, u32[]{:S(2)}) collective-permute-start(bf16[256,2048]{1,0:T(8,128)(2,1)} %get-tuple-element.67), channel_id=1, source_target_pairs={{0,4},{4,0},{8,12},{12,8},{1,5},{5,1},{9,13},{13,9},{2,6},{6,2},{1... | collective-permute-start | bytes 3145736 | tf_op jit(solution)/shard_map/ppermute | solution.py:345
  99.5 3.9 %collective-permute-start.23 = (bf16[128,2048]{1,0:T(8,128)(2,1)}, bf16[128,2048]{1,0:T(8,128)(2,1)S(1)}, u32[]{:S(2)}, u32[]{:S(2)}) collective-permute-start(bf16[128,2048]{1,0:T(8,128)(2,1)} %get-tuple-element.64.refs_2_), channel_id=1, source_target_pairs={{0,4},{4,0},{8,12},{12,8},{1,5},{5,1},{9,13},{13,9},{2,6},{6,2},{1... | collective-permute-start | bytes 1572872 | tf_op jit(solution)/shard_map/ppermute | solution.py:345
  99.6 19.2 %collective-permute-start.21 = (bf16[128,2048]{1,0:T(8,128)(2,1)}, bf16[128,2048]{1,0:T(8,128)(2,1)}, u32[]{:S(2)}, u32[]{:S(2)}) collective-permute-start(bf16[128,2048]{1,0:T(8,128)(2,1)} %get-tuple-element.63.refs_0_), channel_id=1, source_target_pairs={{0,8},{4,12},{8,0},{12,4},{1,9},{5,13},{9,1},{13,5},{2,10},{6,14},... | collective-permute-start | bytes 1572872 | tf_op jit(solution)/shard_map/ppermute | solution.py:348
  118.8 17.5 %collective-permute-start.28 = (bf16[256,2048]{1,0:T(8,128)(2,1)}, bf16[256,2048]{1,0:T(8,128)(2,1)S(1)}, u32[]{:S(2)}, u32[]{:S(2)}) collective-permute-start(bf16[256,2048]{1,0:T(8,128)(2,1)} %get-tuple-element.72), channel_id=1, source_target_pairs={{0,4},{4,0},{8,12},{12,8},{1,5},{5,1},{9,13},{13,9},{2,6},{6,2},{1... | collective-permute-start | bytes 3145736 | tf_op jit(solution)/shard_map/ppermute | solution.py:345
  119.4 3.9 %collective-permute-start.27 = (bf16[128,2048]{1,0:T(8,128)(2,1)}, bf16[128,2048]{1,0:T(8,128)(2,1)S(1)}, u32[]{:S(2)}, u32[]{:S(2)}) collective-permute-start(bf16[128,2048]{1,0:T(8,128)(2,1)} %get-tuple-element.69.refs_2_), channel_id=1, source_target_pairs={{0,4},{4,0},{8,12},{12,8},{1,5},{5,1},{9,13},{13,9},{2,6},{6,2},{1... | collective-permute-start | bytes 1572872 | tf_op jit(solution)/shard_map/ppermute | solution.py:345
  119.5 19.2 %collective-permute-start.25 = (bf16[128,2048]{1,0:T(8,128)(2,1)}, bf16[128,2048]{1,0:T(8,128)(2,1)S(1)}, u32[]{:S(2)}, u32[]{:S(2)}) collective-permute-start(bf16[128,2048]{1,0:T(8,128)(2,1)} %get-tuple-element.68), channel_id=1, source_target_pairs={{0,8},{4,12},{8,0},{12,4},{1,9},{5,13},{9,1},{13,5},{2,10},{6,14},... | collective-permute-start | bytes 1572872 | tf_op jit(solution)/shard_map/ppermute | solution.py:348
  139.5 18.6 %collective-permute-start.31 = (bf16[256,2048]{1,0:T(8,128)(2,1)}, bf16[256,2048]{1,0:T(8,128)(2,1)S(1)}, u32[]{:S(2)}, u32[]{:S(2)}) collective-permute-start(bf16[256,2048]{1,0:T(8,128)(2,1)} %get-tuple-element.78), channel_id=1, source_target_pairs={{0,4},{4,0},{8,12},{12,8},{1,5},{5,1},{9,13},{13,9},{2,6},{6,2},{1... | collective-permute-start | bytes 3145736 | tf_op jit(solution)/shard_map/ppermute | solution.py:345
  139.6 5.5 %collective-permute-start.11 = (bf16[128,2048]{1,0:T(8,128)(2,1)}, bf16[128,2048]{1,0:T(8,128)(2,1)S(1)}, u32[]{:S(2)}, u32[]{:S(2)}) collective-permute-start(bf16[128,2048]{1,0:T(8,128)(2,1)} %copy-done.24), channel_id=1, source_target_pairs={{0,4},{4,0},{8,12},{12,8},{1,5},{5,1},{9,13},{13,9},{2,6},{6,2},{1... | collective-permute-start | bytes 1572872 | tf_op jit(solution)/shard_map/ppermute | solution.py:345
  140.0 5.1 %collective-permute-start.14 = (bf16[128,2048]{1,0:T(8,128)(2,1)}, bf16[128,2048]{1,0:T(8,128)(2,1)S(1)}, u32[]{:S(2)}, u32[]{:S(2)}) collective-permute-start(bf16[128,2048]{1,0:T(8,128)(2,1)} %get-tuple-element.57.refs_2_), channel_id=1, source_target_pairs={{0,4},{4,0},{8,12},{12,8},{1,5},{5,1},{9,13},{13,9},{2,6},{6,2},{1... | collective-permute-start | bytes 1572872 | tf_op jit(solution)/shard_map/ppermute | solution.py:345
  140.2 20.3 %collective-permute-start.29 = (bf16[128,2048]{1,0:T(8,128)(2,1)}, bf16[128,2048]{1,0:T(8,128)(2,1)S(1)}, u32[]{:S(2)}, u32[]{:S(2)}) collective-permute-start(bf16[128,2048]{1,0:T(8,128)(2,1)} %get-tuple-element.73), channel_id=1, source_target_pairs={{0,8},{4,12},{8,0},{12,4},{1,9},{5,13},{9,1},{13,5},{2,10},{6,14},... | collective-permute-start | bytes 1572872 | tf_op jit(solution)/shard_map/ppermute | solution.py:348
  142.9 17.6 %collective-permute-start.30 = (bf16[128,2048]{1,0:T(8,128)(2,1)S(1)}, bf16[128,2048]{1,0:T(8,128)(2,1)S(1)}, u32[]{:S(2)}, u32[]{:S(2)}) collective-permute-start(bf16[128,2048]{1,0:T(8,128)(2,1)S(1)} %fusion.13), channel_id=1, source_target_pairs={{0,1},{1,3},{3,2},{2,0},{4,5},{5,7},{7,6},{6,4},{8,9},{9,11},{11,1... | collective-permute-start | bytes 1572872 | tf_op jit(solution)/shard_map/ppermute | solution.py:351
  162.0 3.6 %collective-permute-start.32 = (bf16[256,2048]{1,0:T(8,128)(2,1)}, bf16[256,2048]{1,0:T(8,128)(2,1)S(1)}, u32[]{:S(2)}, u32[]{:S(2)}) collective-permute-start(bf16[256,2048]{1,0:T(8,128)(2,1)} %get-tuple-element.79), channel_id=1, source_target_pairs={{0,4},{4,0},{8,12},{12,8},{1,5},{5,1},{9,13},{13,9},{2,6},{6,2},{1... | collective-permute-start | bytes 3145736 | tf_op jit(solution)/shard_map/ppermute | solution.py:345
  162.1 14.5 %collective-permute-start.33 = (bf16[128,2048]{1,0:T(8,128)(2,1)}, bf16[128,2048]{1,0:T(8,128)(2,1)S(1)}, u32[]{:S(2)}, u32[]{:S(2)}) collective-permute-start(bf16[128,2048]{1,0:T(8,128)(2,1)} %get-tuple-element.80), channel_id=1, source_target_pairs={{0,8},{4,12},{8,0},{12,4},{1,9},{5,13},{9,1},{13,5},{2,10},{6,14},... | collective-permute-start | bytes 1572872 | tf_op jit(solution)/shard_map/ppermute | solution.py:348
  164.5 15.0 %collective-permute-start.34 = (bf16[128,2048]{1,0:T(8,128)(2,1)S(1)}, bf16[128,2048]{1,0:T(8,128)(2,1)S(1)}, u32[]{:S(2)}, u32[]{:S(2)}) collective-permute-start(bf16[128,2048]{1,0:T(8,128)(2,1)S(1)} %fusion.6), channel_id=1, source_target_pairs={{0,1},{1,3},{3,2},{2,0},{4,5},{5,7},{7,6},{6,4},{8,9},{9,11},{11,1... | collective-permute-start | bytes 1572872 | tf_op jit(solution)/shard_map/ppermute | solution.py:351
  182.3 14.2 %collective-permute-start.36 = (bf16[128,2048]{1,0:T(8,128)(2,1)S(1)}, bf16[128,2048]{1,0:T(8,128)(2,1)S(1)}, u32[]{:S(2)}, u32[]{:S(2)}) collective-permute-start(bf16[128,2048]{1,0:T(8,128)(2,1)S(1)} %fusion.2), channel_id=1, source_target_pairs={{0,1},{1,3},{3,2},{2,0},{4,5},{5,7},{7,6},{6,4},{8,9},{9,11},{11,1... | collective-permute-start | bytes 1572872 | tf_op jit(solution)/shard_map/ppermute | solution.py:351
  182.5 14.0 %collective-permute-start.35 = (bf16[128,2048]{1,0:T(8,128)(2,1)S(1)}, bf16[128,2048]{1,0:T(8,128)(2,1)S(1)}, u32[]{:S(2)}, u32[]{:S(2)}) collective-permute-start(bf16[128,2048]{1,0:T(8,128)(2,1)S(1)} %copy-done.59), channel_id=1, source_target_pairs={{0,8},{4,12},{8,0},{12,4},{1,9},{5,13},{9,1},{13,5},{2,10},{6,14},... | collective-permute-start | bytes 1572872 | tf_op jit(solution)/shard_map/ppermute | solution.py:348
  (85 other events, 550.6 us)

commit v4 on v2

--- a/solution.py
+++ b/solution.py
@@ -11,6 +11,7 @@
 HD = 128
 QH = 16
 KVH = 2
+VMEM_GRANT = 60 * 1024 * 1024
 
 
 def attend_head(queries, keys_one, values_one, block):
@@ -57,8 +58,53 @@
     return ranks.reshape(items).astype(jnp.int32)
 
 
+def pack_kernel(chip_ref, query_ref, key_ref, value_ref, id_ref, gate_ref, away_ref, here_kv_ref, away_kv_ref):
+    tokens = query_ref.shape[0]
+    head_size = key_ref.shape[1] // 2
+    chip_width = away_ref.shape[1]
+    chip = chip_ref[0]
+    experts = here_kv_ref.shape[0] - tokens
+    away_ref[...] = query_ref[:, pl.ds(pl.multiple_of((1 - chip) * chip_width, chip_width), chip_width)]
+    number = lax.broadcasted_iota(jnp.int32, (experts, tokens), 0)
+    table = jnp.zeros((experts, tokens), jnp.float32)
+    for choice in range(id_ref.shape[0]):
+        table += jnp.where(
+            number == id_ref[choice : choice + 1, :],
+            gate_ref[choice : choice + 1, :].astype(jnp.float32),
+            0.0,
+        )
+    for out_ref, head in ((here_kv_ref, chip), (away_kv_ref, 1 - chip)):
+        columns = pl.ds(pl.multiple_of(head * head_size, head_size), head_size)
+        out_ref[0:tokens, 0:head_size] = key_ref[:, columns]
+        out_ref[0:tokens, head_size:] = value_ref[:, columns]
+        out_ref[tokens:, 0:head_size] = table.astype(jnp.bfloat16)
+        out_ref[tokens:, head_size:] = jnp.zeros((experts, head_size), jnp.bfloat16)
+
+
+def pack(chip, queries, keys, values, ids, gates, experts):
+    tokens, width = queries.shape
+    kv = jax.ShapeDtypeStruct((tokens + experts, keys.shape[1]), jnp.bfloat16)
+    return pl.pallas_call(
+        pack_kernel,
+        in_specs=[pl.BlockSpec(memory_space=pltpu.SMEM)]
+        + [pl.BlockSpec(memory_space=pltpu.VMEM)] * 5,
+        out_specs=[pl.BlockSpec(memory_space=pltpu.VMEM)] * 3,
+        out_shape=[jax.ShapeDtypeStruct((tokens, width // 2), jnp.bfloat16), kv, kv],
+        compiler_params=pltpu.CompilerParams(vmem_limit_bytes=VMEM_GRANT),
+    )(chip.reshape(1), queries, keys, values, ids, gates)
+
+
 def attend_kernel(place_ref, query_ref, *refs, scale):
-    kv_refs, (w_own_ref, w_other_ref, out_ref, keys, values, heads) = refs[:4], refs[4:]
+    kv_refs, (w_own_ref, w_other_ref, out_ref, keys, values, heads, w_own, w_other, done) = (
+        refs[:4],
+        refs[4:],
+    )
+    fetches = [
+        pltpu.make_async_copy(w_own_ref, w_own, done.at[0]),
+        pltpu.make_async_copy(w_other_ref, w_other, done.at[1]),
+    ]
+    for fetch in fetches:
+        fetch.start()
     rows = keys.shape[0] // 4
     head_size = keys.shape[1]
     core = place_ref[0]
@@ -68,9 +114,8 @@
     col_pos = jnp.concatenate([place_ref[3 + part] * rows + lane for part in range(4)], axis=1)
     allowed = row_pos >= col_pos
     for part, kv_ref in enumerate(kv_refs):
-        start = kv_ref.shape[1] - 2 * head_size
-        keys[part * rows : (part + 1) * rows, :] = kv_ref[:, start : start + head_size]
-        values[part * rows : (part + 1) * rows, :] = kv_ref[:, start + head_size :]
+        keys[part * rows : (part + 1) * rows, :] = kv_ref[0:rows, 0:head_size]
+        values[part * rows : (part + 1) * rows, :] = kv_ref[0:rows, head_size:]
     key_block = keys[...]
     value_block = values[...]
     for head in range(heads.shape[1] // head_size):
@@ -87,12 +132,14 @@
         heads[:, head * head_size : (head + 1) * head_size] = jnp.dot(
             probs, value_block, preferred_element_type=jnp.float32
         ).astype(jnp.bfloat16)
+    for fetch in fetches:
+        fetch.wait()
     half = heads.shape[1] // 2
     own = heads[:, pl.ds(pl.multiple_of(core * half, half), half)]
     other = heads[:, pl.ds(pl.multiple_of((1 - core) * half, half), half)]
     out_ref[...] = (
-        jnp.dot(own, w_own_ref[...], preferred_element_type=jnp.float32)
-        + jnp.dot(other, w_other_ref[...], preferred_element_type=jnp.float32)
+        jnp.dot(own, w_own[...], preferred_element_type=jnp.float32)
+        + jnp.dot(other, w_other[...], preferred_element_type=jnp.float32)
     ).astype(out_ref.dtype)
 
 
@@ -103,15 +150,19 @@
     return pl.pallas_call(
         functools.partial(attend_kernel, scale=1.0 / HD**0.5),
         in_specs=[pl.BlockSpec(memory_space=pltpu.SMEM)]
-        + [pl.BlockSpec(memory_space=pltpu.VMEM)] * 7,
+        + [pl.BlockSpec(memory_space=pltpu.VMEM)] * 5
+        + [pl.BlockSpec(memory_space=pl.ANY)] * 2,
         out_specs=pl.BlockSpec(memory_space=pltpu.VMEM),
         out_shape=jax.ShapeDtypeStruct((tokens, width), dtype),
         scratch_shapes=[
             pltpu.VMEM((4 * tokens, HD), jnp.bfloat16),
             pltpu.VMEM((4 * tokens, HD), jnp.bfloat16),
             pltpu.VMEM((tokens, chip_width), jnp.bfloat16),
+            pltpu.VMEM(w_own.shape, jnp.bfloat16),
+            pltpu.VMEM(w_other.shape, jnp.bfloat16),
+            pltpu.SemaphoreType.DMA((2,)),
         ],
-        compiler_params=pltpu.CompilerParams(vmem_limit_bytes=32 * 1024 * 1024),
+        compiler_params=pltpu.CompilerParams(vmem_limit_bytes=VMEM_GRANT),
         cost_estimate=pl.CostEstimate(
             flops=16 * tokens * tokens * chip_width + 2 * tokens * chip_width * width,
             bytes_accessed=4 * w_own.size + 4 * tokens * width,
@@ -139,8 +190,22 @@
         in_specs=[pl.BlockSpec(memory_space=pltpu.VMEM)] * 4,
         out_specs=[pl.BlockSpec(memory_space=pltpu.VMEM)] * 2,
         out_shape=[jax.ShapeDtypeStruct(residual.shape, jnp.bfloat16)] * 2,
-        compiler_params=pltpu.CompilerParams(vmem_limit_bytes=32 * 1024 * 1024),
+        compiler_params=pltpu.CompilerParams(vmem_limit_bytes=VMEM_GRANT),
     )(residual, own, other, gain)
+
+
+def pass_kernel(*refs):
+    del refs
+
+
+def meet(*arrays):
+    return pl.pallas_call(
+        pass_kernel,
+        in_specs=[pl.BlockSpec(memory_space=pl.ANY)] * len(arrays),
+        out_specs=[pl.BlockSpec(memory_space=pl.ANY)] * len(arrays),
+        out_shape=[jax.ShapeDtypeStruct(array.shape, array.dtype) for array in arrays],
+        input_output_aliases={index: index for index in range(len(arrays))},
+    )(*arrays)
 
 
 def experts_kernel(gate_ref, *refs, cap):
@@ -234,7 +299,7 @@
             pltpu.VMEM((4 * cap, width), jnp.bfloat16),
             pltpu.VMEM((4 * cap, width), jnp.float32),
         ],
-        compiler_params=pltpu.CompilerParams(vmem_limit_bytes=40 * 1024 * 1024),
+        compiler_params=pltpu.CompilerParams(vmem_limit_bytes=VMEM_GRANT),
         cost_estimate=pl.CostEstimate(
             flops=24 * cap * width * hidden_units,
             bytes_accessed=16 * tokens * width + 6 * width * hidden_units,
@@ -274,47 +339,25 @@
     queries = query_rows[0]
     chip_width = queries.shape[1] // 2
 
-    def kv_of(head):
-        start = head * HD
-        return jnp.concatenate(
-            [
-                lax.dynamic_slice_in_dim(key_rows[0], start, HD, 1),
-                lax.dynamic_slice_in_dim(value_rows[0], start, HD, 1),
-            ],
-            axis=1,
-        )
-
-    kv_here = kv_of(chip)
-    kv_away = kv_of(1 - chip)
-    outgoing = jnp.concatenate(
-        [lax.dynamic_slice_in_dim(queries, (1 - chip) * chip_width, chip_width, 1), kv_away], axis=1
-    )
-    incoming = lax.ppermute(outgoing, "seq", across)
-    kv_twin = lax.ppermute(kv_here, "seq", twin)
-    kv_diagonal = lax.ppermute(kv_away, "seq", diagonal)
+    tokens = queries.shape[0]
+    queries_away, kv_here, kv_away = pack(
+        chip,
+        queries,
+        key_rows[0],
+        value_rows[0],
+        expert_ids[0].T,
+        gate_weights[0].T,
+        experts,
+    )
+    incoming = lax.ppermute(queries_away, "seq", across)
+    kv_parts = [
+        kv_here,
+        lax.ppermute(kv_here, "seq", twin),
+        lax.ppermute(kv_away, "seq", across),
+        lax.ppermute(kv_away, "seq", diagonal),
+    ]
     w_other = lax.ppermute(out_proj, "seq", twin)
-
-    table = jnp.sum(
-        jnp.where(
-            expert_ids[0][None] == jnp.arange(experts, dtype=jnp.int32)[:, None, None],
-            gate_weights[0].astype(jnp.float32)[None],
-            0.0,
-        ),
-        axis=2,
-    ).astype(jnp.bfloat16)
-    quad = jnp.stack(
-        [
-            table,
-            lax.ppermute(table, "seq", twin),
-            lax.ppermute(table, "seq", across),
-            lax.ppermute(table, "seq", diagonal),
-        ]
-    )
-    quads = [quad] + [lax.ppermute(quad, "sub", ring(steps)) for steps in range(1, n_sub)]
-    mine = place * n_sub + lax.axis_index("sub")
-    gates = lax.dynamic_index_in_dim(jnp.stack(quads), mine, 2, keepdims=False).astype(jnp.float32)
-
-    kv_parts = (kv_here, kv_twin, incoming, kv_diagonal)
+    quad = jnp.concatenate([part[tokens:, :tokens] for part in kv_parts], axis=1)
     columns = [place, place ^ 1, place ^ 2, place ^ 3]
 
     def place_of(query_start, row_block):
@@ -327,34 +370,83 @@
     )
     hidden, normed = add_and_norm(residual_in[0], projected, projected_across, norm_gain[None])
 
-    rows = normed
-    sums = []
-    for step in range(n_sub):
-        rows_twin = lax.ppermute(rows, "seq", twin)
-        rows_across = lax.ppermute(rows, "seq", across)
-        rows_diagonal = lax.ppermute(rows_across, "seq", twin)
-        blocks = (rows, rows_twin, rows_across, rows_diagonal)
-        if step < n_sub - 1:
-            rows = lax.ppermute(rows, "sub", ring(1))
-        sums.append(
-            experts_on_rows(gates[step], blocks, expert_gate[0], expert_up[0], expert_down[0], cap)
-        )
-    tokens = queries.shape[0]
-    carried = None
-    for step in list(range(1, n_sub)) + [0]:
-        own, away, other = sums[step]
-        met = lax.ppermute(other, "seq", twin).astype(jnp.float32)
-        away = (away.astype(jnp.float32) + met[tokens:]).astype(jnp.bfloat16)
-        part = (
-            own.astype(jnp.float32)
-            + met[:tokens]
-            + lax.ppermute(away, "seq", across).astype(jnp.float32)
-        )
-        if carried is not None:
-            part = part + carried.astype(jnp.float32)
-        if step:
-            carried = lax.ppermute(part.astype(jnp.bfloat16), "sub", ring(1))
-    return (hidden.astype(jnp.float32) + part).astype(jnp.bfloat16)[None]
+    last = n_sub - 1
+    mine = place * n_sub + lax.axis_index("sub")
+
+    def gates_of(quad):
+        row = lax.dynamic_slice_in_dim(quad, mine, 1, 0)
+        return row.reshape(4, tokens).astype(jnp.float32)
+
+    lag = max(n_sub, 4)
+    held = {("row", 0): normed, ("quad", 0): quad}
+
+    def move_twin(array):
+        return lax.ppermute(array, "seq", twin)
+
+    def move_across(array):
+        return lax.ppermute(array, "seq", across)
+
+    def move_on(array):
+        return lax.ppermute(array, "sub", ring(1))
+
+    def sum_here(step):
+        return (
+            held["own", step].astype(jnp.float32)
+            + held["met", step][:tokens].astype(jnp.float32)
+            + held["back", step].astype(jnp.float32)
+        )
+
+    for turn in range(1, lag + n_sub + 1):
+        now = {}
+        if turn <= n_sub:
+            step = turn - 1
+            now["across", step] = move_across(held["row", step])
+            if step < last:
+                now["row", step + 1] = move_on(held["row", step])
+            held["twin", step] = move_twin(held["row", step])
+        if turn == 1:
+            for steps in range(1, n_sub):
+                now["quad", steps] = lax.ppermute(quad, "sub", ring(steps))
+        if 2 <= turn <= n_sub + 1:
+            step = turn - 2
+            held["diagonal", step] = move_twin(held["across", step])
+        back = turn - lag
+        if 1 <= back <= n_sub:
+            step = back % n_sub
+            now["back", step] = move_across(held["away", step])
+        if 2 <= back:
+            step = back - 1
+            part = sum_here(step)
+            if step > 1:
+                part = part + held["sum", step - 1].astype(jnp.float32)
+            now["sum", step] = move_on(part.astype(jnp.bfloat16))
+        step = turn - 2 if turn < lag + n_sub - 2 else 0
+        if turn == lag + n_sub - 2 or 1 <= step <= last:
+            own, away, other = experts_on_rows(
+                gates_of(held["quad", step]),
+                [held[name, step] for name in ("row", "twin", "across", "diagonal")],
+                expert_gate[0],
+                expert_up[0],
+                expert_down[0],
+                cap,
+            )
+            now["other", step] = other
+            held["own", step] = own
+            held["part", step] = away
+        step = turn - 3 if turn < lag + n_sub - 1 else 0
+        if turn == lag + n_sub - 1 or 1 <= step <= last:
+            held["met", step] = move_twin(held["other", step])
+            now["away", step] = (
+                held["part", step].astype(jnp.float32)
+                + held["met", step][tokens:].astype(jnp.float32)
+            ).astype(jnp.bfloat16)
+        if turn < lag + n_sub:
+            now = dict(zip(now.keys(), meet(*now.values())))
+        held.update(now)
+    total = hidden.astype(jnp.float32) + sum_here(0)
+    if last:
+        total = total + held["sum", last].astype(jnp.float32)
+    return total.astype(jnp.bfloat16)[None]
 
 
 def per_device(
@@ -376,7 +468,7 @@
     experts = n_seq * n_sub
     topk = expert_ids.shape[2]
     cap = max(2, (5 * tokens * topk + 4 * experts - 1) // (4 * experts))
-    if n_seq == 2 * KVH and KVH == 2 and experts <= 2 * topk and cap % 16 == 0:
+    if n_seq == 2 * KVH and KVH == 2 and tokens == HD and experts <= 2 * topk and cap % 16 == 0:
         return gathered_plan(
             query_rows,
             key_rows,

time: 188 us -> 185 us (0.984)
  waiting for transfers between devices: 97.4 us -> 62 us
  Pallas kernels: 39.4 us -> 58.2 us
  other arithmetic: 4.36 us -> 18.2 us
  starting transfers between devices: 31.1 us -> 27.2 us
  local copies, waits for them, and re-layouts: 14.9 us -> 18.7 us
    ppermute x35 -> x33, waiting for transfers between devices: 95 us -> 56.5 us  [the longest x6 19.3 us: move_on(): return lax.ppermute(array, 'sub', ring(1))]
    pallas_call x4, Pallas kernels: 28.8 us -> 42.3 us  [experts_on_rows(): pl.pallas_call(functools.partial(experts_kernel, cap=cap), grid=(hidden_u...]
    convert_element_type x12 -> x11, other arithmetic: 2.99 us -> 15.9 us  [the longest x4 5.87 us: gathered_plan(): now['away', step] = (held['part', step].astype(jnp.float32) + held['met',...]
    ppermute x35 -> x33, starting transfers between devices: 29 us -> 25.1 us  [the longest x8 7.22 us: move_across(): return lax.ppermute(array, 'seq', across)]
    ppermute x1, waiting for transfers between devices: 2.45 us -> 5.53 us  [gathered_plan(): projected_across = lax.ppermute(sent, 'seq', across)]
    slice x0 -> x4, local copies, waits for them, and re-layouts: none -> 2.7 us  [gathered_plan(): part[tokens:, :tokens]]
    pallas_call x2, Pallas kernels: 9.17 us -> 11.4 us  [attend(): pl.pallas_call(functools.partial(attend_kernel, scale=1.0 / HD ** 0.5), i...]
    pallas_call x0 -> x8, Pallas kernels: none -> 1.9 us  [the longest x1 1.89 us: pack(): pl.pallas_call(pack_kernel, in_specs=[pl.BlockSpec(memory_space=pltpu.SME...]
  transfers between devices with their start and end apart: 37 -> 35, of which waited for: 18 -> 17; matrix products, arithmetic and copies ran while one was open for 3% -> 10% of each run, Pallas kernels for 18% -> 27%
where the time goes in v4:
time: 185 us; the launch traced here: 184 us
  waiting for transfers between devices  62 us (34%)
  Pallas kernels  58.2 us (31%)
  starting transfers between devices  27.2 us (15%)
  local copies, waits for them, and re-layouts  18.7 us (10%)
  other arithmetic  18.2 us (10%)
    pallas_call x4, Pallas kernels, experts_on_rows(): pl.pallas_call(functools.partial(experts_kernel, cap=cap), grid=(hidden_u...  42.3 us
    ppermute x6, waiting for transfers between devices, move_on(): return lax.ppermute(array, 'sub', ring(1))  19.3 us
    ppermute x8, waiting for transfers between devices, move_across(): return lax.ppermute(array, 'seq', across)  18.2 us
    unnamed x76, local copies, waits for them, and re-layouts  14.1 us
    pallas_call x2, Pallas kernels, attend(): pl.pallas_call(functools.partial(attend_kernel, scale=1.0 / HD ** 0.5), i...  11.4 us
    ppermute x3, waiting for transfers between devices, gathered_plan(): now['quad', steps] = lax.ppermute(quad, 'sub', ring(steps))  7.27 us
    ppermute x8, starting transfers between devices, move_across(): return lax.ppermute(array, 'seq', across)  7.22 us
    ppermute x6, starting transfers between devices, move_on(): return lax.ppermute(array, 'sub', ring(1))  7.07 us
  transfers between devices with their start and end apart: 35, of which 17 were waited for; matrix products, arithmetic and copies ran while one was open for 10% of the time, Pallas kernels for 27%

profile of v4, /device:TPU:0, one launch (start us, length us, event | category | flops | bytes accessed | tf_op | source)
XLA Modules:
  0.0 184.4 jit_solution(10768220029041994734)
XLA Ops:
  0.5 1.9 %shard_map.109 = (bf16[128,1024]{1,0:T(8,128)(2,1)}, bf16[144,256]{1,0:T(8,128)(2,1)}, bf16[144,256]{1,0:T(8,128)(2,1)}) custom-call(s32[1]{0:T(128)} %bitcast.8.chip_ref, bf16[128,2048]{1,0:T(8,128)(2,1)} %bitcast.38, bf16[128,256]{1,0:T(8,128)(2,1)} %bitcast.41, bf16[128,256]{1,0:T(8,128)(2,1)} %bitcast.42, s32[8,128]{1,0:T(8,128)} %bitcast.47, ...), custom_call_target="tpu_custom_call" | custom-call | tf_op jit(solution)/shard_map/pallas_call | solution.py:87
  2.3 2.5 %collective-permute-start.4 = (bf16[128,1024]{1,0:T(8,128)(2,1)}, bf16[128,1024]{1,0:T(8,128)(2,1)S(1)}, u32[]{:S(2)}, u32[]{:S(2)}) collective-permute-start(bf16[128,1024]{1,0:T(8,128)(2,1)} %get-tuple-element.47), channel_id=1, source_target_pairs={{0,8},{4,12},{8,0},{12,4},{1,9},{5,13},{9,1},{13,5},{2,10},{6,14},... | collective-permute-start | bytes 786440 | tf_op jit(solution)/shard_map/ppermute | solution.py:352
  7.3 6.5 %collective-permute-done.1.refs_2_ = bf16[144,256]{1,0:T(8,128)(2,1)S(1)} collective-permute-done((bf16[144,256]{1,0:T(8,128)(2,1)}, bf16[144,256]{1,0:T(8,128)(2,1)S(1)}, u32[]{:S(2)}, u32[]{:S(2)}) %collective-permute-start.1) | collective-permute-done | bytes 73760 | tf_op jit(solution)/shard_map/ppermute | solution.py:356
  17.1 5.6 %shard_map.111 = bf16[128,2048]{1,0:T(8,128)(2,1)} custom-call(s32[7]{0:T(128)} %stack.38.place_ref, bf16[128,1024]{1,0:T(8,128)(2,1)} %copy-done.33, bf16[144,256]{1,0:T(8,128)(2,1)} %get-tuple-element.45.refs_0_, bf16[144,256]{1,0:T(8,128)(2,1)} %copy-done.30, bf16[144,256]{1,0:T(8,128)(2,1)} %copy-done.31, bf16[144,256]{1,0:T(8,128)(2,1)} %copy-done.32, ...), custom_call_target="tpu_custom_call" | custom-call | flops 805306368 | bytes 5242880 | tf_op jit(solution)/shard_map/pallas_call | solution.py:150
  22.6 1.6 collective-permute-start.5
  25.5 5.8 %shard_map.110.own_ref = f32[128,2048]{1,0:T(8,128)} custom-call(s32[7]{0:T(128)} %stack.37.place_ref, bf16[128,2048]{1,0:T(8,128)(2,1)} %bitcast.39, bf16[144,256]{1,0:T(8,128)(2,1)} %get-tuple-element.45.refs_0_, bf16[144,256]{1,0:T(8,128)(2,1)} %copy-done.30, bf16[144,256]{1,0:T(8,128)(2,1)} %copy-done.31, bf16[144,256]{1,0:T(8,128)(2,1)} %copy-done.32, ...), custom_call_target="tpu_custom_call" | custom-call | flops 805306368 | bytes 5242880 | tf_op jit(solution)/shard_map/pallas_call | solution.py:150
  31.3 5.5 %collective-permute-done.5.other_ref = bf16[128,2048]{1,0:T(8,128)(2,1)S(1)} collective-permute-done((bf16[128,2048]{1,0:T(8,128)(2,1)}, bf16[128,2048]{1,0:T(8,128)(2,1)S(1)}, u32[]{:S(2)}, u32[]{:S(2)}) %collective-permute-start.5) | collective-permute-done | bytes 524320 | tf_op jit(solution)/shard_map/ppermute | solution.py:367
  37.6 2.7 %shard_map.112 = (bf16[128,2048]{1,0:T(8,128)(2,1)}, bf16[128,2048]{1,0:T(8,128)(2,1)}) custom-call(bf16[128,2048]{1,0:T(8,128)(2,1)} %bitcast.40, f32[128,2048]{1,0:T(8,128)} %shard_map.110.own_ref, bf16[128,2048]{1,0:T(8,128)(2,1)} %copy-done.29, bf16[1,2048]{1,0:T(2,128)(2,1)} %broadcast_in_dim.6.gain_ref), custom_call_target="tpu_custom_call" | custom-call | tf_op jit(solution)/shard_map/pallas_call | solution.py:188
  40.3 1.6 collective-permute-start.7
  42.0 1.6 collective-permute-start.8
  46.3 2.6 %collective-permute-start.9 = (bf16[16,512]{1,0:T(8,128)(2,1)S(1)}, bf16[16,512]{1,0:T(8,128)(2,1)S(1)}, u32[]{:S(2)}, u32[]{:S(2)}) collective-permute-start(bf16[16,512]{1,0:T(8,128)(2,1)S(1)} %pad_maximum_fusion), channel_id=1, source_target_pairs={{0,1},{1,3},{3,2},{2,0},{4,5},{5,7},{7,6},{6,4},{8,9},{9,11},{11,1... | collective-permute-start | bytes 49160 | tf_op jit(solution)/shard_map/ppermute | solution.py:409
  49.1 1.7 collective-permute-start.11
  50.8 6.2 %collective-permute-done.9.refs_2_ = bf16[16,512]{1,0:T(8,128)(2,1)S(1)} collective-permute-done((bf16[16,512]{1,0:T(8,128)(2,1)S(1)}, bf16[16,512]{1,0:T(8,128)(2,1)S(1)}, u32[]{:S(2)}, u32[]{:S(2)}) %collective-permute-start.9) | collective-permute-done | bytes 16416 | tf_op jit(solution)/shard_map/ppermute | solution.py:409
  60.9 10.6 %collective-permute-done.13.refs_0_ = bf16[128,2048]{1,0:T(8,128)(2,1)S(1)} collective-permute-done((bf16[128,2048]{1,0:T(8,128)(2,1)}, bf16[128,2048]{1,0:T(8,128)(2,1)S(1)}, u32[]{:S(2)}, u32[]{:S(2)}) %collective-permute-start.13) | collective-permute-done | bytes 524320 | tf_op jit(solution)/shard_map/ppermute | solution.py:387
  73.4 1.5 collective-permute-start.15
  77.3 10.6 %shard_map.116 = (bf16[128,2048]{1,0:T(8,128)(2,1)}, bf16[128,2048]{1,0:T(8,128)(2,1)}, bf16[256,2048]{1,0:T(8,128)(2,1)}) custom-call(f32[4,128]{1,0:T(4,128)} %bitcast.46, bf16[128,2048]{1,0:T(8,128)(2,1)} %get-tuple-element.52.refs_0_, bf16[128,2048]{1,0:T(8,128)(2,1)} %copy-done.20, bf16[128,2048]{1,0:T(8,128)(2,1)} %get-tuple-element.55.refs_2_, ...), custom_call_target="tpu_custom_call" | custom-call | flops 3019898880 | bytes 13631488 | tf_op jit(solution)/shard_map/pallas_call | solution.py:279
  88.0 2.2 %collective-permute-done.16.refs_1_ = bf16[128,2048]{1,0:T(8,128)(2,1)S(1)} collective-permute-done((bf16[128,2048]{1,0:T(8,128)(2,1)}, bf16[128,2048]{1,0:T(8,128)(2,1)S(1)}, u32[]{:S(2)}, u32[]{:S(2)}) %collective-permute-start.16) | collective-permute-done | bytes 524320 | tf_op jit(solution)/shard_map/ppermute | solution.py:390
  96.2 10.6 %shard_map.118 = (bf16[128,2048]{1,0:T(8,128)(2,1)}, bf16[128,2048]{1,0:T(8,128)(2,1)}, bf16[256,2048]{1,0:T(8,128)(2,1)}) custom-call(f32[4,128]{1,0:T(4,128)} %bitcast.44, bf16[128,2048]{1,0:T(8,128)(2,1)} %get-tuple-element.53.refs_0_, bf16[128,2048]{1,0:T(8,128)(2,1)} %copy-done.24, bf16[128,2048]{1,0:T(8,128)(2,1)} %get-tuple-element.59.refs_2_, ...), custom_call_target="tpu_custom_call" | custom-call | flops 3019898880 | bytes 13631488 | tf_op jit(solution)/shard_map/pallas_call | solution.py:279
  111.0 1.6 collective-permute-done.24.refs_1_
  114.2 10.6 %shard_map.120 = (bf16[128,2048]{1,0:T(8,128)(2,1)}, bf16[128,2048]{1,0:T(8,128)(2,1)}, bf16[256,2048]{1,0:T(8,128)(2,1)}) custom-call(f32[4,128]{1,0:T(4,128)} %bitcast.45, bf16[128,2048]{1,0:T(8,128)(2,1)} %get-tuple-element.57.refs_0_, bf16[128,2048]{1,0:T(8,128)(2,1)} %copy-done.25, bf16[128,2048]{1,0:T(8,128)(2,1)} %get-tuple-element.65.refs_2_, ...), custom_call_target="tpu_custom_call" | custom-call | flops 3019898880 | bytes 13631488 | tf_op jit(solution)/shard_map/pallas_call | solution.py:279
  128.4 2.3 %add_convert_fusion.5 = bf16[128,2048]{1,0:T(8,128)(2,1)} fusion(bf16[128,2048]{1,0:T(8,128)(2,1)} %get-tuple-element.71, bf16[128,2048]{1,0:T(8,128)(2,1)} %get-tuple-element.70, bf16[256,2048]{1,0:T(8,128)(2,1)S(1)} %collective-permute-done.22), kind=kLoop, calls=%fused_computation.5 | loop fusion | flops 1572864 | bytes 2097152 | tf_op jit(solution)/shard_map/convert_element_type | solution.py:422
  133.5 10.6 %shard_map.114 = (bf16[128,2048]{1,0:T(8,128)(2,1)}, bf16[128,2048]{1,0:T(8,128)(2,1)}, bf16[256,2048]{1,0:T(8,128)(2,1)}) custom-call(f32[4,128]{1,0:T(4,128)} %bitcast.43, bf16[128,2048]{1,0:T(8,128)(2,1)} %get-tuple-element.49.refs_0_, bf16[128,2048]{1,0:T(8,128)(2,1)} %copy-done.22, bf16[128,2048]{1,0:T(8,128)(2,1)} %get-tuple-element.50.refs_2_, ...), custom_call_target="tpu_custom_call" | custom-call | flops 3019898880 | bytes 13631488 | tf_op jit(solution)/shard_map/pallas_call | solution.py:279
  144.0 2.0 %add_convert_fusion.4.refs_3_ = bf16[128,2048]{1,0:T(8,128)(2,1)} fusion(bf16[128,2048]{1,0:T(8,128)(2,1)S(1)} %copy-done.17, bf16[256,2048]{1,0:T(8,128)(2,1)} %collective-permute-done.29), kind=kLoop, calls=%fused_computation.4 | loop fusion | flops 1048576 | bytes 1572864 | tf_op jit(solution)/shard_map/convert_element_type | solution.py:442
  147.0 1.5 collective-permute-start.31
  148.5 1.7 add_convert_fusion.3
  150.2 2.2 %collective-permute-start.32 = (bf16[128,2048]{1,0:T(8,128)(2,1)S(1)}, bf16[128,2048]{1,0:T(8,128)(2,1)S(1)}, u32[]{:S(2)}, u32[]{:S(2)}) collective-permute-start(bf16[128,2048]{1,0:T(8,128)(2,1)S(1)} %add_convert_fusion.3), channel_id=1, source_target_pairs={{0,1},{1,3},{3,2},{2,0},{4,5},{5,7},{7,6},{6,4},{8,9},{9,11},{11,1... | collective-permute-start | bytes 1572872 | tf_op jit(solution)/shard_map/ppermute | solution.py:390
  152.4 2.0 %add_convert_fusion.2.refs_2_ = bf16[128,2048]{1,0:T(8,128)(2,1)} fusion(bf16[128,2048]{1,0:T(8,128)(2,1)} %get-tuple-element.80, bf16[256,2048]{1,0:T(8,128)(2,1)S(1)} %collective-permute-done.30), kind=kLoop, calls=%fused_computation.2 | loop fusion | flops 1048576 | bytes 1572864 | tf_op jit(solution)/shard_map/convert_element_type | solution.py:442
  154.4 7.1 %collective-permute-done.31.refs_0_ = bf16[128,2048]{1,0:T(8,128)(2,1)S(1)} collective-permute-done((bf16[128,2048]{1,0:T(8,128)(2,1)}, bf16[128,2048]{1,0:T(8,128)(2,1)S(1)}, u32[]{:S(2)}, u32[]{:S(2)}) %collective-permute-start.31) | collective-permute-done | bytes 524320 | tf_op jit(solution)/shard_map/ppermute | solution.py:387
  161.5 3.7 %collective-permute-done.32.refs_1_ = bf16[128,2048]{1,0:T(8,128)(2,1)S(1)} collective-permute-done((bf16[128,2048]{1,0:T(8,128)(2,1)S(1)}, bf16[128,2048]{1,0:T(8,128)(2,1)S(1)}, u32[]{:S(2)}, u32[]{:S(2)}) %collective-permute-start.32) | collective-permute-done | bytes 524320 | tf_op jit(solution)/shard_map/ppermute | solution.py:390
  166.0 1.7 add_convert_fusion.1
  169.5 12.4 %collective-permute-done.34 = bf16[128,2048]{1,0:T(8,128)(2,1)S(1)} collective-permute-done((bf16[128,2048]{1,0:T(8,128)(2,1)S(1)}, bf16[128,2048]{1,0:T(8,128)(2,1)S(1)}, u32[]{:S(2)}, u32[]{:S(2)}) %collective-permute-start.34) | collective-permute-done | bytes 524320 | tf_op jit(solution)/shard_map/ppermute | solution.py:390
  182.2 2.3 %fusion = bf16[1,128,2048]{2,1,0:T(8,128)(2,1)} fusion(bf16[128,2048]{1,0:T(8,128)(2,1)S(1)} %collective-permute-done.34, bf16[128,2048]{1,0:T(8,128)(2,1)S(1)} %collective-permute-done.33, bf16[128,2048]{1,0:T(8,128)(2,1)} %get-tuple-element.51, bf16[128,2048]{1,0:T(8,128)(2,1)S(1)} %copy-done.28, bf16[256,2048]{1,0:T(8,128)(2,1)S(1)} %collective-permute-done.30), kind=kLoop, calls=%fused_computation.8 | loop fusion | flops 2621440 | bytes 3145728 | tf_op jit(solution)/shard_map/broadcast_in_dim | solution.py:449
  (149 shorter events, 41.6 us)
Async XLA Ops:
  0.0 15.0 %collective-permute-start.3 = (bf16[512,2048]{1,0:T(8,128)(2,1)}, bf16[512,2048]{1,0:T(8,128)(2,1)S(1)}, u32[]{:S(2)}, u32[]{:S(2)}) collective-permute-start(bf16[512,2048]{1,0:T(8,128)(2,1)} %refs_4_.3), channel_id=1, source_target_pairs={{0,4},{4,0},{8,12},{12,8},{1,5},{5,1},{9,13},{13,9},{2,6},{6,2},{1... | collective-permute-start | bytes 6291464 | tf_op jit(solution)/shard_map/ppermute | solution.py:359
  2.3 12.7 %collective-permute-start.4 = (bf16[128,1024]{1,0:T(8,128)(2,1)}, bf16[128,1024]{1,0:T(8,128)(2,1)S(1)}, u32[]{:S(2)}, u32[]{:S(2)}) collective-permute-start(bf16[128,1024]{1,0:T(8,128)(2,1)} %get-tuple-element.47), channel_id=1, source_target_pairs={{0,8},{4,12},{8,0},{12,4},{1,9},{5,13},{9,1},{13,5},{2,10},{6,14},... | collective-permute-start | bytes 786440 | tf_op jit(solution)/shard_map/ppermute | solution.py:352
  5.1 8.7 %collective-permute-start.1 = (bf16[144,256]{1,0:T(8,128)(2,1)}, bf16[144,256]{1,0:T(8,128)(2,1)S(1)}, u32[]{:S(2)}, u32[]{:S(2)}) collective-permute-start(bf16[144,256]{1,0:T(8,128)(2,1)} %get-tuple-element.46), channel_id=1, source_target_pairs={{0,8},{4,12},{8,0},{12,4},{1,9},{5,13},{9,1},{13,5},{2,10},{6,14},... | collective-permute-start | bytes 221192 | tf_op jit(solution)/shard_map/ppermute | solution.py:356
  5.4 9.6 %collective-permute-start.2 = (bf16[144,256]{1,0:T(8,128)(2,1)}, bf16[144,256]{1,0:T(8,128)(2,1)S(1)}, u32[]{:S(2)}, u32[]{:S(2)}) collective-permute-start(bf16[144,256]{1,0:T(8,128)(2,1)} %get-tuple-element.46), channel_id=1, source_target_pairs={{0,12},{4,8},{8,4},{12,0},{1,13},{5,9},{9,5},{13,1},{2,14},{6,10},... | collective-permute-start | bytes 221192 | tf_op jit(solution)/shard_map/ppermute | solution.py:357
  22.6 14.2 %collective-permute-start.5 = (bf16[128,2048]{1,0:T(8,128)(2,1)}, bf16[128,2048]{1,0:T(8,128)(2,1)S(1)}, u32[]{:S(2)}, u32[]{:S(2)}) collective-permute-start(bf16[128,2048]{1,0:T(8,128)(2,1)} %shard_map.111), channel_id=1, source_target_pairs={{0,8},{4,12},{8,0},{12,4},{1,9},{5,13},{9,1},{13,5},{2,10},{6,14},... | collective-permute-start | bytes 1572872 | tf_op jit(solution)/shard_map/ppermute | solution.py:367
  40.3 17.7 %collective-permute-start.7 = (bf16[128,2048]{1,0:T(8,128)(2,1)}, bf16[128,2048]{1,0:T(8,128)(2,1)S(1)}, u32[]{:S(2)}, u32[]{:S(2)}) collective-permute-start(bf16[128,2048]{1,0:T(8,128)(2,1)} %get-tuple-element.49.refs_0_), channel_id=1, source_target_pairs={{0,8},{4,12},{8,0},{12,4},{1,9},{5,13},{9,1},{13,5},{2,10},{6,14},... | collective-permute-start | bytes 1572872 | tf_op jit(solution)/shard_map/ppermute | solution.py:387
  42.0 16.1 %collective-permute-start.8 = (bf16[128,2048]{1,0:T(8,128)(2,1)}, bf16[128,2048]{1,0:T(8,128)(2,1)S(1)}, u32[]{:S(2)}, u32[]{:S(2)}) collective-permute-start(bf16[128,2048]{1,0:T(8,128)(2,1)} %get-tuple-element.49.refs_0_), channel_id=1, source_target_pairs={{0,1},{1,3},{3,2},{2,0},{4,5},{5,7},{7,6},{6,4},{8,9},{9,11},{11,1... | collective-permute-start | bytes 1572872 | tf_op jit(solution)/shard_map/ppermute | solution.py:390
  46.3 10.7 %collective-permute-start.9 = (bf16[16,512]{1,0:T(8,128)(2,1)S(1)}, bf16[16,512]{1,0:T(8,128)(2,1)S(1)}, u32[]{:S(2)}, u32[]{:S(2)}) collective-permute-start(bf16[16,512]{1,0:T(8,128)(2,1)S(1)} %pad_maximum_fusion), channel_id=1, source_target_pairs={{0,1},{1,3},{3,2},{2,0},{4,5},{5,7},{7,6},{6,4},{8,9},{9,11},{11,1... | collective-permute-start | bytes 49160 | tf_op jit(solution)/shard_map/ppermute | solution.py:409
  48.9 9.2 %collective-permute-start.10 = (bf16[16,512]{1,0:T(8,128)(2,1)S(1)}, bf16[16,512]{1,0:T(8,128)(2,1)S(1)}, u32[]{:S(2)}, u32[]{:S(2)}) collective-permute-start(bf16[16,512]{1,0:T(8,128)(2,1)S(1)} %pad_maximum_fusion), channel_id=1, source_target_pairs={{0,3},{1,2},{3,0},{2,1},{4,7},{5,6},{7,4},{6,5},{8,11},{9,10},{11,... | collective-permute-start | bytes 49160 | tf_op jit(solution)/shard_map/ppermute | solution.py:409
  49.1 9.0 %collective-permute-start.11 = (bf16[16,512]{1,0:T(8,128)(2,1)S(1)}, bf16[16,512]{1,0:T(8,128)(2,1)S(1)}, u32[]{:S(2)}, u32[]{:S(2)}) collective-permute-start(bf16[16,512]{1,0:T(8,128)(2,1)S(1)} %pad_maximum_fusion), channel_id=1, source_target_pairs={{0,2},{1,0},{3,1},{2,3},{4,6},{5,4},{7,5},{6,7},{8,10},{9,8},{11,9... | collective-permute-start | bytes 49160 | tf_op jit(solution)/shard_map/ppermute | solution.py:409
  59.6 11.8 %collective-permute-start.13 = (bf16[128,2048]{1,0:T(8,128)(2,1)}, bf16[128,2048]{1,0:T(8,128)(2,1)S(1)}, u32[]{:S(2)}, u32[]{:S(2)}) collective-permute-start(bf16[128,2048]{1,0:T(8,128)(2,1)} %get-tuple-element.52.refs_0_), channel_id=1, source_target_pairs={{0,8},{4,12},{8,0},{12,4},{1,9},{5,13},{9,1},{13,5},{2,10},{6,14},... | collective-permute-start | bytes 1572872 | tf_op jit(solution)/shard_map/ppermute | solution.py:387
  60.1 12.4 %collective-permute-start.14 = (bf16[128,2048]{1,0:T(8,128)(2,1)}, bf16[128,2048]{1,0:T(8,128)(2,1)S(1)}, u32[]{:S(2)}, u32[]{:S(2)}) collective-permute-start(bf16[128,2048]{1,0:T(8,128)(2,1)} %get-tuple-element.52.refs_0_), channel_id=1, source_target_pairs={{0,1},{1,3},{3,2},{2,0},{4,5},{5,7},{7,6},{6,4},{8,9},{9,11},{11,1... | collective-permute-start | bytes 1572872 | tf_op jit(solution)/shard_map/ppermute | solution.py:390
  60.9 15.4 %collective-permute-start.17 = (bf16[128,2048]{1,0:T(8,128)(2,1)}, bf16[128,2048]{1,0:T(8,128)(2,1)S(1)}, u32[]{:S(2)}, u32[]{:S(2)}) collective-permute-start(bf16[128,2048]{1,0:T(8,128)(2,1)} %get-tuple-element.52.refs_0_), channel_id=1, source_target_pairs={{0,4},{4,0},{8,12},{12,8},{1,5},{5,1},{9,13},{13,9},{2,6},{6,2},{1... | collective-permute-start | bytes 1572872 | tf_op jit(solution)/shard_map/ppermute | solution.py:384
  73.4 14.5 %collective-permute-start.15 = (bf16[128,2048]{1,0:T(8,128)(2,1)}, bf16[128,2048]{1,0:T(8,128)(2,1)S(1)}, u32[]{:S(2)}, u32[]{:S(2)}) collective-permute-start(bf16[128,2048]{1,0:T(8,128)(2,1)} %get-tuple-element.53.refs_0_), channel_id=1, source_target_pairs={{0,8},{4,12},{8,0},{12,4},{1,9},{5,13},{9,1},{13,5},{2,10},{6,14},... | collective-permute-start | bytes 1572872 | tf_op jit(solution)/shard_map/ppermute | solution.py:387
  75.0 15.2 %collective-permute-start.16 = (bf16[128,2048]{1,0:T(8,128)(2,1)}, bf16[128,2048]{1,0:T(8,128)(2,1)S(1)}, u32[]{:S(2)}, u32[]{:S(2)}) collective-permute-start(bf16[128,2048]{1,0:T(8,128)(2,1)} %get-tuple-element.53.refs_0_), channel_id=1, source_target_pairs={{0,1},{1,3},{3,2},{2,0},{4,5},{5,7},{7,6},{6,4},{8,9},{9,11},{11,1... | collective-permute-start | bytes 1572872 | tf_op jit(solution)/shard_map/ppermute | solution.py:390
  91.0 15.8 %collective-permute-start.22 = (bf16[256,2048]{1,0:T(8,128)(2,1)}, bf16[256,2048]{1,0:T(8,128)(2,1)S(1)}, u32[]{:S(2)}, u32[]{:S(2)}) collective-permute-start(bf16[256,2048]{1,0:T(8,128)(2,1)} %get-tuple-element.62), channel_id=1, source_target_pairs={{0,4},{4,0},{8,12},{12,8},{1,5},{5,1},{9,13},{13,9},{2,6},{6,2},{1... | collective-permute-start | bytes 3145736 | tf_op jit(solution)/shard_map/ppermute | solution.py:384
  91.5 3.9 %collective-permute-start.21 = (bf16[128,2048]{1,0:T(8,128)(2,1)}, bf16[128,2048]{1,0:T(8,128)(2,1)S(1)}, u32[]{:S(2)}, u32[]{:S(2)}) collective-permute-start(bf16[128,2048]{1,0:T(8,128)(2,1)} %get-tuple-element.59.refs_2_), channel_id=1, source_target_pairs={{0,4},{4,0},{8,12},{12,8},{1,5},{5,1},{9,13},{13,9},{2,6},{6,2},{1... | collective-permute-start | bytes 1572872 | tf_op jit(solution)/shard_map/ppermute | solution.py:384
  92.8 14.9 %collective-permute-start.19 = (bf16[128,2048]{1,0:T(8,128)(2,1)}, bf16[128,2048]{1,0:T(8,128)(2,1)S(1)}, u32[]{:S(2)}, u32[]{:S(2)}) collective-permute-start(bf16[128,2048]{1,0:T(8,128)(2,1)} %get-tuple-element.57.refs_0_), channel_id=1, source_target_pairs={{0,8},{4,12},{8,0},{12,4},{1,9},{5,13},{9,1},{13,5},{2,10},{6,14},... | collective-permute-start | bytes 1572872 | tf_op jit(solution)/shard_map/ppermute | solution.py:387
  108.6 16.2 %collective-permute-start.26 = (bf16[256,2048]{1,0:T(8,128)(2,1)}, bf16[256,2048]{1,0:T(8,128)(2,1)S(1)}, u32[]{:S(2)}, u32[]{:S(2)}) collective-permute-start(bf16[256,2048]{1,0:T(8,128)(2,1)} %get-tuple-element.68), channel_id=1, source_target_pairs={{0,4},{4,0},{8,12},{12,8},{1,5},{5,1},{9,13},{13,9},{2,6},{6,2},{1... | collective-permute-start | bytes 3145736 | tf_op jit(solution)/shard_map/ppermute | solution.py:384
  108.7 3.9 %collective-permute-start.24 = (bf16[128,2048]{1,0:T(8,128)(2,1)S(1)}, bf16[128,2048]{1,0:T(8,128)(2,1)S(1)}, u32[]{:S(2)}, u32[]{:S(2)}) collective-permute-start(bf16[128,2048]{1,0:T(8,128)(2,1)S(1)} %copy-done.13), channel_id=1, source_target_pairs={{0,4},{4,0},{8,12},{12,8},{1,5},{5,1},{9,13},{13,9},{2,6},{6,2},{1... | collective-permute-start | bytes 1572872 | tf_op jit(solution)/shard_map/ppermute | solution.py:384
  109.1 3.9 %collective-permute-start.25 = (bf16[128,2048]{1,0:T(8,128)(2,1)}, bf16[128,2048]{1,0:T(8,128)(2,1)S(1)}, u32[]{:S(2)}, u32[]{:S(2)}) collective-permute-start(bf16[128,2048]{1,0:T(8,128)(2,1)} %get-tuple-element.65.refs_2_), channel_id=1, source_target_pairs={{0,4},{4,0},{8,12},{12,8},{1,5},{5,1},{9,13},{13,9},{2,6},{6,2},{1... | collective-permute-start | bytes 1572872 | tf_op jit(solution)/shard_map/ppermute | solution.py:384
  110.5 15.3 %collective-permute-start.23 = (bf16[128,2048]{1,0:T(8,128)(2,1)}, bf16[128,2048]{1,0:T(8,128)(2,1)S(1)}, u32[]{:S(2)}, u32[]{:S(2)}) collective-permute-start(bf16[128,2048]{1,0:T(8,128)(2,1)} %get-tuple-element.63), channel_id=1, source_target_pairs={{0,8},{4,12},{8,0},{12,4},{1,9},{5,13},{9,1},{13,5},{2,10},{6,14},... | collective-permute-start | bytes 1572872 | tf_op jit(solution)/shard_map/ppermute | solution.py:387
  126.5 17.5 %collective-permute-start.29 = (bf16[256,2048]{1,0:T(8,128)(2,1)}, bf16[256,2048]{1,0:T(8,128)(2,1)}, u32[]{:S(2)}, u32[]{:S(2)}) collective-permute-start(bf16[256,2048]{1,0:T(8,128)(2,1)} %get-tuple-element.74), channel_id=1, source_target_pairs={{0,4},{4,0},{8,12},{12,8},{1,5},{5,1},{9,13},{13,9},{2,6},{6,2},{1... | collective-permute-start | bytes 3145736 | tf_op jit(solution)/shard_map/ppermute | solution.py:384
  126.8 5.0 %collective-permute-start.6 = (bf16[128,2048]{1,0:T(8,128)(2,1)}, bf16[128,2048]{1,0:T(8,128)(2,1)S(1)}, u32[]{:S(2)}, u32[]{:S(2)}) collective-permute-start(bf16[128,2048]{1,0:T(8,128)(2,1)} %get-tuple-element.49.refs_0_), channel_id=1, source_target_pairs={{0,4},{4,0},{8,12},{12,8},{1,5},{5,1},{9,13},{13,9},{2,6},{6,2},{1... | collective-permute-start | bytes 1572872 | tf_op jit(solution)/shard_map/ppermute | solution.py:384
  127.0 4.8 %collective-permute-start.12 = (bf16[128,2048]{1,0:T(8,128)(2,1)S(1)}, bf16[128,2048]{1,0:T(8,128)(2,1)S(1)}, u32[]{:S(2)}, u32[]{:S(2)}) collective-permute-start(bf16[128,2048]{1,0:T(8,128)(2,1)S(1)} %copy-done.6), channel_id=1, source_target_pairs={{0,4},{4,0},{8,12},{12,8},{1,5},{5,1},{9,13},{13,9},{2,6},{6,2},{1... | collective-permute-start | bytes 1572872 | tf_op jit(solution)/shard_map/ppermute | solution.py:384
  127.9 18.1 %collective-permute-start.27 = (bf16[128,2048]{1,0:T(8,128)(2,1)}, bf16[128,2048]{1,0:T(8,128)(2,1)S(1)}, u32[]{:S(2)}, u32[]{:S(2)}) collective-permute-start(bf16[128,2048]{1,0:T(8,128)(2,1)} %get-tuple-element.69), channel_id=1, source_target_pairs={{0,8},{4,12},{8,0},{12,4},{1,9},{5,13},{9,1},{13,5},{2,10},{6,14},... | collective-permute-start | bytes 1572872 | tf_op jit(solution)/shard_map/ppermute | solution.py:387
  130.7 15.4 %collective-permute-start.28 = (bf16[128,2048]{1,0:T(8,128)(2,1)}, bf16[128,2048]{1,0:T(8,128)(2,1)S(1)}, u32[]{:S(2)}, u32[]{:S(2)}) collective-permute-start(bf16[128,2048]{1,0:T(8,128)(2,1)} %add_convert_fusion.5), channel_id=1, source_target_pairs={{0,1},{1,3},{3,2},{2,0},{4,5},{5,7},{7,6},{6,4},{8,9},{9,11},{11,1... | collective-permute-start | bytes 1572872 | tf_op jit(solution)/shard_map/ppermute | solution.py:390
  147.0 5.4 %collective-permute-start.30 = (bf16[256,2048]{1,0:T(8,128)(2,1)}, bf16[256,2048]{1,0:T(8,128)(2,1)S(1)}, u32[]{:S(2)}, u32[]{:S(2)}) collective-permute-start(bf16[256,2048]{1,0:T(8,128)(2,1)} %get-tuple-element.75), channel_id=1, source_target_pairs={{0,4},{4,0},{8,12},{12,8},{1,5},{5,1},{9,13},{13,9},{2,6},{6,2},{1... | collective-permute-start | bytes 3145736 | tf_op jit(solution)/shard_map/ppermute | solution.py:384
  147.0 14.5 %collective-permute-start.31 = (bf16[128,2048]{1,0:T(8,128)(2,1)}, bf16[128,2048]{1,0:T(8,128)(2,1)S(1)}, u32[]{:S(2)}, u32[]{:S(2)}) collective-permute-start(bf16[128,2048]{1,0:T(8,128)(2,1)} %get-tuple-element.76), channel_id=1, source_target_pairs={{0,8},{4,12},{8,0},{12,4},{1,9},{5,13},{9,1},{13,5},{2,10},{6,14},... | collective-permute-start | bytes 1572872 | tf_op jit(solution)/shard_map/ppermute | solution.py:387
  150.2 15.0 %collective-permute-start.32 = (bf16[128,2048]{1,0:T(8,128)(2,1)S(1)}, bf16[128,2048]{1,0:T(8,128)(2,1)S(1)}, u32[]{:S(2)}, u32[]{:S(2)}) collective-permute-start(bf16[128,2048]{1,0:T(8,128)(2,1)S(1)} %add_convert_fusion.3), channel_id=1, source_target_pairs={{0,1},{1,3},{3,2},{2,0},{4,5},{5,7},{7,6},{6,4},{8,9},{9,11},{11,1... | collective-permute-start | bytes 1572872 | tf_op jit(solution)/shard_map/ppermute | solution.py:390
  167.7 14.2 %collective-permute-start.34 = (bf16[128,2048]{1,0:T(8,128)(2,1)S(1)}, bf16[128,2048]{1,0:T(8,128)(2,1)S(1)}, u32[]{:S(2)}, u32[]{:S(2)}) collective-permute-start(bf16[128,2048]{1,0:T(8,128)(2,1)S(1)} %add_convert_fusion.1), channel_id=1, source_target_pairs={{0,1},{1,3},{3,2},{2,0},{4,5},{5,7},{7,6},{6,4},{8,9},{9,11},{11,1... | collective-permute-start | bytes 1572872 | tf_op jit(solution)/shard_map/ppermute | solution.py:390
  169.0 13.2 %collective-permute-start.33 = (bf16[128,2048]{1,0:T(8,128)(2,1)}, bf16[128,2048]{1,0:T(8,128)(2,1)S(1)}, u32[]{:S(2)}, u32[]{:S(2)}) collective-permute-start(bf16[128,2048]{1,0:T(8,128)(2,1)} %get-tuple-element.81), channel_id=1, source_target_pairs={{0,8},{4,12},{8,0},{12,4},{1,9},{5,13},{9,1},{13,5},{2,10},{6,14},... | collective-permute-start | bytes 1572872 | tf_op jit(solution)/shard_map/ppermute | solution.py:387
  (41 other events, 170.4 us)

commit v5 on v4

--- a/solution.py
+++ b/solution.py
@@ -11,7 +11,7 @@
 HD = 128
 QH = 16
 KVH = 2
-VMEM_GRANT = 60 * 1024 * 1024
+MIB = 1024 * 1024
 
 
 def attend_head(queries, keys_one, values_one, block):
@@ -90,15 +90,13 @@
         + [pl.BlockSpec(memory_space=pltpu.VMEM)] * 5,
         out_specs=[pl.BlockSpec(memory_space=pltpu.VMEM)] * 3,
         out_shape=[jax.ShapeDtypeStruct((tokens, width // 2), jnp.bfloat16), kv, kv],
-        compiler_params=pltpu.CompilerParams(vmem_limit_bytes=VMEM_GRANT),
+        compiler_params=pltpu.CompilerParams(vmem_limit_bytes=6 * MIB),
     )(chip.reshape(1), queries, keys, values, ids, gates)
 
 
 def attend_kernel(place_ref, query_ref, *refs, scale):
-    kv_refs, (w_own_ref, w_other_ref, out_ref, keys, values, heads, w_own, w_other, done) = (
-        refs[:4],
-        refs[4:],
-    )
+    kv_refs, refs = refs[:4], refs[4:]
+    w_own_ref, w_other_ref, out_ref, quad_ref, keys, values, heads, w_own, w_other, done = refs
     fetches = [
         pltpu.make_async_copy(w_own_ref, w_own, done.at[0]),
         pltpu.make_async_copy(w_other_ref, w_other, done.at[1]),
@@ -116,6 +114,7 @@
     for part, kv_ref in enumerate(kv_refs):
         keys[part * rows : (part + 1) * rows, :] = kv_ref[0:rows, 0:head_size]
         values[part * rows : (part + 1) * rows, :] = kv_ref[0:rows, head_size:]
+        quad_ref[:, part * rows : (part + 1) * rows] = kv_ref[rows:, 0:rows]
     key_block = keys[...]
     value_block = values[...]
     for head in range(heads.shape[1] // head_size):
@@ -152,8 +151,11 @@
         in_specs=[pl.BlockSpec(memory_space=pltpu.SMEM)]
         + [pl.BlockSpec(memory_space=pltpu.VMEM)] * 5
         + [pl.BlockSpec(memory_space=pl.ANY)] * 2,
-        out_specs=pl.BlockSpec(memory_space=pltpu.VMEM),
-        out_shape=jax.ShapeDtypeStruct((tokens, width), dtype),
+        out_specs=[pl.BlockSpec(memory_space=pltpu.VMEM)] * 2,
+        out_shape=[
+            jax.ShapeDtypeStruct((tokens, width), dtype),
+            jax.ShapeDtypeStruct((kv_parts[0].shape[0] - tokens, 4 * tokens), jnp.bfloat16),
+        ],
         scratch_shapes=[
             pltpu.VMEM((4 * tokens, HD), jnp.bfloat16),
             pltpu.VMEM((4 * tokens, HD), jnp.bfloat16),
@@ -162,7 +164,7 @@
             pltpu.VMEM(w_other.shape, jnp.bfloat16),
             pltpu.SemaphoreType.DMA((2,)),
         ],
-        compiler_params=pltpu.CompilerParams(vmem_limit_bytes=VMEM_GRANT),
+        compiler_params=pltpu.CompilerParams(vmem_limit_bytes=16 * MIB),
         cost_estimate=pl.CostEstimate(
             flops=16 * tokens * tokens * chip_width + 2 * tokens * chip_width * width,
             bytes_accessed=4 * w_own.size + 4 * tokens * width,
@@ -190,7 +192,7 @@
         in_specs=[pl.BlockSpec(memory_space=pltpu.VMEM)] * 4,
         out_specs=[pl.BlockSpec(memory_space=pltpu.VMEM)] * 2,
         out_shape=[jax.ShapeDtypeStruct(residual.shape, jnp.bfloat16)] * 2,
-        compiler_params=pltpu.CompilerParams(vmem_limit_bytes=VMEM_GRANT),
+        compiler_params=pltpu.CompilerParams(vmem_limit_bytes=10 * MIB),
     )(residual, own, other, gain)
 
 
@@ -208,104 +210,91 @@
     )(*arrays)
 
 
-def experts_kernel(gate_ref, *refs, cap):
+def pass_kernel(*refs):
+    del refs
+
+
+def meet(*arrays):
+    return pl.pallas_call(
+        pass_kernel,
+        in_specs=[pl.BlockSpec(memory_space=pl.ANY)] * len(arrays),
+        out_specs=[pl.BlockSpec(memory_space=pl.ANY)] * len(arrays),
+        out_shape=[jax.ShapeDtypeStruct(array.shape, array.dtype) for array in arrays],
+        input_output_aliases={index: index for index in range(len(arrays))},
+        compiler_params=pltpu.CompilerParams(vmem_limit_bytes=MIB),
+    )(*arrays)
+
+
+def experts_kernel(mine_ref, quad_ref, *refs, cap):
     row_refs, refs = refs[:4], refs[4:]
-    w_gate_ref, w_up_ref, w_down_ref, own_ref, across_ref, other_ref, packed, total = refs
+    w_gate_ref, w_up_ref, w_down_ref, own_ref, across_ref, other_ref, packed = refs
     tokens = row_refs[0].shape[0]
-    step = pl.program_id(0)
-    gates = gate_ref[...]
+    quad = quad_ref[...].astype(jnp.float32)
+    expert = lax.broadcasted_iota(jnp.int32, quad.shape, 0)
+    line = jnp.sum(jnp.where(expert == mine_ref[0], quad, 0.0), axis=0, keepdims=True)
+    gates = jnp.concatenate(
+        [line[:, block * tokens : (block + 1) * tokens] for block in range(4)], axis=0
+    )
     named = gates > 0
     before = (
         lax.broadcasted_iota(jnp.int32, (tokens, tokens), 0)
         < lax.broadcasted_iota(jnp.int32, (tokens, tokens), 1)
     ).astype(jnp.bfloat16)
-    rank = jnp.dot(named.astype(jnp.bfloat16), before, preferred_element_type=jnp.float32)
+    rank = jnp.dot(
+        named.astype(jnp.float32).astype(jnp.bfloat16), before, preferred_element_type=jnp.float32
+    )
     slot = jnp.where(named, rank.astype(jnp.int32), -1)
     slots = lax.broadcasted_iota(jnp.int32, (cap, tokens), 0)
-
-    def chosen_of(block):
-        return slots == slot[block : block + 1, :]
-
-    @pl.when(step == 0)
-    def _():
-        for block in range(4):
-            packed[block * cap : (block + 1) * cap, :] = jnp.dot(
-                chosen_of(block).astype(jnp.bfloat16),
-                row_refs[block][...],
-                preferred_element_type=jnp.float32,
-            ).astype(jnp.bfloat16)
-
+    picks = []
+    weights = []
+    for block in range(4):
+        chosen = slots == slot[block : block + 1, :]
+        picks.append(jnp.where(chosen, 1.0, 0.0).astype(jnp.bfloat16))
+        weights.append(
+            jnp.sum(jnp.where(chosen, gates[block : block + 1, :], 0.0), axis=1, keepdims=True)
+        )
+        packed[block * cap : (block + 1) * cap, :] = jnp.dot(
+            picks[block], row_refs[block][...], preferred_element_type=jnp.float32
+        ).astype(jnp.bfloat16)
     rows = packed[...]
     gate_proj = jnp.dot(rows, w_gate_ref[...], preferred_element_type=jnp.float32)
     up_proj = jnp.dot(rows, w_up_ref[...], preferred_element_type=jnp.float32)
     inner = (gate_proj / (1.0 + jnp.exp(-gate_proj)) * up_proj).astype(jnp.bfloat16)
     result = jnp.dot(inner, w_down_ref[...], preferred_element_type=jnp.float32)
-
-    @pl.when(step == 0)
-    def _():
-        total[...] = result
-
-    @pl.when(step > 0)
-    def _():
-        total[...] += result
-
-    @pl.when(step == pl.num_programs(0) - 1)
-    def _():
-        targets = (
-            own_ref.at[...],
-            other_ref.at[0:tokens],
-            across_ref.at[...],
-            other_ref.at[tokens : 2 * tokens],
-        )
-        for block in range(4):
-            chosen = chosen_of(block)
-            weights = jnp.sum(
-                jnp.where(chosen, gates[block : block + 1, :], 0.0), axis=1, keepdims=True
-            )
-            part = (total[block * cap : (block + 1) * cap, :] * weights).astype(jnp.bfloat16)
-            targets[block][...] = lax.dot_general(
-                chosen.astype(jnp.bfloat16),
-                part,
-                (((0,), (0,)), ((), ())),
-                preferred_element_type=jnp.float32,
-            ).astype(jnp.bfloat16)
-
-
-def experts_on_rows(gates, row_blocks, w_gate, w_up, w_down, cap):
+    targets = (
+        own_ref.at[...],
+        other_ref.at[0:tokens],
+        across_ref.at[...],
+        other_ref.at[tokens : 2 * tokens],
+    )
+    for block in range(4):
+        part = (result[block * cap : (block + 1) * cap, :] * weights[block]).astype(jnp.bfloat16)
+        targets[block][...] = lax.dot_general(
+            picks[block], part, (((0,), (0,)), ((), ())), preferred_element_type=jnp.float32
+        ).astype(jnp.bfloat16)
+
+
+def experts_on_rows(mine, quad, row_blocks, w_gate, w_up, w_down, cap):
     tokens, width = row_blocks[0].shape
     hidden_units = w_gate.shape[1]
-    chunk = hidden_units // 3 if hidden_units % 384 == 0 else hidden_units
-    whole = pl.BlockSpec((tokens, width), lambda step: (0, 0))
     return pl.pallas_call(
         functools.partial(experts_kernel, cap=cap),
-        grid=(hidden_units // chunk,),
-        in_specs=[
-            pl.BlockSpec((4, tokens), lambda step: (0, 0)),
-            whole,
-            whole,
-            whole,
-            whole,
-            pl.BlockSpec((width, chunk), lambda step: (0, step)),
-            pl.BlockSpec((width, chunk), lambda step: (0, step)),
-            pl.BlockSpec((chunk, width), lambda step: (step, 0)),
-        ],
-        out_specs=[whole, whole, pl.BlockSpec((2 * tokens, width), lambda step: (0, 0))],
+        in_specs=[pl.BlockSpec(memory_space=pltpu.SMEM)]
+        + [pl.BlockSpec(memory_space=pltpu.VMEM)] * 8,
+        out_specs=[pl.BlockSpec(memory_space=pltpu.VMEM)] * 3,
         out_shape=[
             jax.ShapeDtypeStruct((tokens, width), jnp.bfloat16),
             jax.ShapeDtypeStruct((tokens, width), jnp.bfloat16),
             jax.ShapeDtypeStruct((2 * tokens, width), jnp.bfloat16),
         ],
-        scratch_shapes=[
-            pltpu.VMEM((4 * cap, width), jnp.bfloat16),
-            pltpu.VMEM((4 * cap, width), jnp.float32),
-        ],
-        compiler_params=pltpu.CompilerParams(vmem_limit_bytes=VMEM_GRANT),
+        scratch_shapes=[pltpu.VMEM((4 * cap, width), jnp.bfloat16)],
+        compiler_params=pltpu.CompilerParams(vmem_limit_bytes=28 * MIB),
         cost_estimate=pl.CostEstimate(
             flops=24 * cap * width * hidden_units,
             bytes_accessed=16 * tokens * width + 6 * width * hidden_units,
             transcendentals=4 * cap * hidden_units,
         ),
-    )(gates, *row_blocks, w_gate, w_up, w_down)
+    )(mine.reshape(1), quad, *row_blocks, w_gate, w_up, w_down)
 
 
 def gathered_plan(
@@ -357,15 +346,14 @@
         lax.ppermute(kv_away, "seq", diagonal),
     ]
     w_other = lax.ppermute(out_proj, "seq", twin)
-    quad = jnp.concatenate([part[tokens:, :tokens] for part in kv_parts], axis=1)
     columns = [place, place ^ 1, place ^ 2, place ^ 3]
 
     def place_of(query_start, row_block):
         return jnp.stack([core, query_start, row_block] + columns).astype(jnp.int32)
 
-    sent = attend(place_of(0 * place, place ^ 2), incoming, kv_parts, out_proj, w_other, jnp.bfloat16)
+    sent, quad = attend(place_of(0 * place, place ^ 2), incoming, kv_parts, out_proj, w_other, jnp.bfloat16)
     projected_across = lax.ppermute(sent, "seq", across)
-    projected = attend(
+    projected, _ = attend(
         place_of(chip * chip_width, place), queries, kv_parts, out_proj, w_other, jnp.float32
     )
     hidden, normed = add_and_norm(residual_in[0], projected, projected_across, norm_gain[None])
@@ -373,79 +361,64 @@
     last = n_sub - 1
     mine = place * n_sub + lax.axis_index("sub")
 
-    def gates_of(quad):
-        row = lax.dynamic_slice_in_dim(quad, mine, 1, 0)
-        return row.reshape(4, tokens).astype(jnp.float32)
-
-    lag = max(n_sub, 4)
     held = {("row", 0): normed, ("quad", 0): quad}
-
-    def move_twin(array):
-        return lax.ppermute(array, "seq", twin)
-
-    def move_across(array):
-        return lax.ppermute(array, "seq", across)
-
-    def move_on(array):
-        return lax.ppermute(array, "sub", ring(1))
-
-    def sum_here(step):
-        return (
-            held["own", step].astype(jnp.float32)
-            + held["met", step][:tokens].astype(jnp.float32)
-            + held["back", step].astype(jnp.float32)
-        )
-
-    for turn in range(1, lag + n_sub + 1):
+    ways = {"across": ("seq", across), "twin": ("seq", twin), "on": ("sub", ring(1))}
+
+    def move(array, way):
+        return lax.ppermute(array, *ways[way])
+
+    def experts_of(step):
+        held["own", step], held["part", step], other = experts_on_rows(
+            mine,
+            held["quad", step],
+            [held[name, step] for name in ("row", "twin", "across", "diagonal")],
+            expert_gate[0],
+            expert_up[0],
+            expert_down[0],
+            cap,
+        )
+        return other
+
+    def twin_sum(step):
+        met = move(held["other", step], "twin")
+        held["met", step] = met[:tokens]
+        return (held["part", step].astype(jnp.float32) + met[tokens:].astype(jnp.float32)).astype(
+            jnp.bfloat16
+        )
+
+    def sum_of(step, more):
+        parts = [held["own", step], held["met", step], held["back", step]] + more
+        return sum(part.astype(jnp.float32) for part in parts)
+
+    for turn in range(1, n_sub + 5):
         now = {}
-        if turn <= n_sub:
-            step = turn - 1
-            now["across", step] = move_across(held["row", step])
+        step = turn - 1
+        if step <= last:
+            now["across", step] = move(held["row", step], "across")
             if step < last:
-                now["row", step + 1] = move_on(held["row", step])
-            held["twin", step] = move_twin(held["row", step])
-        if turn == 1:
+                now["row", step + 1] = move(held["row", step], "on")
+            held["twin", step] = move(held["row", step], "twin")
+        step = turn - 4 if turn < n_sub + 4 else 0
+        if 1 <= step <= last or turn == n_sub + 4:
+            now["back", step] = move(held["away", step], "across")
+        step = turn - 5
+        if 1 <= step <= last:
+            more = [held["sum", step - 1]] if step > 1 else []
+            now["sum", step] = move(sum_of(step, more).astype(jnp.bfloat16), "on")
+        step = turn - 2
+        if 0 <= step <= last:
+            held["diagonal", step] = move(held["across", step], "twin")
+            now["other", step] = experts_of(step)
+        step = turn - 3 if turn < n_sub + 3 else 0
+        if 1 <= step <= last or turn == n_sub + 3:
+            now["away", step] = twin_sum(step)
+        if turn == 2:
             for steps in range(1, n_sub):
                 now["quad", steps] = lax.ppermute(quad, "sub", ring(steps))
-        if 2 <= turn <= n_sub + 1:
-            step = turn - 2
-            held["diagonal", step] = move_twin(held["across", step])
-        back = turn - lag
-        if 1 <= back <= n_sub:
-            step = back % n_sub
-            now["back", step] = move_across(held["away", step])
-        if 2 <= back:
-            step = back - 1
-            part = sum_here(step)
-            if step > 1:
-                part = part + held["sum", step - 1].astype(jnp.float32)
-            now["sum", step] = move_on(part.astype(jnp.bfloat16))
-        step = turn - 2 if turn < lag + n_sub - 2 else 0
-        if turn == lag + n_sub - 2 or 1 <= step <= last:
-            own, away, other = experts_on_rows(
-                gates_of(held["quad", step]),
-                [held[name, step] for name in ("row", "twin", "across", "diagonal")],
-                expert_gate[0],
-                expert_up[0],
-                expert_down[0],
-                cap,
-            )
-            now["other", step] = other
-            held["own", step] = own
-            held["part", step] = away
-        step = turn - 3 if turn < lag + n_sub - 1 else 0
-        if turn == lag + n_sub - 1 or 1 <= step <= last:
-            held["met", step] = move_twin(held["other", step])
-            now["away", step] = (
-                held["part", step].astype(jnp.float32)
-                + held["met", step][tokens:].astype(jnp.float32)
-            ).astype(jnp.bfloat16)
-        if turn < lag + n_sub:
+        if turn < n_sub + 4:
             now = dict(zip(now.keys(), meet(*now.values())))
         held.update(now)
-    total = hidden.astype(jnp.float32) + sum_here(0)
-    if last:
-        total = total + held["sum", last].astype(jnp.float32)
+    total = hidden.astype(jnp.float32) + sum_of(0, [held["sum", last]])
     return total.astype(jnp.bfloat16)[None]
 
 
@@ -468,7 +441,7 @@
     experts = n_seq * n_sub
     topk = expert_ids.shape[2]
     cap = max(2, (5 * tokens * topk + 4 * experts - 1) // (4 * experts))
-    if n_seq == 2 * KVH and KVH == 2 and tokens == HD and experts <= 2 * topk and cap % 16 == 0:
+    if n_seq == 2 * KVH and KVH == 2 and tokens == HD and n_sub > 2 and experts <= 2 * topk and cap % 16 == 0:
         return gathered_plan(
             query_rows,
             key_rows,

time: 185 us -> 167 us (0.903)
  Pallas kernels: 58.2 us -> 33.2 us
  waiting for transfers between devices: 62 us -> 85.8 us
  other arithmetic: 18.2 us -> 2.63 us
  local copies, waits for them, and re-layouts: 18.7 us -> 15.7 us
    ppermute x26, waiting for transfers between devices: 41.5 us -> 74.1 us  [move(): return lax.ppermute(array, *ways[way])]
    pallas_call x4, Pallas kernels: 42.3 us -> 21.1 us  [experts_on_rows(): pl.pallas_call(functools.partial(experts_kernel, cap=cap), in_specs=[pl.B...]
    convert_element_type x11 -> x7, other arithmetic: 15.9 us -> 1.4 us  [the longest x3 0.9 us: gathered_plan(): now['sum', step] = move(sum_of(step, more).astype(jnp.bfloat16), 'on')]
    ppermute x3, waiting for transfers between devices: 7.27 us -> 0.01 us  [gathered_plan(): now['quad', steps] = lax.ppermute(quad, 'sub', ring(steps))]
    ppermute x1, waiting for transfers between devices: 1.2 us -> 6.4 us  [gathered_plan(): lax.ppermute(kv_away, 'seq', diagonal)]
    ppermute x1, waiting for transfers between devices: 6.47 us -> 1.78 us  [gathered_plan(): lax.ppermute(kv_away, 'seq', across)]
    slice x4 -> x0, local copies, waits for them, and re-layouts: 2.7 us -> none  [gathered_plan(): part[tokens:, :tokens]]
    ppermute x26, starting transfers between devices: 16.2 us -> 18.5 us  [move(): return lax.ppermute(array, *ways[way])]
  transfers between devices with their start and end apart: 35 -> 35, of which waited for: 17 -> 19; matrix products, arithmetic and copies ran while one was open for 10% -> 1% of each run, Pallas kernels for 27% -> 15%
where the time goes in v5:
time: 167 us; the launch traced here: 166 us
  waiting for transfers between devices  85.8 us (51%)
  Pallas kernels  33.2 us (20%)
  starting transfers between devices  28.8 us (17%)
  local copies, waits for them, and re-layouts  15.7 us (9%)
  other arithmetic  2.63 us (2%)
    ppermute x26, waiting for transfers between devices, move(): return lax.ppermute(array, *ways[way])  74.1 us
    pallas_call x4, Pallas kernels, experts_on_rows(): pl.pallas_call(functools.partial(experts_kernel, cap=cap), in_specs=[pl.B...  21.1 us
    ppermute x26, starting transfers between devices, move(): return lax.ppermute(array, *ways[way])  18.5 us
    unnamed x34, local copies, waits for them, and re-layouts  15.5 us
    pallas_call x2, Pallas kernels, attend(): pl.pallas_call(functools.partial(attend_kernel, scale=1.0 / HD ** 0.5), i...  9.84 us
    ppermute x1, waiting for transfers between devices, gathered_plan(): lax.ppermute(kv_away, 'seq', diagonal)  6.4 us
    ppermute x3, starting transfers between devices, gathered_plan(): now['quad', steps] = lax.ppermute(quad, 'sub', ring(steps))  3.59 us
    ppermute x1, waiting for transfers between devices, gathered_plan(): projected_across = lax.ppermute(sent, 'seq', across)  3.45 us
  transfers between devices with their start and end apart: 35, of which 19 were waited for; matrix products, arithmetic and copies ran while one was open for 1% of the time, Pallas kernels for 15%

profile of v5, /device:TPU:0, one launch (start us, length us, event | category | flops | bytes accessed | tf_op | source)
XLA Modules:
  0.0 166.3 jit_solution(1570881298972227275)
XLA Ops:
  4.6 2.6 %collective-permute-start.4 = (bf16[128,1024]{1,0:T(8,128)(2,1)S(1)}, bf16[128,1024]{1,0:T(8,128)(2,1)S(1)}, u32[]{:S(2)}, u32[]{:S(2)}) collective-permute-start(bf16[128,1024]{1,0:T(8,128)(2,1)S(1)} %get-tuple-element.51), channel_id=1, source_target_pairs={{0,8},{4,12},{8,0},{12,4},{1,9},{5,13},{9,1},{13,5},{2,10},{6,14},... | collective-permute-start | bytes 786440 | tf_op jit(solution)/shard_map/ppermute | solution.py:341
  7.4 1.7 %collective-permute-start.1 = (bf16[144,256]{1,0:T(8,128)(2,1)S(1)}, bf16[144,256]{1,0:T(8,128)(2,1)S(1)}, u32[]{:S(2)}, u32[]{:S(2)}) collective-permute-start(bf16[144,256]{1,0:T(8,128)(2,1)S(1)} %get-tuple-element.49), channel_id=1, source_target_pairs={{0,8},{4,12},{8,0},{12,4},{1,9},{5,13},{9,1},{13,5},{2,10},{6,14},... | collective-permute-start | bytes 221192 | tf_op jit(solution)/shard_map/ppermute | solution.py:345
  9.1 6.4 %collective-permute-done.2.refs_3_ = bf16[144,256]{1,0:T(8,128)(2,1)S(1)} collective-permute-done((bf16[144,256]{1,0:T(8,128)(2,1)S(1)}, bf16[144,256]{1,0:T(8,128)(2,1)S(1)}, u32[]{:S(2)}, u32[]{:S(2)}) %collective-permute-start.2) | collective-permute-done | bytes 73760 | tf_op jit(solution)/shard_map/ppermute | solution.py:346
  15.5 1.8 %collective-permute-done.1.refs_2_ = bf16[144,256]{1,0:T(8,128)(2,1)S(1)} collective-permute-done((bf16[144,256]{1,0:T(8,128)(2,1)S(1)}, bf16[144,256]{1,0:T(8,128)(2,1)S(1)}, u32[]{:S(2)}, u32[]{:S(2)}) %collective-permute-start.1) | collective-permute-done | bytes 73760 | tf_op jit(solution)/shard_map/ppermute | solution.py:345
  17.3 1.6 copy-done.3
  18.9 5.3 %shard_map.111 = (bf16[128,2048]{1,0:T(8,128)(2,1)}, bf16[16,512]{1,0:T(8,128)(2,1)S(1)}) custom-call(s32[7]{0:T(128)S(1)} %stack.38.place_ref, bf16[128,1024]{1,0:T(8,128)(2,1)S(1)} %collective-permute-done.4.query_ref, bf16[144,256]{1,0:T(8,128)(2,1)S(1)} %get-tuple-element.48.refs_0_, bf16[144,256]{1,0:T(8,128)(2,1)S(1)} %collective-permute-done.refs_1_, ...), custom_call_target="tpu_custom_call" | custom-call | flops 805306368 | bytes 5242880 | tf_op jit(solution)/shard_map/pallas_call | solution.py:149
  24.2 1.8 %collective-permute-start.5 = (bf16[128,2048]{1,0:T(8,128)(2,1)}, bf16[128,2048]{1,0:T(8,128)(2,1)}, u32[]{:S(2)}, u32[]{:S(2)}) collective-permute-start(bf16[128,2048]{1,0:T(8,128)(2,1)} %get-tuple-element.52), channel_id=1, source_target_pairs={{0,8},{4,12},{8,0},{12,4},{1,9},{5,13},{9,1},{13,5},{2,10},{6,14},... | collective-permute-start | bytes 1572872 | tf_op jit(solution)/shard_map/ppermute | solution.py:355
  26.2 1.6 copy-done.4
  27.8 1.6 copy-done.6
  30.4 4.5 %shard_map.110 = (f32[128,2048]{1,0:T(8,128)S(1)}, bf16[16,512]{1,0:T(8,128)(2,1)}) custom-call(s32[7]{0:T(128)S(1)} %stack.37.place_ref, bf16[128,2048]{1,0:T(8,128)(2,1)S(1)} %bitcast.36, bf16[144,256]{1,0:T(8,128)(2,1)S(1)} %get-tuple-element.48.refs_0_, bf16[144,256]{1,0:T(8,128)(2,1)S(1)} %collective-permute-done.refs_1_, ...), custom_call_target="tpu_custom_call" | custom-call | flops 805306368 | bytes 5242880 | tf_op jit(solution)/shard_map/pallas_call | solution.py:149
  34.9 3.4 %collective-permute-done.5.other_ref = bf16[128,2048]{1,0:T(8,128)(2,1)} collective-permute-done((bf16[128,2048]{1,0:T(8,128)(2,1)}, bf16[128,2048]{1,0:T(8,128)(2,1)}, u32[]{:S(2)}, u32[]{:S(2)}) %collective-permute-start.5) | collective-permute-done | bytes 524320 | tf_op jit(solution)/shard_map/ppermute | solution.py:355
  39.4 2.2 %shard_map.112 = (bf16[128,2048]{1,0:T(8,128)(2,1)S(1)}, bf16[128,2048]{1,0:T(8,128)(2,1)}) custom-call(bf16[128,2048]{1,0:T(8,128)(2,1)S(1)} %bitcast.37, f32[128,2048]{1,0:T(8,128)S(1)} %get-tuple-element.50.own_ref, bf16[128,2048]{1,0:T(8,128)(2,1)} %collective-permute-done.5.other_ref, bf16[1,2048]{1,0:T(2,128)(2,1)S(1)} %broadcast_in_dim.6.gain_ref), custom_call_target="tpu_custom_call" | custom-call | tf_op jit(solution)/shard_map/pallas_call | solution.py:190
  42.5 1.6 collective-permute-start.8
  45.6 11.0 %collective-permute-done.8.refs_1_ = bf16[128,2048]{1,0:T(8,128)(2,1)} collective-permute-done((bf16[128,2048]{1,0:T(8,128)(2,1)}, bf16[128,2048]{1,0:T(8,128)(2,1)}, u32[]{:S(2)}, u32[]{:S(2)}) %collective-permute-start.8) | collective-permute-done | bytes 524320 | tf_op jit(solution)/shard_map/ppermute | solution.py:368
  56.8 2.6 %collective-permute-start.11 = (bf16[128,2048]{1,0:T(8,128)(2,1)}, bf16[128,2048]{1,0:T(8,128)(2,1)}, u32[]{:S(2)}, u32[]{:S(2)}) collective-permute-start(bf16[128,2048]{1,0:T(8,128)(2,1)} %get-tuple-element.58.refs_0_), channel_id=1, source_target_pairs={{0,1},{1,3},{3,2},{2,0},{4,5},{5,7},{7,6},{6,4},{8,9},{9,11},{11,1... | collective-permute-start | bytes 1572872 | tf_op jit(solution)/shard_map/ppermute | solution.py:368
  61.2 3.2 %collective-permute-start.13 = (bf16[16,512]{1,0:T(8,128)(2,1)S(1)}, bf16[16,512]{1,0:T(8,128)(2,1)S(1)}, u32[]{:S(2)}, u32[]{:S(2)}) collective-permute-start(bf16[16,512]{1,0:T(8,128)(2,1)S(1)} %get-tuple-element.54.quad_ref), channel_id=1, source_target_pairs={{0,3},{1,2},{3,0},{2,1},{4,7},{5,6},{7,4},{6,5},{8,11},{9,10},{11,... | collective-permute-start | bytes 49160 | tf_op jit(solution)/shard_map/ppermute | solution.py:417
  64.5 1.9 %copy-done.1 = bf16[1,2048,768]{2,1,0:T(8,128)(2,1)S(1)} copy-done((bf16[1,2048,768]{2,1,0:T(8,128)(2,1)S(1)}, bf16[1,2048,768]{2,1,0:T(8,128)(2,1)}, u32[]{:S(2)}) %copy-start.1) | copy-done | bytes 3145752
  66.3 1.9 %copy-done.2 = bf16[1,768,2048]{2,1,0:T(8,128)(2,1)S(1)} copy-done((bf16[1,768,2048]{2,1,0:T(8,128)(2,1)S(1)}, bf16[1,768,2048]{2,1,0:T(8,128)(2,1)}, u32[]{:S(2)}) %copy-start.2) | copy-done | bytes 3145752
  68.2 5.8 %shard_map.114 = (bf16[128,2048]{1,0:T(8,128)(2,1)S(1)}, bf16[128,2048]{1,0:T(8,128)(2,1)S(1)}, bf16[256,2048]{1,0:T(8,128)(2,1)S(1)}) custom-call(s32[1]{0:T(128)} %bitcast.15.mine_ref, bf16[16,512]{1,0:T(8,128)(2,1)S(1)} %get-tuple-element.54.quad_ref, bf16[128,2048]{1,0:T(8,128)(2,1)} %get-tuple-element.55.refs_0_, ...), custom_call_target="tpu_custom_call" | custom-call | flops 3019898880 | bytes 13631488 | tf_op jit(solution)/shard_map/pallas_call | solution.py:280
  77.0 5.5 %shard_map.116 = (bf16[128,2048]{1,0:T(8,128)(2,1)S(1)}, bf16[128,2048]{1,0:T(8,128)(2,1)S(1)}, bf16[256,2048]{1,0:T(8,128)(2,1)S(1)}) custom-call(s32[1]{0:T(128)} %bitcast.15.mine_ref, bf16[16,512]{1,0:T(8,128)(2,1)S(1)} %get-tuple-element.62.quad_ref, bf16[128,2048]{1,0:T(8,128)(2,1)} %get-tuple-element.58.refs_0_, ...), custom_call_target="tpu_custom_call" | custom-call | flops 3019898880 | bytes 13631488 | tf_op jit(solution)/shard_map/pallas_call | solution.py:280
  82.5 7.7 %collective-permute-done.17.refs_1_ = bf16[128,2048]{1,0:T(8,128)(2,1)S(1)} collective-permute-done((bf16[128,2048]{1,0:T(8,128)(2,1)}, bf16[128,2048]{1,0:T(8,128)(2,1)S(1)}, u32[]{:S(2)}, u32[]{:S(2)}) %collective-permute-start.17) | collective-permute-done | bytes 524320 | tf_op jit(solution)/shard_map/ppermute | solution.py:368
  91.3 2.9 %collective-permute-done.21.refs_1_ = bf16[128,2048]{1,0:T(8,128)(2,1)S(1)} collective-permute-done((bf16[128,2048]{1,0:T(8,128)(2,1)}, bf16[128,2048]{1,0:T(8,128)(2,1)S(1)}, u32[]{:S(2)}, u32[]{:S(2)}) %collective-permute-start.21) | collective-permute-done | bytes 524320 | tf_op jit(solution)/shard_map/ppermute | solution.py:368
  94.4 5.4 %shard_map.118 = (bf16[128,2048]{1,0:T(8,128)(2,1)S(1)}, bf16[128,2048]{1,0:T(8,128)(2,1)S(1)}, bf16[256,2048]{1,0:T(8,128)(2,1)S(1)}) custom-call(s32[1]{0:T(128)} %bitcast.15.mine_ref, bf16[16,512]{1,0:T(8,128)(2,1)S(1)} %get-tuple-element.66.quad_ref, bf16[128,2048]{1,0:T(8,128)(2,1)} %get-tuple-element.61.refs_0_, ...), custom_call_target="tpu_custom_call" | custom-call | flops 3019898880 | bytes 13631488 | tf_op jit(solution)/shard_map/pallas_call | solution.py:280
  99.9 5.2 %collective-permute-done.20.refs_0_ = bf16[128,2048]{1,0:T(8,128)(2,1)S(1)} collective-permute-done((bf16[128,2048]{1,0:T(8,128)(2,1)S(1)}, bf16[128,2048]{1,0:T(8,128)(2,1)S(1)}, u32[]{:S(2)}, u32[]{:S(2)}) %collective-permute-start.20) | collective-permute-done | bytes 524320 | tf_op jit(solution)/shard_map/ppermute | solution.py:368
  106.1 2.3 %collective-permute-done.25.refs_1_ = bf16[128,2048]{1,0:T(8,128)(2,1)S(1)} collective-permute-done((bf16[128,2048]{1,0:T(8,128)(2,1)S(1)}, bf16[128,2048]{1,0:T(8,128)(2,1)S(1)}, u32[]{:S(2)}, u32[]{:S(2)}) %collective-permute-start.25) | collective-permute-done | bytes 524320 | tf_op jit(solution)/shard_map/ppermute | solution.py:368
  109.2 4.3 %shard_map.120 = (bf16[128,2048]{1,0:T(8,128)(2,1)S(1)}, bf16[128,2048]{1,0:T(8,128)(2,1)S(1)}, bf16[256,2048]{1,0:T(8,128)(2,1)S(1)}) custom-call(s32[1]{0:T(128)} %bitcast.15.mine_ref, bf16[16,512]{1,0:T(8,128)(2,1)S(1)} %get-tuple-element.72.quad_ref, bf16[128,2048]{1,0:T(8,128)(2,1)S(1)} %get-tuple-element.65.refs_0_, ...), custom_call_target="tpu_custom_call" | custom-call | flops 3019898880 | bytes 13631488 | tf_op jit(solution)/shard_map/pallas_call | solution.py:280
  113.7 6.2 %collective-permute-done.24.refs_0_ = bf16[128,2048]{1,0:T(8,128)(2,1)S(1)} collective-permute-done((bf16[128,2048]{1,0:T(8,128)(2,1)S(1)}, bf16[128,2048]{1,0:T(8,128)(2,1)S(1)}, u32[]{:S(2)}, u32[]{:S(2)}) %collective-permute-start.24) | collective-permute-done | bytes 524320 | tf_op jit(solution)/shard_map/ppermute | solution.py:368
  120.7 2.5 %collective-permute-start.29 = (bf16[128,2048]{1,0:T(8,128)(2,1)S(1)}, bf16[128,2048]{1,0:T(8,128)(2,1)S(1)}, u32[]{:S(2)}, u32[]{:S(2)}) collective-permute-start(bf16[128,2048]{1,0:T(8,128)(2,1)S(1)} %add_convert_fusion.5), channel_id=1, source_target_pairs={{0,1},{1,3},{3,2},{2,0},{4,5},{5,7},{7,6},{6,4},{8,9},{9,11},{11,1... | collective-permute-start | bytes 1572872 | tf_op jit(solution)/shard_map/ppermute | solution.py:368
  123.4 10.9 %collective-permute-done.28.refs_0_ = bf16[128,2048]{1,0:T(8,128)(2,1)S(1)} collective-permute-done((bf16[128,2048]{1,0:T(8,128)(2,1)S(1)}, bf16[128,2048]{1,0:T(8,128)(2,1)S(1)}, u32[]{:S(2)}, u32[]{:S(2)}) %collective-permute-start.28) | collective-permute-done | bytes 524320 | tf_op jit(solution)/shard_map/ppermute | solution.py:368
  138.4 10.6 %collective-permute-done.31.refs_0_ = bf16[128,2048]{1,0:T(8,128)(2,1)S(1)} collective-permute-done((bf16[128,2048]{1,0:T(8,128)(2,1)S(1)}, bf16[128,2048]{1,0:T(8,128)(2,1)S(1)}, u32[]{:S(2)}, u32[]{:S(2)}) %collective-permute-start.31) | collective-permute-done | bytes 524320 | tf_op jit(solution)/shard_map/ppermute | solution.py:368
  149.0 2.5 %collective-permute-done.32.refs_1_ = bf16[128,2048]{1,0:T(8,128)(2,1)S(1)} collective-permute-done((bf16[128,2048]{1,0:T(8,128)(2,1)S(1)}, bf16[128,2048]{1,0:T(8,128)(2,1)S(1)}, u32[]{:S(2)}, u32[]{:S(2)}) %collective-permute-start.32) | collective-permute-done | bytes 524320 | tf_op jit(solution)/shard_map/ppermute | solution.py:368
  153.1 10.4 %collective-permute-done.33 = bf16[128,2048]{1,0:T(8,128)(2,1)S(1)} collective-permute-done((bf16[128,2048]{1,0:T(8,128)(2,1)S(1)}, bf16[128,2048]{1,0:T(8,128)(2,1)S(1)}, u32[]{:S(2)}, u32[]{:S(2)}) %collective-permute-start.33) | collective-permute-done | bytes 524320 | tf_op jit(solution)/shard_map/ppermute | solution.py:368
  (98 shorter events, 27.0 us)
Async XLA Ops:
  0.0 17.3 %collective-permute-start.3 = (bf16[512,2048]{1,0:T(8,128)(2,1)}, bf16[512,2048]{1,0:T(8,128)(2,1)S(1)}, u32[]{:S(2)}, u32[]{:S(2)}) collective-permute-start(bf16[512,2048]{1,0:T(8,128)(2,1)} %refs_4_.3), channel_id=1, source_target_pairs={{0,4},{4,0},{8,12},{12,8},{1,5},{5,1},{9,13},{13,9},{2,6},{6,2},{1... | collective-permute-start | bytes 6291464 | tf_op jit(solution)/shard_map/ppermute | solution.py:348
  4.6 12.7 %collective-permute-start.4 = (bf16[128,1024]{1,0:T(8,128)(2,1)S(1)}, bf16[128,1024]{1,0:T(8,128)(2,1)S(1)}, u32[]{:S(2)}, u32[]{:S(2)}) collective-permute-start(bf16[128,1024]{1,0:T(8,128)(2,1)S(1)} %get-tuple-element.51), channel_id=1, source_target_pairs={{0,8},{4,12},{8,0},{12,4},{1,9},{5,13},{9,1},{13,5},{2,10},{6,14},... | collective-permute-start | bytes 786440 | tf_op jit(solution)/shard_map/ppermute | solution.py:341
  7.2 8.3 %collective-permute-start.2 = (bf16[144,256]{1,0:T(8,128)(2,1)S(1)}, bf16[144,256]{1,0:T(8,128)(2,1)S(1)}, u32[]{:S(2)}, u32[]{:S(2)}) collective-permute-start(bf16[144,256]{1,0:T(8,128)(2,1)S(1)} %get-tuple-element.49), channel_id=1, source_target_pairs={{0,12},{4,8},{8,4},{12,0},{1,13},{5,9},{9,5},{13,1},{2,14},{6,10},... | collective-permute-start | bytes 221192 | tf_op jit(solution)/shard_map/ppermute | solution.py:346
  7.4 9.9 %collective-permute-start.1 = (bf16[144,256]{1,0:T(8,128)(2,1)S(1)}, bf16[144,256]{1,0:T(8,128)(2,1)S(1)}, u32[]{:S(2)}, u32[]{:S(2)}) collective-permute-start(bf16[144,256]{1,0:T(8,128)(2,1)S(1)} %get-tuple-element.49), channel_id=1, source_target_pairs={{0,8},{4,12},{8,0},{12,4},{1,9},{5,13},{9,1},{13,5},{2,10},{6,14},... | collective-permute-start | bytes 221192 | tf_op jit(solution)/shard_map/ppermute | solution.py:345
  9.1 8.3 %collective-permute-start = (bf16[144,256]{1,0:T(8,128)(2,1)S(1)}, bf16[144,256]{1,0:T(8,128)(2,1)S(1)}, u32[]{:S(2)}, u32[]{:S(2)}) collective-permute-start(bf16[144,256]{1,0:T(8,128)(2,1)S(1)} %get-tuple-element.48.refs_0_), channel_id=1, source_target_pairs={{0,4},{4,0},{8,12},{12,8},{1,5},{5,1},{9,13},{13,9},{2,6},{6,2},{1... | collective-permute-start | bytes 221192 | tf_op jit(solution)/shard_map/ppermute | solution.py:344
  24.2 14.1 %collective-permute-start.5 = (bf16[128,2048]{1,0:T(8,128)(2,1)}, bf16[128,2048]{1,0:T(8,128)(2,1)}, u32[]{:S(2)}, u32[]{:S(2)}) collective-permute-start(bf16[128,2048]{1,0:T(8,128)(2,1)} %get-tuple-element.52), channel_id=1, source_target_pairs={{0,8},{4,12},{8,0},{12,4},{1,9},{5,13},{9,1},{13,5},{2,10},{6,14},... | collective-permute-start | bytes 1572872 | tf_op jit(solution)/shard_map/ppermute | solution.py:355
  42.5 14.1 %collective-permute-start.8 = (bf16[128,2048]{1,0:T(8,128)(2,1)}, bf16[128,2048]{1,0:T(8,128)(2,1)}, u32[]{:S(2)}, u32[]{:S(2)}) collective-permute-start(bf16[128,2048]{1,0:T(8,128)(2,1)} %get-tuple-element.55.refs_0_), channel_id=1, source_target_pairs={{0,1},{1,3},{3,2},{2,0},{4,5},{5,7},{7,6},{6,4},{8,9},{9,11},{11,1... | collective-permute-start | bytes 1572872 | tf_op jit(solution)/shard_map/ppermute | solution.py:368
  44.0 12.7 %collective-permute-start.7 = (bf16[128,2048]{1,0:T(8,128)(2,1)}, bf16[128,2048]{1,0:T(8,128)(2,1)}, u32[]{:S(2)}, u32[]{:S(2)}) collective-permute-start(bf16[128,2048]{1,0:T(8,128)(2,1)} %get-tuple-element.55.refs_0_), channel_id=1, source_target_pairs={{0,8},{4,12},{8,0},{12,4},{1,9},{5,13},{9,1},{13,5},{2,10},{6,14},... | collective-permute-start | bytes 1572872 | tf_op jit(solution)/shard_map/ppermute | solution.py:368
  45.6 15.6 %collective-permute-start.6 = (bf16[128,2048]{1,0:T(8,128)(2,1)}, bf16[128,2048]{1,0:T(8,128)(2,1)}, u32[]{:S(2)}, u32[]{:S(2)}) collective-permute-start(bf16[128,2048]{1,0:T(8,128)(2,1)} %get-tuple-element.55.refs_0_), channel_id=1, source_target_pairs={{0,4},{4,0},{8,12},{12,8},{1,5},{5,1},{9,13},{13,9},{2,6},{6,2},{1... | collective-permute-start | bytes 1572872 | tf_op jit(solution)/shard_map/ppermute | solution.py:368
  56.8 7.7 %collective-permute-start.9 = (bf16[128,2048]{1,0:T(8,128)(2,1)}, bf16[128,2048]{1,0:T(8,128)(2,1)}, u32[]{:S(2)}, u32[]{:S(2)}) collective-permute-start(bf16[128,2048]{1,0:T(8,128)(2,1)} %get-tuple-element.56.refs_2_), channel_id=1, source_target_pairs={{0,4},{4,0},{8,12},{12,8},{1,5},{5,1},{9,13},{13,9},{2,6},{6,2},{1... | collective-permute-start | bytes 1572872 | tf_op jit(solution)/shard_map/ppermute | solution.py:368
  56.8 17.4 %collective-permute-start.11 = (bf16[128,2048]{1,0:T(8,128)(2,1)}, bf16[128,2048]{1,0:T(8,128)(2,1)}, u32[]{:S(2)}, u32[]{:S(2)}) collective-permute-start(bf16[128,2048]{1,0:T(8,128)(2,1)} %get-tuple-element.58.refs_0_), channel_id=1, source_target_pairs={{0,1},{1,3},{3,2},{2,0},{4,5},{5,7},{7,6},{6,4},{8,9},{9,11},{11,1... | collective-permute-start | bytes 1572872 | tf_op jit(solution)/shard_map/ppermute | solution.py:368
  59.3 14.9 %collective-permute-start.10 = (bf16[128,2048]{1,0:T(8,128)(2,1)}, bf16[128,2048]{1,0:T(8,128)(2,1)}, u32[]{:S(2)}, u32[]{:S(2)}) collective-permute-start(bf16[128,2048]{1,0:T(8,128)(2,1)} %get-tuple-element.58.refs_0_), channel_id=1, source_target_pairs={{0,8},{4,12},{8,0},{12,4},{1,9},{5,13},{9,1},{13,5},{2,10},{6,14},... | collective-permute-start | bytes 1572872 | tf_op jit(solution)/shard_map/ppermute | solution.py:368
  60.8 13.2 %collective-permute-start.14 = (bf16[16,512]{1,0:T(8,128)(2,1)S(1)}, bf16[16,512]{1,0:T(8,128)(2,1)S(1)}, u32[]{:S(2)}, u32[]{:S(2)}) collective-permute-start(bf16[16,512]{1,0:T(8,128)(2,1)S(1)} %get-tuple-element.54.quad_ref), channel_id=1, source_target_pairs={{0,2},{1,0},{3,1},{2,3},{4,6},{5,4},{7,5},{6,7},{8,10},{9,8},{11,9... | collective-permute-start | bytes 49160 | tf_op jit(solution)/shard_map/ppermute | solution.py:417
  61.2 13.0 %collective-permute-start.13 = (bf16[16,512]{1,0:T(8,128)(2,1)S(1)}, bf16[16,512]{1,0:T(8,128)(2,1)S(1)}, u32[]{:S(2)}, u32[]{:S(2)}) collective-permute-start(bf16[16,512]{1,0:T(8,128)(2,1)S(1)} %get-tuple-element.54.quad_ref), channel_id=1, source_target_pairs={{0,3},{1,2},{3,0},{2,1},{4,7},{5,6},{7,4},{6,5},{8,11},{9,10},{11,... | collective-permute-start | bytes 49160 | tf_op jit(solution)/shard_map/ppermute | solution.py:417
  64.4 9.7 %collective-permute-start.12 = (bf16[16,512]{1,0:T(8,128)(2,1)S(1)}, bf16[16,512]{1,0:T(8,128)(2,1)S(1)}, u32[]{:S(2)}, u32[]{:S(2)}) collective-permute-start(bf16[16,512]{1,0:T(8,128)(2,1)S(1)} %get-tuple-element.54.quad_ref), channel_id=1, source_target_pairs={{0,1},{1,3},{3,2},{2,0},{4,5},{5,7},{7,6},{6,4},{8,9},{9,11},{11,1... | collective-permute-start | bytes 49160 | tf_op jit(solution)/shard_map/ppermute | solution.py:417
  74.8 15.5 %collective-permute-start.17 = (bf16[128,2048]{1,0:T(8,128)(2,1)}, bf16[128,2048]{1,0:T(8,128)(2,1)S(1)}, u32[]{:S(2)}, u32[]{:S(2)}) collective-permute-start(bf16[128,2048]{1,0:T(8,128)(2,1)} %get-tuple-element.61.refs_0_), channel_id=1, source_target_pairs={{0,1},{1,3},{3,2},{2,0},{4,5},{5,7},{7,6},{6,4},{8,9},{9,11},{11,1... | collective-permute-start | bytes 1572872 | tf_op jit(solution)/shard_map/ppermute | solution.py:368
  75.9 14.3 %collective-permute-start.16 = (bf16[128,2048]{1,0:T(8,128)(2,1)}, bf16[128,2048]{1,0:T(8,128)(2,1)S(1)}, u32[]{:S(2)}, u32[]{:S(2)}) collective-permute-start(bf16[128,2048]{1,0:T(8,128)(2,1)} %get-tuple-element.61.refs_0_), channel_id=1, source_target_pairs={{0,8},{4,12},{8,0},{12,4},{1,9},{5,13},{9,1},{13,5},{2,10},{6,14},... | collective-permute-start | bytes 1572872 | tf_op jit(solution)/shard_map/ppermute | solution.py:368
  90.2 9.5 %collective-permute-start.23 = (bf16[256,2048]{1,0:T(8,128)(2,1)S(1)}, bf16[256,2048]{1,0:T(8,128)(2,1)S(1)}, u32[]{:S(2)}, u32[]{:S(2)}) collective-permute-start(bf16[256,2048]{1,0:T(8,128)(2,1)S(1)} %get-tuple-element.70), channel_id=1, source_target_pairs={{0,4},{4,0},{8,12},{12,8},{1,5},{5,1},{9,13},{13,9},{2,6},{6,2},{1... | collective-permute-start | bytes 3145736 | tf_op jit(solution)/shard_map/ppermute | solution.py:368
  90.2 4.0 %collective-permute-start.21 = (bf16[128,2048]{1,0:T(8,128)(2,1)}, bf16[128,2048]{1,0:T(8,128)(2,1)S(1)}, u32[]{:S(2)}, u32[]{:S(2)}) collective-permute-start(bf16[128,2048]{1,0:T(8,128)(2,1)} %get-tuple-element.61.refs_0_), channel_id=1, source_target_pairs={{0,4},{4,0},{8,12},{12,8},{1,5},{5,1},{9,13},{13,9},{2,6},{6,2},{1... | collective-permute-start | bytes 1572872 | tf_op jit(solution)/shard_map/ppermute | solution.py:368
  90.7 3.6 %collective-permute-start.22 = (bf16[128,2048]{1,0:T(8,128)(2,1)S(1)}, bf16[128,2048]{1,0:T(8,128)(2,1)S(1)}, u32[]{:S(2)}, u32[]{:S(2)}) collective-permute-start(bf16[128,2048]{1,0:T(8,128)(2,1)S(1)} %get-tuple-element.67.refs_2_), channel_id=1, source_target_pairs={{0,4},{4,0},{8,12},{12,8},{1,5},{5,1},{9,13},{13,9},{2,6},{6,2},{1... | collective-permute-start | bytes 1572872 | tf_op jit(solution)/shard_map/ppermute | solution.py:368
  90.8 14.3 %collective-permute-start.20 = (bf16[128,2048]{1,0:T(8,128)(2,1)S(1)}, bf16[128,2048]{1,0:T(8,128)(2,1)S(1)}, u32[]{:S(2)}, u32[]{:S(2)}) collective-permute-start(bf16[128,2048]{1,0:T(8,128)(2,1)S(1)} %get-tuple-element.65.refs_0_), channel_id=1, source_target_pairs={{0,8},{4,12},{8,0},{12,4},{1,9},{5,13},{9,1},{13,5},{2,10},{6,14},... | collective-permute-start | bytes 1572872 | tf_op jit(solution)/shard_map/ppermute | solution.py:368
  105.1 8.5 %collective-permute-start.27 = (bf16[256,2048]{1,0:T(8,128)(2,1)S(1)}, bf16[256,2048]{1,0:T(8,128)(2,1)S(1)}, u32[]{:S(2)}, u32[]{:S(2)}) collective-permute-start(bf16[256,2048]{1,0:T(8,128)(2,1)S(1)} %get-tuple-element.76), channel_id=1, source_target_pairs={{0,4},{4,0},{8,12},{12,8},{1,5},{5,1},{9,13},{13,9},{2,6},{6,2},{1... | collective-permute-start | bytes 3145736 | tf_op jit(solution)/shard_map/ppermute | solution.py:368
  105.1 3.4 %collective-permute-start.25 = (bf16[128,2048]{1,0:T(8,128)(2,1)S(1)}, bf16[128,2048]{1,0:T(8,128)(2,1)S(1)}, u32[]{:S(2)}, u32[]{:S(2)}) collective-permute-start(bf16[128,2048]{1,0:T(8,128)(2,1)S(1)} %get-tuple-element.65.refs_0_), channel_id=1, source_target_pairs={{0,4},{4,0},{8,12},{12,8},{1,5},{5,1},{9,13},{13,9},{2,6},{6,2},{1... | collective-permute-start | bytes 1572872 | tf_op jit(solution)/shard_map/ppermute | solution.py:368
  105.6 3.6 %collective-permute-start.26 = (bf16[128,2048]{1,0:T(8,128)(2,1)S(1)}, bf16[128,2048]{1,0:T(8,128)(2,1)S(1)}, u32[]{:S(2)}, u32[]{:S(2)}) collective-permute-start(bf16[128,2048]{1,0:T(8,128)(2,1)S(1)} %get-tuple-element.73.refs_2_), channel_id=1, source_target_pairs={{0,4},{4,0},{8,12},{12,8},{1,5},{5,1},{9,13},{13,9},{2,6},{6,2},{1... | collective-permute-start | bytes 1572872 | tf_op jit(solution)/shard_map/ppermute | solution.py:368
  105.6 14.3 %collective-permute-start.24 = (bf16[128,2048]{1,0:T(8,128)(2,1)S(1)}, bf16[128,2048]{1,0:T(8,128)(2,1)S(1)}, u32[]{:S(2)}, u32[]{:S(2)}) collective-permute-start(bf16[128,2048]{1,0:T(8,128)(2,1)S(1)} %get-tuple-element.71), channel_id=1, source_target_pairs={{0,8},{4,12},{8,0},{12,4},{1,9},{5,13},{9,1},{13,5},{2,10},{6,14},... | collective-permute-start | bytes 1572872 | tf_op jit(solution)/shard_map/ppermute | solution.py:368
  119.9 14.3 %collective-permute-start.28 = (bf16[128,2048]{1,0:T(8,128)(2,1)S(1)}, bf16[128,2048]{1,0:T(8,128)(2,1)S(1)}, u32[]{:S(2)}, u32[]{:S(2)}) collective-permute-start(bf16[128,2048]{1,0:T(8,128)(2,1)S(1)} %get-tuple-element.77), channel_id=1, source_target_pairs={{0,8},{4,12},{8,0},{12,4},{1,9},{5,13},{9,1},{13,5},{2,10},{6,14},... | collective-permute-start | bytes 1572872 | tf_op jit(solution)/shard_map/ppermute | solution.py:368
  120.7 15.0 %collective-permute-start.29 = (bf16[128,2048]{1,0:T(8,128)(2,1)S(1)}, bf16[128,2048]{1,0:T(8,128)(2,1)S(1)}, u32[]{:S(2)}, u32[]{:S(2)}) collective-permute-start(bf16[128,2048]{1,0:T(8,128)(2,1)S(1)} %add_convert_fusion.5), channel_id=1, source_target_pairs={{0,1},{1,3},{3,2},{2,0},{4,5},{5,7},{7,6},{6,4},{8,9},{9,11},{11,1... | collective-permute-start | bytes 1572872 | tf_op jit(solution)/shard_map/ppermute | solution.py:368
  123.3 15.0 %collective-permute-start.15 = (bf16[256,2048]{1,0:T(8,128)(2,1)S(1)}, bf16[256,2048]{1,0:T(8,128)(2,1)S(1)}, u32[]{:S(2)}, u32[]{:S(2)}) collective-permute-start(bf16[256,2048]{1,0:T(8,128)(2,1)S(1)} %get-tuple-element.60), channel_id=1, source_target_pairs={{0,4},{4,0},{8,12},{12,8},{1,5},{5,1},{9,13},{13,9},{2,6},{6,2},{1... | collective-permute-start | bytes 3145736 | tf_op jit(solution)/shard_map/ppermute | solution.py:368
  135.7 13.2 %collective-permute-start.31 = (bf16[128,2048]{1,0:T(8,128)(2,1)S(1)}, bf16[128,2048]{1,0:T(8,128)(2,1)S(1)}, u32[]{:S(2)}, u32[]{:S(2)}) collective-permute-start(bf16[128,2048]{1,0:T(8,128)(2,1)S(1)} %get-tuple-element.82), channel_id=1, source_target_pairs={{0,8},{4,12},{8,0},{12,4},{1,9},{5,13},{9,1},{13,5},{2,10},{6,14},... | collective-permute-start | bytes 1572872 | tf_op jit(solution)/shard_map/ppermute | solution.py:368
  137.6 13.9 %collective-permute-start.32 = (bf16[128,2048]{1,0:T(8,128)(2,1)S(1)}, bf16[128,2048]{1,0:T(8,128)(2,1)S(1)}, u32[]{:S(2)}, u32[]{:S(2)}) collective-permute-start(bf16[128,2048]{1,0:T(8,128)(2,1)S(1)} %add_convert_fusion.3), channel_id=1, source_target_pairs={{0,1},{1,3},{3,2},{2,0},{4,5},{5,7},{7,6},{6,4},{8,9},{9,11},{11,1... | collective-permute-start | bytes 1572872 | tf_op jit(solution)/shard_map/ppermute | solution.py:368
  151.5 12.0 %collective-permute-start.33 = (bf16[128,2048]{1,0:T(8,128)(2,1)S(1)}, bf16[128,2048]{1,0:T(8,128)(2,1)S(1)}, u32[]{:S(2)}, u32[]{:S(2)}) collective-permute-start(bf16[128,2048]{1,0:T(8,128)(2,1)S(1)} %get-tuple-element.87), channel_id=1, source_target_pairs={{0,8},{4,12},{8,0},{12,4},{1,9},{5,13},{9,1},{13,5},{2,10},{6,14},... | collective-permute-start | bytes 1572872 | tf_op jit(solution)/shard_map/ppermute | solution.py:368
  152.4 12.7 %collective-permute-start.34 = (bf16[128,2048]{1,0:T(8,128)(2,1)S(1)}, bf16[128,2048]{1,0:T(8,128)(2,1)S(1)}, u32[]{:S(2)}, u32[]{:S(2)}) collective-permute-start(bf16[128,2048]{1,0:T(8,128)(2,1)S(1)} %add_convert_fusion.1), channel_id=1, source_target_pairs={{0,1},{1,3},{3,2},{2,0},{4,5},{5,7},{7,6},{6,4},{8,9},{9,11},{11,1... | collective-permute-start | bytes 1572872 | tf_op jit(solution)/shard_map/ppermute | solution.py:368
  (20 other events, 119.3 us)

commit v6 on v5

--- a/solution.py
+++ b/solution.py
@@ -90,13 +90,14 @@
         + [pl.BlockSpec(memory_space=pltpu.VMEM)] * 5,
         out_specs=[pl.BlockSpec(memory_space=pltpu.VMEM)] * 3,
         out_shape=[jax.ShapeDtypeStruct((tokens, width // 2), jnp.bfloat16), kv, kv],
-        compiler_params=pltpu.CompilerParams(vmem_limit_bytes=6 * MIB),
+        compiler_params=pltpu.CompilerParams(vmem_limit_bytes=60 * MIB),
     )(chip.reshape(1), queries, keys, values, ids, gates)
 
 
 def attend_kernel(place_ref, query_ref, *refs, scale):
     kv_refs, refs = refs[:4], refs[4:]
-    w_own_ref, w_other_ref, out_ref, quad_ref, keys, values, heads, w_own, w_other, done = refs
+    base_refs = refs[: len(refs) - 10]
+    w_own_ref, w_other_ref, out_ref, quad_ref, keys, values, heads, w_own, w_other, done = refs[-10:]
     fetches = [
         pltpu.make_async_copy(w_own_ref, w_own, done.at[0]),
         pltpu.make_async_copy(w_other_ref, w_other, done.at[1]),
@@ -136,20 +137,22 @@
     half = heads.shape[1] // 2
     own = heads[:, pl.ds(pl.multiple_of(core * half, half), half)]
     other = heads[:, pl.ds(pl.multiple_of((1 - core) * half, half), half)]
-    out_ref[...] = (
-        jnp.dot(own, w_own[...], preferred_element_type=jnp.float32)
-        + jnp.dot(other, w_other[...], preferred_element_type=jnp.float32)
-    ).astype(out_ref.dtype)
-
-
-def attend(place, queries, kv_parts, w_own, w_other, dtype):
+    total = jnp.dot(own, w_own[...], preferred_element_type=jnp.float32) + jnp.dot(
+        other, w_other[...], preferred_element_type=jnp.float32
+    )
+    for base_ref in base_refs:
+        total += base_ref[...].astype(jnp.float32)
+    out_ref[...] = total.astype(out_ref.dtype)
+
+
+def attend(place, queries, kv_parts, bases, w_own, w_other, dtype):
     tokens = queries.shape[0]
     width = w_own.shape[1]
     chip_width = 2 * w_own.shape[0]
     return pl.pallas_call(
         functools.partial(attend_kernel, scale=1.0 / HD**0.5),
         in_specs=[pl.BlockSpec(memory_space=pltpu.SMEM)]
-        + [pl.BlockSpec(memory_space=pltpu.VMEM)] * 5
+        + [pl.BlockSpec(memory_space=pltpu.VMEM)] * (5 + len(bases))
         + [pl.BlockSpec(memory_space=pl.ANY)] * 2,
         out_specs=[pl.BlockSpec(memory_space=pltpu.VMEM)] * 2,
         out_shape=[
@@ -170,13 +173,11 @@
             bytes_accessed=4 * w_own.size + 4 * tokens * width,
             transcendentals=4 * tokens * tokens * chip_width // HD,
         ),
-    )(place, queries, *kv_parts, w_own, w_other)
-
-
-def norm_kernel(residual_ref, own_ref, other_ref, gain_ref, hidden_ref, normed_ref):
-    hidden = (
-        residual_ref[...].astype(jnp.float32) + own_ref[...] + other_ref[...].astype(jnp.float32)
-    ).astype(jnp.bfloat16)
+    )(place, queries, *kv_parts, *bases, w_own, w_other)
+
+
+def norm_kernel(own_ref, other_ref, gain_ref, hidden_ref, normed_ref):
+    hidden = (own_ref[...] + other_ref[...].astype(jnp.float32)).astype(jnp.bfloat16)
     hidden_ref[...] = hidden
     wide = hidden.astype(jnp.float32)
     normed_ref[...] = (
@@ -186,14 +187,14 @@
     ).astype(jnp.bfloat16)
 
 
-def add_and_norm(residual, own, other, gain):
+def add_and_norm(own, other, gain):
     return pl.pallas_call(
         norm_kernel,
-        in_specs=[pl.BlockSpec(memory_space=pltpu.VMEM)] * 4,
+        in_specs=[pl.BlockSpec(memory_space=pltpu.VMEM)] * 3,
         out_specs=[pl.BlockSpec(memory_space=pltpu.VMEM)] * 2,
-        out_shape=[jax.ShapeDtypeStruct(residual.shape, jnp.bfloat16)] * 2,
+        out_shape=[jax.ShapeDtypeStruct(own.shape, jnp.bfloat16)] * 2,
         compiler_params=pltpu.CompilerParams(vmem_limit_bytes=10 * MIB),
-    )(residual, own, other, gain)
+    )(own, other, gain)
 
 
 def pass_kernel(*refs):
@@ -351,12 +352,20 @@
     def place_of(query_start, row_block):
         return jnp.stack([core, query_start, row_block] + columns).astype(jnp.int32)
 
-    sent, quad = attend(place_of(0 * place, place ^ 2), incoming, kv_parts, out_proj, w_other, jnp.bfloat16)
+    sent, quad = attend(
+        place_of(0 * place, place ^ 2), incoming, kv_parts, [], out_proj, w_other, jnp.bfloat16
+    )
     projected_across = lax.ppermute(sent, "seq", across)
     projected, _ = attend(
-        place_of(chip * chip_width, place), queries, kv_parts, out_proj, w_other, jnp.float32
-    )
-    hidden, normed = add_and_norm(residual_in[0], projected, projected_across, norm_gain[None])
+        place_of(chip * chip_width, place),
+        queries,
+        kv_parts,
+        [residual_in[0]],
+        out_proj,
+        w_other,
+        jnp.float32,
+    )
+    hidden, normed = add_and_norm(projected, projected_across, norm_gain[None])
 
     last = n_sub - 1
     mine = place * n_sub + lax.axis_index("sub")
@@ -408,11 +417,14 @@
         step = turn - 2
         if 0 <= step <= last:
             held["diagonal", step] = move(held["across", step], "twin")
+        if 1 <= step <= last:
             now["other", step] = experts_of(step)
+        if turn == n_sub + 2:
+            now["other", 0] = experts_of(0)
         step = turn - 3 if turn < n_sub + 3 else 0
         if 1 <= step <= last or turn == n_sub + 3:
             now["away", step] = twin_sum(step)
-        if turn == 2:
+        if turn == 1:
             for steps in range(1, n_sub):
                 now["quad", steps] = lax.ppermute(quad, "sub", ring(steps))
         if turn < n_sub + 4:

time: 167 us -> 171 us (1.024)
  waiting for transfers between devices: 85.8 us -> 97.1 us
  starting transfers between devices: 28.8 us -> 22.9 us
  local copies, waits for them, and re-layouts: 15.7 us -> 13.4 us
    ppermute x3, waiting for transfers between devices: 0.01 us -> 9.84 us  [gathered_plan(): now['quad', steps] = lax.ppermute(quad, 'sub', ring(steps))]
    ppermute x26, starting transfers between devices: 18.5 us -> 11.9 us  [move(): return lax.ppermute(array, *ways[way])]
    ppermute x1, waiting for transfers between devices: 6.4 us -> 1.06 us  [gathered_plan(): lax.ppermute(kv_away, 'seq', diagonal)]
    ppermute x1, waiting for transfers between devices: 1.78 us -> 7 us  [gathered_plan(): lax.ppermute(kv_away, 'seq', across)]
    ppermute x1, waiting for transfers between devices: 3.45 us -> 6.42 us  [gathered_plan(): projected_across = lax.ppermute(sent, 'seq', across)]
    unnamed x34 -> x42, local copies, waits for them, and re-layouts: 15.5 us -> 13.3 us
    pallas_call x1, Pallas kernels: 0.05 us -> 1.88 us  [pack(): pl.pallas_call(pack_kernel, in_specs=[pl.BlockSpec(memory_space=pltpu.SME...]
  transfers between devices with their start and end apart: 35 -> 35, of which waited for: 19 -> 24; matrix products, arithmetic and copies ran while one was open for 1% -> 1% of each run, Pallas kernels for 15% -> 16%
where the time goes in v6:
time: 171 us
  waiting for transfers between devices  97.1 us (57%)
  Pallas kernels  34.2 us (20%)
  starting transfers between devices  22.9 us (13%)
  local copies, waits for them, and re-layouts  13.4 us (8%)
  other arithmetic  2.64 us (2%)
    ppermute x26, waiting for transfers between devices, move(): return lax.ppermute(array, *ways[way])  72.8 us
    pallas_call x4, Pallas kernels, experts_on_rows(): pl.pallas_call(functools.partial(experts_kernel, cap=cap), in_specs=[pl.B...  21.1 us
    unnamed x42, local copies, waits for them, and re-layouts  13.3 us
    ppermute x26, starting transfers between devices, move(): return lax.ppermute(array, *ways[way])  11.9 us
    pallas_call x2, Pallas kernels, attend(): pl.pallas_call(functools.partial(attend_kernel, scale=1.0 / HD ** 0.5), i...  9.85 us
    ppermute x3, waiting for transfers between devices, gathered_plan(): now['quad', steps] = lax.ppermute(quad, 'sub', ring(steps))  9.84 us
    ppermute x1, waiting for transfers between devices, gathered_plan(): lax.ppermute(kv_away, 'seq', across)  7 us
    ppermute x1, waiting for transfers between devices, gathered_plan(): projected_across = lax.ppermute(sent, 'seq', across)  6.42 us
  transfers between devices with their start and end apart: 35, of which 24 were waited for; matrix products, arithmetic and copies ran while one was open for 1% of the time, Pallas kernels for 16%

profile of v6, /device:TPU:0, one launch (start us, length us, event | category | flops | bytes accessed | tf_op | source)
XLA Modules:
  0.0 170.6 jit_solution(6478769723969495921)
XLA Ops:
  0.5 1.9 %shard_map.109 = (bf16[128,1024]{1,0:T(8,128)(2,1)}, bf16[144,256]{1,0:T(8,128)(2,1)}, bf16[144,256]{1,0:T(8,128)(2,1)}) custom-call(s32[1]{0:T(128)} %bitcast.7.chip_ref, bf16[128,2048]{1,0:T(8,128)(2,1)} %bitcast.35, bf16[128,256]{1,0:T(8,128)(2,1)} %bitcast.38, bf16[128,256]{1,0:T(8,128)(2,1)} %bitcast.39, s32[8,128]{1,0:T(8,128)} %bitcast.40, ...), custom_call_target="tpu_custom_call" | custom-call | tf_op jit(solution)/shard_map/pallas_call | solution.py:87
  2.3 2.6 %collective-permute-start.4 = (bf16[128,1024]{1,0:T(8,128)(2,1)}, bf16[128,1024]{1,0:T(8,128)(2,1)S(1)}, u32[]{:S(2)}, u32[]{:S(2)}) collective-permute-start(bf16[128,1024]{1,0:T(8,128)(2,1)} %get-tuple-element.51), channel_id=1, source_target_pairs={{0,8},{4,12},{8,0},{12,4},{1,9},{5,13},{9,1},{13,5},{2,10},{6,14},... | collective-permute-start | bytes 786440 | tf_op jit(solution)/shard_map/ppermute | solution.py:342
  6.9 7.0 %collective-permute-done.1.refs_2_ = bf16[144,256]{1,0:T(8,128)(2,1)S(1)} collective-permute-done((bf16[144,256]{1,0:T(8,128)(2,1)}, bf16[144,256]{1,0:T(8,128)(2,1)S(1)}, u32[]{:S(2)}, u32[]{:S(2)}) %collective-permute-start.1) | collective-permute-done | bytes 73760 | tf_op jit(solution)/shard_map/ppermute | solution.py:346
  17.0 1.6 copy-done.3
  18.6 1.6 copy-done.6
  22.0 5.3 %shard_map.111 = (bf16[128,2048]{1,0:T(8,128)(2,1)}, bf16[16,512]{1,0:T(8,128)(2,1)S(1)}) custom-call(s32[7]{0:T(128)S(1)} %stack.38.place_ref, bf16[128,1024]{1,0:T(8,128)(2,1)S(1)} %copy-done.19, bf16[144,256]{1,0:T(8,128)(2,1)S(1)} %copy-done.16, bf16[144,256]{1,0:T(8,128)(2,1)S(1)} %collective-permute-done.refs_1_, ...), custom_call_target="tpu_custom_call" | custom-call | flops 805306368 | bytes 5242880 | tf_op jit(solution)/shard_map/pallas_call | solution.py:152
  27.3 1.6 collective-permute-start.5
  30.7 4.5 %shard_map.110 = (f32[128,2048]{1,0:T(8,128)S(1)}, bf16[16,512]{1,0:T(8,128)(2,1)}) custom-call(s32[7]{0:T(128)S(1)} %stack.37.place_ref, bf16[128,2048]{1,0:T(8,128)(2,1)S(1)} %bitcast.36, bf16[144,256]{1,0:T(8,128)(2,1)S(1)} %copy-done.17, bf16[144,256]{1,0:T(8,128)(2,1)S(1)} %collective-permute-done.refs_1_, ...), custom_call_target="tpu_custom_call" | custom-call | flops 805306368 | bytes 5242880 | tf_op jit(solution)/shard_map/pallas_call | solution.py:152
  35.3 6.4 %collective-permute-done.5.other_ref = bf16[128,2048]{1,0:T(8,128)(2,1)} collective-permute-done((bf16[128,2048]{1,0:T(8,128)(2,1)}, bf16[128,2048]{1,0:T(8,128)(2,1)}, u32[]{:S(2)}, u32[]{:S(2)}) %collective-permute-start.5) | collective-permute-done | bytes 524320 | tf_op jit(solution)/shard_map/ppermute | solution.py:358
  43.1 1.8 %collective-permute-start.7 = (bf16[128,2048]{1,0:T(8,128)(2,1)S(1)}, bf16[128,2048]{1,0:T(8,128)(2,1)S(1)}, u32[]{:S(2)}, u32[]{:S(2)}) collective-permute-start(bf16[128,2048]{1,0:T(8,128)(2,1)S(1)} %get-tuple-element.55.refs_0_), channel_id=1, source_target_pairs={{0,8},{4,12},{8,0},{12,4},{1,9},{5,13},{9,1},{13,5},{2,10},{6,14},... | collective-permute-start | bytes 1572872 | tf_op jit(solution)/shard_map/ppermute | solution.py:377
  46.4 2.6 %collective-permute-start.9 = (bf16[16,512]{1,0:T(8,128)(2,1)S(1)}, bf16[16,512]{1,0:T(8,128)(2,1)S(1)}, u32[]{:S(2)}, u32[]{:S(2)}) collective-permute-start(bf16[16,512]{1,0:T(8,128)(2,1)S(1)} %get-tuple-element.54.quad_ref), channel_id=1, source_target_pairs={{0,1},{1,3},{3,2},{2,0},{4,5},{5,7},{7,6},{6,4},{8,9},{9,11},{11,1... | collective-permute-start | bytes 49160 | tf_op jit(solution)/shard_map/ppermute | solution.py:429
  49.3 1.7 collective-permute-start.11
  50.9 8.8 %collective-permute-done.9.refs_2_ = bf16[16,512]{1,0:T(8,128)(2,1)S(1)} collective-permute-done((bf16[16,512]{1,0:T(8,128)(2,1)S(1)}, bf16[16,512]{1,0:T(8,128)(2,1)S(1)}, u32[]{:S(2)}, u32[]{:S(2)}) %collective-permute-start.9) | collective-permute-done | bytes 16416 | tf_op jit(solution)/shard_map/ppermute | solution.py:429
  62.8 10.8 %collective-permute-done.13.refs_0_ = bf16[128,2048]{1,0:T(8,128)(2,1)} collective-permute-done((bf16[128,2048]{1,0:T(8,128)(2,1)}, bf16[128,2048]{1,0:T(8,128)(2,1)}, u32[]{:S(2)}, u32[]{:S(2)}) %collective-permute-start.13) | collective-permute-done | bytes 524320 | tf_op jit(solution)/shard_map/ppermute | solution.py:377
  77.0 1.9 %copy-done.1 = bf16[1,2048,768]{2,1,0:T(8,128)(2,1)S(1)} copy-done((bf16[1,2048,768]{2,1,0:T(8,128)(2,1)S(1)}, bf16[1,2048,768]{2,1,0:T(8,128)(2,1)}, u32[]{:S(2)}) %copy-start.1) | copy-done | bytes 3145752
  78.9 1.9 %copy-done.2 = bf16[1,768,2048]{2,1,0:T(8,128)(2,1)S(1)} copy-done((bf16[1,768,2048]{2,1,0:T(8,128)(2,1)S(1)}, bf16[1,768,2048]{2,1,0:T(8,128)(2,1)}, u32[]{:S(2)}) %copy-start.2) | copy-done | bytes 3145752
  80.8 5.8 %shard_map.116 = (bf16[128,2048]{1,0:T(8,128)(2,1)S(1)}, bf16[128,2048]{1,0:T(8,128)(2,1)S(1)}, bf16[256,2048]{1,0:T(8,128)(2,1)S(1)}) custom-call(s32[1]{0:T(128)} %bitcast.15.mine_ref, bf16[16,512]{1,0:T(8,128)(2,1)S(1)} %get-tuple-element.60.quad_ref, bf16[128,2048]{1,0:T(8,128)(2,1)} %get-tuple-element.58.refs_0_, ...), custom_call_target="tpu_custom_call" | custom-call | flops 3019898880 | bytes 13631488 | tf_op jit(solution)/shard_map/pallas_call | solution.py:281
  86.6 2.8 %collective-permute-done.15.refs_0_ = bf16[128,2048]{1,0:T(8,128)(2,1)} collective-permute-done((bf16[128,2048]{1,0:T(8,128)(2,1)}, bf16[128,2048]{1,0:T(8,128)(2,1)}, u32[]{:S(2)}, u32[]{:S(2)}) %collective-permute-start.15) | collective-permute-done | bytes 524320 | tf_op jit(solution)/shard_map/ppermute | solution.py:377
  89.4 2.1 %collective-permute-done.16.refs_1_ = bf16[128,2048]{1,0:T(8,128)(2,1)} collective-permute-done((bf16[128,2048]{1,0:T(8,128)(2,1)}, bf16[128,2048]{1,0:T(8,128)(2,1)}, u32[]{:S(2)}, u32[]{:S(2)}) %collective-permute-start.16) | collective-permute-done | bytes 524320 | tf_op jit(solution)/shard_map/ppermute | solution.py:377
  92.5 2.2 %collective-permute-done.20.refs_1_ = bf16[128,2048]{1,0:T(8,128)(2,1)S(1)} collective-permute-done((bf16[128,2048]{1,0:T(8,128)(2,1)}, bf16[128,2048]{1,0:T(8,128)(2,1)S(1)}, u32[]{:S(2)}, u32[]{:S(2)}) %collective-permute-start.20) | collective-permute-done | bytes 524320 | tf_op jit(solution)/shard_map/ppermute | solution.py:377
  95.9 5.5 %shard_map.118 = (bf16[128,2048]{1,0:T(8,128)(2,1)S(1)}, bf16[128,2048]{1,0:T(8,128)(2,1)S(1)}, bf16[256,2048]{1,0:T(8,128)(2,1)S(1)}) custom-call(s32[1]{0:T(128)} %bitcast.15.mine_ref, bf16[16,512]{1,0:T(8,128)(2,1)S(1)} %get-tuple-element.64.quad_ref, bf16[128,2048]{1,0:T(8,128)(2,1)} %get-tuple-element.59.refs_0_, ...), custom_call_target="tpu_custom_call" | custom-call | flops 3019898880 | bytes 13631488 | tf_op jit(solution)/shard_map/pallas_call | solution.py:281
  101.6 5.0 %collective-permute-done.19.refs_0_ = bf16[128,2048]{1,0:T(8,128)(2,1)S(1)} collective-permute-done((bf16[128,2048]{1,0:T(8,128)(2,1)}, bf16[128,2048]{1,0:T(8,128)(2,1)S(1)}, u32[]{:S(2)}, u32[]{:S(2)}) %collective-permute-start.19) | collective-permute-done | bytes 524320 | tf_op jit(solution)/shard_map/ppermute | solution.py:377
  107.6 3.0 %collective-permute-done.24.refs_1_ = bf16[128,2048]{1,0:T(8,128)(2,1)S(1)} collective-permute-done((bf16[128,2048]{1,0:T(8,128)(2,1)}, bf16[128,2048]{1,0:T(8,128)(2,1)S(1)}, u32[]{:S(2)}, u32[]{:S(2)}) %collective-permute-start.24) | collective-permute-done | bytes 524320 | tf_op jit(solution)/shard_map/ppermute | solution.py:377
  110.7 5.4 %shard_map.120 = (bf16[128,2048]{1,0:T(8,128)(2,1)S(1)}, bf16[128,2048]{1,0:T(8,128)(2,1)S(1)}, bf16[256,2048]{1,0:T(8,128)(2,1)S(1)}) custom-call(s32[1]{0:T(128)} %bitcast.15.mine_ref, bf16[16,512]{1,0:T(8,128)(2,1)S(1)} %get-tuple-element.70.quad_ref, bf16[128,2048]{1,0:T(8,128)(2,1)} %get-tuple-element.63.refs_0_, ...), custom_call_target="tpu_custom_call" | custom-call | flops 3019898880 | bytes 13631488 | tf_op jit(solution)/shard_map/pallas_call | solution.py:281
  116.3 5.2 %collective-permute-done.23.refs_0_ = bf16[128,2048]{1,0:T(8,128)(2,1)S(1)} collective-permute-done((bf16[128,2048]{1,0:T(8,128)(2,1)S(1)}, bf16[128,2048]{1,0:T(8,128)(2,1)S(1)}, u32[]{:S(2)}, u32[]{:S(2)}) %collective-permute-start.23) | collective-permute-done | bytes 524320 | tf_op jit(solution)/shard_map/ppermute | solution.py:377
  123.1 1.7 %collective-permute-done.6.refs_1_ = bf16[128,2048]{1,0:T(8,128)(2,1)S(1)} collective-permute-done((bf16[128,2048]{1,0:T(8,128)(2,1)S(1)}, bf16[128,2048]{1,0:T(8,128)(2,1)S(1)}, u32[]{:S(2)}, u32[]{:S(2)}) %collective-permute-start.6) | collective-permute-done | bytes 524320 | tf_op jit(solution)/shard_map/ppermute | solution.py:377
  125.6 4.3 %shard_map.114 = (bf16[128,2048]{1,0:T(8,128)(2,1)S(1)}, bf16[128,2048]{1,0:T(8,128)(2,1)S(1)}, bf16[256,2048]{1,0:T(8,128)(2,1)S(1)}) custom-call(s32[1]{0:T(128)} %bitcast.15.mine_ref, bf16[16,512]{1,0:T(8,128)(2,1)S(1)} %get-tuple-element.54.quad_ref, bf16[128,2048]{1,0:T(8,128)(2,1)S(1)} %copy-done.13, ...), custom_call_target="tpu_custom_call" | custom-call | flops 3019898880 | bytes 13631488 | tf_op jit(solution)/shard_map/pallas_call | solution.py:281
  130.1 6.2 %collective-permute-done.27.refs_0_ = bf16[128,2048]{1,0:T(8,128)(2,1)S(1)} collective-permute-done((bf16[128,2048]{1,0:T(8,128)(2,1)S(1)}, bf16[128,2048]{1,0:T(8,128)(2,1)S(1)}, u32[]{:S(2)}, u32[]{:S(2)}) %collective-permute-start.27) | collective-permute-done | bytes 524320 | tf_op jit(solution)/shard_map/ppermute | solution.py:377
  136.3 1.6 collective-permute-done.28.refs_1_
  140.7 11.5 %collective-permute-done.31.refs_0_ = bf16[128,2048]{1,0:T(8,128)(2,1)S(1)} collective-permute-done((bf16[128,2048]{1,0:T(8,128)(2,1)S(1)}, bf16[128,2048]{1,0:T(8,128)(2,1)S(1)}, u32[]{:S(2)}, u32[]{:S(2)}) %collective-permute-start.31) | collective-permute-done | bytes 524320 | tf_op jit(solution)/shard_map/ppermute | solution.py:377
  152.3 2.5 %collective-permute-done.32.refs_1_ = bf16[128,2048]{1,0:T(8,128)(2,1)S(1)} collective-permute-done((bf16[128,2048]{1,0:T(8,128)(2,1)S(1)}, bf16[128,2048]{1,0:T(8,128)(2,1)S(1)}, u32[]{:S(2)}, u32[]{:S(2)}) %collective-permute-start.32) | collective-permute-done | bytes 524320 | tf_op jit(solution)/shard_map/ppermute | solution.py:377
  155.8 13.5 %collective-permute-done.34 = bf16[128,2048]{1,0:T(8,128)(2,1)S(1)} collective-permute-done((bf16[128,2048]{1,0:T(8,128)(2,1)S(1)}, bf16[128,2048]{1,0:T(8,128)(2,1)S(1)}, u32[]{:S(2)}, u32[]{:S(2)}) %collective-permute-start.34) | collective-permute-done | bytes 524320 | tf_op jit(solution)/shard_map/ppermute | solution.py:377
  (106 shorter events, 29.8 us)
Async XLA Ops:
  0.0 15.6 %collective-permute-start.3 = (bf16[512,2048]{1,0:T(8,128)(2,1)}, bf16[512,2048]{1,0:T(8,128)(2,1)S(1)}, u32[]{:S(2)}, u32[]{:S(2)}) collective-permute-start(bf16[512,2048]{1,0:T(8,128)(2,1)} %refs_4_.1), channel_id=1, source_target_pairs={{0,4},{4,0},{8,12},{12,8},{1,5},{5,1},{9,13},{13,9},{2,6},{6,2},{1... | collective-permute-start | bytes 6291464 | tf_op jit(solution)/shard_map/ppermute | solution.py:349
  2.3 12.6 %collective-permute-start.4 = (bf16[128,1024]{1,0:T(8,128)(2,1)}, bf16[128,1024]{1,0:T(8,128)(2,1)S(1)}, u32[]{:S(2)}, u32[]{:S(2)}) collective-permute-start(bf16[128,1024]{1,0:T(8,128)(2,1)} %get-tuple-element.51), channel_id=1, source_target_pairs={{0,8},{4,12},{8,0},{12,4},{1,9},{5,13},{9,1},{13,5},{2,10},{6,14},... | collective-permute-start | bytes 786440 | tf_op jit(solution)/shard_map/ppermute | solution.py:342
  5.1 8.8 %collective-permute-start.1 = (bf16[144,256]{1,0:T(8,128)(2,1)}, bf16[144,256]{1,0:T(8,128)(2,1)S(1)}, u32[]{:S(2)}, u32[]{:S(2)}) collective-permute-start(bf16[144,256]{1,0:T(8,128)(2,1)} %get-tuple-element.49), channel_id=1, source_target_pairs={{0,8},{4,12},{8,0},{12,4},{1,9},{5,13},{9,1},{13,5},{2,10},{6,14},... | collective-permute-start | bytes 221192 | tf_op jit(solution)/shard_map/ppermute | solution.py:346
  5.4 9.6 %collective-permute-start.2 = (bf16[144,256]{1,0:T(8,128)(2,1)}, bf16[144,256]{1,0:T(8,128)(2,1)S(1)}, u32[]{:S(2)}, u32[]{:S(2)}) collective-permute-start(bf16[144,256]{1,0:T(8,128)(2,1)} %get-tuple-element.49), channel_id=1, source_target_pairs={{0,12},{4,8},{8,4},{12,0},{1,13},{5,9},{9,5},{13,1},{2,14},{6,10},... | collective-permute-start | bytes 221192 | tf_op jit(solution)/shard_map/ppermute | solution.py:347
  27.3 14.3 %collective-permute-start.5 = (bf16[128,2048]{1,0:T(8,128)(2,1)}, bf16[128,2048]{1,0:T(8,128)(2,1)}, u32[]{:S(2)}, u32[]{:S(2)}) collective-permute-start(bf16[128,2048]{1,0:T(8,128)(2,1)} %get-tuple-element.52), channel_id=1, source_target_pairs={{0,8},{4,12},{8,0},{12,4},{1,9},{5,13},{9,1},{13,5},{2,10},{6,14},... | collective-permute-start | bytes 1572872 | tf_op jit(solution)/shard_map/ppermute | solution.py:358
  43.1 17.7 %collective-permute-start.7 = (bf16[128,2048]{1,0:T(8,128)(2,1)S(1)}, bf16[128,2048]{1,0:T(8,128)(2,1)S(1)}, u32[]{:S(2)}, u32[]{:S(2)}) collective-permute-start(bf16[128,2048]{1,0:T(8,128)(2,1)S(1)} %get-tuple-element.55.refs_0_), channel_id=1, source_target_pairs={{0,8},{4,12},{8,0},{12,4},{1,9},{5,13},{9,1},{13,5},{2,10},{6,14},... | collective-permute-start | bytes 1572872 | tf_op jit(solution)/shard_map/ppermute | solution.py:377
  44.9 15.9 %collective-permute-start.8 = (bf16[128,2048]{1,0:T(8,128)(2,1)S(1)}, bf16[128,2048]{1,0:T(8,128)(2,1)}, u32[]{:S(2)}, u32[]{:S(2)}) collective-permute-start(bf16[128,2048]{1,0:T(8,128)(2,1)S(1)} %get-tuple-element.55.refs_0_), channel_id=1, source_target_pairs={{0,1},{1,3},{3,2},{2,0},{4,5},{5,7},{7,6},{6,4},{8,9},{9,11},{11,1... | collective-permute-start | bytes 1572872 | tf_op jit(solution)/shard_map/ppermute | solution.py:377
  46.4 13.3 %collective-permute-start.9 = (bf16[16,512]{1,0:T(8,128)(2,1)S(1)}, bf16[16,512]{1,0:T(8,128)(2,1)S(1)}, u32[]{:S(2)}, u32[]{:S(2)}) collective-permute-start(bf16[16,512]{1,0:T(8,128)(2,1)S(1)} %get-tuple-element.54.quad_ref), channel_id=1, source_target_pairs={{0,1},{1,3},{3,2},{2,0},{4,5},{5,7},{7,6},{6,4},{8,9},{9,11},{11,1... | collective-permute-start | bytes 49160 | tf_op jit(solution)/shard_map/ppermute | solution.py:429
  49.0 11.7 %collective-permute-start.10 = (bf16[16,512]{1,0:T(8,128)(2,1)S(1)}, bf16[16,512]{1,0:T(8,128)(2,1)S(1)}, u32[]{:S(2)}, u32[]{:S(2)}) collective-permute-start(bf16[16,512]{1,0:T(8,128)(2,1)S(1)} %get-tuple-element.54.quad_ref), channel_id=1, source_target_pairs={{0,3},{1,2},{3,0},{2,1},{4,7},{5,6},{7,4},{6,5},{8,11},{9,10},{11,... | collective-permute-start | bytes 49160 | tf_op jit(solution)/shard_map/ppermute | solution.py:429
  49.3 11.5 %collective-permute-start.11 = (bf16[16,512]{1,0:T(8,128)(2,1)S(1)}, bf16[16,512]{1,0:T(8,128)(2,1)S(1)}, u32[]{:S(2)}, u32[]{:S(2)}) collective-permute-start(bf16[16,512]{1,0:T(8,128)(2,1)S(1)} %get-tuple-element.54.quad_ref), channel_id=1, source_target_pairs={{0,2},{1,0},{3,1},{2,3},{4,6},{5,4},{7,5},{6,7},{8,10},{9,8},{11,9... | collective-permute-start | bytes 49160 | tf_op jit(solution)/shard_map/ppermute | solution.py:429
  61.6 12.0 %collective-permute-start.13 = (bf16[128,2048]{1,0:T(8,128)(2,1)}, bf16[128,2048]{1,0:T(8,128)(2,1)}, u32[]{:S(2)}, u32[]{:S(2)}) collective-permute-start(bf16[128,2048]{1,0:T(8,128)(2,1)} %get-tuple-element.58.refs_0_), channel_id=1, source_target_pairs={{0,8},{4,12},{8,0},{12,4},{1,9},{5,13},{9,1},{13,5},{2,10},{6,14},... | collective-permute-start | bytes 1572872 | tf_op jit(solution)/shard_map/ppermute | solution.py:377
  62.1 12.6 %collective-permute-start.14 = (bf16[128,2048]{1,0:T(8,128)(2,1)}, bf16[128,2048]{1,0:T(8,128)(2,1)}, u32[]{:S(2)}, u32[]{:S(2)}) collective-permute-start(bf16[128,2048]{1,0:T(8,128)(2,1)} %get-tuple-element.58.refs_0_), channel_id=1, source_target_pairs={{0,1},{1,3},{3,2},{2,0},{4,5},{5,7},{7,6},{6,4},{8,9},{9,11},{11,1... | collective-permute-start | bytes 1572872 | tf_op jit(solution)/shard_map/ppermute | solution.py:377
  62.8 13.5 %collective-permute-start.17 = (bf16[128,2048]{1,0:T(8,128)(2,1)}, bf16[128,2048]{1,0:T(8,128)(2,1)}, u32[]{:S(2)}, u32[]{:S(2)}) collective-permute-start(bf16[128,2048]{1,0:T(8,128)(2,1)} %get-tuple-element.58.refs_0_), channel_id=1, source_target_pairs={{0,4},{4,0},{8,12},{12,8},{1,5},{5,1},{9,13},{13,9},{2,6},{6,2},{1... | collective-permute-start | bytes 1572872 | tf_op jit(solution)/shard_map/ppermute | solution.py:377
  74.7 14.7 %collective-permute-start.15 = (bf16[128,2048]{1,0:T(8,128)(2,1)}, bf16[128,2048]{1,0:T(8,128)(2,1)}, u32[]{:S(2)}, u32[]{:S(2)}) collective-permute-start(bf16[128,2048]{1,0:T(8,128)(2,1)} %get-tuple-element.59.refs_0_), channel_id=1, source_target_pairs={{0,8},{4,12},{8,0},{12,4},{1,9},{5,13},{9,1},{13,5},{2,10},{6,14},... | collective-permute-start | bytes 1572872 | tf_op jit(solution)/shard_map/ppermute | solution.py:377
  76.3 15.3 %collective-permute-start.16 = (bf16[128,2048]{1,0:T(8,128)(2,1)}, bf16[128,2048]{1,0:T(8,128)(2,1)}, u32[]{:S(2)}, u32[]{:S(2)}) collective-permute-start(bf16[128,2048]{1,0:T(8,128)(2,1)} %get-tuple-element.59.refs_0_), channel_id=1, source_target_pairs={{0,1},{1,3},{3,2},{2,0},{4,5},{5,7},{7,6},{6,4},{8,9},{9,11},{11,1... | collective-permute-start | bytes 1572872 | tf_op jit(solution)/shard_map/ppermute | solution.py:377
  91.5 9.9 %collective-permute-start.22 = (bf16[256,2048]{1,0:T(8,128)(2,1)S(1)}, bf16[256,2048]{1,0:T(8,128)(2,1)S(1)}, u32[]{:S(2)}, u32[]{:S(2)}) collective-permute-start(bf16[256,2048]{1,0:T(8,128)(2,1)S(1)} %get-tuple-element.68), channel_id=1, source_target_pairs={{0,4},{4,0},{8,12},{12,8},{1,5},{5,1},{9,13},{13,9},{2,6},{6,2},{1... | collective-permute-start | bytes 3145736 | tf_op jit(solution)/shard_map/ppermute | solution.py:377
  91.5 3.2 %collective-permute-start.20 = (bf16[128,2048]{1,0:T(8,128)(2,1)}, bf16[128,2048]{1,0:T(8,128)(2,1)S(1)}, u32[]{:S(2)}, u32[]{:S(2)}) collective-permute-start(bf16[128,2048]{1,0:T(8,128)(2,1)} %get-tuple-element.59.refs_0_), channel_id=1, source_target_pairs={{0,4},{4,0},{8,12},{12,8},{1,5},{5,1},{9,13},{13,9},{2,6},{6,2},{1... | collective-permute-start | bytes 1572872 | tf_op jit(solution)/shard_map/ppermute | solution.py:377
  92.0 3.9 %collective-permute-start.21 = (bf16[128,2048]{1,0:T(8,128)(2,1)}, bf16[128,2048]{1,0:T(8,128)(2,1)S(1)}, u32[]{:S(2)}, u32[]{:S(2)}) collective-permute-start(bf16[128,2048]{1,0:T(8,128)(2,1)} %get-tuple-element.65.refs_2_), channel_id=1, source_target_pairs={{0,4},{4,0},{8,12},{12,8},{1,5},{5,1},{9,13},{13,9},{2,6},{6,2},{1... | collective-permute-start | bytes 1572872 | tf_op jit(solution)/shard_map/ppermute | solution.py:377
  92.0 14.5 %collective-permute-start.19 = (bf16[128,2048]{1,0:T(8,128)(2,1)}, bf16[128,2048]{1,0:T(8,128)(2,1)S(1)}, u32[]{:S(2)}, u32[]{:S(2)}) collective-permute-start(bf16[128,2048]{1,0:T(8,128)(2,1)} %get-tuple-element.63.refs_0_), channel_id=1, source_target_pairs={{0,8},{4,12},{8,0},{12,4},{1,9},{5,13},{9,1},{13,5},{2,10},{6,14},... | collective-permute-start | bytes 1572872 | tf_op jit(solution)/shard_map/ppermute | solution.py:377
  106.6 9.6 %collective-permute-start.26 = (bf16[256,2048]{1,0:T(8,128)(2,1)S(1)}, bf16[256,2048]{1,0:T(8,128)(2,1)S(1)}, u32[]{:S(2)}, u32[]{:S(2)}) collective-permute-start(bf16[256,2048]{1,0:T(8,128)(2,1)S(1)} %get-tuple-element.74), channel_id=1, source_target_pairs={{0,4},{4,0},{8,12},{12,8},{1,5},{5,1},{9,13},{13,9},{2,6},{6,2},{1... | collective-permute-start | bytes 3145736 | tf_op jit(solution)/shard_map/ppermute | solution.py:377
  106.6 4.0 %collective-permute-start.24 = (bf16[128,2048]{1,0:T(8,128)(2,1)}, bf16[128,2048]{1,0:T(8,128)(2,1)S(1)}, u32[]{:S(2)}, u32[]{:S(2)}) collective-permute-start(bf16[128,2048]{1,0:T(8,128)(2,1)} %get-tuple-element.63.refs_0_), channel_id=1, source_target_pairs={{0,4},{4,0},{8,12},{12,8},{1,5},{5,1},{9,13},{13,9},{2,6},{6,2},{1... | collective-permute-start | bytes 1572872 | tf_op jit(solution)/shard_map/ppermute | solution.py:377
  107.1 3.6 %collective-permute-start.25 = (bf16[128,2048]{1,0:T(8,128)(2,1)S(1)}, bf16[128,2048]{1,0:T(8,128)(2,1)S(1)}, u32[]{:S(2)}, u32[]{:S(2)}) collective-permute-start(bf16[128,2048]{1,0:T(8,128)(2,1)S(1)} %get-tuple-element.71.refs_2_), channel_id=1, source_target_pairs={{0,4},{4,0},{8,12},{12,8},{1,5},{5,1},{9,13},{13,9},{2,6},{6,2},{1... | collective-permute-start | bytes 1572872 | tf_op jit(solution)/shard_map/ppermute | solution.py:377
  107.1 14.3 %collective-permute-start.23 = (bf16[128,2048]{1,0:T(8,128)(2,1)S(1)}, bf16[128,2048]{1,0:T(8,128)(2,1)S(1)}, u32[]{:S(2)}, u32[]{:S(2)}) collective-permute-start(bf16[128,2048]{1,0:T(8,128)(2,1)S(1)} %get-tuple-element.69), channel_id=1, source_target_pairs={{0,8},{4,12},{8,0},{12,4},{1,9},{5,13},{9,1},{13,5},{2,10},{6,14},... | collective-permute-start | bytes 1572872 | tf_op jit(solution)/shard_map/ppermute | solution.py:377
  121.4 8.5 %collective-permute-start.29 = (bf16[256,2048]{1,0:T(8,128)(2,1)S(1)}, bf16[256,2048]{1,0:T(8,128)(2,1)S(1)}, u32[]{:S(2)}, u32[]{:S(2)}) collective-permute-start(bf16[256,2048]{1,0:T(8,128)(2,1)S(1)} %get-tuple-element.80), channel_id=1, source_target_pairs={{0,4},{4,0},{8,12},{12,8},{1,5},{5,1},{9,13},{13,9},{2,6},{6,2},{1... | collective-permute-start | bytes 3145736 | tf_op jit(solution)/shard_map/ppermute | solution.py:377
  121.4 3.4 %collective-permute-start.6 = (bf16[128,2048]{1,0:T(8,128)(2,1)S(1)}, bf16[128,2048]{1,0:T(8,128)(2,1)S(1)}, u32[]{:S(2)}, u32[]{:S(2)}) collective-permute-start(bf16[128,2048]{1,0:T(8,128)(2,1)S(1)} %copy-done.13), channel_id=1, source_target_pairs={{0,4},{4,0},{8,12},{12,8},{1,5},{5,1},{9,13},{13,9},{2,6},{6,2},{1... | collective-permute-start | bytes 1572872 | tf_op jit(solution)/shard_map/ppermute | solution.py:377
  122.0 3.6 %collective-permute-start.12 = (bf16[128,2048]{1,0:T(8,128)(2,1)S(1)}, bf16[128,2048]{1,0:T(8,128)(2,1)S(1)}, u32[]{:S(2)}, u32[]{:S(2)}) collective-permute-start(bf16[128,2048]{1,0:T(8,128)(2,1)S(1)} %copy-done.10), channel_id=1, source_target_pairs={{0,4},{4,0},{8,12},{12,8},{1,5},{5,1},{9,13},{13,9},{2,6},{6,2},{1... | collective-permute-start | bytes 1572872 | tf_op jit(solution)/shard_map/ppermute | solution.py:377
  122.0 14.3 %collective-permute-start.27 = (bf16[128,2048]{1,0:T(8,128)(2,1)S(1)}, bf16[128,2048]{1,0:T(8,128)(2,1)S(1)}, u32[]{:S(2)}, u32[]{:S(2)}) collective-permute-start(bf16[128,2048]{1,0:T(8,128)(2,1)S(1)} %get-tuple-element.75), channel_id=1, source_target_pairs={{0,8},{4,12},{8,0},{12,4},{1,9},{5,13},{9,1},{13,5},{2,10},{6,14},... | collective-permute-start | bytes 1572872 | tf_op jit(solution)/shard_map/ppermute | solution.py:377
  122.8 15.2 %collective-permute-start.28 = (bf16[128,2048]{1,0:T(8,128)(2,1)S(1)}, bf16[128,2048]{1,0:T(8,128)(2,1)S(1)}, u32[]{:S(2)}, u32[]{:S(2)}) collective-permute-start(bf16[128,2048]{1,0:T(8,128)(2,1)S(1)} %add_convert_fusion.5), channel_id=1, source_target_pairs={{0,1},{1,3},{3,2},{2,0},{4,5},{5,7},{7,6},{6,4},{8,9},{9,11},{11,1... | collective-permute-start | bytes 1572872 | tf_op jit(solution)/shard_map/ppermute | solution.py:377
  137.9 14.3 %collective-permute-start.31 = (bf16[128,2048]{1,0:T(8,128)(2,1)S(1)}, bf16[128,2048]{1,0:T(8,128)(2,1)S(1)}, u32[]{:S(2)}, u32[]{:S(2)}) collective-permute-start(bf16[128,2048]{1,0:T(8,128)(2,1)S(1)} %get-tuple-element.82), channel_id=1, source_target_pairs={{0,8},{4,12},{8,0},{12,4},{1,9},{5,13},{9,1},{13,5},{2,10},{6,14},... | collective-permute-start | bytes 1572872 | tf_op jit(solution)/shard_map/ppermute | solution.py:377
  139.8 15.0 %collective-permute-start.32 = (bf16[128,2048]{1,0:T(8,128)(2,1)S(1)}, bf16[128,2048]{1,0:T(8,128)(2,1)S(1)}, u32[]{:S(2)}, u32[]{:S(2)}) collective-permute-start(bf16[128,2048]{1,0:T(8,128)(2,1)S(1)} %add_convert_fusion.3), channel_id=1, source_target_pairs={{0,1},{1,3},{3,2},{2,0},{4,5},{5,7},{7,6},{6,4},{8,9},{9,11},{11,1... | collective-permute-start | bytes 1572872 | tf_op jit(solution)/shard_map/ppermute | solution.py:377
  155.2 14.2 %collective-permute-start.34 = (bf16[128,2048]{1,0:T(8,128)(2,1)S(1)}, bf16[128,2048]{1,0:T(8,128)(2,1)S(1)}, u32[]{:S(2)}, u32[]{:S(2)}) collective-permute-start(bf16[128,2048]{1,0:T(8,128)(2,1)S(1)} %add_convert_fusion.1), channel_id=1, source_target_pairs={{0,1},{1,3},{3,2},{2,0},{4,5},{5,7},{7,6},{6,4},{8,9},{9,11},{11,1... | collective-permute-start | bytes 1572872 | tf_op jit(solution)/shard_map/ppermute | solution.py:377
  155.3 14.1 %collective-permute-start.33 = (bf16[128,2048]{1,0:T(8,128)(2,1)S(1)}, bf16[128,2048]{1,0:T(8,128)(2,1)S(1)}, u32[]{:S(2)}, u32[]{:S(2)}) collective-permute-start(bf16[128,2048]{1,0:T(8,128)(2,1)S(1)} %get-tuple-element.87), channel_id=1, source_target_pairs={{0,8},{4,12},{8,0},{12,4},{1,9},{5,13},{9,1},{13,5},{2,10},{6,14},... | collective-permute-start | bytes 1572872 | tf_op jit(solution)/shard_map/ppermute | solution.py:377
  (24 other events, 218.2 us)

commit v7 on v6

--- a/solution.py
+++ b/solution.py
@@ -167,7 +167,7 @@
             pltpu.VMEM(w_other.shape, jnp.bfloat16),
             pltpu.SemaphoreType.DMA((2,)),
         ],
-        compiler_params=pltpu.CompilerParams(vmem_limit_bytes=16 * MIB),
+        compiler_params=pltpu.CompilerParams(vmem_limit_bytes=60 * MIB),
         cost_estimate=pl.CostEstimate(
             flops=16 * tokens * tokens * chip_width + 2 * tokens * chip_width * width,
             bytes_accessed=4 * w_own.size + 4 * tokens * width,
@@ -176,7 +176,8 @@
     )(place, queries, *kv_parts, *bases, w_own, w_other)
 
 
-def norm_kernel(own_ref, other_ref, gain_ref, hidden_ref, normed_ref):
+def norm_kernel(own_ref, other_ref, gain_ref, *refs):
+    hidden_ref, normed_ref = refs[-2:]
     hidden = (own_ref[...] + other_ref[...].astype(jnp.float32)).astype(jnp.bfloat16)
     hidden_ref[...] = hidden
     wide = hidden.astype(jnp.float32)
@@ -187,14 +188,15 @@
     ).astype(jnp.bfloat16)
 
 
-def add_and_norm(own, other, gain):
+def add_and_norm(own, other, gain, present):
     return pl.pallas_call(
         norm_kernel,
-        in_specs=[pl.BlockSpec(memory_space=pltpu.VMEM)] * 3,
+        in_specs=[pl.BlockSpec(memory_space=pltpu.VMEM)] * 3
+        + [pl.BlockSpec(memory_space=pl.ANY)] * len(present),
         out_specs=[pl.BlockSpec(memory_space=pltpu.VMEM)] * 2,
         out_shape=[jax.ShapeDtypeStruct(own.shape, jnp.bfloat16)] * 2,
-        compiler_params=pltpu.CompilerParams(vmem_limit_bytes=10 * MIB),
-    )(own, other, gain)
+        compiler_params=pltpu.CompilerParams(vmem_limit_bytes=60 * MIB),
+    )(own, other, gain, *present)
 
 
 def pass_kernel(*refs):
@@ -365,12 +367,14 @@
         w_other,
         jnp.float32,
     )
-    hidden, normed = add_and_norm(projected, projected_across, norm_gain[None])
+    quads = [lax.ppermute(quad, "sub", ring(steps)) for steps in range(1, n_sub)]
+    hidden, normed = add_and_norm(projected, projected_across, norm_gain[None], quads)
 
     last = n_sub - 1
     mine = place * n_sub + lax.axis_index("sub")
 
     held = {("row", 0): normed, ("quad", 0): quad}
+    held.update({("quad", steps): moved for steps, moved in enumerate(quads, 1)})
     ways = {"across": ("seq", across), "twin": ("seq", twin), "on": ("sub", ring(1))}
 
     def move(array, way):
@@ -424,9 +428,6 @@
         step = turn - 3 if turn < n_sub + 3 else 0
         if 1 <= step <= last or turn == n_sub + 3:
             now["away", step] = twin_sum(step)
-        if turn == 1:
-            for steps in range(1, n_sub):
-                now["quad", steps] = lax.ppermute(quad, "sub", ring(steps))
         if turn < n_sub + 4:
             now = dict(zip(now.keys(), meet(*now.values())))
         held.update(now)

time: 171 us -> 166 us (0.971)
  waiting for transfers between devices: 97.1 us -> 89.8 us
  local copies, waits for them, and re-layouts: 13.4 us -> 9.81 us
  Pallas kernels: 34.2 us -> 37.3 us
  starting transfers between devices: 22.9 us -> 25.6 us
    ppermute x3, waiting for transfers between devices: 9.84 us -> 0.01 us  [gathered_plan(): lax.ppermute(quad, 'sub', ring(steps))]
    ppermute x26, waiting for transfers between devices: 72.8 us -> 82.1 us  [move(): return lax.ppermute(array, *ways[way])]
    ppermute x1, waiting for transfers between devices: 6.42 us -> 0.01 us  [gathered_plan(): projected_across = lax.ppermute(sent, 'seq', across)]
    unnamed x42 -> x40, local copies, waits for them, and re-layouts: 13.3 us -> 7.95 us
  transfers between devices with their start and end apart: 35 -> 35, of which waited for: 24 -> 23; matrix products, arithmetic and copies ran while one was open for 1% -> 2% of each run, Pallas kernels for 16% -> 18%
where the time goes in v7:
time: 166 us; the launch traced here: 165 us
  waiting for transfers between devices  89.8 us (54%)
  Pallas kernels  37.3 us (22%)
  starting transfers between devices  25.6 us (15%)
  local copies, waits for them, and re-layouts  9.81 us (6%)
  other arithmetic  2.64 us (2%)
    ppermute x26, waiting for transfers between devices, move(): return lax.ppermute(array, *ways[way])  82.1 us
    pallas_call x4, Pallas kernels, experts_on_rows(): pl.pallas_call(functools.partial(experts_kernel, cap=cap), in_specs=[pl.B...  21.1 us
    ppermute x26, starting transfers between devices, move(): return lax.ppermute(array, *ways[way])  13.5 us
    pallas_call x2, Pallas kernels, attend(): pl.pallas_call(functools.partial(attend_kernel, scale=1.0 / HD ** 0.5), i...  11.6 us
    unnamed x40, local copies, waits for them, and re-layouts  7.95 us
    ppermute x1, waiting for transfers between devices, gathered_plan(): lax.ppermute(kv_away, 'seq', across)  6.45 us
    ppermute x3, starting transfers between devices, gathered_plan(): lax.ppermute(quad, 'sub', ring(steps))  5.62 us
  transfers between devices with their start and end apart: 35, of which 23 were waited for; matrix products, arithmetic and copies ran while one was open for 2% of the time, Pallas kernels for 18%

profile of v7, /device:TPU:0, one launch (start us, length us, event | category | flops | bytes accessed | tf_op | source)
XLA Modules:
  0.0 165.4 jit_solution(14401060333292632914)
XLA Ops:
  0.5 1.9 %shard_map.109 = (bf16[128,1024]{1,0:T(8,128)(2,1)}, bf16[144,256]{1,0:T(8,128)(2,1)}, bf16[144,256]{1,0:T(8,128)(2,1)}) custom-call(s32[1]{0:T(128)} %bitcast.7.chip_ref, bf16[128,2048]{1,0:T(8,128)(2,1)} %bitcast.35, bf16[128,256]{1,0:T(8,128)(2,1)} %bitcast.38, bf16[128,256]{1,0:T(8,128)(2,1)} %bitcast.39, s32[8,128]{1,0:T(8,128)} %bitcast.40, ...), custom_call_target="tpu_custom_call" | custom-call | tf_op jit(solution)/shard_map/pallas_call | solution.py:87
  2.3 2.5 %collective-permute-start.4 = (bf16[128,1024]{1,0:T(8,128)(2,1)}, bf16[128,1024]{1,0:T(8,128)(2,1)S(1)}, u32[]{:S(2)}, u32[]{:S(2)}) collective-permute-start(bf16[128,1024]{1,0:T(8,128)(2,1)} %get-tuple-element.48), channel_id=1, source_target_pairs={{0,8},{4,12},{8,0},{12,4},{1,9},{5,13},{9,1},{13,5},{2,10},{6,14},... | collective-permute-start | bytes 786440 | tf_op jit(solution)/shard_map/ppermute | solution.py:344
  7.4 6.4 %collective-permute-done.1.refs_2_ = bf16[144,256]{1,0:T(8,128)(2,1)S(1)} collective-permute-done((bf16[144,256]{1,0:T(8,128)(2,1)}, bf16[144,256]{1,0:T(8,128)(2,1)S(1)}, u32[]{:S(2)}, u32[]{:S(2)}) %collective-permute-start.1) | collective-permute-done | bytes 73760 | tf_op jit(solution)/shard_map/ppermute | solution.py:348
  17.1 5.6 %shard_map.111 = (bf16[128,2048]{1,0:T(8,128)(2,1)}, bf16[16,512]{1,0:T(8,128)(2,1)}) custom-call(s32[7]{0:T(128)} %stack.38.place_ref, bf16[128,1024]{1,0:T(8,128)(2,1)} %copy-done.18, bf16[144,256]{1,0:T(8,128)(2,1)} %get-tuple-element.45.refs_0_, bf16[144,256]{1,0:T(8,128)(2,1)} %copy-done.15, bf16[144,256]{1,0:T(8,128)(2,1)} %copy-done.16, ...), custom_call_target="tpu_custom_call" | custom-call | flops 805306368 | bytes 5242880 | tf_op jit(solution)/shard_map/pallas_call | solution.py:152
  22.6 1.6 collective-permute-start.5
  25.5 1.6 collective-permute-start.6
  27.1 2.5 %collective-permute-start.7 = (bf16[16,512]{1,0:T(8,128)(2,1)}, bf16[16,512]{1,0:T(8,128)(2,1)S(1)}, u32[]{:S(2)}, u32[]{:S(2)}) collective-permute-start(bf16[16,512]{1,0:T(8,128)(2,1)} %get-tuple-element.50.quad_ref), channel_id=1, source_target_pairs={{0,3},{1,2},{3,0},{2,1},{4,7},{5,6},{7,4},{6,5},{8,11},{9,10},{11,... | collective-permute-start | bytes 49160 | tf_op jit(solution)/shard_map/ppermute | solution.py:370
  29.5 1.6 collective-permute-start.8
  31.1 6.0 %shard_map.110 = (f32[128,2048]{1,0:T(8,128)}, bf16[16,512]{1,0:T(8,128)(2,1)}) custom-call(s32[7]{0:T(128)} %stack.37.place_ref, bf16[128,2048]{1,0:T(8,128)(2,1)} %bitcast.36, bf16[144,256]{1,0:T(8,128)(2,1)} %get-tuple-element.45.refs_0_, bf16[144,256]{1,0:T(8,128)(2,1)} %copy-done.15, bf16[144,256]{1,0:T(8,128)(2,1)} %copy-done.16, ...), custom_call_target="tpu_custom_call" | custom-call | flops 805306368 | bytes 5242880 | tf_op jit(solution)/shard_map/pallas_call | solution.py:152
  37.8 2.8 %shard_map.112 = (bf16[128,2048]{1,0:T(8,128)(2,1)}, bf16[128,2048]{1,0:T(8,128)(2,1)}) custom-call(f32[128,2048]{1,0:T(8,128)} %get-tuple-element.47.own_ref, bf16[128,2048]{1,0:T(8,128)(2,1)} %collective-permute-done.5.other_ref, bf16[1,2048]{1,0:T(2,128)(2,1)} %broadcast_in_dim.6.gain_ref, bf16[16,512]{1,0:T(8,128)(2,1)} %copy-done.10, ...), custom_call_target="tpu_custom_call" | custom-call | tf_op jit(solution)/shard_map/pallas_call | solution.py:192
  41.1 1.6 collective-permute-start.11
  42.7 11.0 %collective-permute-done.10.refs_0_ = bf16[128,2048]{1,0:T(8,128)(2,1)S(1)} collective-permute-done((bf16[128,2048]{1,0:T(8,128)(2,1)}, bf16[128,2048]{1,0:T(8,128)(2,1)S(1)}, u32[]{:S(2)}, u32[]{:S(2)}) %collective-permute-start.10) | collective-permute-done | bytes 524320 | tf_op jit(solution)/shard_map/ppermute | solution.py:381
  53.7 1.6 collective-permute-done.11.refs_1_
  57.4 11.1 %collective-permute-done.13.refs_0_ = bf16[128,2048]{1,0:T(8,128)(2,1)} collective-permute-done((bf16[128,2048]{1,0:T(8,128)(2,1)}, bf16[128,2048]{1,0:T(8,128)(2,1)}, u32[]{:S(2)}, u32[]{:S(2)}) %collective-permute-start.13) | collective-permute-done | bytes 524320 | tf_op jit(solution)/shard_map/ppermute | solution.py:381
  68.5 1.5 collective-permute-done.14.refs_1_
  72.2 1.9 %copy-done.1 = bf16[1,2048,768]{2,1,0:T(8,128)(2,1)S(1)} copy-done((bf16[1,2048,768]{2,1,0:T(8,128)(2,1)S(1)}, bf16[1,2048,768]{2,1,0:T(8,128)(2,1)}, u32[]{:S(2)}) %copy-start.1) | copy-done | bytes 3145752
  74.1 1.9 %copy-done.2 = bf16[1,768,2048]{2,1,0:T(8,128)(2,1)S(1)} copy-done((bf16[1,768,2048]{2,1,0:T(8,128)(2,1)S(1)}, bf16[1,768,2048]{2,1,0:T(8,128)(2,1)}, u32[]{:S(2)}) %copy-start.2) | copy-done | bytes 3145752
  76.7 5.9 %shard_map.116 = (bf16[128,2048]{1,0:T(8,128)(2,1)S(1)}, bf16[128,2048]{1,0:T(8,128)(2,1)S(1)}, bf16[256,2048]{1,0:T(8,128)(2,1)S(1)}) custom-call(s32[1]{0:T(128)} %bitcast.15.mine_ref, bf16[16,512]{1,0:T(8,128)(2,1)S(1)} %copy-done.11, bf16[128,2048]{1,0:T(8,128)(2,1)} %get-tuple-element.55.refs_0_, bf16[128,2048]{1,0:T(8,128)(2,1)} %collective-permute-done.17.refs_1_, ...), custom_call_target="tpu_custom_call" | custom-call | flops 3019898880 | bytes 13631488 | tf_op jit(solution)/shard_map/pallas_call | solution.py:283
  82.5 2.0 %collective-permute-done.15.refs_0_ = bf16[128,2048]{1,0:T(8,128)(2,1)} collective-permute-done((bf16[128,2048]{1,0:T(8,128)(2,1)}, bf16[128,2048]{1,0:T(8,128)(2,1)}, u32[]{:S(2)}, u32[]{:S(2)}) %collective-permute-start.15) | collective-permute-done | bytes 524320 | tf_op jit(solution)/shard_map/ppermute | solution.py:381
  84.6 1.8 %collective-permute-done.16.refs_1_ = bf16[128,2048]{1,0:T(8,128)(2,1)} collective-permute-done((bf16[128,2048]{1,0:T(8,128)(2,1)}, bf16[128,2048]{1,0:T(8,128)(2,1)}, u32[]{:S(2)}, u32[]{:S(2)}) %collective-permute-start.16) | collective-permute-done | bytes 524320 | tf_op jit(solution)/shard_map/ppermute | solution.py:381
  87.7 1.9 %collective-permute-done.20.refs_1_ = bf16[128,2048]{1,0:T(8,128)(2,1)S(1)} collective-permute-done((bf16[128,2048]{1,0:T(8,128)(2,1)}, bf16[128,2048]{1,0:T(8,128)(2,1)S(1)}, u32[]{:S(2)}, u32[]{:S(2)}) %collective-permute-start.20) | collective-permute-done | bytes 524320 | tf_op jit(solution)/shard_map/ppermute | solution.py:381
  90.8 5.5 %shard_map.118 = (bf16[128,2048]{1,0:T(8,128)(2,1)S(1)}, bf16[128,2048]{1,0:T(8,128)(2,1)S(1)}, bf16[256,2048]{1,0:T(8,128)(2,1)S(1)}) custom-call(s32[1]{0:T(128)} %bitcast.15.mine_ref, bf16[16,512]{1,0:T(8,128)(2,1)S(1)} %copy-done.9, bf16[128,2048]{1,0:T(8,128)(2,1)} %get-tuple-element.56.refs_0_, bf16[128,2048]{1,0:T(8,128)(2,1)S(1)} %collective-permute-done.20.refs_1_, ...), custom_call_target="tpu_custom_call" | custom-call | flops 3019898880 | bytes 13631488 | tf_op jit(solution)/shard_map/pallas_call | solution.py:283
  96.4 5.0 %collective-permute-done.19.refs_0_ = bf16[128,2048]{1,0:T(8,128)(2,1)S(1)} collective-permute-done((bf16[128,2048]{1,0:T(8,128)(2,1)}, bf16[128,2048]{1,0:T(8,128)(2,1)S(1)}, u32[]{:S(2)}, u32[]{:S(2)}) %collective-permute-start.19) | collective-permute-done | bytes 524320 | tf_op jit(solution)/shard_map/ppermute | solution.py:381
  102.8 2.6 %collective-permute-done.24.refs_1_ = bf16[128,2048]{1,0:T(8,128)(2,1)S(1)} collective-permute-done((bf16[128,2048]{1,0:T(8,128)(2,1)}, bf16[128,2048]{1,0:T(8,128)(2,1)S(1)}, u32[]{:S(2)}, u32[]{:S(2)}) %collective-permute-start.24) | collective-permute-done | bytes 524320 | tf_op jit(solution)/shard_map/ppermute | solution.py:381
  105.6 5.4 %shard_map.120 = (bf16[128,2048]{1,0:T(8,128)(2,1)S(1)}, bf16[128,2048]{1,0:T(8,128)(2,1)S(1)}, bf16[256,2048]{1,0:T(8,128)(2,1)S(1)}) custom-call(s32[1]{0:T(128)} %bitcast.15.mine_ref, bf16[16,512]{1,0:T(8,128)(2,1)S(1)} %copy-done.7, bf16[128,2048]{1,0:T(8,128)(2,1)} %get-tuple-element.59.refs_0_, bf16[128,2048]{1,0:T(8,128)(2,1)S(1)} %collective-permute-done.24.refs_1_, ...), custom_call_target="tpu_custom_call" | custom-call | flops 3019898880 | bytes 13631488 | tf_op jit(solution)/shard_map/pallas_call | solution.py:283
  111.2 5.1 %collective-permute-done.23.refs_0_ = bf16[128,2048]{1,0:T(8,128)(2,1)S(1)} collective-permute-done((bf16[128,2048]{1,0:T(8,128)(2,1)S(1)}, bf16[128,2048]{1,0:T(8,128)(2,1)S(1)}, u32[]{:S(2)}, u32[]{:S(2)}) %collective-permute-start.23) | collective-permute-done | bytes 524320 | tf_op jit(solution)/shard_map/ppermute | solution.py:381
  120.5 4.3 %shard_map.114 = (bf16[128,2048]{1,0:T(8,128)(2,1)S(1)}, bf16[128,2048]{1,0:T(8,128)(2,1)S(1)}, bf16[256,2048]{1,0:T(8,128)(2,1)S(1)}) custom-call(s32[1]{0:T(128)} %bitcast.15.mine_ref, bf16[16,512]{1,0:T(8,128)(2,1)S(1)} %copy-done.12, bf16[128,2048]{1,0:T(8,128)(2,1)S(1)} %copy-done.5, bf16[128,2048]{1,0:T(8,128)(2,1)S(1)} %collective-permute-done.9.refs_1_, ...), custom_call_target="tpu_custom_call" | custom-call | flops 3019898880 | bytes 13631488 | tf_op jit(solution)/shard_map/pallas_call | solution.py:283
  124.9 6.2 %collective-permute-done.27.refs_0_ = bf16[128,2048]{1,0:T(8,128)(2,1)S(1)} collective-permute-done((bf16[128,2048]{1,0:T(8,128)(2,1)S(1)}, bf16[128,2048]{1,0:T(8,128)(2,1)S(1)}, u32[]{:S(2)}, u32[]{:S(2)}) %collective-permute-start.27) | collective-permute-done | bytes 524320 | tf_op jit(solution)/shard_map/ppermute | solution.py:381
  131.1 2.0 %collective-permute-done.28.refs_1_ = bf16[128,2048]{1,0:T(8,128)(2,1)S(1)} collective-permute-done((bf16[128,2048]{1,0:T(8,128)(2,1)S(1)}, bf16[128,2048]{1,0:T(8,128)(2,1)S(1)}, u32[]{:S(2)}, u32[]{:S(2)}) %collective-permute-start.28) | collective-permute-done | bytes 524320 | tf_op jit(solution)/shard_map/ppermute | solution.py:381
  135.9 11.5 %collective-permute-done.31.refs_0_ = bf16[128,2048]{1,0:T(8,128)(2,1)S(1)} collective-permute-done((bf16[128,2048]{1,0:T(8,128)(2,1)S(1)}, bf16[128,2048]{1,0:T(8,128)(2,1)S(1)}, u32[]{:S(2)}, u32[]{:S(2)}) %collective-permute-start.31) | collective-permute-done | bytes 524320 | tf_op jit(solution)/shard_map/ppermute | solution.py:381
  147.5 2.2 %collective-permute-done.32.refs_1_ = bf16[128,2048]{1,0:T(8,128)(2,1)S(1)} collective-permute-done((bf16[128,2048]{1,0:T(8,128)(2,1)S(1)}, bf16[128,2048]{1,0:T(8,128)(2,1)S(1)}, u32[]{:S(2)}, u32[]{:S(2)}) %collective-permute-start.32) | collective-permute-done | bytes 524320 | tf_op jit(solution)/shard_map/ppermute | solution.py:381
  151.3 12.9 %collective-permute-done.34 = bf16[128,2048]{1,0:T(8,128)(2,1)S(1)} collective-permute-done((bf16[128,2048]{1,0:T(8,128)(2,1)S(1)}, bf16[128,2048]{1,0:T(8,128)(2,1)S(1)}, u32[]{:S(2)}, u32[]{:S(2)}) %collective-permute-start.34) | collective-permute-done | bytes 524320 | tf_op jit(solution)/shard_map/ppermute | solution.py:381
  (104 shorter events, 27.8 us)
Async XLA Ops:
  0.0 15.0 %collective-permute-start.3 = (bf16[512,2048]{1,0:T(8,128)(2,1)}, bf16[512,2048]{1,0:T(8,128)(2,1)S(1)}, u32[]{:S(2)}, u32[]{:S(2)}) collective-permute-start(bf16[512,2048]{1,0:T(8,128)(2,1)} %refs_4_.1), channel_id=1, source_target_pairs={{0,4},{4,0},{8,12},{12,8},{1,5},{5,1},{9,13},{13,9},{2,6},{6,2},{1... | collective-permute-start | bytes 6291464 | tf_op jit(solution)/shard_map/ppermute | solution.py:351
  2.3 12.7 %collective-permute-start.4 = (bf16[128,1024]{1,0:T(8,128)(2,1)}, bf16[128,1024]{1,0:T(8,128)(2,1)S(1)}, u32[]{:S(2)}, u32[]{:S(2)}) collective-permute-start(bf16[128,1024]{1,0:T(8,128)(2,1)} %get-tuple-element.48), channel_id=1, source_target_pairs={{0,8},{4,12},{8,0},{12,4},{1,9},{5,13},{9,1},{13,5},{2,10},{6,14},... | collective-permute-start | bytes 786440 | tf_op jit(solution)/shard_map/ppermute | solution.py:344
  5.1 8.7 %collective-permute-start.1 = (bf16[144,256]{1,0:T(8,128)(2,1)}, bf16[144,256]{1,0:T(8,128)(2,1)S(1)}, u32[]{:S(2)}, u32[]{:S(2)}) collective-permute-start(bf16[144,256]{1,0:T(8,128)(2,1)} %get-tuple-element.46), channel_id=1, source_target_pairs={{0,8},{4,12},{8,0},{12,4},{1,9},{5,13},{9,1},{13,5},{2,10},{6,14},... | collective-permute-start | bytes 221192 | tf_op jit(solution)/shard_map/ppermute | solution.py:348
  5.4 9.6 %collective-permute-start.2 = (bf16[144,256]{1,0:T(8,128)(2,1)}, bf16[144,256]{1,0:T(8,128)(2,1)S(1)}, u32[]{:S(2)}, u32[]{:S(2)}) collective-permute-start(bf16[144,256]{1,0:T(8,128)(2,1)} %get-tuple-element.46), channel_id=1, source_target_pairs={{0,12},{4,8},{8,4},{12,0},{1,13},{5,9},{9,5},{13,1},{2,14},{6,10},... | collective-permute-start | bytes 221192 | tf_op jit(solution)/shard_map/ppermute | solution.py:349
  22.6 14.6 %collective-permute-start.5 = (bf16[128,2048]{1,0:T(8,128)(2,1)}, bf16[128,2048]{1,0:T(8,128)(2,1)}, u32[]{:S(2)}, u32[]{:S(2)}) collective-permute-start(bf16[128,2048]{1,0:T(8,128)(2,1)} %get-tuple-element.49), channel_id=1, source_target_pairs={{0,8},{4,12},{8,0},{12,4},{1,9},{5,13},{9,1},{13,5},{2,10},{6,14},... | collective-permute-start | bytes 1572872 | tf_op jit(solution)/shard_map/ppermute | solution.py:360
  25.5 11.6 %collective-permute-start.6 = (bf16[16,512]{1,0:T(8,128)(2,1)}, bf16[16,512]{1,0:T(8,128)(2,1)S(1)}, u32[]{:S(2)}, u32[]{:S(2)}) collective-permute-start(bf16[16,512]{1,0:T(8,128)(2,1)} %get-tuple-element.50.quad_ref), channel_id=1, source_target_pairs={{0,1},{1,3},{3,2},{2,0},{4,5},{5,7},{7,6},{6,4},{8,9},{9,11},{11,1... | collective-permute-start | bytes 49160 | tf_op jit(solution)/shard_map/ppermute | solution.py:370
  27.1 10.1 %collective-permute-start.7 = (bf16[16,512]{1,0:T(8,128)(2,1)}, bf16[16,512]{1,0:T(8,128)(2,1)S(1)}, u32[]{:S(2)}, u32[]{:S(2)}) collective-permute-start(bf16[16,512]{1,0:T(8,128)(2,1)} %get-tuple-element.50.quad_ref), channel_id=1, source_target_pairs={{0,3},{1,2},{3,0},{2,1},{4,7},{5,6},{7,4},{6,5},{8,11},{9,10},{11,... | collective-permute-start | bytes 49160 | tf_op jit(solution)/shard_map/ppermute | solution.py:370
  29.5 7.6 %collective-permute-start.8 = (bf16[16,512]{1,0:T(8,128)(2,1)}, bf16[16,512]{1,0:T(8,128)(2,1)S(1)}, u32[]{:S(2)}, u32[]{:S(2)}) collective-permute-start(bf16[16,512]{1,0:T(8,128)(2,1)} %get-tuple-element.50.quad_ref), channel_id=1, source_target_pairs={{0,2},{1,0},{3,1},{2,3},{4,6},{5,4},{7,5},{6,7},{8,10},{9,8},{11,9... | collective-permute-start | bytes 49160 | tf_op jit(solution)/shard_map/ppermute | solution.py:370
  40.6 13.1 %collective-permute-start.10 = (bf16[128,2048]{1,0:T(8,128)(2,1)}, bf16[128,2048]{1,0:T(8,128)(2,1)S(1)}, u32[]{:S(2)}, u32[]{:S(2)}) collective-permute-start(bf16[128,2048]{1,0:T(8,128)(2,1)} %get-tuple-element.52.refs_0_), channel_id=1, source_target_pairs={{0,8},{4,12},{8,0},{12,4},{1,9},{5,13},{9,1},{13,5},{2,10},{6,14},... | collective-permute-start | bytes 1572872 | tf_op jit(solution)/shard_map/ppermute | solution.py:381
  41.1 14.2 %collective-permute-start.11 = (bf16[128,2048]{1,0:T(8,128)(2,1)}, bf16[128,2048]{1,0:T(8,128)(2,1)}, u32[]{:S(2)}, u32[]{:S(2)}) collective-permute-start(bf16[128,2048]{1,0:T(8,128)(2,1)} %get-tuple-element.52.refs_0_), channel_id=1, source_target_pairs={{0,1},{1,3},{3,2},{2,0},{4,5},{5,7},{7,6},{6,4},{8,9},{9,11},{11,1... | collective-permute-start | bytes 1572872 | tf_op jit(solution)/shard_map/ppermute | solution.py:381
  56.1 12.4 %collective-permute-start.13 = (bf16[128,2048]{1,0:T(8,128)(2,1)}, bf16[128,2048]{1,0:T(8,128)(2,1)}, u32[]{:S(2)}, u32[]{:S(2)}) collective-permute-start(bf16[128,2048]{1,0:T(8,128)(2,1)} %get-tuple-element.55.refs_0_), channel_id=1, source_target_pairs={{0,8},{4,12},{8,0},{12,4},{1,9},{5,13},{9,1},{13,5},{2,10},{6,14},... | collective-permute-start | bytes 1572872 | tf_op jit(solution)/shard_map/ppermute | solution.py:381
  57.3 12.7 %collective-permute-start.14 = (bf16[128,2048]{1,0:T(8,128)(2,1)}, bf16[128,2048]{1,0:T(8,128)(2,1)}, u32[]{:S(2)}, u32[]{:S(2)}) collective-permute-start(bf16[128,2048]{1,0:T(8,128)(2,1)} %get-tuple-element.55.refs_0_), channel_id=1, source_target_pairs={{0,1},{1,3},{3,2},{2,0},{4,5},{5,7},{7,6},{6,4},{8,9},{9,11},{11,1... | collective-permute-start | bytes 1572872 | tf_op jit(solution)/shard_map/ppermute | solution.py:381
  57.4 14.5 %collective-permute-start.17 = (bf16[128,2048]{1,0:T(8,128)(2,1)}, bf16[128,2048]{1,0:T(8,128)(2,1)}, u32[]{:S(2)}, u32[]{:S(2)}) collective-permute-start(bf16[128,2048]{1,0:T(8,128)(2,1)} %get-tuple-element.55.refs_0_), channel_id=1, source_target_pairs={{0,4},{4,0},{8,12},{12,8},{1,5},{5,1},{9,13},{13,9},{2,6},{6,2},{1... | collective-permute-start | bytes 1572872 | tf_op jit(solution)/shard_map/ppermute | solution.py:381
  69.9 14.7 %collective-permute-start.15 = (bf16[128,2048]{1,0:T(8,128)(2,1)}, bf16[128,2048]{1,0:T(8,128)(2,1)}, u32[]{:S(2)}, u32[]{:S(2)}) collective-permute-start(bf16[128,2048]{1,0:T(8,128)(2,1)} %get-tuple-element.56.refs_0_), channel_id=1, source_target_pairs={{0,8},{4,12},{8,0},{12,4},{1,9},{5,13},{9,1},{13,5},{2,10},{6,14},... | collective-permute-start | bytes 1572872 | tf_op jit(solution)/shard_map/ppermute | solution.py:381
  71.1 15.3 %collective-permute-start.16 = (bf16[128,2048]{1,0:T(8,128)(2,1)}, bf16[128,2048]{1,0:T(8,128)(2,1)}, u32[]{:S(2)}, u32[]{:S(2)}) collective-permute-start(bf16[128,2048]{1,0:T(8,128)(2,1)} %get-tuple-element.56.refs_0_), channel_id=1, source_target_pairs={{0,1},{1,3},{3,2},{2,0},{4,5},{5,7},{7,6},{6,4},{8,9},{9,11},{11,1... | collective-permute-start | bytes 1572872 | tf_op jit(solution)/shard_map/ppermute | solution.py:381
  86.4 9.9 %collective-permute-start.22 = (bf16[256,2048]{1,0:T(8,128)(2,1)S(1)}, bf16[256,2048]{1,0:T(8,128)(2,1)S(1)}, u32[]{:S(2)}, u32[]{:S(2)}) collective-permute-start(bf16[256,2048]{1,0:T(8,128)(2,1)S(1)} %get-tuple-element.63), channel_id=1, source_target_pairs={{0,4},{4,0},{8,12},{12,8},{1,5},{5,1},{9,13},{13,9},{2,6},{6,2},{1... | collective-permute-start | bytes 3145736 | tf_op jit(solution)/shard_map/ppermute | solution.py:381
  86.4 3.2 %collective-permute-start.20 = (bf16[128,2048]{1,0:T(8,128)(2,1)}, bf16[128,2048]{1,0:T(8,128)(2,1)S(1)}, u32[]{:S(2)}, u32[]{:S(2)}) collective-permute-start(bf16[128,2048]{1,0:T(8,128)(2,1)} %get-tuple-element.56.refs_0_), channel_id=1, source_target_pairs={{0,4},{4,0},{8,12},{12,8},{1,5},{5,1},{9,13},{13,9},{2,6},{6,2},{1... | collective-permute-start | bytes 1572872 | tf_op jit(solution)/shard_map/ppermute | solution.py:381
  86.9 3.9 %collective-permute-start.21 = (bf16[128,2048]{1,0:T(8,128)(2,1)}, bf16[128,2048]{1,0:T(8,128)(2,1)S(1)}, u32[]{:S(2)}, u32[]{:S(2)}) collective-permute-start(bf16[128,2048]{1,0:T(8,128)(2,1)} %get-tuple-element.60.refs_2_), channel_id=1, source_target_pairs={{0,4},{4,0},{8,12},{12,8},{1,5},{5,1},{9,13},{13,9},{2,6},{6,2},{1... | collective-permute-start | bytes 1572872 | tf_op jit(solution)/shard_map/ppermute | solution.py:381
  86.9 14.5 %collective-permute-start.19 = (bf16[128,2048]{1,0:T(8,128)(2,1)}, bf16[128,2048]{1,0:T(8,128)(2,1)S(1)}, u32[]{:S(2)}, u32[]{:S(2)}) collective-permute-start(bf16[128,2048]{1,0:T(8,128)(2,1)} %get-tuple-element.59.refs_0_), channel_id=1, source_target_pairs={{0,8},{4,12},{8,0},{12,4},{1,9},{5,13},{9,1},{13,5},{2,10},{6,14},... | collective-permute-start | bytes 1572872 | tf_op jit(solution)/shard_map/ppermute | solution.py:381
  101.4 9.6 %collective-permute-start.26 = (bf16[256,2048]{1,0:T(8,128)(2,1)S(1)}, bf16[256,2048]{1,0:T(8,128)(2,1)S(1)}, u32[]{:S(2)}, u32[]{:S(2)}) collective-permute-start(bf16[256,2048]{1,0:T(8,128)(2,1)S(1)} %get-tuple-element.68), channel_id=1, source_target_pairs={{0,4},{4,0},{8,12},{12,8},{1,5},{5,1},{9,13},{13,9},{2,6},{6,2},{1... | collective-permute-start | bytes 3145736 | tf_op jit(solution)/shard_map/ppermute | solution.py:381
  101.4 4.0 %collective-permute-start.24 = (bf16[128,2048]{1,0:T(8,128)(2,1)}, bf16[128,2048]{1,0:T(8,128)(2,1)S(1)}, u32[]{:S(2)}, u32[]{:S(2)}) collective-permute-start(bf16[128,2048]{1,0:T(8,128)(2,1)} %get-tuple-element.59.refs_0_), channel_id=1, source_target_pairs={{0,4},{4,0},{8,12},{12,8},{1,5},{5,1},{9,13},{13,9},{2,6},{6,2},{1... | collective-permute-start | bytes 1572872 | tf_op jit(solution)/shard_map/ppermute | solution.py:381
  102.0 3.6 %collective-permute-start.25 = (bf16[128,2048]{1,0:T(8,128)(2,1)S(1)}, bf16[128,2048]{1,0:T(8,128)(2,1)S(1)}, u32[]{:S(2)}, u32[]{:S(2)}) collective-permute-start(bf16[128,2048]{1,0:T(8,128)(2,1)S(1)} %get-tuple-element.65.refs_2_), channel_id=1, source_target_pairs={{0,4},{4,0},{8,12},{12,8},{1,5},{5,1},{9,13},{13,9},{2,6},{6,2},{1... | collective-permute-start | bytes 1572872 | tf_op jit(solution)/shard_map/ppermute | solution.py:381
  102.0 14.3 %collective-permute-start.23 = (bf16[128,2048]{1,0:T(8,128)(2,1)S(1)}, bf16[128,2048]{1,0:T(8,128)(2,1)S(1)}, u32[]{:S(2)}, u32[]{:S(2)}) collective-permute-start(bf16[128,2048]{1,0:T(8,128)(2,1)S(1)} %get-tuple-element.64), channel_id=1, source_target_pairs={{0,8},{4,12},{8,0},{12,4},{1,9},{5,13},{9,1},{13,5},{2,10},{6,14},... | collective-permute-start | bytes 1572872 | tf_op jit(solution)/shard_map/ppermute | solution.py:381
  116.3 8.5 %collective-permute-start.29 = (bf16[256,2048]{1,0:T(8,128)(2,1)S(1)}, bf16[256,2048]{1,0:T(8,128)(2,1)S(1)}, u32[]{:S(2)}, u32[]{:S(2)}) collective-permute-start(bf16[256,2048]{1,0:T(8,128)(2,1)S(1)} %get-tuple-element.74), channel_id=1, source_target_pairs={{0,4},{4,0},{8,12},{12,8},{1,5},{5,1},{9,13},{13,9},{2,6},{6,2},{1... | collective-permute-start | bytes 3145736 | tf_op jit(solution)/shard_map/ppermute | solution.py:381
  116.3 3.4 %collective-permute-start.9 = (bf16[128,2048]{1,0:T(8,128)(2,1)S(1)}, bf16[128,2048]{1,0:T(8,128)(2,1)S(1)}, u32[]{:S(2)}, u32[]{:S(2)}) collective-permute-start(bf16[128,2048]{1,0:T(8,128)(2,1)S(1)} %copy-done.5), channel_id=1, source_target_pairs={{0,4},{4,0},{8,12},{12,8},{1,5},{5,1},{9,13},{13,9},{2,6},{6,2},{1... | collective-permute-start | bytes 1572872 | tf_op jit(solution)/shard_map/ppermute | solution.py:381
  116.8 3.6 %collective-permute-start.12 = (bf16[128,2048]{1,0:T(8,128)(2,1)S(1)}, bf16[128,2048]{1,0:T(8,128)(2,1)S(1)}, u32[]{:S(2)}, u32[]{:S(2)}) collective-permute-start(bf16[128,2048]{1,0:T(8,128)(2,1)S(1)} %copy-done.4), channel_id=1, source_target_pairs={{0,4},{4,0},{8,12},{12,8},{1,5},{5,1},{9,13},{13,9},{2,6},{6,2},{1... | collective-permute-start | bytes 1572872 | tf_op jit(solution)/shard_map/ppermute | solution.py:381
  116.9 14.3 %collective-permute-start.27 = (bf16[128,2048]{1,0:T(8,128)(2,1)S(1)}, bf16[128,2048]{1,0:T(8,128)(2,1)S(1)}, u32[]{:S(2)}, u32[]{:S(2)}) collective-permute-start(bf16[128,2048]{1,0:T(8,128)(2,1)S(1)} %get-tuple-element.69), channel_id=1, source_target_pairs={{0,8},{4,12},{8,0},{12,4},{1,9},{5,13},{9,1},{13,5},{2,10},{6,14},... | collective-permute-start | bytes 1572872 | tf_op jit(solution)/shard_map/ppermute | solution.py:381
  118.0 15.2 %collective-permute-start.28 = (bf16[128,2048]{1,0:T(8,128)(2,1)S(1)}, bf16[128,2048]{1,0:T(8,128)(2,1)S(1)}, u32[]{:S(2)}, u32[]{:S(2)}) collective-permute-start(bf16[128,2048]{1,0:T(8,128)(2,1)S(1)} %add_convert_fusion.5), channel_id=1, source_target_pairs={{0,1},{1,3},{3,2},{2,0},{4,5},{5,7},{7,6},{6,4},{8,9},{9,11},{11,1... | collective-permute-start | bytes 1572872 | tf_op jit(solution)/shard_map/ppermute | solution.py:381
  133.1 14.3 %collective-permute-start.31 = (bf16[128,2048]{1,0:T(8,128)(2,1)S(1)}, bf16[128,2048]{1,0:T(8,128)(2,1)S(1)}, u32[]{:S(2)}, u32[]{:S(2)}) collective-permute-start(bf16[128,2048]{1,0:T(8,128)(2,1)S(1)} %get-tuple-element.76), channel_id=1, source_target_pairs={{0,8},{4,12},{8,0},{12,4},{1,9},{5,13},{9,1},{13,5},{2,10},{6,14},... | collective-permute-start | bytes 1572872 | tf_op jit(solution)/shard_map/ppermute | solution.py:381
  134.7 15.0 %collective-permute-start.32 = (bf16[128,2048]{1,0:T(8,128)(2,1)S(1)}, bf16[128,2048]{1,0:T(8,128)(2,1)S(1)}, u32[]{:S(2)}, u32[]{:S(2)}) collective-permute-start(bf16[128,2048]{1,0:T(8,128)(2,1)S(1)} %add_convert_fusion.3), channel_id=1, source_target_pairs={{0,1},{1,3},{3,2},{2,0},{4,5},{5,7},{7,6},{6,4},{8,9},{9,11},{11,1... | collective-permute-start | bytes 1572872 | tf_op jit(solution)/shard_map/ppermute | solution.py:381
  150.0 14.2 %collective-permute-start.34 = (bf16[128,2048]{1,0:T(8,128)(2,1)S(1)}, bf16[128,2048]{1,0:T(8,128)(2,1)S(1)}, u32[]{:S(2)}, u32[]{:S(2)}) collective-permute-start(bf16[128,2048]{1,0:T(8,128)(2,1)S(1)} %add_convert_fusion.1), channel_id=1, source_target_pairs={{0,1},{1,3},{3,2},{2,0},{4,5},{5,7},{7,6},{6,4},{8,9},{9,11},{11,1... | collective-permute-start | bytes 1572872 | tf_op jit(solution)/shard_map/ppermute | solution.py:381
  150.8 13.4 %collective-permute-start.33 = (bf16[128,2048]{1,0:T(8,128)(2,1)S(1)}, bf16[128,2048]{1,0:T(8,128)(2,1)S(1)}, u32[]{:S(2)}, u32[]{:S(2)}) collective-permute-start(bf16[128,2048]{1,0:T(8,128)(2,1)S(1)} %get-tuple-element.81), channel_id=1, source_target_pairs={{0,8},{4,12},{8,0},{12,4},{1,9},{5,13},{9,1},{13,5},{2,10},{6,14},... | collective-permute-start | bytes 1572872 | tf_op jit(solution)/shard_map/ppermute | solution.py:381
  (23 other events, 159.6 us)

commit v8 on v6

--- a/solution.py
+++ b/solution.py
@@ -167,7 +167,7 @@
             pltpu.VMEM(w_other.shape, jnp.bfloat16),
             pltpu.SemaphoreType.DMA((2,)),
         ],
-        compiler_params=pltpu.CompilerParams(vmem_limit_bytes=16 * MIB),
+        compiler_params=pltpu.CompilerParams(vmem_limit_bytes=60 * MIB),
         cost_estimate=pl.CostEstimate(
             flops=16 * tokens * tokens * chip_width + 2 * tokens * chip_width * width,
             bytes_accessed=4 * w_own.size + 4 * tokens * width,
@@ -188,12 +188,16 @@
 
 
 def add_and_norm(own, other, gain):
+    tokens, width = own.shape
+    rows = tokens // 4
+    block = pl.BlockSpec((rows, width), lambda step: (step, 0))
     return pl.pallas_call(
         norm_kernel,
-        in_specs=[pl.BlockSpec(memory_space=pltpu.VMEM)] * 3,
-        out_specs=[pl.BlockSpec(memory_space=pltpu.VMEM)] * 2,
+        grid=(4,),
+        in_specs=[block, block, pl.BlockSpec((1, width), lambda step: (0, 0))],
+        out_specs=[block, block],
         out_shape=[jax.ShapeDtypeStruct(own.shape, jnp.bfloat16)] * 2,
-        compiler_params=pltpu.CompilerParams(vmem_limit_bytes=10 * MIB),
+        compiler_params=pltpu.CompilerParams(vmem_limit_bytes=60 * MIB),
     )(own, other, gain)
 
 
@@ -226,10 +230,13 @@
     )(*arrays)
 
 
-def experts_kernel(mine_ref, quad_ref, *refs, cap):
-    row_refs, refs = refs[:4], refs[4:]
+def experts_kernel(mine_ref, quad_ref, *refs, cap, pieces):
+    row_refs = []
+    for count in pieces:
+        row_refs.append(refs[:count])
+        refs = refs[count:]
     w_gate_ref, w_up_ref, w_down_ref, own_ref, across_ref, other_ref, packed = refs
-    tokens = row_refs[0].shape[0]
+    tokens = row_refs[0][0].shape[0]
     quad = quad_ref[...].astype(jnp.float32)
     expert = lax.broadcasted_iota(jnp.int32, quad.shape, 0)
     line = jnp.sum(jnp.where(expert == mine_ref[0], quad, 0.0), axis=0, keepdims=True)
@@ -254,9 +261,13 @@
         weights.append(
             jnp.sum(jnp.where(chosen, gates[block : block + 1, :], 0.0), axis=1, keepdims=True)
         )
-        packed[block * cap : (block + 1) * cap, :] = jnp.dot(
-            picks[block], row_refs[block][...], preferred_element_type=jnp.float32
-        ).astype(jnp.bfloat16)
+        start = 0
+        for row_ref in row_refs[block]:
+            stop = start + row_ref.shape[1]
+            packed[block * cap : (block + 1) * cap, start:stop] = jnp.dot(
+                picks[block], row_ref[...], preferred_element_type=jnp.float32
+            ).astype(jnp.bfloat16)
+            start = stop
     rows = packed[...]
     gate_proj = jnp.dot(rows, w_gate_ref[...], preferred_element_type=jnp.float32)
     up_proj = jnp.dot(rows, w_up_ref[...], preferred_element_type=jnp.float32)
@@ -276,12 +287,13 @@
 
 
 def experts_on_rows(mine, quad, row_blocks, w_gate, w_up, w_down, cap):
-    tokens, width = row_blocks[0].shape
-    hidden_units = w_gate.shape[1]
+    tokens = row_blocks[0][0].shape[0]
+    width, hidden_units = w_gate.shape
+    pieces = tuple(len(block) for block in row_blocks)
     return pl.pallas_call(
-        functools.partial(experts_kernel, cap=cap),
+        functools.partial(experts_kernel, cap=cap, pieces=pieces),
         in_specs=[pl.BlockSpec(memory_space=pltpu.SMEM)]
-        + [pl.BlockSpec(memory_space=pltpu.VMEM)] * 8,
+        + [pl.BlockSpec(memory_space=pltpu.VMEM)] * (4 + sum(pieces)),
         out_specs=[pl.BlockSpec(memory_space=pltpu.VMEM)] * 3,
         out_shape=[
             jax.ShapeDtypeStruct((tokens, width), jnp.bfloat16),
@@ -295,7 +307,7 @@
             bytes_accessed=16 * tokens * width + 6 * width * hidden_units,
             transcendentals=4 * cap * hidden_units,
         ),
-    )(mine.reshape(1), quad, *row_blocks, w_gate, w_up, w_down)
+    )(mine.reshape(1), quad, *sum(row_blocks, []), w_gate, w_up, w_down)
 
 
 def gathered_plan(
@@ -371,6 +383,7 @@
     mine = place * n_sub + lax.axis_index("sub")
 
     held = {("row", 0): normed, ("quad", 0): quad}
+    half = normed.shape[1] // 2
     ways = {"across": ("seq", across), "twin": ("seq", twin), "on": ("sub", ring(1))}
 
     def move(array, way):
@@ -380,7 +393,10 @@
         held["own", step], held["part", step], other = experts_on_rows(
             mine,
             held["quad", step],
-            [held[name, step] for name in ("row", "twin", "across", "diagonal")],
+            [
+                [held[name, step]] if (name, step) in held else list(held[name, step, "pieces"])
+                for name in ("row", "twin", "across", "diagonal")
+            ],
             expert_gate[0],
             expert_up[0],
             expert_down[0],
@@ -402,10 +418,14 @@
     for turn in range(1, n_sub + 5):
         now = {}
         step = turn - 1
+        if step < last:
+            now["across", step] = move(held["row", step], "across")
+            now["row", step + 1] = move(held["row", step], "on")
+            now["quad", step + 1] = move(held["quad", step], "on")
+        if step == last:
+            now["half", 0] = move(held["row", step][:, :half], "across")
+            now["half", 1] = move(held["across", step - 1][:, half:], "on")
         if step <= last:
-            now["across", step] = move(held["row", step], "across")
-            if step < last:
-                now["row", step + 1] = move(held["row", step], "on")
             held["twin", step] = move(held["row", step], "twin")
         step = turn - 4 if turn < n_sub + 4 else 0
         if 1 <= step <= last or turn == n_sub + 4:
@@ -415,8 +435,13 @@
             more = [held["sum", step - 1]] if step > 1 else []
             now["sum", step] = move(sum_of(step, more).astype(jnp.bfloat16), "on")
         step = turn - 2
-        if 0 <= step <= last:
+        if 0 <= step < last:
             held["diagonal", step] = move(held["across", step], "twin")
+        if step == last:
+            held["across", step, "pieces"] = [held["half", side] for side in range(2)]
+            held["diagonal", step, "pieces"] = [
+                move(held["half", side], "twin") for side in range(2)
+            ]
         if 1 <= step <= last:
             now["other", step] = experts_of(step)
         if turn == n_sub + 2:
@@ -424,9 +449,6 @@
         step = turn - 3 if turn < n_sub + 3 else 0
         if 1 <= step <= last or turn == n_sub + 3:
             now["away", step] = twin_sum(step)
-        if turn == 1:
-            for steps in range(1, n_sub):
-                now["quad", steps] = lax.ppermute(quad, "sub", ring(steps))
         if turn < n_sub + 4:
             now = dict(zip(now.keys(), meet(*now.values())))
         held.update(now)

time: 171 us -> 165 us (0.965)
  waiting for transfers between devices: 97.1 us -> 79.7 us
  starting transfers between devices: 22.9 us -> 33.7 us
  Pallas kernels: 34.2 us -> 38.2 us
  local copies, waits for them, and re-layouts: 13.4 us -> 10.5 us
    ppermute x26 -> x31, starting transfers between devices: 11.9 us -> 27.3 us  [move(): return lax.ppermute(array, *ways[way])]
    ppermute x3 -> x0, waiting for transfers between devices: 9.84 us -> none  [gathered_plan(): now['quad', steps] = lax.ppermute(quad, 'sub', ring(steps))]
    unnamed x42 -> x28, local copies, waits for them, and re-layouts: 13.3 us -> 6.66 us
    ppermute x26 -> x31, waiting for transfers between devices: 72.8 us -> 66.6 us  [move(): return lax.ppermute(array, *ways[way])]
    ppermute x3 -> x0, starting transfers between devices: 4.5 us -> none  [gathered_plan(): now['quad', steps] = lax.ppermute(quad, 'sub', ring(steps))]
    pallas_call x5, Pallas kernels: 22.4 us -> 24.7 us  [the longest x4 21.1 us: experts_on_rows(): pl.pallas_call(functools.partial(experts_kernel, cap=cap, pieces=pieces),...]
    slice x0 -> x2, local copies, waits for them, and re-layouts: none -> 1.94 us  [the longest x1 0.97 us: gathered_plan(): now['half', 0] = move(held['row', step][:, :half], 'across')]
    pallas_call x2, Pallas kernels: 9.85 us -> 11.6 us  [attend(): pl.pallas_call(functools.partial(attend_kernel, scale=1.0 / HD ** 0.5), i...]
  transfers between devices with their start and end apart: 35 -> 37, of which waited for: 24 -> 20; matrix products, arithmetic and copies ran while one was open for 1% -> 3% of each run, Pallas kernels for 16% -> 18%
where the time goes in v8:
time: 165 us
  waiting for transfers between devices  79.7 us (48%)
  Pallas kernels  38.2 us (23%)
  starting transfers between devices  33.7 us (20%)
  local copies, waits for them, and re-layouts  10.5 us (6%)
  other arithmetic  2.64 us (2%)
    ppermute x31, waiting for transfers between devices, move(): return lax.ppermute(array, *ways[way])  66.6 us
    ppermute x31, starting transfers between devices, move(): return lax.ppermute(array, *ways[way])  27.3 us
    pallas_call x4, Pallas kernels, experts_on_rows(): pl.pallas_call(functools.partial(experts_kernel, cap=cap, pieces=pieces),...  21.1 us
    pallas_call x2, Pallas kernels, attend(): pl.pallas_call(functools.partial(attend_kernel, scale=1.0 / HD ** 0.5), i...  11.6 us
    unnamed x28, local copies, waits for them, and re-layouts  6.66 us
    ppermute x1, waiting for transfers between devices, gathered_plan(): lax.ppermute(kv_away, 'seq', across)  6.45 us
    ppermute x1, waiting for transfers between devices, gathered_plan(): projected_across = lax.ppermute(sent, 'seq', across)  5.46 us
    pallas_call x1, Pallas kernels, add_and_norm(): pl.pallas_call(norm_kernel, grid=(4,), in_specs=[block, block, pl.BlockSp...  3.61 us
  transfers between devices with their start and end apart: 37, of which 20 were waited for; matrix products, arithmetic and copies ran while one was open for 3% of the time, Pallas kernels for 18%

profile of v8, /device:TPU:0, one launch (start us, length us, event | category | flops | bytes accessed | tf_op | source)
XLA Modules:
  0.0 164.9 jit_solution(9014111236033530143)
XLA Ops:
  0.5 1.9 %shard_map.109 = (bf16[128,1024]{1,0:T(8,128)(2,1)}, bf16[144,256]{1,0:T(8,128)(2,1)}, bf16[144,256]{1,0:T(8,128)(2,1)}) custom-call(s32[1]{0:T(128)} %bitcast.7.chip_ref, bf16[128,2048]{1,0:T(8,128)(2,1)} %bitcast.35, bf16[128,256]{1,0:T(8,128)(2,1)} %bitcast.38, bf16[128,256]{1,0:T(8,128)(2,1)} %bitcast.39, s32[8,128]{1,0:T(8,128)} %bitcast.40, ...), custom_call_target="tpu_custom_call" | custom-call | tf_op jit(solution)/shard_map/pallas_call | solution.py:87
  2.3 2.5 %collective-permute-start.4 = (bf16[128,1024]{1,0:T(8,128)(2,1)}, bf16[128,1024]{1,0:T(8,128)(2,1)S(1)}, u32[]{:S(2)}, u32[]{:S(2)}) collective-permute-start(bf16[128,1024]{1,0:T(8,128)(2,1)} %get-tuple-element.52), channel_id=1, source_target_pairs={{0,8},{4,12},{8,0},{12,4},{1,9},{5,13},{9,1},{13,5},{2,10},{6,14},... | collective-permute-start | bytes 786440 | tf_op jit(solution)/shard_map/ppermute | solution.py:354
  7.4 6.4 %collective-permute-done.1.refs_2_ = bf16[144,256]{1,0:T(8,128)(2,1)S(1)} collective-permute-done((bf16[144,256]{1,0:T(8,128)(2,1)}, bf16[144,256]{1,0:T(8,128)(2,1)S(1)}, u32[]{:S(2)}, u32[]{:S(2)}) %collective-permute-start.1) | collective-permute-done | bytes 73760 | tf_op jit(solution)/shard_map/ppermute | solution.py:358
  17.1 5.6 %shard_map.111 = (bf16[128,2048]{1,0:T(8,128)(2,1)}, bf16[16,512]{1,0:T(8,128)(2,1)}) custom-call(s32[7]{0:T(128)} %stack.38.place_ref, bf16[128,1024]{1,0:T(8,128)(2,1)} %copy-done.12, bf16[144,256]{1,0:T(8,128)(2,1)} %get-tuple-element.49.refs_0_, bf16[144,256]{1,0:T(8,128)(2,1)} %copy-done.9, bf16[144,256]{1,0:T(8,128)(2,1)} %copy-done.10, ...), custom_call_target="tpu_custom_call" | custom-call | flops 805306368 | bytes 5242880 | tf_op jit(solution)/shard_map/pallas_call | solution.py:152
  22.7 1.6 collective-permute-start.5
  25.5 6.0 %shard_map.110 = (f32[128,2048]{1,0:T(8,128)}, bf16[16,512]{1,0:T(8,128)(2,1)}) custom-call(s32[7]{0:T(128)} %stack.37.place_ref, bf16[128,2048]{1,0:T(8,128)(2,1)} %bitcast.36, bf16[144,256]{1,0:T(8,128)(2,1)} %get-tuple-element.49.refs_0_, bf16[144,256]{1,0:T(8,128)(2,1)} %copy-done.9, bf16[144,256]{1,0:T(8,128)(2,1)} %copy-done.10, ...), custom_call_target="tpu_custom_call" | custom-call | flops 805306368 | bytes 5242880 | tf_op jit(solution)/shard_map/pallas_call | solution.py:152
  31.5 5.5 %collective-permute-done.5.other_ref = bf16[128,2048]{1,0:T(8,128)(2,1)} collective-permute-done((bf16[128,2048]{1,0:T(8,128)(2,1)}, bf16[128,2048]{1,0:T(8,128)(2,1)}, u32[]{:S(2)}, u32[]{:S(2)}) %collective-permute-start.5) | collective-permute-done | bytes 524320 | tf_op jit(solution)/shard_map/ppermute | solution.py:370
  37.0 3.6 %shard_map.112 = (bf16[128,2048]{1,0:T(8,128)(2,1)}, bf16[128,2048]{1,0:T(8,128)(2,1)}) custom-call(f32[128,2048]{1,0:T(8,128)} %get-tuple-element.51.own_ref, bf16[128,2048]{1,0:T(8,128)(2,1)} %collective-permute-done.5.other_ref, bf16[1,2048]{1,0:T(2,128)(2,1)} %broadcast_in_dim.6.gain_ref), custom_call_target="tpu_custom_call" | custom-call | tf_op jit(solution)/shard_map/pallas_call | solution.py:194
  40.6 1.6 collective-permute-start.7
  42.2 1.6 collective-permute-start.8
  43.8 2.6 %collective-permute-start.9 = (bf16[16,512]{1,0:T(8,128)(2,1)S(1)}, bf16[16,512]{1,0:T(8,128)(2,1)S(1)}, u32[]{:S(2)}, u32[]{:S(2)}) collective-permute-start(bf16[16,512]{1,0:T(8,128)(2,1)S(1)} %copy-done.6), channel_id=1, source_target_pairs={{0,1},{1,3},{3,2},{2,0},{4,5},{5,7},{7,6},{6,4},{8,9},{9,11},{11,1... | collective-permute-start | bytes 49160 | tf_op jit(solution)/shard_map/ppermute | solution.py:390
  46.4 10.3 %collective-permute-done.9.refs_2_ = bf16[16,512]{1,0:T(8,128)(2,1)S(1)} collective-permute-done((bf16[16,512]{1,0:T(8,128)(2,1)S(1)}, bf16[16,512]{1,0:T(8,128)(2,1)S(1)}, u32[]{:S(2)}, u32[]{:S(2)}) %collective-permute-start.9) | collective-permute-done | bytes 16416 | tf_op jit(solution)/shard_map/ppermute | solution.py:390
  58.8 3.4 %collective-permute-start.13 = (bf16[16,512]{1,0:T(8,128)(2,1)S(1)}, bf16[16,512]{1,0:T(8,128)(2,1)S(1)}, u32[]{:S(2)}, u32[]{:S(2)}) collective-permute-start(bf16[16,512]{1,0:T(8,128)(2,1)S(1)} %get-tuple-element.60.quad_ref), channel_id=1, source_target_pairs={{0,1},{1,3},{3,2},{2,0},{4,5},{5,7},{7,6},{6,4},{8,9},{9,11},{11,1... | collective-permute-start | bytes 49160 | tf_op jit(solution)/shard_map/ppermute | solution.py:390
  62.2 9.2 %collective-permute-done.13.refs_2_ = bf16[16,512]{1,0:T(8,128)(2,1)S(1)} collective-permute-done((bf16[16,512]{1,0:T(8,128)(2,1)S(1)}, bf16[16,512]{1,0:T(8,128)(2,1)S(1)}, u32[]{:S(2)}, u32[]{:S(2)}) %collective-permute-start.13) | collective-permute-done | bytes 16416 | tf_op jit(solution)/shard_map/ppermute | solution.py:390
  71.4 1.6 collective-permute-start.14
  73.7 3.4 %collective-permute-start.16 = (bf16[16,512]{1,0:T(8,128)(2,1)S(1)}, bf16[16,512]{1,0:T(8,128)(2,1)S(1)}, u32[]{:S(2)}, u32[]{:S(2)}) collective-permute-start(bf16[16,512]{1,0:T(8,128)(2,1)S(1)} %get-tuple-element.62.quad_ref), channel_id=1, source_target_pairs={{0,1},{1,3},{3,2},{2,0},{4,5},{5,7},{7,6},{6,4},{8,9},{9,11},{11,1... | collective-permute-start | bytes 49160 | tf_op jit(solution)/shard_map/ppermute | solution.py:390
  77.1 1.9 %copy-done.1 = bf16[1,2048,768]{2,1,0:T(8,128)(2,1)S(1)} copy-done((bf16[1,2048,768]{2,1,0:T(8,128)(2,1)S(1)}, bf16[1,2048,768]{2,1,0:T(8,128)(2,1)}, u32[]{:S(2)}) %copy-start.1) | copy-done | bytes 3145752
  79.0 1.9 %copy-done.2 = bf16[1,768,2048]{2,1,0:T(8,128)(2,1)S(1)} copy-done((bf16[1,768,2048]{2,1,0:T(8,128)(2,1)S(1)}, bf16[1,768,2048]{2,1,0:T(8,128)(2,1)}, u32[]{:S(2)}) %copy-start.2) | copy-done | bytes 3145752
  80.9 5.8 %shard_map.116 = (bf16[128,2048]{1,0:T(8,128)(2,1)S(1)}, bf16[128,2048]{1,0:T(8,128)(2,1)S(1)}, bf16[256,2048]{1,0:T(8,128)(2,1)S(1)}) custom-call(s32[1]{0:T(128)} %bitcast.15.mine_ref, bf16[16,512]{1,0:T(8,128)(2,1)S(1)} %get-tuple-element.60.quad_ref, bf16[128,2048]{1,0:T(8,128)(2,1)} %get-tuple-element.59.refs_0_, ...), custom_call_target="tpu_custom_call" | custom-call | flops 3019898880 | bytes 13631488 | tf_op jit(solution)/shard_map/pallas_call | solution.py:293
  86.8 1.7 %collective-permute-done.16.refs_2_ = bf16[16,512]{1,0:T(8,128)(2,1)S(1)} collective-permute-done((bf16[16,512]{1,0:T(8,128)(2,1)S(1)}, bf16[16,512]{1,0:T(8,128)(2,1)S(1)}, u32[]{:S(2)}, u32[]{:S(2)}) %collective-permute-start.16) | collective-permute-done | bytes 16416 | tf_op jit(solution)/shard_map/ppermute | solution.py:390
  92.9 5.5 %shard_map.118 = (bf16[128,2048]{1,0:T(8,128)(2,1)S(1)}, bf16[128,2048]{1,0:T(8,128)(2,1)S(1)}, bf16[256,2048]{1,0:T(8,128)(2,1)S(1)}) custom-call(s32[1]{0:T(128)} %bitcast.15.mine_ref, bf16[16,512]{1,0:T(8,128)(2,1)S(1)} %get-tuple-element.62.quad_ref, bf16[128,2048]{1,0:T(8,128)(2,1)} %get-tuple-element.61.refs_0_, ...), custom_call_target="tpu_custom_call" | custom-call | flops 3019898880 | bytes 13631488 | tf_op jit(solution)/shard_map/pallas_call | solution.py:293
  102.0 1.5 collective-permute-start.24
  105.1 5.4 %shard_map.120 = (bf16[128,2048]{1,0:T(8,128)(2,1)S(1)}, bf16[128,2048]{1,0:T(8,128)(2,1)S(1)}, bf16[256,2048]{1,0:T(8,128)(2,1)S(1)}) custom-call(s32[1]{0:T(128)} %bitcast.15.mine_ref, bf16[16,512]{1,0:T(8,128)(2,1)S(1)} %get-tuple-element.71.quad_ref, bf16[128,2048]{1,0:T(8,128)(2,1)} %get-tuple-element.65.refs_0_, ...), custom_call_target="tpu_custom_call" | custom-call | flops 3019898880 | bytes 13631488 | tf_op jit(solution)/shard_map/pallas_call | solution.py:293
  110.6 5.2 %collective-permute-done.24.refs_0_ = bf16[128,2048]{1,0:T(8,128)(2,1)S(1)} collective-permute-done((bf16[128,2048]{1,0:T(8,128)(2,1)S(1)}, bf16[128,2048]{1,0:T(8,128)(2,1)S(1)}, u32[]{:S(2)}, u32[]{:S(2)}) %collective-permute-start.24) | collective-permute-done | bytes 524320 | tf_op jit(solution)/shard_map/ppermute | solution.py:390
  116.4 1.5 collective-permute-start.29
  119.9 4.3 %shard_map.114 = (bf16[128,2048]{1,0:T(8,128)(2,1)S(1)}, bf16[128,2048]{1,0:T(8,128)(2,1)S(1)}, bf16[256,2048]{1,0:T(8,128)(2,1)S(1)}) custom-call(s32[1]{0:T(128)} %bitcast.15.mine_ref, bf16[16,512]{1,0:T(8,128)(2,1)S(1)} %copy-done.6, bf16[128,2048]{1,0:T(8,128)(2,1)S(1)} %copy-done.5, bf16[128,2048]{1,0:T(8,128)(2,1)S(1)} %collective-permute-done.6.refs_1_, ...), custom_call_target="tpu_custom_call" | custom-call | flops 3019898880 | bytes 13631488 | tf_op jit(solution)/shard_map/pallas_call | solution.py:293
  124.4 6.2 %collective-permute-done.29.refs_0_ = bf16[128,2048]{1,0:T(8,128)(2,1)S(1)} collective-permute-done((bf16[128,2048]{1,0:T(8,128)(2,1)S(1)}, bf16[128,2048]{1,0:T(8,128)(2,1)S(1)}, u32[]{:S(2)}, u32[]{:S(2)}) %collective-permute-start.29) | collective-permute-done | bytes 524320 | tf_op jit(solution)/shard_map/ppermute | solution.py:390
  130.6 2.6 %collective-permute-done.30.refs_1_ = bf16[128,2048]{1,0:T(8,128)(2,1)S(1)} collective-permute-done((bf16[128,2048]{1,0:T(8,128)(2,1)S(1)}, bf16[128,2048]{1,0:T(8,128)(2,1)S(1)}, u32[]{:S(2)}, u32[]{:S(2)}) %collective-permute-start.30) | collective-permute-done | bytes 524320 | tf_op jit(solution)/shard_map/ppermute | solution.py:390
  136.1 11.5 %collective-permute-done.33.refs_0_ = bf16[128,2048]{1,0:T(8,128)(2,1)S(1)} collective-permute-done((bf16[128,2048]{1,0:T(8,128)(2,1)S(1)}, bf16[128,2048]{1,0:T(8,128)(2,1)S(1)}, u32[]{:S(2)}, u32[]{:S(2)}) %collective-permute-start.33) | collective-permute-done | bytes 524320 | tf_op jit(solution)/shard_map/ppermute | solution.py:390
  147.6 1.6 collective-permute-done.34.refs_1_
  150.3 1.5 collective-permute-start.35
  151.8 11.9 %collective-permute-done.36 = bf16[128,2048]{1,0:T(8,128)(2,1)S(1)} collective-permute-done((bf16[128,2048]{1,0:T(8,128)(2,1)S(1)}, bf16[128,2048]{1,0:T(8,128)(2,1)S(1)}, u32[]{:S(2)}, u32[]{:S(2)}) %collective-permute-start.36) | collective-permute-done | bytes 524320 | tf_op jit(solution)/shard_map/ppermute | solution.py:390
  (98 shorter events, 27.9 us)
Async XLA Ops:
  0.0 15.0 %collective-permute-start.3 = (bf16[512,2048]{1,0:T(8,128)(2,1)}, bf16[512,2048]{1,0:T(8,128)(2,1)S(1)}, u32[]{:S(2)}, u32[]{:S(2)}) collective-permute-start(bf16[512,2048]{1,0:T(8,128)(2,1)} %refs_4_.1), channel_id=1, source_target_pairs={{0,4},{4,0},{8,12},{12,8},{1,5},{5,1},{9,13},{13,9},{2,6},{6,2},{1... | collective-permute-start | bytes 6291464 | tf_op jit(solution)/shard_map/ppermute | solution.py:361
  2.3 12.7 %collective-permute-start.4 = (bf16[128,1024]{1,0:T(8,128)(2,1)}, bf16[128,1024]{1,0:T(8,128)(2,1)S(1)}, u32[]{:S(2)}, u32[]{:S(2)}) collective-permute-start(bf16[128,1024]{1,0:T(8,128)(2,1)} %get-tuple-element.52), channel_id=1, source_target_pairs={{0,8},{4,12},{8,0},{12,4},{1,9},{5,13},{9,1},{13,5},{2,10},{6,14},... | collective-permute-start | bytes 786440 | tf_op jit(solution)/shard_map/ppermute | solution.py:354
  5.1 8.7 %collective-permute-start.1 = (bf16[144,256]{1,0:T(8,128)(2,1)}, bf16[144,256]{1,0:T(8,128)(2,1)S(1)}, u32[]{:S(2)}, u32[]{:S(2)}) collective-permute-start(bf16[144,256]{1,0:T(8,128)(2,1)} %get-tuple-element.50), channel_id=1, source_target_pairs={{0,8},{4,12},{8,0},{12,4},{1,9},{5,13},{9,1},{13,5},{2,10},{6,14},... | collective-permute-start | bytes 221192 | tf_op jit(solution)/shard_map/ppermute | solution.py:358
  5.4 9.6 %collective-permute-start.2 = (bf16[144,256]{1,0:T(8,128)(2,1)}, bf16[144,256]{1,0:T(8,128)(2,1)S(1)}, u32[]{:S(2)}, u32[]{:S(2)}) collective-permute-start(bf16[144,256]{1,0:T(8,128)(2,1)} %get-tuple-element.50), channel_id=1, source_target_pairs={{0,12},{4,8},{8,4},{12,0},{1,13},{5,9},{9,5},{13,1},{2,14},{6,10},... | collective-permute-start | bytes 221192 | tf_op jit(solution)/shard_map/ppermute | solution.py:359
  22.7 14.3 %collective-permute-start.5 = (bf16[128,2048]{1,0:T(8,128)(2,1)}, bf16[128,2048]{1,0:T(8,128)(2,1)}, u32[]{:S(2)}, u32[]{:S(2)}) collective-permute-start(bf16[128,2048]{1,0:T(8,128)(2,1)} %get-tuple-element.53), channel_id=1, source_target_pairs={{0,8},{4,12},{8,0},{12,4},{1,9},{5,13},{9,1},{13,5},{2,10},{6,14},... | collective-permute-start | bytes 1572872 | tf_op jit(solution)/shard_map/ppermute | solution.py:370
  40.6 16.1 %collective-permute-start.7 = (bf16[128,2048]{1,0:T(8,128)(2,1)}, bf16[128,2048]{1,0:T(8,128)(2,1)S(1)}, u32[]{:S(2)}, u32[]{:S(2)}) collective-permute-start(bf16[128,2048]{1,0:T(8,128)(2,1)} %get-tuple-element.56.refs_0_), channel_id=1, source_target_pairs={{0,8},{4,12},{8,0},{12,4},{1,9},{5,13},{9,1},{13,5},{2,10},{6,14},... | collective-permute-start | bytes 1572872 | tf_op jit(solution)/shard_map/ppermute | solution.py:390
  42.2 14.4 %collective-permute-start.8 = (bf16[128,2048]{1,0:T(8,128)(2,1)}, bf16[128,2048]{1,0:T(8,128)(2,1)}, u32[]{:S(2)}, u32[]{:S(2)}) collective-permute-start(bf16[128,2048]{1,0:T(8,128)(2,1)} %get-tuple-element.56.refs_0_), channel_id=1, source_target_pairs={{0,1},{1,3},{3,2},{2,0},{4,5},{5,7},{7,6},{6,4},{8,9},{9,11},{11,1... | collective-permute-start | bytes 1572872 | tf_op jit(solution)/shard_map/ppermute | solution.py:390
  43.8 12.9 %collective-permute-start.9 = (bf16[16,512]{1,0:T(8,128)(2,1)S(1)}, bf16[16,512]{1,0:T(8,128)(2,1)S(1)}, u32[]{:S(2)}, u32[]{:S(2)}) collective-permute-start(bf16[16,512]{1,0:T(8,128)(2,1)S(1)} %copy-done.6), channel_id=1, source_target_pairs={{0,1},{1,3},{3,2},{2,0},{4,5},{5,7},{7,6},{6,4},{8,9},{9,11},{11,1... | collective-permute-start | bytes 49160 | tf_op jit(solution)/shard_map/ppermute | solution.py:390
  57.5 13.9 %collective-permute-start.11 = (bf16[128,2048]{1,0:T(8,128)(2,1)}, bf16[128,2048]{1,0:T(8,128)(2,1)}, u32[]{:S(2)}, u32[]{:S(2)}) collective-permute-start(bf16[128,2048]{1,0:T(8,128)(2,1)} %get-tuple-element.59.refs_0_), channel_id=1, source_target_pairs={{0,8},{4,12},{8,0},{12,4},{1,9},{5,13},{9,1},{13,5},{2,10},{6,14},... | collective-permute-start | bytes 1572872 | tf_op jit(solution)/shard_map/ppermute | solution.py:390
  58.0 13.4 %collective-permute-start.12 = (bf16[128,2048]{1,0:T(8,128)(2,1)}, bf16[128,2048]{1,0:T(8,128)(2,1)}, u32[]{:S(2)}, u32[]{:S(2)}) collective-permute-start(bf16[128,2048]{1,0:T(8,128)(2,1)} %get-tuple-element.59.refs_0_), channel_id=1, source_target_pairs={{0,1},{1,3},{3,2},{2,0},{4,5},{5,7},{7,6},{6,4},{8,9},{9,11},{11,1... | collective-permute-start | bytes 1572872 | tf_op jit(solution)/shard_map/ppermute | solution.py:390
  58.8 12.6 %collective-permute-start.13 = (bf16[16,512]{1,0:T(8,128)(2,1)S(1)}, bf16[16,512]{1,0:T(8,128)(2,1)S(1)}, u32[]{:S(2)}, u32[]{:S(2)}) collective-permute-start(bf16[16,512]{1,0:T(8,128)(2,1)S(1)} %get-tuple-element.60.quad_ref), channel_id=1, source_target_pairs={{0,1},{1,3},{3,2},{2,0},{4,5},{5,7},{7,6},{6,4},{8,9},{9,11},{11,1... | collective-permute-start | bytes 49160 | tf_op jit(solution)/shard_map/ppermute | solution.py:390
  62.2 15.0 %collective-permute-start.17 = (bf16[128,2048]{1,0:T(8,128)(2,1)}, bf16[128,2048]{1,0:T(8,128)(2,1)}, u32[]{:S(2)}, u32[]{:S(2)}) collective-permute-start(bf16[128,2048]{1,0:T(8,128)(2,1)} %get-tuple-element.59.refs_0_), channel_id=1, source_target_pairs={{0,4},{4,0},{8,12},{12,8},{1,5},{5,1},{9,13},{13,9},{2,6},{6,2},{1... | collective-permute-start | bytes 1572872 | tf_op jit(solution)/shard_map/ppermute | solution.py:390
  71.4 5.8 %collective-permute-start.18 = (bf16[128,2048]{1,0:T(8,128)(2,1)}, bf16[128,2048]{1,0:T(8,128)(2,1)}, u32[]{:S(2)}, u32[]{:S(2)}) collective-permute-start(bf16[128,2048]{1,0:T(8,128)(2,1)} %get-tuple-element.63.refs_2_), channel_id=1, source_target_pairs={{0,4},{4,0},{8,12},{12,8},{1,5},{5,1},{9,13},{13,9},{2,6},{6,2},{1... | collective-permute-start | bytes 1572872 | tf_op jit(solution)/shard_map/ppermute | solution.py:390
  71.4 17.0 %collective-permute-start.14 = (bf16[128,2048]{1,0:T(8,128)(2,1)}, bf16[128,2048]{1,0:T(8,128)(2,1)}, u32[]{:S(2)}, u32[]{:S(2)}) collective-permute-start(bf16[128,2048]{1,0:T(8,128)(2,1)} %get-tuple-element.61.refs_0_), channel_id=1, source_target_pairs={{0,8},{4,12},{8,0},{12,4},{1,9},{5,13},{9,1},{13,5},{2,10},{6,14},... | collective-permute-start | bytes 1572872 | tf_op jit(solution)/shard_map/ppermute | solution.py:390
  73.0 15.5 %collective-permute-start.15 = (bf16[128,2048]{1,0:T(8,128)(2,1)}, bf16[128,2048]{1,0:T(8,128)(2,1)}, u32[]{:S(2)}, u32[]{:S(2)}) collective-permute-start(bf16[128,2048]{1,0:T(8,128)(2,1)} %get-tuple-element.61.refs_0_), channel_id=1, source_target_pairs={{0,1},{1,3},{3,2},{2,0},{4,5},{5,7},{7,6},{6,4},{8,9},{9,11},{11,1... | collective-permute-start | bytes 1572872 | tf_op jit(solution)/shard_map/ppermute | solution.py:390
  73.7 14.8 %collective-permute-start.16 = (bf16[16,512]{1,0:T(8,128)(2,1)S(1)}, bf16[16,512]{1,0:T(8,128)(2,1)S(1)}, u32[]{:S(2)}, u32[]{:S(2)}) collective-permute-start(bf16[16,512]{1,0:T(8,128)(2,1)S(1)} %get-tuple-element.62.quad_ref), channel_id=1, source_target_pairs={{0,1},{1,3},{3,2},{2,0},{4,5},{5,7},{7,6},{6,4},{8,9},{9,11},{11,1... | collective-permute-start | bytes 49160 | tf_op jit(solution)/shard_map/ppermute | solution.py:390
  88.5 10.0 %collective-permute-start.23 = (bf16[256,2048]{1,0:T(8,128)(2,1)S(1)}, bf16[256,2048]{1,0:T(8,128)(2,1)S(1)}, u32[]{:S(2)}, u32[]{:S(2)}) collective-permute-start(bf16[256,2048]{1,0:T(8,128)(2,1)S(1)} %get-tuple-element.69), channel_id=1, source_target_pairs={{0,4},{4,0},{8,12},{12,8},{1,5},{5,1},{9,13},{13,9},{2,6},{6,2},{1... | collective-permute-start | bytes 3145736 | tf_op jit(solution)/shard_map/ppermute | solution.py:390
  88.5 3.8 %collective-permute-start.21 = (bf16[128,2048]{1,0:T(8,128)(2,1)}, bf16[128,2048]{1,0:T(8,128)(2,1)S(1)}, u32[]{:S(2)}, u32[]{:S(2)}) collective-permute-start(bf16[128,2048]{1,0:T(8,128)(2,1)} %get-tuple-element.61.refs_0_), channel_id=1, source_target_pairs={{0,4},{4,0},{8,12},{12,8},{1,5},{5,1},{9,13},{13,9},{2,6},{6,2},{1... | collective-permute-start | bytes 1572872 | tf_op jit(solution)/shard_map/ppermute | solution.py:390
  89.0 3.9 %collective-permute-start.22 = (bf16[128,2048]{1,0:T(8,128)(2,1)}, bf16[128,2048]{1,0:T(8,128)(2,1)S(1)}, u32[]{:S(2)}, u32[]{:S(2)}) collective-permute-start(bf16[128,2048]{1,0:T(8,128)(2,1)} %get-tuple-element.66.refs_2_), channel_id=1, source_target_pairs={{0,4},{4,0},{8,12},{12,8},{1,5},{5,1},{9,13},{13,9},{2,6},{6,2},{1... | collective-permute-start | bytes 1572872 | tf_op jit(solution)/shard_map/ppermute | solution.py:390
  91.1 8.7 %collective-permute-start.19 = (bf16[128,1024]{1,0:T(8,128)(2,1)S(1)}, bf16[128,1024]{1,0:T(8,128)(2,1)S(1)}, u32[]{:S(2)}, u32[]{:S(2)}) collective-permute-start(bf16[128,1024]{1,0:T(8,128)(2,1)S(1)} %slice.30), channel_id=1, source_target_pairs={{0,8},{4,12},{8,0},{12,4},{1,9},{5,13},{9,1},{13,5},{2,10},{6,14},... | collective-permute-start | bytes 786440 | tf_op jit(solution)/shard_map/ppermute | solution.py:390
  91.7 9.3 %collective-permute-start.20 = (bf16[128,1024]{1,0:T(8,128)(2,1)S(1)}, bf16[128,1024]{1,0:T(8,128)(2,1)S(1)}, u32[]{:S(2)}, u32[]{:S(2)}) collective-permute-start(bf16[128,1024]{1,0:T(8,128)(2,1)S(1)} %slice.31), channel_id=1, source_target_pairs={{0,1},{1,3},{3,2},{2,0},{4,5},{5,7},{7,6},{6,4},{8,9},{9,11},{11,1... | collective-permute-start | bytes 786440 | tf_op jit(solution)/shard_map/ppermute | solution.py:390
  100.9 9.6 %collective-permute-start.28 = (bf16[256,2048]{1,0:T(8,128)(2,1)S(1)}, bf16[256,2048]{1,0:T(8,128)(2,1)S(1)}, u32[]{:S(2)}, u32[]{:S(2)}) collective-permute-start(bf16[256,2048]{1,0:T(8,128)(2,1)S(1)} %get-tuple-element.76), channel_id=1, source_target_pairs={{0,4},{4,0},{8,12},{12,8},{1,5},{5,1},{9,13},{13,9},{2,6},{6,2},{1... | collective-permute-start | bytes 3145736 | tf_op jit(solution)/shard_map/ppermute | solution.py:390
  100.9 4.0 %collective-permute-start.25 = (bf16[128,2048]{1,0:T(8,128)(2,1)}, bf16[128,2048]{1,0:T(8,128)(2,1)S(1)}, u32[]{:S(2)}, u32[]{:S(2)}) collective-permute-start(bf16[128,2048]{1,0:T(8,128)(2,1)} %get-tuple-element.65.refs_0_), channel_id=1, source_target_pairs={{0,4},{4,0},{8,12},{12,8},{1,5},{5,1},{9,13},{13,9},{2,6},{6,2},{1... | collective-permute-start | bytes 1572872 | tf_op jit(solution)/shard_map/ppermute | solution.py:390
  101.4 3.6 %collective-permute-start.27 = (bf16[128,1024]{1,0:T(8,128)(2,1)S(1)}, bf16[128,1024]{1,0:T(8,128)(2,1)S(1)}, u32[]{:S(2)}, u32[]{:S(2)}) collective-permute-start(bf16[128,1024]{1,0:T(8,128)(2,1)S(1)} %get-tuple-element.73.refs_3_), channel_id=1, source_target_pairs={{0,4},{4,0},{8,12},{12,8},{1,5},{5,1},{9,13},{13,9},{2,6},{6,2},{1... | collective-permute-start | bytes 786440 | tf_op jit(solution)/shard_map/ppermute | solution.py:390
  102.0 13.8 %collective-permute-start.24 = (bf16[128,2048]{1,0:T(8,128)(2,1)S(1)}, bf16[128,2048]{1,0:T(8,128)(2,1)S(1)}, u32[]{:S(2)}, u32[]{:S(2)}) collective-permute-start(bf16[128,2048]{1,0:T(8,128)(2,1)S(1)} %get-tuple-element.70), channel_id=1, source_target_pairs={{0,8},{4,12},{8,0},{12,4},{1,9},{5,13},{9,1},{13,5},{2,10},{6,14},... | collective-permute-start | bytes 1572872 | tf_op jit(solution)/shard_map/ppermute | solution.py:390
  115.8 8.5 %collective-permute-start.31 = (bf16[256,2048]{1,0:T(8,128)(2,1)S(1)}, bf16[256,2048]{1,0:T(8,128)(2,1)S(1)}, u32[]{:S(2)}, u32[]{:S(2)}) collective-permute-start(bf16[256,2048]{1,0:T(8,128)(2,1)S(1)} %get-tuple-element.82), channel_id=1, source_target_pairs={{0,4},{4,0},{8,12},{12,8},{1,5},{5,1},{9,13},{13,9},{2,6},{6,2},{1... | collective-permute-start | bytes 3145736 | tf_op jit(solution)/shard_map/ppermute | solution.py:390
  116.4 14.3 %collective-permute-start.29 = (bf16[128,2048]{1,0:T(8,128)(2,1)S(1)}, bf16[128,2048]{1,0:T(8,128)(2,1)S(1)}, u32[]{:S(2)}, u32[]{:S(2)}) collective-permute-start(bf16[128,2048]{1,0:T(8,128)(2,1)S(1)} %get-tuple-element.77), channel_id=1, source_target_pairs={{0,8},{4,12},{8,0},{12,4},{1,9},{5,13},{9,1},{13,5},{2,10},{6,14},... | collective-permute-start | bytes 1572872 | tf_op jit(solution)/shard_map/ppermute | solution.py:390
  118.1 15.2 %collective-permute-start.30 = (bf16[128,2048]{1,0:T(8,128)(2,1)S(1)}, bf16[128,2048]{1,0:T(8,128)(2,1)S(1)}, u32[]{:S(2)}, u32[]{:S(2)}) collective-permute-start(bf16[128,2048]{1,0:T(8,128)(2,1)S(1)} %add_convert_fusion.5), channel_id=1, source_target_pairs={{0,1},{1,3},{3,2},{2,0},{4,5},{5,7},{7,6},{6,4},{8,9},{9,11},{11,1... | collective-permute-start | bytes 1572872 | tf_op jit(solution)/shard_map/ppermute | solution.py:390
  133.3 14.3 %collective-permute-start.33 = (bf16[128,2048]{1,0:T(8,128)(2,1)S(1)}, bf16[128,2048]{1,0:T(8,128)(2,1)S(1)}, u32[]{:S(2)}, u32[]{:S(2)}) collective-permute-start(bf16[128,2048]{1,0:T(8,128)(2,1)S(1)} %get-tuple-element.84), channel_id=1, source_target_pairs={{0,8},{4,12},{8,0},{12,4},{1,9},{5,13},{9,1},{13,5},{2,10},{6,14},... | collective-permute-start | bytes 1572872 | tf_op jit(solution)/shard_map/ppermute | solution.py:390
  134.2 15.0 %collective-permute-start.34 = (bf16[128,2048]{1,0:T(8,128)(2,1)S(1)}, bf16[128,2048]{1,0:T(8,128)(2,1)S(1)}, u32[]{:S(2)}, u32[]{:S(2)}) collective-permute-start(bf16[128,2048]{1,0:T(8,128)(2,1)S(1)} %add_convert_fusion.3), channel_id=1, source_target_pairs={{0,1},{1,3},{3,2},{2,0},{4,5},{5,7},{7,6},{6,4},{8,9},{9,11},{11,1... | collective-permute-start | bytes 1572872 | tf_op jit(solution)/shard_map/ppermute | solution.py:390
  149.5 14.2 %collective-permute-start.36 = (bf16[128,2048]{1,0:T(8,128)(2,1)S(1)}, bf16[128,2048]{1,0:T(8,128)(2,1)S(1)}, u32[]{:S(2)}, u32[]{:S(2)}) collective-permute-start(bf16[128,2048]{1,0:T(8,128)(2,1)S(1)} %add_convert_fusion.1), channel_id=1, source_target_pairs={{0,1},{1,3},{3,2},{2,0},{4,5},{5,7},{7,6},{6,4},{8,9},{9,11},{11,1... | collective-permute-start | bytes 1572872 | tf_op jit(solution)/shard_map/ppermute | solution.py:390
  150.3 13.4 %collective-permute-start.35 = (bf16[128,2048]{1,0:T(8,128)(2,1)S(1)}, bf16[128,2048]{1,0:T(8,128)(2,1)S(1)}, u32[]{:S(2)}, u32[]{:S(2)}) collective-permute-start(bf16[128,2048]{1,0:T(8,128)(2,1)S(1)} %get-tuple-element.89), channel_id=1, source_target_pairs={{0,8},{4,12},{8,0},{12,4},{1,9},{5,13},{9,1},{13,5},{2,10},{6,14},... | collective-permute-start | bytes 1572872 | tf_op jit(solution)/shard_map/ppermute | solution.py:390
  (19 other events, 161.4 us)

commit v9 on v8

--- a/solution.py
+++ b/solution.py
@@ -128,7 +128,7 @@
         )
         scores = jnp.where(allowed, scores, -1e30)
         weights = jnp.exp(scores - jnp.max(scores, axis=1, keepdims=True))
-        probs = (weights / jnp.sum(weights, axis=1, keepdims=True)).astype(jnp.bfloat16)
+        probs = (weights * (1.0 / jnp.sum(weights, axis=1, keepdims=True))).astype(jnp.bfloat16)
         heads[:, head * head_size : (head + 1) * head_size] = jnp.dot(
             probs, value_block, preferred_element_type=jnp.float32
         ).astype(jnp.bfloat16)
@@ -176,7 +176,8 @@
     )(place, queries, *kv_parts, *bases, w_own, w_other)
 
 
-def norm_kernel(own_ref, other_ref, gain_ref, hidden_ref, normed_ref):
+def norm_kernel(own_ref, other_ref, gain_ref, *refs):
+    hidden_ref, normed_ref = refs[-2:]
     hidden = (own_ref[...] + other_ref[...].astype(jnp.float32)).astype(jnp.bfloat16)
     hidden_ref[...] = hidden
     wide = hidden.astype(jnp.float32)
@@ -187,28 +188,25 @@
     ).astype(jnp.bfloat16)
 
 
-def add_and_norm(own, other, gain):
-    tokens, width = own.shape
-    rows = tokens // 4
-    block = pl.BlockSpec((rows, width), lambda step: (step, 0))
+def add_and_norm(own, other, gain, present):
     return pl.pallas_call(
         norm_kernel,
-        grid=(4,),
-        in_specs=[block, block, pl.BlockSpec((1, width), lambda step: (0, 0))],
-        out_specs=[block, block],
+        in_specs=[pl.BlockSpec(memory_space=pltpu.VMEM)] * 3
+        + [pl.BlockSpec(memory_space=pl.ANY)] * len(present),
+        out_specs=[pl.BlockSpec(memory_space=pltpu.VMEM)] * 2,
         out_shape=[jax.ShapeDtypeStruct(own.shape, jnp.bfloat16)] * 2,
         compiler_params=pltpu.CompilerParams(vmem_limit_bytes=60 * MIB),
-    )(own, other, gain)
+    )(own, other, gain, *present)
 
 
 def pass_kernel(*refs):
     del refs
 
 
-def meet(*arrays):
+def meet(arrays, present):
     return pl.pallas_call(
         pass_kernel,
-        in_specs=[pl.BlockSpec(memory_space=pl.ANY)] * len(arrays),
+        in_specs=[pl.BlockSpec(memory_space=pl.ANY)] * (len(arrays) + len(present)),
         out_specs=[pl.BlockSpec(memory_space=pl.ANY)] * len(arrays),
         out_shape=[jax.ShapeDtypeStruct(array.shape, array.dtype) for array in arrays],
         input_output_aliases={index: index for index in range(len(arrays))},
@@ -219,15 +217,15 @@
     del refs
 
 
-def meet(*arrays):
+def meet(arrays, present):
     return pl.pallas_call(
         pass_kernel,
-        in_specs=[pl.BlockSpec(memory_space=pl.ANY)] * len(arrays),
+        in_specs=[pl.BlockSpec(memory_space=pl.ANY)] * (len(arrays) + len(present)),
         out_specs=[pl.BlockSpec(memory_space=pl.ANY)] * len(arrays),
         out_shape=[jax.ShapeDtypeStruct(array.shape, array.dtype) for array in arrays],
         input_output_aliases={index: index for index in range(len(arrays))},
         compiler_params=pltpu.CompilerParams(vmem_limit_bytes=MIB),
-    )(*arrays)
+    )(*arrays, *present)
 
 
 def experts_kernel(mine_ref, quad_ref, *refs, cap, pieces):
@@ -377,12 +375,14 @@
         w_other,
         jnp.float32,
     )
-    hidden, normed = add_and_norm(projected, projected_across, norm_gain[None])
+    quads = [lax.ppermute(quad, "sub", ring(steps)) for steps in range(1, n_sub)]
+    hidden, normed = add_and_norm(projected, projected_across, norm_gain[None], quads)
 
     last = n_sub - 1
     mine = place * n_sub + lax.axis_index("sub")
 
     held = {("row", 0): normed, ("quad", 0): quad}
+    held.update({("quad", steps): moved for steps, moved in enumerate(quads, 1)})
     half = normed.shape[1] // 2
     ways = {"across": ("seq", across), "twin": ("seq", twin), "on": ("sub", ring(1))}
 
@@ -421,7 +421,6 @@
         if step < last:
             now["across", step] = move(held["row", step], "across")
             now["row", step + 1] = move(held["row", step], "on")
-            now["quad", step + 1] = move(held["quad", step], "on")
         if step == last:
             now["half", 0] = move(held["row", step][:, :half], "across")
             now["half", 1] = move(held["across", step - 1][:, half:], "on")
@@ -450,7 +449,8 @@
         if 1 <= step <= last or turn == n_sub + 3:
             now["away", step] = twin_sum(step)
         if turn < n_sub + 4:
-            now = dict(zip(now.keys(), meet(*now.values())))
+            weights = [expert_gate[0], expert_up[0], expert_down[0]] if turn == 1 else []
+            now = dict(zip(now.keys(), meet(list(now.values()), weights)))
         held.update(now)
     total = hidden.astype(jnp.float32) + sum_of(0, [held["sum", last]])
     return total.astype(jnp.bfloat16)[None]

time: 165 us -> 167 us (1.012)
  starting transfers between devices: 33.7 us -> 28 us
  local copies, waits for them, and re-layouts: 10.5 us -> 14.9 us
  waiting for transfers between devices: 79.7 us -> 83.8 us
    ppermute x31 -> x28, starting transfers between devices: 27.3 us -> 15.9 us  [move(): return lax.ppermute(array, *ways[way])]
    ppermute x31 -> x28, waiting for transfers between devices: 66.6 us -> 76.2 us  [move(): return lax.ppermute(array, *ways[way])]
    ppermute x0 -> x3, starting transfers between devices: none -> 5.63 us  [gathered_plan(): lax.ppermute(quad, 'sub', ring(steps))]
    ppermute x1, waiting for transfers between devices: 5.46 us -> 0.01 us  [gathered_plan(): projected_across = lax.ppermute(sent, 'seq', across)]
    unnamed x28 -> x48, local copies, waits for them, and re-layouts: 6.66 us -> 11 us
  transfers between devices with their start and end apart: 37 -> 37, of which waited for: 20 -> 23; matrix products, arithmetic and copies ran while one was open for 3% -> 3% of each run, Pallas kernels for 18% -> 17%
where the time goes in v9:
time: 167 us
  waiting for transfers between devices  83.8 us (50%)
  Pallas kernels  37.2 us (22%)
  starting transfers between devices  28 us (17%)
  local copies, waits for them, and re-layouts  14.9 us (9%)
  other arithmetic  2.63 us (2%)
    ppermute x28, waiting for transfers between devices, move(): return lax.ppermute(array, *ways[way])  76.2 us
    pallas_call x4, Pallas kernels, experts_on_rows(): pl.pallas_call(functools.partial(experts_kernel, cap=cap, pieces=pieces),...  21 us
    ppermute x28, starting transfers between devices, move(): return lax.ppermute(array, *ways[way])  15.9 us
    pallas_call x2, Pallas kernels, attend(): pl.pallas_call(functools.partial(attend_kernel, scale=1.0 / HD ** 0.5), i...  11.7 us
    unnamed x48, local copies, waits for them, and re-layouts  11 us
    ppermute x1, waiting for transfers between devices, gathered_plan(): lax.ppermute(kv_away, 'seq', across)  6.4 us
    ppermute x3, starting transfers between devices, gathered_plan(): lax.ppermute(quad, 'sub', ring(steps))  5.63 us
  transfers between devices with their start and end apart: 37, of which 23 were waited for; matrix products, arithmetic and copies ran while one was open for 3% of the time, Pallas kernels for 17%

profile of v9, /device:TPU:0, one launch (start us, length us, event | category | flops | bytes accessed | tf_op | source)
XLA Modules:
  0.0 166.8 jit_solution(5334750129153644570)
XLA Ops:
  0.5 1.9 %shard_map.109 = (bf16[128,1024]{1,0:T(8,128)(2,1)}, bf16[144,256]{1,0:T(8,128)(2,1)}, bf16[144,256]{1,0:T(8,128)(2,1)}) custom-call(s32[1]{0:T(128)} %bitcast.7.chip_ref, bf16[128,2048]{1,0:T(8,128)(2,1)} %bitcast.38, bf16[128,256]{1,0:T(8,128)(2,1)} %bitcast.41, bf16[128,256]{1,0:T(8,128)(2,1)} %bitcast.42, s32[8,128]{1,0:T(8,128)} %bitcast.43, ...), custom_call_target="tpu_custom_call" | custom-call | tf_op jit(solution)/shard_map/pallas_call | solution.py:87
  2.3 2.5 %collective-permute-start.4 = (bf16[128,1024]{1,0:T(8,128)(2,1)}, bf16[128,1024]{1,0:T(8,128)(2,1)S(1)}, u32[]{:S(2)}, u32[]{:S(2)}) collective-permute-start(bf16[128,1024]{1,0:T(8,128)(2,1)} %get-tuple-element.49), channel_id=1, source_target_pairs={{0,8},{4,12},{8,0},{12,4},{1,9},{5,13},{9,1},{13,5},{2,10},{6,14},... | collective-permute-start | bytes 786440 | tf_op jit(solution)/shard_map/ppermute | solution.py:352
  7.4 6.4 %collective-permute-done.1.refs_2_ = bf16[144,256]{1,0:T(8,128)(2,1)S(1)} collective-permute-done((bf16[144,256]{1,0:T(8,128)(2,1)}, bf16[144,256]{1,0:T(8,128)(2,1)S(1)}, u32[]{:S(2)}, u32[]{:S(2)}) %collective-permute-start.1) | collective-permute-done | bytes 73760 | tf_op jit(solution)/shard_map/ppermute | solution.py:356
  17.1 5.6 %shard_map.111 = (bf16[128,2048]{1,0:T(8,128)(2,1)}, bf16[16,512]{1,0:T(8,128)(2,1)}) custom-call(s32[7]{0:T(128)} %stack.38.place_ref, bf16[128,1024]{1,0:T(8,128)(2,1)} %copy-done.22, bf16[144,256]{1,0:T(8,128)(2,1)} %get-tuple-element.46.refs_0_, bf16[144,256]{1,0:T(8,128)(2,1)} %copy-done.19, bf16[144,256]{1,0:T(8,128)(2,1)} %copy-done.20, ...), custom_call_target="tpu_custom_call" | custom-call | flops 805306368 | bytes 5242880 | tf_op jit(solution)/shard_map/pallas_call | solution.py:152
  22.6 1.6 collective-permute-start.5
  25.5 1.6 collective-permute-start.6
  27.1 2.5 %collective-permute-start.7 = (bf16[16,512]{1,0:T(8,128)(2,1)}, bf16[16,512]{1,0:T(8,128)(2,1)S(1)}, u32[]{:S(2)}, u32[]{:S(2)}) collective-permute-start(bf16[16,512]{1,0:T(8,128)(2,1)} %get-tuple-element.51.quad_ref), channel_id=1, source_target_pairs={{0,3},{1,2},{3,0},{2,1},{4,7},{5,6},{7,4},{6,5},{8,11},{9,10},{11,... | collective-permute-start | bytes 49160 | tf_op jit(solution)/shard_map/ppermute | solution.py:378
  29.6 1.6 collective-permute-start.8
  31.2 6.2 %shard_map.110 = (f32[128,2048]{1,0:T(8,128)}, bf16[16,512]{1,0:T(8,128)(2,1)}) custom-call(s32[7]{0:T(128)} %stack.37.place_ref, bf16[128,2048]{1,0:T(8,128)(2,1)} %bitcast.39, bf16[144,256]{1,0:T(8,128)(2,1)} %get-tuple-element.46.refs_0_, bf16[144,256]{1,0:T(8,128)(2,1)} %copy-done.19, bf16[144,256]{1,0:T(8,128)(2,1)} %copy-done.20, ...), custom_call_target="tpu_custom_call" | custom-call | flops 805306368 | bytes 5242880 | tf_op jit(solution)/shard_map/pallas_call | solution.py:152
  38.0 2.5 %shard_map.112 = (bf16[128,2048]{1,0:T(8,128)(2,1)}, bf16[128,2048]{1,0:T(8,128)(2,1)}) custom-call(f32[128,2048]{1,0:T(8,128)} %get-tuple-element.48.own_ref, bf16[128,2048]{1,0:T(8,128)(2,1)} %collective-permute-done.5.other_ref, bf16[1,2048]{1,0:T(2,128)(2,1)} %broadcast_in_dim.6.gain_ref, bf16[16,512]{1,0:T(8,128)(2,1)} %copy-done.14, ...), custom_call_target="tpu_custom_call" | custom-call | tf_op jit(solution)/shard_map/pallas_call | solution.py:192
  41.1 1.6 collective-permute-start.11
  42.7 10.9 %collective-permute-done.10.refs_0_ = bf16[128,2048]{1,0:T(8,128)(2,1)S(1)} collective-permute-done((bf16[128,2048]{1,0:T(8,128)(2,1)}, bf16[128,2048]{1,0:T(8,128)(2,1)S(1)}, u32[]{:S(2)}, u32[]{:S(2)}) %collective-permute-start.10) | collective-permute-done | bytes 524320 | tf_op jit(solution)/shard_map/ppermute | solution.py:390
  53.6 1.7 collective-permute-done.11.refs_1_
  55.3 1.9 %copy-done.1 = bf16[1,2048,768]{2,1,0:T(8,128)(2,1)S(1)} copy-done((bf16[1,2048,768]{2,1,0:T(8,128)(2,1)S(1)}, bf16[1,2048,768]{2,1,0:T(8,128)(2,1)}, u32[]{:S(2)}) %copy-start.1) | copy-done | bytes 3145752
  57.2 1.9 %copy-done.4 = bf16[1,768,2048]{2,1,0:T(8,128)(2,1)S(1)} copy-done((bf16[1,768,2048]{2,1,0:T(8,128)(2,1)S(1)}, bf16[1,768,2048]{2,1,0:T(8,128)(2,1)}, u32[]{:S(2)}) %copy-start.4) | copy-done | bytes 3145752
  61.2 11.1 %collective-permute-done.13.refs_0_ = bf16[128,2048]{1,0:T(8,128)(2,1)} collective-permute-done((bf16[128,2048]{1,0:T(8,128)(2,1)}, bf16[128,2048]{1,0:T(8,128)(2,1)}, u32[]{:S(2)}, u32[]{:S(2)}) %collective-permute-start.13) | collective-permute-done | bytes 524320 | tf_op jit(solution)/shard_map/ppermute | solution.py:390
  75.9 1.9 %copy-done.2 = bf16[1,2048,768]{2,1,0:T(8,128)(2,1)S(1)} copy-done((bf16[1,2048,768]{2,1,0:T(8,128)(2,1)S(1)}, bf16[1,2048,768]{2,1,0:T(8,128)(2,1)}, u32[]{:S(2)}) %copy-start.2) | copy-done | bytes 3145752
  77.8 1.9 %copy-done.5 = bf16[1,768,2048]{2,1,0:T(8,128)(2,1)S(1)} copy-done((bf16[1,768,2048]{2,1,0:T(8,128)(2,1)S(1)}, bf16[1,768,2048]{2,1,0:T(8,128)(2,1)}, u32[]{:S(2)}) %copy-start.5) | copy-done | bytes 3145752
  79.7 5.8 %shard_map.116 = (bf16[128,2048]{1,0:T(8,128)(2,1)S(1)}, bf16[128,2048]{1,0:T(8,128)(2,1)S(1)}, bf16[256,2048]{1,0:T(8,128)(2,1)S(1)}) custom-call(s32[1]{0:T(128)} %bitcast.15.mine_ref, bf16[16,512]{1,0:T(8,128)(2,1)S(1)} %copy-done.15, bf16[128,2048]{1,0:T(8,128)(2,1)} %get-tuple-element.56.refs_0_, bf16[128,2048]{1,0:T(8,128)(2,1)} %collective-permute-done.17.refs_1_, ...), custom_call_target="tpu_custom_call" | custom-call | flops 3019898880 | bytes 13631488 | tf_op jit(solution)/shard_map/pallas_call | solution.py:291
  85.5 2.8 %collective-permute-done.15.refs_0_ = bf16[128,2048]{1,0:T(8,128)(2,1)} collective-permute-done((bf16[128,2048]{1,0:T(8,128)(2,1)}, bf16[128,2048]{1,0:T(8,128)(2,1)}, u32[]{:S(2)}, u32[]{:S(2)}) %collective-permute-start.15) | collective-permute-done | bytes 524320 | tf_op jit(solution)/shard_map/ppermute | solution.py:390
  88.3 1.9 %collective-permute-done.16.refs_1_ = bf16[128,2048]{1,0:T(8,128)(2,1)} collective-permute-done((bf16[128,2048]{1,0:T(8,128)(2,1)}, bf16[128,2048]{1,0:T(8,128)(2,1)}, u32[]{:S(2)}, u32[]{:S(2)}) %collective-permute-start.16) | collective-permute-done | bytes 524320 | tf_op jit(solution)/shard_map/ppermute | solution.py:390
  94.5 5.5 %shard_map.118 = (bf16[128,2048]{1,0:T(8,128)(2,1)S(1)}, bf16[128,2048]{1,0:T(8,128)(2,1)S(1)}, bf16[256,2048]{1,0:T(8,128)(2,1)S(1)}) custom-call(s32[1]{0:T(128)} %bitcast.15.mine_ref, bf16[16,512]{1,0:T(8,128)(2,1)S(1)} %copy-done.13, bf16[128,2048]{1,0:T(8,128)(2,1)} %get-tuple-element.57.refs_0_, bf16[128,2048]{1,0:T(8,128)(2,1)S(1)} %collective-permute-done.21.refs_1_, ...), custom_call_target="tpu_custom_call" | custom-call | flops 3019898880 | bytes 13631488 | tf_op jit(solution)/shard_map/pallas_call | solution.py:291
  105.1 1.7 %collective-permute-done.25.refs_1_ = bf16[128,2048]{1,0:T(8,128)(2,1)S(1)} collective-permute-done((bf16[128,2048]{1,0:T(8,128)(2,1)}, bf16[128,2048]{1,0:T(8,128)(2,1)S(1)}, u32[]{:S(2)}, u32[]{:S(2)}) %collective-permute-start.25) | collective-permute-done | bytes 524320 | tf_op jit(solution)/shard_map/ppermute | solution.py:390
  107.0 5.5 %shard_map.120 = (bf16[128,2048]{1,0:T(8,128)(2,1)S(1)}, bf16[128,2048]{1,0:T(8,128)(2,1)S(1)}, bf16[256,2048]{1,0:T(8,128)(2,1)S(1)}) custom-call(s32[1]{0:T(128)} %bitcast.15.mine_ref, bf16[16,512]{1,0:T(8,128)(2,1)S(1)} %copy-done.11, bf16[128,2048]{1,0:T(8,128)(2,1)} %get-tuple-element.60.refs_0_, bf16[128,2048]{1,0:T(8,128)(2,1)S(1)} %collective-permute-done.25.refs_1_, ...), custom_call_target="tpu_custom_call" | custom-call | flops 3019898880 | bytes 13631488 | tf_op jit(solution)/shard_map/pallas_call | solution.py:291
  112.6 5.0 %collective-permute-done.24.refs_0_ = bf16[128,2048]{1,0:T(8,128)(2,1)S(1)} collective-permute-done((bf16[128,2048]{1,0:T(8,128)(2,1)S(1)}, bf16[128,2048]{1,0:T(8,128)(2,1)S(1)}, u32[]{:S(2)}, u32[]{:S(2)}) %collective-permute-start.24) | collective-permute-done | bytes 524320 | tf_op jit(solution)/shard_map/ppermute | solution.py:390
  121.8 4.3 %shard_map.114 = (bf16[128,2048]{1,0:T(8,128)(2,1)S(1)}, bf16[128,2048]{1,0:T(8,128)(2,1)S(1)}, bf16[256,2048]{1,0:T(8,128)(2,1)S(1)}) custom-call(s32[1]{0:T(128)} %bitcast.15.mine_ref, bf16[16,512]{1,0:T(8,128)(2,1)S(1)} %copy-done.16, bf16[128,2048]{1,0:T(8,128)(2,1)S(1)} %copy-done.9, bf16[128,2048]{1,0:T(8,128)(2,1)S(1)} %collective-permute-done.9.refs_1_, ...), custom_call_target="tpu_custom_call" | custom-call | flops 3019898880 | bytes 13631488 | tf_op jit(solution)/shard_map/pallas_call | solution.py:291
  126.3 6.2 %collective-permute-done.29.refs_0_ = bf16[128,2048]{1,0:T(8,128)(2,1)S(1)} collective-permute-done((bf16[128,2048]{1,0:T(8,128)(2,1)S(1)}, bf16[128,2048]{1,0:T(8,128)(2,1)S(1)}, u32[]{:S(2)}, u32[]{:S(2)}) %collective-permute-start.29) | collective-permute-done | bytes 524320 | tf_op jit(solution)/shard_map/ppermute | solution.py:390
  132.5 2.4 %collective-permute-done.30.refs_1_ = bf16[128,2048]{1,0:T(8,128)(2,1)S(1)} collective-permute-done((bf16[128,2048]{1,0:T(8,128)(2,1)S(1)}, bf16[128,2048]{1,0:T(8,128)(2,1)S(1)}, u32[]{:S(2)}, u32[]{:S(2)}) %collective-permute-start.30) | collective-permute-done | bytes 524320 | tf_op jit(solution)/shard_map/ppermute | solution.py:390
  137.7 11.5 %collective-permute-done.33.refs_0_ = bf16[128,2048]{1,0:T(8,128)(2,1)S(1)} collective-permute-done((bf16[128,2048]{1,0:T(8,128)(2,1)S(1)}, bf16[128,2048]{1,0:T(8,128)(2,1)S(1)}, u32[]{:S(2)}, u32[]{:S(2)}) %collective-permute-start.33) | collective-permute-done | bytes 524320 | tf_op jit(solution)/shard_map/ppermute | solution.py:390
  149.2 1.8 %collective-permute-done.34.refs_1_ = bf16[128,2048]{1,0:T(8,128)(2,1)S(1)} collective-permute-done((bf16[128,2048]{1,0:T(8,128)(2,1)S(1)}, bf16[128,2048]{1,0:T(8,128)(2,1)S(1)}, u32[]{:S(2)}, u32[]{:S(2)}) %collective-permute-start.34) | collective-permute-done | bytes 524320 | tf_op jit(solution)/shard_map/ppermute | solution.py:390
  151.9 1.5 collective-permute-start.35
  153.4 12.1 %collective-permute-done.36 = bf16[128,2048]{1,0:T(8,128)(2,1)S(1)} collective-permute-done((bf16[128,2048]{1,0:T(8,128)(2,1)S(1)}, bf16[128,2048]{1,0:T(8,128)(2,1)S(1)}, u32[]{:S(2)}, u32[]{:S(2)}) %collective-permute-start.36) | collective-permute-done | bytes 524320 | tf_op jit(solution)/shard_map/ppermute | solution.py:390
  (118 shorter events, 33.4 us)
Async XLA Ops:
  0.0 15.0 %collective-permute-start.3 = (bf16[512,2048]{1,0:T(8,128)(2,1)}, bf16[512,2048]{1,0:T(8,128)(2,1)S(1)}, u32[]{:S(2)}, u32[]{:S(2)}) collective-permute-start(bf16[512,2048]{1,0:T(8,128)(2,1)} %refs_4_.1), channel_id=1, source_target_pairs={{0,4},{4,0},{8,12},{12,8},{1,5},{5,1},{9,13},{13,9},{2,6},{6,2},{1... | collective-permute-start | bytes 6291464 | tf_op jit(solution)/shard_map/ppermute | solution.py:359
  2.3 12.7 %collective-permute-start.4 = (bf16[128,1024]{1,0:T(8,128)(2,1)}, bf16[128,1024]{1,0:T(8,128)(2,1)S(1)}, u32[]{:S(2)}, u32[]{:S(2)}) collective-permute-start(bf16[128,1024]{1,0:T(8,128)(2,1)} %get-tuple-element.49), channel_id=1, source_target_pairs={{0,8},{4,12},{8,0},{12,4},{1,9},{5,13},{9,1},{13,5},{2,10},{6,14},... | collective-permute-start | bytes 786440 | tf_op jit(solution)/shard_map/ppermute | solution.py:352
  5.1 8.7 %collective-permute-start.1 = (bf16[144,256]{1,0:T(8,128)(2,1)}, bf16[144,256]{1,0:T(8,128)(2,1)S(1)}, u32[]{:S(2)}, u32[]{:S(2)}) collective-permute-start(bf16[144,256]{1,0:T(8,128)(2,1)} %get-tuple-element.47), channel_id=1, source_target_pairs={{0,8},{4,12},{8,0},{12,4},{1,9},{5,13},{9,1},{13,5},{2,10},{6,14},... | collective-permute-start | bytes 221192 | tf_op jit(solution)/shard_map/ppermute | solution.py:356
  5.4 9.6 %collective-permute-start.2 = (bf16[144,256]{1,0:T(8,128)(2,1)}, bf16[144,256]{1,0:T(8,128)(2,1)S(1)}, u32[]{:S(2)}, u32[]{:S(2)}) collective-permute-start(bf16[144,256]{1,0:T(8,128)(2,1)} %get-tuple-element.47), channel_id=1, source_target_pairs={{0,12},{4,8},{8,4},{12,0},{1,13},{5,9},{9,5},{13,1},{2,14},{6,10},... | collective-permute-start | bytes 221192 | tf_op jit(solution)/shard_map/ppermute | solution.py:357
  22.6 14.8 %collective-permute-start.5 = (bf16[128,2048]{1,0:T(8,128)(2,1)}, bf16[128,2048]{1,0:T(8,128)(2,1)}, u32[]{:S(2)}, u32[]{:S(2)}) collective-permute-start(bf16[128,2048]{1,0:T(8,128)(2,1)} %get-tuple-element.50), channel_id=1, source_target_pairs={{0,8},{4,12},{8,0},{12,4},{1,9},{5,13},{9,1},{13,5},{2,10},{6,14},... | collective-permute-start | bytes 1572872 | tf_op jit(solution)/shard_map/ppermute | solution.py:368
  25.5 11.8 %collective-permute-start.6 = (bf16[16,512]{1,0:T(8,128)(2,1)}, bf16[16,512]{1,0:T(8,128)(2,1)S(1)}, u32[]{:S(2)}, u32[]{:S(2)}) collective-permute-start(bf16[16,512]{1,0:T(8,128)(2,1)} %get-tuple-element.51.quad_ref), channel_id=1, source_target_pairs={{0,1},{1,3},{3,2},{2,0},{4,5},{5,7},{7,6},{6,4},{8,9},{9,11},{11,1... | collective-permute-start | bytes 49160 | tf_op jit(solution)/shard_map/ppermute | solution.py:378
  27.1 10.3 %collective-permute-start.7 = (bf16[16,512]{1,0:T(8,128)(2,1)}, bf16[16,512]{1,0:T(8,128)(2,1)S(1)}, u32[]{:S(2)}, u32[]{:S(2)}) collective-permute-start(bf16[16,512]{1,0:T(8,128)(2,1)} %get-tuple-element.51.quad_ref), channel_id=1, source_target_pairs={{0,3},{1,2},{3,0},{2,1},{4,7},{5,6},{7,4},{6,5},{8,11},{9,10},{11,... | collective-permute-start | bytes 49160 | tf_op jit(solution)/shard_map/ppermute | solution.py:378
  29.6 7.8 %collective-permute-start.8 = (bf16[16,512]{1,0:T(8,128)(2,1)}, bf16[16,512]{1,0:T(8,128)(2,1)S(1)}, u32[]{:S(2)}, u32[]{:S(2)}) collective-permute-start(bf16[16,512]{1,0:T(8,128)(2,1)} %get-tuple-element.51.quad_ref), channel_id=1, source_target_pairs={{0,2},{1,0},{3,1},{2,3},{4,6},{5,4},{7,5},{6,7},{8,10},{9,8},{11,9... | collective-permute-start | bytes 49160 | tf_op jit(solution)/shard_map/ppermute | solution.py:378
  40.5 13.1 %collective-permute-start.10 = (bf16[128,2048]{1,0:T(8,128)(2,1)}, bf16[128,2048]{1,0:T(8,128)(2,1)S(1)}, u32[]{:S(2)}, u32[]{:S(2)}) collective-permute-start(bf16[128,2048]{1,0:T(8,128)(2,1)} %get-tuple-element.53.refs_0_), channel_id=1, source_target_pairs={{0,8},{4,12},{8,0},{12,4},{1,9},{5,13},{9,1},{13,5},{2,10},{6,14},... | collective-permute-start | bytes 1572872 | tf_op jit(solution)/shard_map/ppermute | solution.py:390
  41.1 14.2 %collective-permute-start.11 = (bf16[128,2048]{1,0:T(8,128)(2,1)}, bf16[128,2048]{1,0:T(8,128)(2,1)}, u32[]{:S(2)}, u32[]{:S(2)}) collective-permute-start(bf16[128,2048]{1,0:T(8,128)(2,1)} %get-tuple-element.53.refs_0_), channel_id=1, source_target_pairs={{0,1},{1,3},{3,2},{2,0},{4,5},{5,7},{7,6},{6,4},{8,9},{9,11},{11,1... | collective-permute-start | bytes 1572872 | tf_op jit(solution)/shard_map/ppermute | solution.py:390
  59.9 12.4 %collective-permute-start.13 = (bf16[128,2048]{1,0:T(8,128)(2,1)}, bf16[128,2048]{1,0:T(8,128)(2,1)}, u32[]{:S(2)}, u32[]{:S(2)}) collective-permute-start(bf16[128,2048]{1,0:T(8,128)(2,1)} %get-tuple-element.56.refs_0_), channel_id=1, source_target_pairs={{0,8},{4,12},{8,0},{12,4},{1,9},{5,13},{9,1},{13,5},{2,10},{6,14},... | collective-permute-start | bytes 1572872 | tf_op jit(solution)/shard_map/ppermute | solution.py:390
  61.0 12.7 %collective-permute-start.14 = (bf16[128,2048]{1,0:T(8,128)(2,1)}, bf16[128,2048]{1,0:T(8,128)(2,1)}, u32[]{:S(2)}, u32[]{:S(2)}) collective-permute-start(bf16[128,2048]{1,0:T(8,128)(2,1)} %get-tuple-element.56.refs_0_), channel_id=1, source_target_pairs={{0,1},{1,3},{3,2},{2,0},{4,5},{5,7},{7,6},{6,4},{8,9},{9,11},{11,1... | collective-permute-start | bytes 1572872 | tf_op jit(solution)/shard_map/ppermute | solution.py:390
  61.2 14.5 %collective-permute-start.17 = (bf16[128,2048]{1,0:T(8,128)(2,1)}, bf16[128,2048]{1,0:T(8,128)(2,1)}, u32[]{:S(2)}, u32[]{:S(2)}) collective-permute-start(bf16[128,2048]{1,0:T(8,128)(2,1)} %get-tuple-element.56.refs_0_), channel_id=1, source_target_pairs={{0,4},{4,0},{8,12},{12,8},{1,5},{5,1},{9,13},{13,9},{2,6},{6,2},{1... | collective-permute-start | bytes 1572872 | tf_op jit(solution)/shard_map/ppermute | solution.py:390
  73.6 14.7 %collective-permute-start.15 = (bf16[128,2048]{1,0:T(8,128)(2,1)}, bf16[128,2048]{1,0:T(8,128)(2,1)}, u32[]{:S(2)}, u32[]{:S(2)}) collective-permute-start(bf16[128,2048]{1,0:T(8,128)(2,1)} %get-tuple-element.57.refs_0_), channel_id=1, source_target_pairs={{0,8},{4,12},{8,0},{12,4},{1,9},{5,13},{9,1},{13,5},{2,10},{6,14},... | collective-permute-start | bytes 1572872 | tf_op jit(solution)/shard_map/ppermute | solution.py:390
  74.9 15.3 %collective-permute-start.16 = (bf16[128,2048]{1,0:T(8,128)(2,1)}, bf16[128,2048]{1,0:T(8,128)(2,1)}, u32[]{:S(2)}, u32[]{:S(2)}) collective-permute-start(bf16[128,2048]{1,0:T(8,128)(2,1)} %get-tuple-element.57.refs_0_), channel_id=1, source_target_pairs={{0,1},{1,3},{3,2},{2,0},{4,5},{5,7},{7,6},{6,4},{8,9},{9,11},{11,1... | collective-permute-start | bytes 1572872 | tf_op jit(solution)/shard_map/ppermute | solution.py:390
  90.2 9.9 %collective-permute-start.23 = (bf16[256,2048]{1,0:T(8,128)(2,1)S(1)}, bf16[256,2048]{1,0:T(8,128)(2,1)S(1)}, u32[]{:S(2)}, u32[]{:S(2)}) collective-permute-start(bf16[256,2048]{1,0:T(8,128)(2,1)S(1)} %get-tuple-element.64), channel_id=1, source_target_pairs={{0,4},{4,0},{8,12},{12,8},{1,5},{5,1},{9,13},{13,9},{2,6},{6,2},{1... | collective-permute-start | bytes 3145736 | tf_op jit(solution)/shard_map/ppermute | solution.py:390
  90.2 3.8 %collective-permute-start.21 = (bf16[128,2048]{1,0:T(8,128)(2,1)}, bf16[128,2048]{1,0:T(8,128)(2,1)S(1)}, u32[]{:S(2)}, u32[]{:S(2)}) collective-permute-start(bf16[128,2048]{1,0:T(8,128)(2,1)} %get-tuple-element.57.refs_0_), channel_id=1, source_target_pairs={{0,4},{4,0},{8,12},{12,8},{1,5},{5,1},{9,13},{13,9},{2,6},{6,2},{1... | collective-permute-start | bytes 1572872 | tf_op jit(solution)/shard_map/ppermute | solution.py:390
  90.7 3.9 %collective-permute-start.22 = (bf16[128,2048]{1,0:T(8,128)(2,1)}, bf16[128,2048]{1,0:T(8,128)(2,1)S(1)}, u32[]{:S(2)}, u32[]{:S(2)}) collective-permute-start(bf16[128,2048]{1,0:T(8,128)(2,1)} %get-tuple-element.61.refs_2_), channel_id=1, source_target_pairs={{0,4},{4,0},{8,12},{12,8},{1,5},{5,1},{9,13},{13,9},{2,6},{6,2},{1... | collective-permute-start | bytes 1572872 | tf_op jit(solution)/shard_map/ppermute | solution.py:390
  92.6 8.8 %collective-permute-start.19 = (bf16[128,1024]{1,0:T(8,128)(2,1)S(1)}, bf16[128,1024]{1,0:T(8,128)(2,1)S(1)}, u32[]{:S(2)}, u32[]{:S(2)}) collective-permute-start(bf16[128,1024]{1,0:T(8,128)(2,1)S(1)} %slice.30), channel_id=1, source_target_pairs={{0,8},{4,12},{8,0},{12,4},{1,9},{5,13},{9,1},{13,5},{2,10},{6,14},... | collective-permute-start | bytes 786440 | tf_op jit(solution)/shard_map/ppermute | solution.py:390
  93.5 9.3 %collective-permute-start.20 = (bf16[128,1024]{1,0:T(8,128)(2,1)S(1)}, bf16[128,1024]{1,0:T(8,128)(2,1)S(1)}, u32[]{:S(2)}, u32[]{:S(2)}) collective-permute-start(bf16[128,1024]{1,0:T(8,128)(2,1)S(1)} %slice.31), channel_id=1, source_target_pairs={{0,1},{1,3},{3,2},{2,0},{4,5},{5,7},{7,6},{6,4},{8,9},{9,11},{11,1... | collective-permute-start | bytes 786440 | tf_op jit(solution)/shard_map/ppermute | solution.py:390
  102.8 9.7 %collective-permute-start.28 = (bf16[256,2048]{1,0:T(8,128)(2,1)S(1)}, bf16[256,2048]{1,0:T(8,128)(2,1)S(1)}, u32[]{:S(2)}, u32[]{:S(2)}) collective-permute-start(bf16[256,2048]{1,0:T(8,128)(2,1)S(1)} %get-tuple-element.70), channel_id=1, source_target_pairs={{0,4},{4,0},{8,12},{12,8},{1,5},{5,1},{9,13},{13,9},{2,6},{6,2},{1... | collective-permute-start | bytes 3145736 | tf_op jit(solution)/shard_map/ppermute | solution.py:390
  102.8 4.0 %collective-permute-start.25 = (bf16[128,2048]{1,0:T(8,128)(2,1)}, bf16[128,2048]{1,0:T(8,128)(2,1)S(1)}, u32[]{:S(2)}, u32[]{:S(2)}) collective-permute-start(bf16[128,2048]{1,0:T(8,128)(2,1)} %get-tuple-element.60.refs_0_), channel_id=1, source_target_pairs={{0,4},{4,0},{8,12},{12,8},{1,5},{5,1},{9,13},{13,9},{2,6},{6,2},{1... | collective-permute-start | bytes 1572872 | tf_op jit(solution)/shard_map/ppermute | solution.py:390
  103.3 3.6 %collective-permute-start.27 = (bf16[128,1024]{1,0:T(8,128)(2,1)S(1)}, bf16[128,1024]{1,0:T(8,128)(2,1)S(1)}, u32[]{:S(2)}, u32[]{:S(2)}) collective-permute-start(bf16[128,1024]{1,0:T(8,128)(2,1)S(1)} %get-tuple-element.67.refs_3_), channel_id=1, source_target_pairs={{0,4},{4,0},{8,12},{12,8},{1,5},{5,1},{9,13},{13,9},{2,6},{6,2},{1... | collective-permute-start | bytes 786440 | tf_op jit(solution)/shard_map/ppermute | solution.py:390
  103.8 13.8 %collective-permute-start.24 = (bf16[128,2048]{1,0:T(8,128)(2,1)S(1)}, bf16[128,2048]{1,0:T(8,128)(2,1)S(1)}, u32[]{:S(2)}, u32[]{:S(2)}) collective-permute-start(bf16[128,2048]{1,0:T(8,128)(2,1)S(1)} %get-tuple-element.65), channel_id=1, source_target_pairs={{0,8},{4,12},{8,0},{12,4},{1,9},{5,13},{9,1},{13,5},{2,10},{6,14},... | collective-permute-start | bytes 1572872 | tf_op jit(solution)/shard_map/ppermute | solution.py:390
  117.7 8.5 %collective-permute-start.31 = (bf16[256,2048]{1,0:T(8,128)(2,1)S(1)}, bf16[256,2048]{1,0:T(8,128)(2,1)S(1)}, u32[]{:S(2)}, u32[]{:S(2)}) collective-permute-start(bf16[256,2048]{1,0:T(8,128)(2,1)S(1)} %get-tuple-element.76), channel_id=1, source_target_pairs={{0,4},{4,0},{8,12},{12,8},{1,5},{5,1},{9,13},{13,9},{2,6},{6,2},{1... | collective-permute-start | bytes 3145736 | tf_op jit(solution)/shard_map/ppermute | solution.py:390
  118.2 3.6 %collective-permute-start.12 = (bf16[128,2048]{1,0:T(8,128)(2,1)S(1)}, bf16[128,2048]{1,0:T(8,128)(2,1)S(1)}, u32[]{:S(2)}, u32[]{:S(2)}) collective-permute-start(bf16[128,2048]{1,0:T(8,128)(2,1)S(1)} %copy-done.8), channel_id=1, source_target_pairs={{0,4},{4,0},{8,12},{12,8},{1,5},{5,1},{9,13},{13,9},{2,6},{6,2},{1... | collective-permute-start | bytes 1572872 | tf_op jit(solution)/shard_map/ppermute | solution.py:390
  118.2 14.3 %collective-permute-start.29 = (bf16[128,2048]{1,0:T(8,128)(2,1)S(1)}, bf16[128,2048]{1,0:T(8,128)(2,1)S(1)}, u32[]{:S(2)}, u32[]{:S(2)}) collective-permute-start(bf16[128,2048]{1,0:T(8,128)(2,1)S(1)} %get-tuple-element.71), channel_id=1, source_target_pairs={{0,8},{4,12},{8,0},{12,4},{1,9},{5,13},{9,1},{13,5},{2,10},{6,14},... | collective-permute-start | bytes 1572872 | tf_op jit(solution)/shard_map/ppermute | solution.py:390
  119.7 15.2 %collective-permute-start.30 = (bf16[128,2048]{1,0:T(8,128)(2,1)S(1)}, bf16[128,2048]{1,0:T(8,128)(2,1)S(1)}, u32[]{:S(2)}, u32[]{:S(2)}) collective-permute-start(bf16[128,2048]{1,0:T(8,128)(2,1)S(1)} %add_convert_fusion.5), channel_id=1, source_target_pairs={{0,1},{1,3},{3,2},{2,0},{4,5},{5,7},{7,6},{6,4},{8,9},{9,11},{11,1... | collective-permute-start | bytes 1572872 | tf_op jit(solution)/shard_map/ppermute | solution.py:390
  134.9 14.3 %collective-permute-start.33 = (bf16[128,2048]{1,0:T(8,128)(2,1)S(1)}, bf16[128,2048]{1,0:T(8,128)(2,1)S(1)}, u32[]{:S(2)}, u32[]{:S(2)}) collective-permute-start(bf16[128,2048]{1,0:T(8,128)(2,1)S(1)} %get-tuple-element.78), channel_id=1, source_target_pairs={{0,8},{4,12},{8,0},{12,4},{1,9},{5,13},{9,1},{13,5},{2,10},{6,14},... | collective-permute-start | bytes 1572872 | tf_op jit(solution)/shard_map/ppermute | solution.py:390
  136.0 15.0 %collective-permute-start.34 = (bf16[128,2048]{1,0:T(8,128)(2,1)S(1)}, bf16[128,2048]{1,0:T(8,128)(2,1)S(1)}, u32[]{:S(2)}, u32[]{:S(2)}) collective-permute-start(bf16[128,2048]{1,0:T(8,128)(2,1)S(1)} %add_convert_fusion.3), channel_id=1, source_target_pairs={{0,1},{1,3},{3,2},{2,0},{4,5},{5,7},{7,6},{6,4},{8,9},{9,11},{11,1... | collective-permute-start | bytes 1572872 | tf_op jit(solution)/shard_map/ppermute | solution.py:390
  151.4 14.2 %collective-permute-start.36 = (bf16[128,2048]{1,0:T(8,128)(2,1)S(1)}, bf16[128,2048]{1,0:T(8,128)(2,1)S(1)}, u32[]{:S(2)}, u32[]{:S(2)}) collective-permute-start(bf16[128,2048]{1,0:T(8,128)(2,1)S(1)} %add_convert_fusion.1), channel_id=1, source_target_pairs={{0,1},{1,3},{3,2},{2,0},{4,5},{5,7},{7,6},{6,4},{8,9},{9,11},{11,1... | collective-permute-start | bytes 1572872 | tf_op jit(solution)/shard_map/ppermute | solution.py:390
  151.9 13.6 %collective-permute-start.35 = (bf16[128,2048]{1,0:T(8,128)(2,1)S(1)}, bf16[128,2048]{1,0:T(8,128)(2,1)S(1)}, u32[]{:S(2)}, u32[]{:S(2)}) collective-permute-start(bf16[128,2048]{1,0:T(8,128)(2,1)S(1)} %get-tuple-element.83), channel_id=1, source_target_pairs={{0,8},{4,12},{8,0},{12,4},{1,9},{5,13},{9,1},{13,5},{2,10},{6,14},... | collective-permute-start | bytes 1572872 | tf_op jit(solution)/shard_map/ppermute | solution.py:390
  (29 other events, 197.5 us)

commit v10 on v9

--- a/solution.py
+++ b/solution.py
@@ -203,10 +203,10 @@
     del refs
 
 
-def meet(arrays, present):
+def meet(arrays, flops):
     return pl.pallas_call(
         pass_kernel,
-        in_specs=[pl.BlockSpec(memory_space=pl.ANY)] * (len(arrays) + len(present)),
+        in_specs=[pl.BlockSpec(memory_space=pl.ANY)] * len(arrays),
         out_specs=[pl.BlockSpec(memory_space=pl.ANY)] * len(arrays),
         out_shape=[jax.ShapeDtypeStruct(array.shape, array.dtype) for array in arrays],
         input_output_aliases={index: index for index in range(len(arrays))},
@@ -217,15 +217,16 @@
     del refs
 
 
-def meet(arrays, present):
+def meet(arrays, flops):
     return pl.pallas_call(
         pass_kernel,
-        in_specs=[pl.BlockSpec(memory_space=pl.ANY)] * (len(arrays) + len(present)),
+        in_specs=[pl.BlockSpec(memory_space=pl.ANY)] * len(arrays),
         out_specs=[pl.BlockSpec(memory_space=pl.ANY)] * len(arrays),
         out_shape=[jax.ShapeDtypeStruct(array.shape, array.dtype) for array in arrays],
         input_output_aliases={index: index for index in range(len(arrays))},
         compiler_params=pltpu.CompilerParams(vmem_limit_bytes=MIB),
-    )(*arrays, *present)
+        cost_estimate=pl.CostEstimate(flops=flops, bytes_accessed=0, transcendentals=0),
+    )(*arrays)
 
 
 def experts_kernel(mine_ref, quad_ref, *refs, cap, pieces):
@@ -413,6 +414,10 @@
 
     def sum_of(step, more):
         parts = [held["own", step], held["met", step], held["back", step]] + more
+        if held["back", step].shape[1] == half:
+            left = sum(part[:, :half].astype(jnp.float32) for part in parts)
+            right = sum(part[:, half:].astype(jnp.float32) for part in parts if part.shape[1] > half)
+            return jnp.concatenate([left, right], axis=1)
         return sum(part.astype(jnp.float32) for part in parts)
 
     for turn in range(1, n_sub + 5):
@@ -428,7 +433,17 @@
             held["twin", step] = move(held["row", step], "twin")
         step = turn - 4 if turn < n_sub + 4 else 0
         if 1 <= step <= last or turn == n_sub + 4:
-            now["back", step] = move(held["away", step], "across")
+            if step == 1 and last > 1:
+                now["back", step] = move(held["away", step][:, :half], "across")
+                now["late", step] = move(held["away", step][:, half:], "on")
+            elif step == 2:
+                away = held["away", step]
+                added = away[:, half:].astype(jnp.float32) + held["late", 1].astype(jnp.float32)
+                now["back", step] = move(
+                    jnp.concatenate([away[:, :half], added.astype(jnp.bfloat16)], axis=1), "across"
+                )
+            else:
+                now["back", step] = move(held["away", step], "across")
         step = turn - 5
         if 1 <= step <= last:
             more = [held["sum", step - 1]] if step > 1 else []
@@ -449,8 +464,8 @@
         if 1 <= step <= last or turn == n_sub + 3:
             now["away", step] = twin_sum(step)
         if turn < n_sub + 4:
-            weights = [expert_gate[0], expert_up[0], expert_down[0]] if turn == 1 else []
-            now = dict(zip(now.keys(), meet(list(now.values()), weights)))
+            wait = 10_000_000_000 if turn <= 2 else 0
+            now = dict(zip(now.keys(), meet(list(now.values()), wait)))
         held.update(now)
     total = hidden.astype(jnp.float32) + sum_of(0, [held["sum", last]])
     return total.astype(jnp.bfloat16)[None]

time: 167 us -> 163 us (0.976)
  local copies, waits for them, and re-layouts: 14.9 us -> 10.5 us
    unnamed x48 -> x42, local copies, waits for them, and re-layouts: 11 us -> 6.63 us
    ppermute x28 -> x29, waiting for transfers between devices: 76.2 us -> 74.8 us  [move(): return lax.ppermute(array, *ways[way])]
    ppermute x28 -> x29, starting transfers between devices: 15.9 us -> 17.2 us  [move(): return lax.ppermute(array, *ways[way])]
  transfers between devices with their start and end apart: 37 -> 38, of which waited for: 23 -> 19; matrix products, arithmetic and copies ran while one was open for 3% -> 3% of each run, Pallas kernels for 17% -> 18%
where the time goes in v10:
time: 163 us; the launch traced here: 162 us
  waiting for transfers between devices  82.5 us (51%)
  Pallas kernels  37.1 us (23%)
  starting transfers between devices  29.3 us (18%)
  local copies, waits for them, and re-layouts  10.5 us (6%)
  other arithmetic  2.76 us (2%)
    ppermute x29, waiting for transfers between devices, move(): return lax.ppermute(array, *ways[way])  74.8 us
    pallas_call x4, Pallas kernels, experts_on_rows(): pl.pallas_call(functools.partial(experts_kernel, cap=cap, pieces=pieces),...  21.1 us
    ppermute x29, starting transfers between devices, move(): return lax.ppermute(array, *ways[way])  17.2 us
    pallas_call x2, Pallas kernels, attend(): pl.pallas_call(functools.partial(attend_kernel, scale=1.0 / HD ** 0.5), i...  11.6 us
    unnamed x42, local copies, waits for them, and re-layouts  6.63 us
    ppermute x1, waiting for transfers between devices, gathered_plan(): lax.ppermute(kv_away, 'seq', across)  6.47 us
    ppermute x3, starting transfers between devices, gathered_plan(): lax.ppermute(quad, 'sub', ring(steps))  5.63 us
  transfers between devices with their start and end apart: 38, of which 19 were waited for; matrix products, arithmetic and copies ran while one was open for 3% of the time, Pallas kernels for 18%

profile of v10, /device:TPU:0, one launch (start us, length us, event | category | flops | bytes accessed | tf_op | source)
XLA Modules:
  0.0 162.5 jit_solution(16843783362015580337)
XLA Ops:
  0.5 1.9 %shard_map.109 = (bf16[128,1024]{1,0:T(8,128)(2,1)}, bf16[144,256]{1,0:T(8,128)(2,1)}, bf16[144,256]{1,0:T(8,128)(2,1)}) custom-call(s32[1]{0:T(128)} %bitcast.7.chip_ref, bf16[128,2048]{1,0:T(8,128)(2,1)} %bitcast.35, bf16[128,256]{1,0:T(8,128)(2,1)} %bitcast.38, bf16[128,256]{1,0:T(8,128)(2,1)} %bitcast.39, s32[8,128]{1,0:T(8,128)} %bitcast.40, ...), custom_call_target="tpu_custom_call" | custom-call | tf_op jit(solution)/shard_map/pallas_call | solution.py:87
  2.3 2.5 %collective-permute-start.4 = (bf16[128,1024]{1,0:T(8,128)(2,1)}, bf16[128,1024]{1,0:T(8,128)(2,1)S(1)}, u32[]{:S(2)}, u32[]{:S(2)}) collective-permute-start(bf16[128,1024]{1,0:T(8,128)(2,1)} %get-tuple-element.50), channel_id=1, source_target_pairs={{0,8},{4,12},{8,0},{12,4},{1,9},{5,13},{9,1},{13,5},{2,10},{6,14},... | collective-permute-start | bytes 786440 | tf_op jit(solution)/shard_map/ppermute | solution.py:353
  7.3 6.5 %collective-permute-done.1.refs_2_ = bf16[144,256]{1,0:T(8,128)(2,1)S(1)} collective-permute-done((bf16[144,256]{1,0:T(8,128)(2,1)}, bf16[144,256]{1,0:T(8,128)(2,1)S(1)}, u32[]{:S(2)}, u32[]{:S(2)}) %collective-permute-start.1) | collective-permute-done | bytes 73760 | tf_op jit(solution)/shard_map/ppermute | solution.py:357
  17.1 5.6 %shard_map.111 = (bf16[128,2048]{1,0:T(8,128)(2,1)}, bf16[16,512]{1,0:T(8,128)(2,1)}) custom-call(s32[7]{0:T(128)} %stack.38.place_ref, bf16[128,1024]{1,0:T(8,128)(2,1)} %copy-done.19, bf16[144,256]{1,0:T(8,128)(2,1)} %get-tuple-element.47.refs_0_, bf16[144,256]{1,0:T(8,128)(2,1)} %copy-done.16, bf16[144,256]{1,0:T(8,128)(2,1)} %copy-done.17, ...), custom_call_target="tpu_custom_call" | custom-call | flops 805306368 | bytes 5242880 | tf_op jit(solution)/shard_map/pallas_call | solution.py:152
  22.6 1.6 collective-permute-start.5
  25.5 1.6 collective-permute-start.6
  27.1 2.5 %collective-permute-start.7 = (bf16[16,512]{1,0:T(8,128)(2,1)}, bf16[16,512]{1,0:T(8,128)(2,1)S(1)}, u32[]{:S(2)}, u32[]{:S(2)}) collective-permute-start(bf16[16,512]{1,0:T(8,128)(2,1)} %get-tuple-element.52.quad_ref), channel_id=1, source_target_pairs={{0,3},{1,2},{3,0},{2,1},{4,7},{5,6},{7,4},{6,5},{8,11},{9,10},{11,... | collective-permute-start | bytes 49160 | tf_op jit(solution)/shard_map/ppermute | solution.py:379
  29.6 1.6 collective-permute-start.8
  31.1 6.0 %shard_map.110 = (f32[128,2048]{1,0:T(8,128)}, bf16[16,512]{1,0:T(8,128)(2,1)}) custom-call(s32[7]{0:T(128)} %stack.37.place_ref, bf16[128,2048]{1,0:T(8,128)(2,1)} %bitcast.36, bf16[144,256]{1,0:T(8,128)(2,1)} %get-tuple-element.47.refs_0_, bf16[144,256]{1,0:T(8,128)(2,1)} %copy-done.16, bf16[144,256]{1,0:T(8,128)(2,1)} %copy-done.17, ...), custom_call_target="tpu_custom_call" | custom-call | flops 805306368 | bytes 5242880 | tf_op jit(solution)/shard_map/pallas_call | solution.py:152
  38.0 2.5 %shard_map.112 = (bf16[128,2048]{1,0:T(8,128)(2,1)}, bf16[128,2048]{1,0:T(8,128)(2,1)}) custom-call(f32[128,2048]{1,0:T(8,128)} %get-tuple-element.49.own_ref, bf16[128,2048]{1,0:T(8,128)(2,1)} %copy-done.14, bf16[1,2048]{1,0:T(2,128)(2,1)} %broadcast_in_dim.6.gain_ref, bf16[16,512]{1,0:T(8,128)(2,1)} %copy-done.10, bf16[16,512]{1,0:T(8,128)(2,1)} %copy-done.8, ...), custom_call_target="tpu_custom_call" | custom-call | tf_op jit(solution)/shard_map/pallas_call | solution.py:192
  41.8 1.6 collective-permute-start.11
  43.4 10.3 %collective-permute-done.10.refs_0_ = bf16[128,2048]{1,0:T(8,128)(2,1)S(1)} collective-permute-done((bf16[128,2048]{1,0:T(8,128)(2,1)}, bf16[128,2048]{1,0:T(8,128)(2,1)S(1)}, u32[]{:S(2)}, u32[]{:S(2)}) %collective-permute-start.10) | collective-permute-done | bytes 524320 | tf_op jit(solution)/shard_map/ppermute | solution.py:391
  53.7 2.3 %collective-permute-done.11.refs_1_ = bf16[128,2048]{1,0:T(8,128)(2,1)} collective-permute-done((bf16[128,2048]{1,0:T(8,128)(2,1)}, bf16[128,2048]{1,0:T(8,128)(2,1)}, u32[]{:S(2)}, u32[]{:S(2)}) %collective-permute-start.11) | collective-permute-done | bytes 524320 | tf_op jit(solution)/shard_map/ppermute | solution.py:391
  57.3 11.1 %collective-permute-done.13.refs_0_ = bf16[128,2048]{1,0:T(8,128)(2,1)} collective-permute-done((bf16[128,2048]{1,0:T(8,128)(2,1)}, bf16[128,2048]{1,0:T(8,128)(2,1)}, u32[]{:S(2)}, u32[]{:S(2)}) %collective-permute-start.13) | collective-permute-done | bytes 524320 | tf_op jit(solution)/shard_map/ppermute | solution.py:391
  69.4 1.7 %collective-permute-start.15 = (bf16[128,2048]{1,0:T(8,128)(2,1)}, bf16[128,2048]{1,0:T(8,128)(2,1)}, u32[]{:S(2)}, u32[]{:S(2)}) collective-permute-start(bf16[128,2048]{1,0:T(8,128)(2,1)} %get-tuple-element.58.refs_0_), channel_id=1, source_target_pairs={{0,8},{4,12},{8,0},{12,4},{1,9},{5,13},{9,1},{13,5},{2,10},{6,14},... | collective-permute-start | bytes 1572872 | tf_op jit(solution)/shard_map/ppermute | solution.py:391
  71.9 1.9 %copy-done.1 = bf16[1,2048,768]{2,1,0:T(8,128)(2,1)S(1)} copy-done((bf16[1,2048,768]{2,1,0:T(8,128)(2,1)S(1)}, bf16[1,2048,768]{2,1,0:T(8,128)(2,1)}, u32[]{:S(2)}) %copy-start.1) | copy-done | bytes 3145752
  73.7 1.9 %copy-done.2 = bf16[1,768,2048]{2,1,0:T(8,128)(2,1)S(1)} copy-done((bf16[1,768,2048]{2,1,0:T(8,128)(2,1)S(1)}, bf16[1,768,2048]{2,1,0:T(8,128)(2,1)}, u32[]{:S(2)}) %copy-start.2) | copy-done | bytes 3145752
  75.6 5.8 %shard_map.116 = (bf16[128,2048]{1,0:T(8,128)(2,1)S(1)}, bf16[128,2048]{1,0:T(8,128)(2,1)S(1)}, bf16[256,2048]{1,0:T(8,128)(2,1)S(1)}) custom-call(s32[1]{0:T(128)} %bitcast.15.mine_ref, bf16[16,512]{1,0:T(8,128)(2,1)S(1)} %copy-done.11, bf16[128,2048]{1,0:T(8,128)(2,1)} %get-tuple-element.57.refs_0_, bf16[128,2048]{1,0:T(8,128)(2,1)} %collective-permute-done.17.refs_1_, ...), custom_call_target="tpu_custom_call" | custom-call | flops 3019898880 | bytes 13631488 | tf_op jit(solution)/shard_map/pallas_call | solution.py:292
  81.5 2.6 %collective-permute-done.15.refs_0_ = bf16[128,2048]{1,0:T(8,128)(2,1)} collective-permute-done((bf16[128,2048]{1,0:T(8,128)(2,1)}, bf16[128,2048]{1,0:T(8,128)(2,1)}, u32[]{:S(2)}, u32[]{:S(2)}) %collective-permute-start.15) | collective-permute-done | bytes 524320 | tf_op jit(solution)/shard_map/ppermute | solution.py:391
  84.1 2.3 %collective-permute-done.16.refs_1_ = bf16[128,2048]{1,0:T(8,128)(2,1)} collective-permute-done((bf16[128,2048]{1,0:T(8,128)(2,1)}, bf16[128,2048]{1,0:T(8,128)(2,1)}, u32[]{:S(2)}, u32[]{:S(2)}) %collective-permute-start.16) | collective-permute-done | bytes 524320 | tf_op jit(solution)/shard_map/ppermute | solution.py:391
  90.7 5.5 %shard_map.118 = (bf16[128,2048]{1,0:T(8,128)(2,1)S(1)}, bf16[128,2048]{1,0:T(8,128)(2,1)S(1)}, bf16[256,2048]{1,0:T(8,128)(2,1)S(1)}) custom-call(s32[1]{0:T(128)} %bitcast.15.mine_ref, bf16[16,512]{1,0:T(8,128)(2,1)S(1)} %copy-done.9, bf16[128,2048]{1,0:T(8,128)(2,1)} %get-tuple-element.58.refs_0_, bf16[128,2048]{1,0:T(8,128)(2,1)S(1)} %collective-permute-done.21.refs_1_, ...), custom_call_target="tpu_custom_call" | custom-call | flops 3019898880 | bytes 13631488 | tf_op jit(solution)/shard_map/pallas_call | solution.py:292
  99.8 2.9 %collective-permute-done.26.refs_1_ = bf16[128,2048]{1,0:T(8,128)(2,1)S(1)} collective-permute-done((bf16[128,2048]{1,0:T(8,128)(2,1)}, bf16[128,2048]{1,0:T(8,128)(2,1)S(1)}, u32[]{:S(2)}, u32[]{:S(2)}) %collective-permute-start.26) | collective-permute-done | bytes 524320 | tf_op jit(solution)/shard_map/ppermute | solution.py:391
  103.1 1.5 collective-permute-start.24
  105.4 5.4 %shard_map.120 = (bf16[128,2048]{1,0:T(8,128)(2,1)S(1)}, bf16[128,2048]{1,0:T(8,128)(2,1)S(1)}, bf16[256,2048]{1,0:T(8,128)(2,1)S(1)}) custom-call(s32[1]{0:T(128)} %bitcast.15.mine_ref, bf16[16,512]{1,0:T(8,128)(2,1)S(1)} %copy-done.7, bf16[128,2048]{1,0:T(8,128)(2,1)} %get-tuple-element.61.refs_0_, bf16[128,2048]{1,0:T(8,128)(2,1)S(1)} %collective-permute-done.26.refs_1_, ...), custom_call_target="tpu_custom_call" | custom-call | flops 3019898880 | bytes 13631488 | tf_op jit(solution)/shard_map/pallas_call | solution.py:292
  111.5 2.1 %collective-permute-done.25.refs_1_ = bf16[128,1024]{1,0:T(8,128)(2,1)S(1)} collective-permute-done((bf16[128,1024]{1,0:T(8,128)(2,1)S(1)}, bf16[128,1024]{1,0:T(8,128)(2,1)S(1)}, u32[]{:S(2)}, u32[]{:S(2)}) %collective-permute-start.25) | collective-permute-done | bytes 262176 | tf_op jit(solution)/shard_map/ppermute | solution.py:391
  115.7 4.3 %shard_map.114 = (bf16[128,2048]{1,0:T(8,128)(2,1)S(1)}, bf16[128,2048]{1,0:T(8,128)(2,1)S(1)}, bf16[256,2048]{1,0:T(8,128)(2,1)S(1)}) custom-call(s32[1]{0:T(128)} %bitcast.15.mine_ref, bf16[16,512]{1,0:T(8,128)(2,1)S(1)} %copy-done.12, bf16[128,2048]{1,0:T(8,128)(2,1)S(1)} %copy-done.3, bf16[128,2048]{1,0:T(8,128)(2,1)S(1)} %collective-permute-done.9.refs_1_, ...), custom_call_target="tpu_custom_call" | custom-call | flops 3019898880 | bytes 13631488 | tf_op jit(solution)/shard_map/pallas_call | solution.py:292
  120.2 8.0 %collective-permute-done.30.refs_0_ = bf16[128,2048]{1,0:T(8,128)(2,1)S(1)} collective-permute-done((bf16[128,2048]{1,0:T(8,128)(2,1)S(1)}, bf16[128,2048]{1,0:T(8,128)(2,1)S(1)}, u32[]{:S(2)}, u32[]{:S(2)}) %collective-permute-start.30) | collective-permute-done | bytes 524320 | tf_op jit(solution)/shard_map/ppermute | solution.py:391
  128.1 1.7 %collective-permute-done.31.refs_1_ = bf16[128,2048]{1,0:T(8,128)(2,1)S(1)} collective-permute-done((bf16[128,2048]{1,0:T(8,128)(2,1)S(1)}, bf16[128,2048]{1,0:T(8,128)(2,1)S(1)}, u32[]{:S(2)}, u32[]{:S(2)}) %collective-permute-start.31) | collective-permute-done | bytes 524320 | tf_op jit(solution)/shard_map/ppermute | solution.py:391
  129.9 1.5 collective-permute-start.34
  132.7 11.5 %collective-permute-done.34.refs_0_ = bf16[128,2048]{1,0:T(8,128)(2,1)S(1)} collective-permute-done((bf16[128,2048]{1,0:T(8,128)(2,1)S(1)}, bf16[128,2048]{1,0:T(8,128)(2,1)S(1)}, u32[]{:S(2)}, u32[]{:S(2)}) %collective-permute-start.34) | collective-permute-done | bytes 524320 | tf_op jit(solution)/shard_map/ppermute | solution.py:391
  144.2 2.5 %collective-permute-done.35.refs_1_ = bf16[128,2048]{1,0:T(8,128)(2,1)S(1)} collective-permute-done((bf16[128,2048]{1,0:T(8,128)(2,1)S(1)}, bf16[128,2048]{1,0:T(8,128)(2,1)S(1)}, u32[]{:S(2)}, u32[]{:S(2)}) %collective-permute-start.35) | collective-permute-done | bytes 524320 | tf_op jit(solution)/shard_map/ppermute | solution.py:391
  148.4 12.9 %collective-permute-done.37 = bf16[128,2048]{1,0:T(8,128)(2,1)S(1)} collective-permute-done((bf16[128,2048]{1,0:T(8,128)(2,1)S(1)}, bf16[128,2048]{1,0:T(8,128)(2,1)S(1)}, u32[]{:S(2)}, u32[]{:S(2)}) %collective-permute-start.37) | collective-permute-done | bytes 524320 | tf_op jit(solution)/shard_map/ppermute | solution.py:391
  (119 shorter events, 28.6 us)
Async XLA Ops:
  0.0 15.0 %collective-permute-start.3 = (bf16[512,2048]{1,0:T(8,128)(2,1)}, bf16[512,2048]{1,0:T(8,128)(2,1)S(1)}, u32[]{:S(2)}, u32[]{:S(2)}) collective-permute-start(bf16[512,2048]{1,0:T(8,128)(2,1)} %refs_4_.1), channel_id=1, source_target_pairs={{0,4},{4,0},{8,12},{12,8},{1,5},{5,1},{9,13},{13,9},{2,6},{6,2},{1... | collective-permute-start | bytes 6291464 | tf_op jit(solution)/shard_map/ppermute | solution.py:360
  2.3 12.7 %collective-permute-start.4 = (bf16[128,1024]{1,0:T(8,128)(2,1)}, bf16[128,1024]{1,0:T(8,128)(2,1)S(1)}, u32[]{:S(2)}, u32[]{:S(2)}) collective-permute-start(bf16[128,1024]{1,0:T(8,128)(2,1)} %get-tuple-element.50), channel_id=1, source_target_pairs={{0,8},{4,12},{8,0},{12,4},{1,9},{5,13},{9,1},{13,5},{2,10},{6,14},... | collective-permute-start | bytes 786440 | tf_op jit(solution)/shard_map/ppermute | solution.py:353
  5.1 8.7 %collective-permute-start.1 = (bf16[144,256]{1,0:T(8,128)(2,1)}, bf16[144,256]{1,0:T(8,128)(2,1)S(1)}, u32[]{:S(2)}, u32[]{:S(2)}) collective-permute-start(bf16[144,256]{1,0:T(8,128)(2,1)} %get-tuple-element.48), channel_id=1, source_target_pairs={{0,8},{4,12},{8,0},{12,4},{1,9},{5,13},{9,1},{13,5},{2,10},{6,14},... | collective-permute-start | bytes 221192 | tf_op jit(solution)/shard_map/ppermute | solution.py:357
  5.4 9.6 %collective-permute-start.2 = (bf16[144,256]{1,0:T(8,128)(2,1)}, bf16[144,256]{1,0:T(8,128)(2,1)S(1)}, u32[]{:S(2)}, u32[]{:S(2)}) collective-permute-start(bf16[144,256]{1,0:T(8,128)(2,1)} %get-tuple-element.48), channel_id=1, source_target_pairs={{0,12},{4,8},{8,4},{12,0},{1,13},{5,9},{9,5},{13,1},{2,14},{6,10},... | collective-permute-start | bytes 221192 | tf_op jit(solution)/shard_map/ppermute | solution.py:358
  22.6 14.6 %collective-permute-start.5 = (bf16[128,2048]{1,0:T(8,128)(2,1)}, bf16[128,2048]{1,0:T(8,128)(2,1)S(1)}, u32[]{:S(2)}, u32[]{:S(2)}) collective-permute-start(bf16[128,2048]{1,0:T(8,128)(2,1)} %get-tuple-element.51), channel_id=1, source_target_pairs={{0,8},{4,12},{8,0},{12,4},{1,9},{5,13},{9,1},{13,5},{2,10},{6,14},... | collective-permute-start | bytes 1572872 | tf_op jit(solution)/shard_map/ppermute | solution.py:369
  25.5 11.7 %collective-permute-start.6 = (bf16[16,512]{1,0:T(8,128)(2,1)}, bf16[16,512]{1,0:T(8,128)(2,1)S(1)}, u32[]{:S(2)}, u32[]{:S(2)}) collective-permute-start(bf16[16,512]{1,0:T(8,128)(2,1)} %get-tuple-element.52.quad_ref), channel_id=1, source_target_pairs={{0,1},{1,3},{3,2},{2,0},{4,5},{5,7},{7,6},{6,4},{8,9},{9,11},{11,1... | collective-permute-start | bytes 49160 | tf_op jit(solution)/shard_map/ppermute | solution.py:379
  27.1 10.1 %collective-permute-start.7 = (bf16[16,512]{1,0:T(8,128)(2,1)}, bf16[16,512]{1,0:T(8,128)(2,1)S(1)}, u32[]{:S(2)}, u32[]{:S(2)}) collective-permute-start(bf16[16,512]{1,0:T(8,128)(2,1)} %get-tuple-element.52.quad_ref), channel_id=1, source_target_pairs={{0,3},{1,2},{3,0},{2,1},{4,7},{5,6},{7,4},{6,5},{8,11},{9,10},{11,... | collective-permute-start | bytes 49160 | tf_op jit(solution)/shard_map/ppermute | solution.py:379
  29.6 7.6 %collective-permute-start.8 = (bf16[16,512]{1,0:T(8,128)(2,1)}, bf16[16,512]{1,0:T(8,128)(2,1)S(1)}, u32[]{:S(2)}, u32[]{:S(2)}) collective-permute-start(bf16[16,512]{1,0:T(8,128)(2,1)} %get-tuple-element.52.quad_ref), channel_id=1, source_target_pairs={{0,2},{1,0},{3,1},{2,3},{4,6},{5,4},{7,5},{6,7},{8,10},{9,8},{11,9... | collective-permute-start | bytes 49160 | tf_op jit(solution)/shard_map/ppermute | solution.py:379
  40.6 13.1 %collective-permute-start.10 = (bf16[128,2048]{1,0:T(8,128)(2,1)}, bf16[128,2048]{1,0:T(8,128)(2,1)S(1)}, u32[]{:S(2)}, u32[]{:S(2)}) collective-permute-start(bf16[128,2048]{1,0:T(8,128)(2,1)} %get-tuple-element.54.refs_0_), channel_id=1, source_target_pairs={{0,8},{4,12},{8,0},{12,4},{1,9},{5,13},{9,1},{13,5},{2,10},{6,14},... | collective-permute-start | bytes 1572872 | tf_op jit(solution)/shard_map/ppermute | solution.py:391
  41.8 14.2 %collective-permute-start.11 = (bf16[128,2048]{1,0:T(8,128)(2,1)}, bf16[128,2048]{1,0:T(8,128)(2,1)}, u32[]{:S(2)}, u32[]{:S(2)}) collective-permute-start(bf16[128,2048]{1,0:T(8,128)(2,1)} %get-tuple-element.54.refs_0_), channel_id=1, source_target_pairs={{0,1},{1,3},{3,2},{2,0},{4,5},{5,7},{7,6},{6,4},{8,9},{9,11},{11,1... | collective-permute-start | bytes 1572872 | tf_op jit(solution)/shard_map/ppermute | solution.py:391
  56.0 12.4 %collective-permute-start.13 = (bf16[128,2048]{1,0:T(8,128)(2,1)}, bf16[128,2048]{1,0:T(8,128)(2,1)}, u32[]{:S(2)}, u32[]{:S(2)}) collective-permute-start(bf16[128,2048]{1,0:T(8,128)(2,1)} %get-tuple-element.57.refs_0_), channel_id=1, source_target_pairs={{0,8},{4,12},{8,0},{12,4},{1,9},{5,13},{9,1},{13,5},{2,10},{6,14},... | collective-permute-start | bytes 1572872 | tf_op jit(solution)/shard_map/ppermute | solution.py:391
  56.5 12.9 %collective-permute-start.14 = (bf16[128,2048]{1,0:T(8,128)(2,1)}, bf16[128,2048]{1,0:T(8,128)(2,1)}, u32[]{:S(2)}, u32[]{:S(2)}) collective-permute-start(bf16[128,2048]{1,0:T(8,128)(2,1)} %get-tuple-element.57.refs_0_), channel_id=1, source_target_pairs={{0,1},{1,3},{3,2},{2,0},{4,5},{5,7},{7,6},{6,4},{8,9},{9,11},{11,1... | collective-permute-start | bytes 1572872 | tf_op jit(solution)/shard_map/ppermute | solution.py:391
  57.3 14.5 %collective-permute-start.17 = (bf16[128,2048]{1,0:T(8,128)(2,1)}, bf16[128,2048]{1,0:T(8,128)(2,1)}, u32[]{:S(2)}, u32[]{:S(2)}) collective-permute-start(bf16[128,2048]{1,0:T(8,128)(2,1)} %get-tuple-element.57.refs_0_), channel_id=1, source_target_pairs={{0,4},{4,0},{8,12},{12,8},{1,5},{5,1},{9,13},{13,9},{2,6},{6,2},{1... | collective-permute-start | bytes 1572872 | tf_op jit(solution)/shard_map/ppermute | solution.py:391
  69.4 14.7 %collective-permute-start.15 = (bf16[128,2048]{1,0:T(8,128)(2,1)}, bf16[128,2048]{1,0:T(8,128)(2,1)}, u32[]{:S(2)}, u32[]{:S(2)}) collective-permute-start(bf16[128,2048]{1,0:T(8,128)(2,1)} %get-tuple-element.58.refs_0_), channel_id=1, source_target_pairs={{0,8},{4,12},{8,0},{12,4},{1,9},{5,13},{9,1},{13,5},{2,10},{6,14},... | collective-permute-start | bytes 1572872 | tf_op jit(solution)/shard_map/ppermute | solution.py:391
  71.1 15.3 %collective-permute-start.16 = (bf16[128,2048]{1,0:T(8,128)(2,1)}, bf16[128,2048]{1,0:T(8,128)(2,1)}, u32[]{:S(2)}, u32[]{:S(2)}) collective-permute-start(bf16[128,2048]{1,0:T(8,128)(2,1)} %get-tuple-element.58.refs_0_), channel_id=1, source_target_pairs={{0,1},{1,3},{3,2},{2,0},{4,5},{5,7},{7,6},{6,4},{8,9},{9,11},{11,1... | collective-permute-start | bytes 1572872 | tf_op jit(solution)/shard_map/ppermute | solution.py:391
  86.4 9.9 %collective-permute-start.23 = (bf16[256,2048]{1,0:T(8,128)(2,1)S(1)}, bf16[256,2048]{1,0:T(8,128)(2,1)S(1)}, u32[]{:S(2)}, u32[]{:S(2)}) collective-permute-start(bf16[256,2048]{1,0:T(8,128)(2,1)S(1)} %get-tuple-element.65), channel_id=1, source_target_pairs={{0,4},{4,0},{8,12},{12,8},{1,5},{5,1},{9,13},{13,9},{2,6},{6,2},{1... | collective-permute-start | bytes 3145736 | tf_op jit(solution)/shard_map/ppermute | solution.py:391
  88.8 8.8 %collective-permute-start.19 = (bf16[128,1024]{1,0:T(8,128)(2,1)S(1)}, bf16[128,1024]{1,0:T(8,128)(2,1)S(1)}, u32[]{:S(2)}, u32[]{:S(2)}) collective-permute-start(bf16[128,1024]{1,0:T(8,128)(2,1)S(1)} %slice.54), channel_id=1, source_target_pairs={{0,8},{4,12},{8,0},{12,4},{1,9},{5,13},{9,1},{13,5},{2,10},{6,14},... | collective-permute-start | bytes 786440 | tf_op jit(solution)/shard_map/ppermute | solution.py:391
  89.2 9.5 %collective-permute-start.20 = (bf16[128,1024]{1,0:T(8,128)(2,1)S(1)}, bf16[128,1024]{1,0:T(8,128)(2,1)S(1)}, u32[]{:S(2)}, u32[]{:S(2)}) collective-permute-start(bf16[128,1024]{1,0:T(8,128)(2,1)S(1)} %slice.55), channel_id=1, source_target_pairs={{0,1},{1,3},{3,2},{2,0},{4,5},{5,7},{7,6},{6,4},{8,9},{9,11},{11,1... | collective-permute-start | bytes 786440 | tf_op jit(solution)/shard_map/ppermute | solution.py:391
  98.8 12.0 %collective-permute-start.29 = (bf16[256,2048]{1,0:T(8,128)(2,1)S(1)}, bf16[256,2048]{1,0:T(8,128)(2,1)S(1)}, u32[]{:S(2)}, u32[]{:S(2)}) collective-permute-start(bf16[256,2048]{1,0:T(8,128)(2,1)S(1)} %get-tuple-element.71), channel_id=1, source_target_pairs={{0,4},{4,0},{8,12},{12,8},{1,5},{5,1},{9,13},{13,9},{2,6},{6,2},{1... | collective-permute-start | bytes 3145736 | tf_op jit(solution)/shard_map/ppermute | solution.py:391
  98.8 4.0 %collective-permute-start.26 = (bf16[128,2048]{1,0:T(8,128)(2,1)}, bf16[128,2048]{1,0:T(8,128)(2,1)S(1)}, u32[]{:S(2)}, u32[]{:S(2)}) collective-permute-start(bf16[128,2048]{1,0:T(8,128)(2,1)} %get-tuple-element.61.refs_0_), channel_id=1, source_target_pairs={{0,4},{4,0},{8,12},{12,8},{1,5},{5,1},{9,13},{13,9},{2,6},{6,2},{1... | collective-permute-start | bytes 1572872 | tf_op jit(solution)/shard_map/ppermute | solution.py:391
  99.3 5.3 %collective-permute-start.28 = (bf16[128,1024]{1,0:T(8,128)(2,1)S(1)}, bf16[128,1024]{1,0:T(8,128)(2,1)S(1)}, u32[]{:S(2)}, u32[]{:S(2)}) collective-permute-start(bf16[128,1024]{1,0:T(8,128)(2,1)S(1)} %get-tuple-element.68.refs_3_), channel_id=1, source_target_pairs={{0,4},{4,0},{8,12},{12,8},{1,5},{5,1},{9,13},{13,9},{2,6},{6,2},{1... | collective-permute-start | bytes 786440 | tf_op jit(solution)/shard_map/ppermute | solution.py:391
  99.8 15.9 %collective-permute-start.9 = (bf16[128,2048]{1,0:T(8,128)(2,1)S(1)}, bf16[128,2048]{1,0:T(8,128)(2,1)S(1)}, u32[]{:S(2)}, u32[]{:S(2)}) collective-permute-start(bf16[128,2048]{1,0:T(8,128)(2,1)S(1)} %copy-done.3), channel_id=1, source_target_pairs={{0,4},{4,0},{8,12},{12,8},{1,5},{5,1},{9,13},{13,9},{2,6},{6,2},{1... | collective-permute-start | bytes 1572872 | tf_op jit(solution)/shard_map/ppermute | solution.py:391
  102.8 12.9 %collective-permute-start.12 = (bf16[128,2048]{1,0:T(8,128)(2,1)S(1)}, bf16[128,2048]{1,0:T(8,128)(2,1)S(1)}, u32[]{:S(2)}, u32[]{:S(2)}) collective-permute-start(bf16[128,2048]{1,0:T(8,128)(2,1)S(1)} %copy-done.5), channel_id=1, source_target_pairs={{0,4},{4,0},{8,12},{12,8},{1,5},{5,1},{9,13},{13,9},{2,6},{6,2},{1... | collective-permute-start | bytes 1572872 | tf_op jit(solution)/shard_map/ppermute | solution.py:391
  103.1 8.3 %collective-permute-start.24 = (bf16[128,1024]{1,0:T(8,128)(2,1)S(1)}, bf16[128,1024]{1,0:T(8,128)(2,1)S(1)}, u32[]{:S(2)}, u32[]{:S(2)}) collective-permute-start(bf16[128,1024]{1,0:T(8,128)(2,1)S(1)} %get-tuple-element.92), channel_id=1, source_target_pairs={{0,8},{4,12},{8,0},{12,4},{1,9},{5,13},{9,1},{13,5},{2,10},{6,14},... | collective-permute-start | bytes 786440 | tf_op jit(solution)/shard_map/ppermute | solution.py:391
  104.6 9.0 %collective-permute-start.25 = (bf16[128,1024]{1,0:T(8,128)(2,1)S(1)}, bf16[128,1024]{1,0:T(8,128)(2,1)S(1)}, u32[]{:S(2)}, u32[]{:S(2)}) collective-permute-start(bf16[128,1024]{1,0:T(8,128)(2,1)S(1)} %get-tuple-element.91), channel_id=1, source_target_pairs={{0,1},{1,3},{3,2},{2,0},{4,5},{5,7},{7,6},{6,4},{8,9},{9,11},{11,1... | collective-permute-start | bytes 786440 | tf_op jit(solution)/shard_map/ppermute | solution.py:391
  113.6 6.4 %collective-permute-start.32 = (bf16[256,2048]{1,0:T(8,128)(2,1)S(1)}, bf16[256,2048]{1,0:T(8,128)(2,1)S(1)}, u32[]{:S(2)}, u32[]{:S(2)}) collective-permute-start(bf16[256,2048]{1,0:T(8,128)(2,1)S(1)} %get-tuple-element.78), channel_id=1, source_target_pairs={{0,4},{4,0},{8,12},{12,8},{1,5},{5,1},{9,13},{13,9},{2,6},{6,2},{1... | collective-permute-start | bytes 3145736 | tf_op jit(solution)/shard_map/ppermute | solution.py:391
  113.7 14.4 %collective-permute-start.30 = (bf16[128,2048]{1,0:T(8,128)(2,1)S(1)}, bf16[128,2048]{1,0:T(8,128)(2,1)S(1)}, u32[]{:S(2)}, u32[]{:S(2)}) collective-permute-start(bf16[128,2048]{1,0:T(8,128)(2,1)S(1)} %pad_maximum_fusion), channel_id=1, source_target_pairs={{0,8},{4,12},{8,0},{12,4},{1,9},{5,13},{9,1},{13,5},{2,10},{6,14},... | collective-permute-start | bytes 1572872 | tf_op jit(solution)/shard_map/ppermute | solution.py:391
  114.6 15.2 %collective-permute-start.31 = (bf16[128,2048]{1,0:T(8,128)(2,1)S(1)}, bf16[128,2048]{1,0:T(8,128)(2,1)S(1)}, u32[]{:S(2)}, u32[]{:S(2)}) collective-permute-start(bf16[128,2048]{1,0:T(8,128)(2,1)S(1)} %pad_maximum_fusion.1), channel_id=1, source_target_pairs={{0,1},{1,3},{3,2},{2,0},{4,5},{5,7},{7,6},{6,4},{8,9},{9,11},{11,1... | collective-permute-start | bytes 1572872 | tf_op jit(solution)/shard_map/ppermute | solution.py:391
  129.9 14.3 %collective-permute-start.34 = (bf16[128,2048]{1,0:T(8,128)(2,1)S(1)}, bf16[128,2048]{1,0:T(8,128)(2,1)S(1)}, u32[]{:S(2)}, u32[]{:S(2)}) collective-permute-start(bf16[128,2048]{1,0:T(8,128)(2,1)S(1)} %get-tuple-element.80), channel_id=1, source_target_pairs={{0,8},{4,12},{8,0},{12,4},{1,9},{5,13},{9,1},{13,5},{2,10},{6,14},... | collective-permute-start | bytes 1572872 | tf_op jit(solution)/shard_map/ppermute | solution.py:391
  131.7 15.0 %collective-permute-start.35 = (bf16[128,2048]{1,0:T(8,128)(2,1)S(1)}, bf16[128,2048]{1,0:T(8,128)(2,1)S(1)}, u32[]{:S(2)}, u32[]{:S(2)}) collective-permute-start(bf16[128,2048]{1,0:T(8,128)(2,1)S(1)} %add_convert_fusion.3), channel_id=1, source_target_pairs={{0,1},{1,3},{3,2},{2,0},{4,5},{5,7},{7,6},{6,4},{8,9},{9,11},{11,1... | collective-permute-start | bytes 1572872 | tf_op jit(solution)/shard_map/ppermute | solution.py:391
  147.0 14.2 %collective-permute-start.37 = (bf16[128,2048]{1,0:T(8,128)(2,1)S(1)}, bf16[128,2048]{1,0:T(8,128)(2,1)S(1)}, u32[]{:S(2)}, u32[]{:S(2)}) collective-permute-start(bf16[128,2048]{1,0:T(8,128)(2,1)S(1)} %add_convert_fusion.1), channel_id=1, source_target_pairs={{0,1},{1,3},{3,2},{2,0},{4,5},{5,7},{7,6},{6,4},{8,9},{9,11},{11,1... | collective-permute-start | bytes 1572872 | tf_op jit(solution)/shard_map/ppermute | solution.py:391
  147.8 13.4 %collective-permute-start.36 = (bf16[128,2048]{1,0:T(8,128)(2,1)S(1)}, bf16[128,2048]{1,0:T(8,128)(2,1)S(1)}, u32[]{:S(2)}, u32[]{:S(2)}) collective-permute-start(bf16[128,2048]{1,0:T(8,128)(2,1)S(1)} %get-tuple-element.85), channel_id=1, source_target_pairs={{0,8},{4,12},{8,0},{12,4},{1,9},{5,13},{9,1},{13,5},{2,10},{6,14},... | collective-permute-start | bytes 1572872 | tf_op jit(solution)/shard_map/ppermute | solution.py:391
  (27 other events, 167.0 us)

commit v11 on v10

--- a/solution.py
+++ b/solution.py
@@ -108,30 +108,36 @@
     head_size = keys.shape[1]
     core = place_ref[0]
     query_start = pl.multiple_of(place_ref[1], head_size)
-    row_pos = place_ref[2] * rows + lax.broadcasted_iota(jnp.int32, (rows, 1), 0)
     lane = lax.broadcasted_iota(jnp.int32, (1, rows), 1)
     col_pos = jnp.concatenate([place_ref[3 + part] * rows + lane for part in range(4)], axis=1)
-    allowed = row_pos >= col_pos
     for part, kv_ref in enumerate(kv_refs):
         keys[part * rows : (part + 1) * rows, :] = kv_ref[0:rows, 0:head_size]
         values[part * rows : (part + 1) * rows, :] = kv_ref[0:rows, head_size:]
         quad_ref[:, part * rows : (part + 1) * rows] = kv_ref[rows:, 0:rows]
     key_block = keys[...]
     value_block = values[...]
-    for head in range(heads.shape[1] // head_size):
-        query = query_ref[:, pl.ds(query_start + head * head_size, head_size)]
-        scores = (
-            lax.dot_general(
-                query, key_block, (((1,), (1,)), ((), ())), preferred_element_type=jnp.float32
+    part = rows // 2
+    for start in range(0, rows, part):
+        row_pos = (
+            place_ref[2] * rows + start + lax.broadcasted_iota(jnp.int32, (part, 1), 0)
+        )
+        allowed = row_pos >= col_pos
+        for head in range(heads.shape[1] // head_size):
+            query = query_ref[
+                start : start + part, pl.ds(query_start + head * head_size, head_size)
+            ]
+            scores = (
+                lax.dot_general(
+                    query, key_block, (((1,), (1,)), ((), ())), preferred_element_type=jnp.float32
+                )
+                * scale
             )
-            * scale
-        )
-        scores = jnp.where(allowed, scores, -1e30)
-        weights = jnp.exp(scores - jnp.max(scores, axis=1, keepdims=True))
-        probs = (weights * (1.0 / jnp.sum(weights, axis=1, keepdims=True))).astype(jnp.bfloat16)
-        heads[:, head * head_size : (head + 1) * head_size] = jnp.dot(
-            probs, value_block, preferred_element_type=jnp.float32
-        ).astype(jnp.bfloat16)
+            scores = jnp.where(allowed, scores, -1e30)
+            weights = jnp.exp(scores - jnp.max(scores, axis=1, keepdims=True))
+            probs = (weights * (1.0 / jnp.sum(weights, axis=1, keepdims=True))).astype(jnp.bfloat16)
+            heads[start : start + part, head * head_size : (head + 1) * head_size] = jnp.dot(
+                probs, value_block, preferred_element_type=jnp.float32
+            ).astype(jnp.bfloat16)
     for fetch in fetches:
         fetch.wait()
     half = heads.shape[1] // 2
@@ -178,14 +184,16 @@
 
 def norm_kernel(own_ref, other_ref, gain_ref, *refs):
     hidden_ref, normed_ref = refs[-2:]
-    hidden = (own_ref[...] + other_ref[...].astype(jnp.float32)).astype(jnp.bfloat16)
-    hidden_ref[...] = hidden
-    wide = hidden.astype(jnp.float32)
-    normed_ref[...] = (
-        wide
-        * lax.rsqrt(jnp.mean(wide * wide, axis=1, keepdims=True) + 1e-06)
-        * gain_ref[...].astype(jnp.float32)
-    ).astype(jnp.bfloat16)
+    gain = gain_ref[...].astype(jnp.float32)
+    rows = 16
+    for start in range(0, own_ref.shape[0], rows):
+        part = slice(start, start + rows)
+        hidden = (own_ref[part, :] + other_ref[part, :].astype(jnp.float32)).astype(jnp.bfloat16)
+        hidden_ref[part, :] = hidden
+        wide = hidden.astype(jnp.float32)
+        normed_ref[part, :] = (
+            wide * lax.rsqrt(jnp.mean(wide * wide, axis=1, keepdims=True) + 1e-06) * gain
+        ).astype(jnp.bfloat16)
 
 
 def add_and_norm(own, other, gain, present):
@@ -331,7 +339,6 @@
     chip = place // 2
     twin = [(index, index ^ 1) for index in range(n_seq)]
     across = [(index, (index + 2) % n_seq) for index in range(n_seq)]
-    diagonal = [(index, (index ^ 1) ^ 2) for index in range(n_seq)]
     order = [0] + list(range(1, n_sub, 2)) + list(reversed(range(2, n_sub, 2)))
 
     def ring(steps):
@@ -351,11 +358,12 @@
         experts,
     )
     incoming = lax.ppermute(queries_away, "seq", across)
+    kv_across = lax.ppermute(kv_away, "seq", across)
     kv_parts = [
         kv_here,
         lax.ppermute(kv_here, "seq", twin),
-        lax.ppermute(kv_away, "seq", across),
-        lax.ppermute(kv_away, "seq", diagonal),
+        kv_across,
+        lax.ppermute(kv_across, "seq", twin),
     ]
     w_other = lax.ppermute(out_proj, "seq", twin)
     columns = [place, place ^ 1, place ^ 2, place ^ 3]

time: 163 us -> 167 us (1.025)
  starting transfers between devices: 29.3 us -> 21.8 us
  waiting for transfers between devices: 82.5 us -> 88.5 us
  Pallas kernels: 37.1 us -> 42.3 us
    ppermute x29, starting transfers between devices: 17.2 us -> 11.1 us  [move(): return lax.ppermute(array, *ways[way])]
    pallas_call x2, Pallas kernels: 11.6 us -> 16.9 us  [attend(): pl.pallas_call(functools.partial(attend_kernel, scale=1.0 / HD ** 0.5), i...]
    ppermute x29, waiting for transfers between devices: 74.8 us -> 79.4 us  [move(): return lax.ppermute(array, *ways[way])]
  transfers between devices with their start and end apart: 38 -> 38, of which waited for: 19 -> 21; matrix products, arithmetic and copies ran while one was open for 3% -> 3% of each run, Pallas kernels for 18% -> 19%
where the time goes in v11:
time: 167 us; the launch traced here: 166 us
  waiting for transfers between devices  88.5 us (53%)
  Pallas kernels  42.3 us (25%)
  starting transfers between devices  21.8 us (13%)
  local copies, waits for them, and re-layouts  10.5 us (6%)
  other arithmetic  2.76 us (2%)
    ppermute x29, waiting for transfers between devices, move(): return lax.ppermute(array, *ways[way])  79.4 us
    pallas_call x4, Pallas kernels, experts_on_rows(): pl.pallas_call(functools.partial(experts_kernel, cap=cap, pieces=pieces),...  21.1 us
    pallas_call x2, Pallas kernels, attend(): pl.pallas_call(functools.partial(attend_kernel, scale=1.0 / HD ** 0.5), i...  16.9 us
    ppermute x29, starting transfers between devices, move(): return lax.ppermute(array, *ways[way])  11.1 us
    ppermute x1, waiting for transfers between devices, gathered_plan(): kv_across = lax.ppermute(kv_away, 'seq', across)  8.5 us
    unnamed x42, local copies, waits for them, and re-layouts  6.64 us
    ppermute x3, starting transfers between devices, gathered_plan(): lax.ppermute(quad, 'sub', ring(steps))  5.63 us
  transfers between devices with their start and end apart: 38, of which 21 were waited for; matrix products, arithmetic and copies ran while one was open for 3% of the time, Pallas kernels for 19%

profile of v11, /device:TPU:0, one launch (start us, length us, event | category | flops | bytes accessed | tf_op | source)
XLA Modules:
  0.0 166.3 jit_solution(5040136436069451770)
XLA Ops:
  0.5 1.9 %shard_map.109 = (bf16[128,1024]{1,0:T(8,128)(2,1)}, bf16[144,256]{1,0:T(8,128)(2,1)}, bf16[144,256]{1,0:T(8,128)(2,1)}) custom-call(s32[1]{0:T(128)} %bitcast.7.chip_ref, bf16[128,2048]{1,0:T(8,128)(2,1)} %bitcast.35, bf16[128,256]{1,0:T(8,128)(2,1)} %bitcast.38, bf16[128,256]{1,0:T(8,128)(2,1)} %bitcast.39, s32[8,128]{1,0:T(8,128)} %bitcast.40, ...), custom_call_target="tpu_custom_call" | custom-call | tf_op jit(solution)/shard_map/pallas_call | solution.py:87
  2.3 2.5 %collective-permute-start.4 = (bf16[128,1024]{1,0:T(8,128)(2,1)}, bf16[128,1024]{1,0:T(8,128)(2,1)S(1)}, u32[]{:S(2)}, u32[]{:S(2)}) collective-permute-start(bf16[128,1024]{1,0:T(8,128)(2,1)} %get-tuple-element.50), channel_id=1, source_target_pairs={{0,8},{4,12},{8,0},{12,4},{1,9},{5,13},{9,1},{13,5},{2,10},{6,14},... | collective-permute-start | bytes 786440 | tf_op jit(solution)/shard_map/ppermute | solution.py:360
  5.1 8.5 %collective-permute-done.1.refs_2_ = bf16[144,256]{1,0:T(8,128)(2,1)S(1)} collective-permute-done((bf16[144,256]{1,0:T(8,128)(2,1)}, bf16[144,256]{1,0:T(8,128)(2,1)S(1)}, u32[]{:S(2)}, u32[]{:S(2)}) %collective-permute-start.1) | collective-permute-done | bytes 73760 | tf_op jit(solution)/shard_map/ppermute | solution.py:361
  16.9 8.2 %shard_map.111 = (bf16[128,2048]{1,0:T(8,128)(2,1)}, bf16[16,512]{1,0:T(8,128)(2,1)}) custom-call(s32[7]{0:T(128)} %stack.38.place_ref, bf16[128,1024]{1,0:T(8,128)(2,1)} %copy-done.19, bf16[144,256]{1,0:T(8,128)(2,1)} %get-tuple-element.47.refs_0_, bf16[144,256]{1,0:T(8,128)(2,1)} %copy-done.17, bf16[144,256]{1,0:T(8,128)(2,1)} %copy-done.16, ...), custom_call_target="tpu_custom_call" | custom-call | flops 805306368 | bytes 5242880 | tf_op jit(solution)/shard_map/pallas_call | solution.py:158
  25.1 1.8 %collective-permute-start.5 = (bf16[128,2048]{1,0:T(8,128)(2,1)}, bf16[128,2048]{1,0:T(8,128)(2,1)S(1)}, u32[]{:S(2)}, u32[]{:S(2)}) collective-permute-start(bf16[128,2048]{1,0:T(8,128)(2,1)} %get-tuple-element.51), channel_id=1, source_target_pairs={{0,8},{4,12},{8,0},{12,4},{1,9},{5,13},{9,1},{13,5},{2,10},{6,14},... | collective-permute-start | bytes 1572872 | tf_op jit(solution)/shard_map/ppermute | solution.py:377
  28.2 1.6 collective-permute-start.6
  29.8 2.5 %collective-permute-start.7 = (bf16[16,512]{1,0:T(8,128)(2,1)}, bf16[16,512]{1,0:T(8,128)(2,1)S(1)}, u32[]{:S(2)}, u32[]{:S(2)}) collective-permute-start(bf16[16,512]{1,0:T(8,128)(2,1)} %get-tuple-element.52.quad_ref), channel_id=1, source_target_pairs={{0,3},{1,2},{3,0},{2,1},{4,7},{5,6},{7,4},{6,5},{8,11},{9,10},{11,... | collective-permute-start | bytes 49160 | tf_op jit(solution)/shard_map/ppermute | solution.py:387
  32.2 1.6 collective-permute-start.8
  33.8 8.7 %shard_map.110 = (f32[128,2048]{1,0:T(8,128)}, bf16[16,512]{1,0:T(8,128)(2,1)}) custom-call(s32[7]{0:T(128)} %stack.37.place_ref, bf16[128,2048]{1,0:T(8,128)(2,1)} %bitcast.36, bf16[144,256]{1,0:T(8,128)(2,1)} %get-tuple-element.47.refs_0_, bf16[144,256]{1,0:T(8,128)(2,1)} %copy-done.17, bf16[144,256]{1,0:T(8,128)(2,1)} %copy-done.16, ...), custom_call_target="tpu_custom_call" | custom-call | flops 805306368 | bytes 5242880 | tf_op jit(solution)/shard_map/pallas_call | solution.py:158
  43.4 2.5 %shard_map.112 = (bf16[128,2048]{1,0:T(8,128)(2,1)}, bf16[128,2048]{1,0:T(8,128)(2,1)}) custom-call(f32[128,2048]{1,0:T(8,128)} %get-tuple-element.49.own_ref, bf16[128,2048]{1,0:T(8,128)(2,1)} %copy-done.14, bf16[1,2048]{1,0:T(2,128)(2,1)} %broadcast_in_dim.6.gain_ref, bf16[16,512]{1,0:T(8,128)(2,1)} %copy-done.10, bf16[16,512]{1,0:T(8,128)(2,1)} %copy-done.8, ...), custom_call_target="tpu_custom_call" | custom-call | tf_op jit(solution)/shard_map/pallas_call | solution.py:200
  46.9 12.1 %collective-permute-done.10.refs_0_ = bf16[128,2048]{1,0:T(8,128)(2,1)S(1)} collective-permute-done((bf16[128,2048]{1,0:T(8,128)(2,1)}, bf16[128,2048]{1,0:T(8,128)(2,1)S(1)}, u32[]{:S(2)}, u32[]{:S(2)}) %collective-permute-start.10) | collective-permute-done | bytes 524320 | tf_op jit(solution)/shard_map/ppermute | solution.py:399
  60.2 1.6 collective-permute-start.13
  61.8 10.5 %collective-permute-done.13.refs_0_ = bf16[128,2048]{1,0:T(8,128)(2,1)} collective-permute-done((bf16[128,2048]{1,0:T(8,128)(2,1)}, bf16[128,2048]{1,0:T(8,128)(2,1)}, u32[]{:S(2)}, u32[]{:S(2)}) %collective-permute-start.13) | collective-permute-done | bytes 524320 | tf_op jit(solution)/shard_map/ppermute | solution.py:399
  72.3 2.1 %collective-permute-done.14.refs_1_ = bf16[128,2048]{1,0:T(8,128)(2,1)} collective-permute-done((bf16[128,2048]{1,0:T(8,128)(2,1)}, bf16[128,2048]{1,0:T(8,128)(2,1)}, u32[]{:S(2)}, u32[]{:S(2)}) %collective-permute-start.14) | collective-permute-done | bytes 524320 | tf_op jit(solution)/shard_map/ppermute | solution.py:399
  75.0 1.7 %collective-permute-done.18.refs_3_ = bf16[128,2048]{1,0:T(8,128)(2,1)} collective-permute-done((bf16[128,2048]{1,0:T(8,128)(2,1)}, bf16[128,2048]{1,0:T(8,128)(2,1)}, u32[]{:S(2)}, u32[]{:S(2)}) %collective-permute-start.18) | collective-permute-done | bytes 524320 | tf_op jit(solution)/shard_map/ppermute | solution.py:399
  76.7 1.9 %copy-done.1 = bf16[1,2048,768]{2,1,0:T(8,128)(2,1)S(1)} copy-done((bf16[1,2048,768]{2,1,0:T(8,128)(2,1)S(1)}, bf16[1,2048,768]{2,1,0:T(8,128)(2,1)}, u32[]{:S(2)}) %copy-start.1) | copy-done | bytes 3145752
  78.6 1.9 %copy-done.2 = bf16[1,768,2048]{2,1,0:T(8,128)(2,1)S(1)} copy-done((bf16[1,768,2048]{2,1,0:T(8,128)(2,1)S(1)}, bf16[1,768,2048]{2,1,0:T(8,128)(2,1)}, u32[]{:S(2)}) %copy-start.2) | copy-done | bytes 3145752
  80.5 5.8 %shard_map.116 = (bf16[128,2048]{1,0:T(8,128)(2,1)S(1)}, bf16[128,2048]{1,0:T(8,128)(2,1)S(1)}, bf16[256,2048]{1,0:T(8,128)(2,1)S(1)}) custom-call(s32[1]{0:T(128)} %bitcast.15.mine_ref, bf16[16,512]{1,0:T(8,128)(2,1)S(1)} %copy-done.11, bf16[128,2048]{1,0:T(8,128)(2,1)} %get-tuple-element.57.refs_0_, bf16[128,2048]{1,0:T(8,128)(2,1)} %collective-permute-done.17.refs_1_, ...), custom_call_target="tpu_custom_call" | custom-call | flops 3019898880 | bytes 13631488 | tf_op jit(solution)/shard_map/pallas_call | solution.py:300
  86.3 2.8 %collective-permute-done.15.refs_0_ = bf16[128,2048]{1,0:T(8,128)(2,1)} collective-permute-done((bf16[128,2048]{1,0:T(8,128)(2,1)}, bf16[128,2048]{1,0:T(8,128)(2,1)}, u32[]{:S(2)}, u32[]{:S(2)}) %collective-permute-start.15) | collective-permute-done | bytes 524320 | tf_op jit(solution)/shard_map/ppermute | solution.py:399
  92.7 1.6 collective-permute-start.19
  94.6 5.5 %shard_map.118 = (bf16[128,2048]{1,0:T(8,128)(2,1)S(1)}, bf16[128,2048]{1,0:T(8,128)(2,1)S(1)}, bf16[256,2048]{1,0:T(8,128)(2,1)S(1)}) custom-call(s32[1]{0:T(128)} %bitcast.15.mine_ref, bf16[16,512]{1,0:T(8,128)(2,1)S(1)} %copy-done.9, bf16[128,2048]{1,0:T(8,128)(2,1)} %get-tuple-element.58.refs_0_, bf16[128,2048]{1,0:T(8,128)(2,1)S(1)} %collective-permute-done.21.refs_1_, ...), custom_call_target="tpu_custom_call" | custom-call | flops 3019898880 | bytes 13631488 | tf_op jit(solution)/shard_map/pallas_call | solution.py:300
  101.5 2.1 %collective-permute-done.20.refs_1_ = bf16[128,1024]{1,0:T(8,128)(2,1)S(1)} collective-permute-done((bf16[128,1024]{1,0:T(8,128)(2,1)S(1)}, bf16[128,1024]{1,0:T(8,128)(2,1)S(1)}, u32[]{:S(2)}, u32[]{:S(2)}) %collective-permute-start.20) | collective-permute-done | bytes 262176 | tf_op jit(solution)/shard_map/ppermute | solution.py:399
  104.7 2.9 %collective-permute-done.26.refs_1_ = bf16[128,2048]{1,0:T(8,128)(2,1)S(1)} collective-permute-done((bf16[128,2048]{1,0:T(8,128)(2,1)}, bf16[128,2048]{1,0:T(8,128)(2,1)S(1)}, u32[]{:S(2)}, u32[]{:S(2)}) %collective-permute-start.26) | collective-permute-done | bytes 524320 | tf_op jit(solution)/shard_map/ppermute | solution.py:399
  108.5 5.4 %shard_map.120 = (bf16[128,2048]{1,0:T(8,128)(2,1)S(1)}, bf16[128,2048]{1,0:T(8,128)(2,1)S(1)}, bf16[256,2048]{1,0:T(8,128)(2,1)S(1)}) custom-call(s32[1]{0:T(128)} %bitcast.15.mine_ref, bf16[16,512]{1,0:T(8,128)(2,1)S(1)} %copy-done.7, bf16[128,2048]{1,0:T(8,128)(2,1)} %get-tuple-element.61.refs_0_, bf16[128,2048]{1,0:T(8,128)(2,1)S(1)} %collective-permute-done.26.refs_1_, ...), custom_call_target="tpu_custom_call" | custom-call | flops 3019898880 | bytes 13631488 | tf_op jit(solution)/shard_map/pallas_call | solution.py:300
  114.0 2.3 %collective-permute-done.24.refs_0_ = bf16[128,1024]{1,0:T(8,128)(2,1)S(1)} collective-permute-done((bf16[128,1024]{1,0:T(8,128)(2,1)S(1)}, bf16[128,1024]{1,0:T(8,128)(2,1)S(1)}, u32[]{:S(2)}, u32[]{:S(2)}) %collective-permute-start.24) | collective-permute-done | bytes 262176 | tf_op jit(solution)/shard_map/ppermute | solution.py:399
  117.6 1.6 collective-permute-start.30
  119.8 4.3 %shard_map.114 = (bf16[128,2048]{1,0:T(8,128)(2,1)S(1)}, bf16[128,2048]{1,0:T(8,128)(2,1)S(1)}, bf16[256,2048]{1,0:T(8,128)(2,1)S(1)}) custom-call(s32[1]{0:T(128)} %bitcast.15.mine_ref, bf16[16,512]{1,0:T(8,128)(2,1)S(1)} %copy-done.12, bf16[128,2048]{1,0:T(8,128)(2,1)S(1)} %copy-done.3, bf16[128,2048]{1,0:T(8,128)(2,1)S(1)} %collective-permute-done.9.refs_1_, ...), custom_call_target="tpu_custom_call" | custom-call | flops 3019898880 | bytes 13631488 | tf_op jit(solution)/shard_map/pallas_call | solution.py:300
  124.3 7.8 %collective-permute-done.30.refs_0_ = bf16[128,2048]{1,0:T(8,128)(2,1)S(1)} collective-permute-done((bf16[128,2048]{1,0:T(8,128)(2,1)S(1)}, bf16[128,2048]{1,0:T(8,128)(2,1)S(1)}, u32[]{:S(2)}, u32[]{:S(2)}) %collective-permute-start.30) | collective-permute-done | bytes 524320 | tf_op jit(solution)/shard_map/ppermute | solution.py:399
  132.0 2.7 %collective-permute-done.31.refs_1_ = bf16[128,2048]{1,0:T(8,128)(2,1)S(1)} collective-permute-done((bf16[128,2048]{1,0:T(8,128)(2,1)S(1)}, bf16[128,2048]{1,0:T(8,128)(2,1)S(1)}, u32[]{:S(2)}, u32[]{:S(2)}) %collective-permute-start.31) | collective-permute-done | bytes 524320 | tf_op jit(solution)/shard_map/ppermute | solution.py:399
  135.6 1.7 %collective-permute-done.33 = bf16[256,2048]{1,0:T(8,128)(2,1)S(1)} collective-permute-done((bf16[256,2048]{1,0:T(8,128)(2,1)S(1)}, bf16[256,2048]{1,0:T(8,128)(2,1)S(1)}, u32[]{:S(2)}, u32[]{:S(2)}) %collective-permute-start.33) | collective-permute-done | bytes 1048608 | tf_op jit(solution)/shard_map/ppermute | solution.py:399
  137.5 11.5 %collective-permute-done.34.refs_0_ = bf16[128,2048]{1,0:T(8,128)(2,1)S(1)} collective-permute-done((bf16[128,2048]{1,0:T(8,128)(2,1)S(1)}, bf16[128,2048]{1,0:T(8,128)(2,1)S(1)}, u32[]{:S(2)}, u32[]{:S(2)}) %collective-permute-start.34) | collective-permute-done | bytes 524320 | tf_op jit(solution)/shard_map/ppermute | solution.py:399
  152.6 12.6 %collective-permute-done.37 = bf16[128,2048]{1,0:T(8,128)(2,1)S(1)} collective-permute-done((bf16[128,2048]{1,0:T(8,128)(2,1)S(1)}, bf16[128,2048]{1,0:T(8,128)(2,1)S(1)}, u32[]{:S(2)}, u32[]{:S(2)}) %collective-permute-start.37) | collective-permute-done | bytes 524320 | tf_op jit(solution)/shard_map/ppermute | solution.py:399
  (119 shorter events, 23.9 us)
Async XLA Ops:
  0.0 14.9 %collective-permute-start.3 = (bf16[512,2048]{1,0:T(8,128)(2,1)}, bf16[512,2048]{1,0:T(8,128)(2,1)S(1)}, u32[]{:S(2)}, u32[]{:S(2)}) collective-permute-start(bf16[512,2048]{1,0:T(8,128)(2,1)} %refs_4_.1), channel_id=1, source_target_pairs={{0,4},{4,0},{8,12},{12,8},{1,5},{5,1},{9,13},{13,9},{2,6},{6,2},{1... | collective-permute-start | bytes 6291464 | tf_op jit(solution)/shard_map/ppermute | solution.py:368
  2.3 12.6 %collective-permute-start.4 = (bf16[128,1024]{1,0:T(8,128)(2,1)}, bf16[128,1024]{1,0:T(8,128)(2,1)S(1)}, u32[]{:S(2)}, u32[]{:S(2)}) collective-permute-start(bf16[128,1024]{1,0:T(8,128)(2,1)} %get-tuple-element.50), channel_id=1, source_target_pairs={{0,8},{4,12},{8,0},{12,4},{1,9},{5,13},{9,1},{13,5},{2,10},{6,14},... | collective-permute-start | bytes 786440 | tf_op jit(solution)/shard_map/ppermute | solution.py:360
  4.9 8.8 %collective-permute-start.1 = (bf16[144,256]{1,0:T(8,128)(2,1)}, bf16[144,256]{1,0:T(8,128)(2,1)S(1)}, u32[]{:S(2)}, u32[]{:S(2)}) collective-permute-start(bf16[144,256]{1,0:T(8,128)(2,1)} %get-tuple-element.48), channel_id=1, source_target_pairs={{0,8},{4,12},{8,0},{12,4},{1,9},{5,13},{9,1},{13,5},{2,10},{6,14},... | collective-permute-start | bytes 221192 | tf_op jit(solution)/shard_map/ppermute | solution.py:361
  4.9 9.3 %collective-permute-start = (bf16[144,256]{1,0:T(8,128)(2,1)}, bf16[144,256]{1,0:T(8,128)(2,1)S(1)}, u32[]{:S(2)}, u32[]{:S(2)}) collective-permute-start(bf16[144,256]{1,0:T(8,128)(2,1)} %get-tuple-element.47.refs_0_), channel_id=1, source_target_pairs={{0,4},{4,0},{8,12},{12,8},{1,5},{5,1},{9,13},{13,9},{2,6},{6,2},{1... | collective-permute-start | bytes 221192 | tf_op jit(solution)/shard_map/ppermute | solution.py:364
  25.1 17.5 %collective-permute-start.5 = (bf16[128,2048]{1,0:T(8,128)(2,1)}, bf16[128,2048]{1,0:T(8,128)(2,1)S(1)}, u32[]{:S(2)}, u32[]{:S(2)}) collective-permute-start(bf16[128,2048]{1,0:T(8,128)(2,1)} %get-tuple-element.51), channel_id=1, source_target_pairs={{0,8},{4,12},{8,0},{12,4},{1,9},{5,13},{9,1},{13,5},{2,10},{6,14},... | collective-permute-start | bytes 1572872 | tf_op jit(solution)/shard_map/ppermute | solution.py:377
  28.2 14.3 %collective-permute-start.6 = (bf16[16,512]{1,0:T(8,128)(2,1)}, bf16[16,512]{1,0:T(8,128)(2,1)S(1)}, u32[]{:S(2)}, u32[]{:S(2)}) collective-permute-start(bf16[16,512]{1,0:T(8,128)(2,1)} %get-tuple-element.52.quad_ref), channel_id=1, source_target_pairs={{0,1},{1,3},{3,2},{2,0},{4,5},{5,7},{7,6},{6,4},{8,9},{9,11},{11,1... | collective-permute-start | bytes 49160 | tf_op jit(solution)/shard_map/ppermute | solution.py:387
  29.8 12.8 %collective-permute-start.7 = (bf16[16,512]{1,0:T(8,128)(2,1)}, bf16[16,512]{1,0:T(8,128)(2,1)S(1)}, u32[]{:S(2)}, u32[]{:S(2)}) collective-permute-start(bf16[16,512]{1,0:T(8,128)(2,1)} %get-tuple-element.52.quad_ref), channel_id=1, source_target_pairs={{0,3},{1,2},{3,0},{2,1},{4,7},{5,6},{7,4},{6,5},{8,11},{9,10},{11,... | collective-permute-start | bytes 49160 | tf_op jit(solution)/shard_map/ppermute | solution.py:387
  32.2 10.3 %collective-permute-start.8 = (bf16[16,512]{1,0:T(8,128)(2,1)}, bf16[16,512]{1,0:T(8,128)(2,1)S(1)}, u32[]{:S(2)}, u32[]{:S(2)}) collective-permute-start(bf16[16,512]{1,0:T(8,128)(2,1)} %get-tuple-element.52.quad_ref), channel_id=1, source_target_pairs={{0,2},{1,0},{3,1},{2,3},{4,6},{5,4},{7,5},{6,7},{8,10},{9,8},{11,9... | collective-permute-start | bytes 49160 | tf_op jit(solution)/shard_map/ppermute | solution.py:387
  45.9 13.1 %collective-permute-start.10 = (bf16[128,2048]{1,0:T(8,128)(2,1)}, bf16[128,2048]{1,0:T(8,128)(2,1)S(1)}, u32[]{:S(2)}, u32[]{:S(2)}) collective-permute-start(bf16[128,2048]{1,0:T(8,128)(2,1)} %get-tuple-element.54.refs_0_), channel_id=1, source_target_pairs={{0,8},{4,12},{8,0},{12,4},{1,9},{5,13},{9,1},{13,5},{2,10},{6,14},... | collective-permute-start | bytes 1572872 | tf_op jit(solution)/shard_map/ppermute | solution.py:399
  46.4 13.8 %collective-permute-start.11 = (bf16[128,2048]{1,0:T(8,128)(2,1)}, bf16[128,2048]{1,0:T(8,128)(2,1)}, u32[]{:S(2)}, u32[]{:S(2)}) collective-permute-start(bf16[128,2048]{1,0:T(8,128)(2,1)} %get-tuple-element.54.refs_0_), channel_id=1, source_target_pairs={{0,1},{1,3},{3,2},{2,0},{4,5},{5,7},{7,6},{6,4},{8,9},{9,11},{11,1... | collective-permute-start | bytes 1572872 | tf_op jit(solution)/shard_map/ppermute | solution.py:399
  60.2 12.1 %collective-permute-start.13 = (bf16[128,2048]{1,0:T(8,128)(2,1)}, bf16[128,2048]{1,0:T(8,128)(2,1)}, u32[]{:S(2)}, u32[]{:S(2)}) collective-permute-start(bf16[128,2048]{1,0:T(8,128)(2,1)} %get-tuple-element.57.refs_0_), channel_id=1, source_target_pairs={{0,8},{4,12},{8,0},{12,4},{1,9},{5,13},{9,1},{13,5},{2,10},{6,14},... | collective-permute-start | bytes 1572872 | tf_op jit(solution)/shard_map/ppermute | solution.py:399
  61.8 12.6 %collective-permute-start.14 = (bf16[128,2048]{1,0:T(8,128)(2,1)}, bf16[128,2048]{1,0:T(8,128)(2,1)}, u32[]{:S(2)}, u32[]{:S(2)}) collective-permute-start(bf16[128,2048]{1,0:T(8,128)(2,1)} %get-tuple-element.57.refs_0_), channel_id=1, source_target_pairs={{0,1},{1,3},{3,2},{2,0},{4,5},{5,7},{7,6},{6,4},{8,9},{9,11},{11,1... | collective-permute-start | bytes 1572872 | tf_op jit(solution)/shard_map/ppermute | solution.py:399
  61.8 13.1 %collective-permute-start.17 = (bf16[128,2048]{1,0:T(8,128)(2,1)}, bf16[128,2048]{1,0:T(8,128)(2,1)}, u32[]{:S(2)}, u32[]{:S(2)}) collective-permute-start(bf16[128,2048]{1,0:T(8,128)(2,1)} %get-tuple-element.57.refs_0_), channel_id=1, source_target_pairs={{0,4},{4,0},{8,12},{12,8},{1,5},{5,1},{9,13},{13,9},{2,6},{6,2},{1... | collective-permute-start | bytes 1572872 | tf_op jit(solution)/shard_map/ppermute | solution.py:399
  74.4 14.7 %collective-permute-start.15 = (bf16[128,2048]{1,0:T(8,128)(2,1)}, bf16[128,2048]{1,0:T(8,128)(2,1)}, u32[]{:S(2)}, u32[]{:S(2)}) collective-permute-start(bf16[128,2048]{1,0:T(8,128)(2,1)} %get-tuple-element.58.refs_0_), channel_id=1, source_target_pairs={{0,8},{4,12},{8,0},{12,4},{1,9},{5,13},{9,1},{13,5},{2,10},{6,14},... | collective-permute-start | bytes 1572872 | tf_op jit(solution)/shard_map/ppermute | solution.py:399
  75.0 15.3 %collective-permute-start.16 = (bf16[128,2048]{1,0:T(8,128)(2,1)}, bf16[128,2048]{1,0:T(8,128)(2,1)}, u32[]{:S(2)}, u32[]{:S(2)}) collective-permute-start(bf16[128,2048]{1,0:T(8,128)(2,1)} %get-tuple-element.58.refs_0_), channel_id=1, source_target_pairs={{0,1},{1,3},{3,2},{2,0},{4,5},{5,7},{7,6},{6,4},{8,9},{9,11},{11,1... | collective-permute-start | bytes 1572872 | tf_op jit(solution)/shard_map/ppermute | solution.py:399
  90.2 9.9 %collective-permute-start.23 = (bf16[256,2048]{1,0:T(8,128)(2,1)S(1)}, bf16[256,2048]{1,0:T(8,128)(2,1)S(1)}, u32[]{:S(2)}, u32[]{:S(2)}) collective-permute-start(bf16[256,2048]{1,0:T(8,128)(2,1)S(1)} %get-tuple-element.65), channel_id=1, source_target_pairs={{0,4},{4,0},{8,12},{12,8},{1,5},{5,1},{9,13},{13,9},{2,6},{6,2},{1... | collective-permute-start | bytes 3145736 | tf_op jit(solution)/shard_map/ppermute | solution.py:399
  90.2 4.0 %collective-permute-start.21 = (bf16[128,2048]{1,0:T(8,128)(2,1)}, bf16[128,2048]{1,0:T(8,128)(2,1)S(1)}, u32[]{:S(2)}, u32[]{:S(2)}) collective-permute-start(bf16[128,2048]{1,0:T(8,128)(2,1)} %get-tuple-element.58.refs_0_), channel_id=1, source_target_pairs={{0,4},{4,0},{8,12},{12,8},{1,5},{5,1},{9,13},{13,9},{2,6},{6,2},{1... | collective-permute-start | bytes 1572872 | tf_op jit(solution)/shard_map/ppermute | solution.py:399
  92.7 8.8 %collective-permute-start.19 = (bf16[128,1024]{1,0:T(8,128)(2,1)S(1)}, bf16[128,1024]{1,0:T(8,128)(2,1)S(1)}, u32[]{:S(2)}, u32[]{:S(2)}) collective-permute-start(bf16[128,1024]{1,0:T(8,128)(2,1)S(1)} %slice.54), channel_id=1, source_target_pairs={{0,8},{4,12},{8,0},{12,4},{1,9},{5,13},{9,1},{13,5},{2,10},{6,14},... | collective-permute-start | bytes 786440 | tf_op jit(solution)/shard_map/ppermute | solution.py:399
  94.3 9.3 %collective-permute-start.20 = (bf16[128,1024]{1,0:T(8,128)(2,1)S(1)}, bf16[128,1024]{1,0:T(8,128)(2,1)S(1)}, u32[]{:S(2)}, u32[]{:S(2)}) collective-permute-start(bf16[128,1024]{1,0:T(8,128)(2,1)S(1)} %slice.55), channel_id=1, source_target_pairs={{0,1},{1,3},{3,2},{2,0},{4,5},{5,7},{7,6},{6,4},{8,9},{9,11},{11,1... | collective-permute-start | bytes 786440 | tf_op jit(solution)/shard_map/ppermute | solution.py:399
  103.6 10.3 %collective-permute-start.29 = (bf16[256,2048]{1,0:T(8,128)(2,1)S(1)}, bf16[256,2048]{1,0:T(8,128)(2,1)S(1)}, u32[]{:S(2)}, u32[]{:S(2)}) collective-permute-start(bf16[256,2048]{1,0:T(8,128)(2,1)S(1)} %get-tuple-element.71), channel_id=1, source_target_pairs={{0,4},{4,0},{8,12},{12,8},{1,5},{5,1},{9,13},{13,9},{2,6},{6,2},{1... | collective-permute-start | bytes 3145736 | tf_op jit(solution)/shard_map/ppermute | solution.py:399
  104.1 4.4 %collective-permute-start.28 = (bf16[128,1024]{1,0:T(8,128)(2,1)S(1)}, bf16[128,1024]{1,0:T(8,128)(2,1)S(1)}, u32[]{:S(2)}, u32[]{:S(2)}) collective-permute-start(bf16[128,1024]{1,0:T(8,128)(2,1)S(1)} %get-tuple-element.68.refs_3_), channel_id=1, source_target_pairs={{0,4},{4,0},{8,12},{12,8},{1,5},{5,1},{9,13},{13,9},{2,6},{6,2},{1... | collective-permute-start | bytes 786440 | tf_op jit(solution)/shard_map/ppermute | solution.py:399
  104.6 15.1 %collective-permute-start.9 = (bf16[128,2048]{1,0:T(8,128)(2,1)S(1)}, bf16[128,2048]{1,0:T(8,128)(2,1)S(1)}, u32[]{:S(2)}, u32[]{:S(2)}) collective-permute-start(bf16[128,2048]{1,0:T(8,128)(2,1)S(1)} %copy-done.3), channel_id=1, source_target_pairs={{0,4},{4,0},{8,12},{12,8},{1,5},{5,1},{9,13},{13,9},{2,6},{6,2},{1... | collective-permute-start | bytes 1572872 | tf_op jit(solution)/shard_map/ppermute | solution.py:399
  107.6 12.2 %collective-permute-start.12 = (bf16[128,2048]{1,0:T(8,128)(2,1)S(1)}, bf16[128,2048]{1,0:T(8,128)(2,1)S(1)}, u32[]{:S(2)}, u32[]{:S(2)}) collective-permute-start(bf16[128,2048]{1,0:T(8,128)(2,1)S(1)} %copy-done.5), channel_id=1, source_target_pairs={{0,4},{4,0},{8,12},{12,8},{1,5},{5,1},{9,13},{13,9},{2,6},{6,2},{1... | collective-permute-start | bytes 1572872 | tf_op jit(solution)/shard_map/ppermute | solution.py:399
  108.0 8.3 %collective-permute-start.24 = (bf16[128,1024]{1,0:T(8,128)(2,1)S(1)}, bf16[128,1024]{1,0:T(8,128)(2,1)S(1)}, u32[]{:S(2)}, u32[]{:S(2)}) collective-permute-start(bf16[128,1024]{1,0:T(8,128)(2,1)S(1)} %get-tuple-element.92), channel_id=1, source_target_pairs={{0,8},{4,12},{8,0},{12,4},{1,9},{5,13},{9,1},{13,5},{2,10},{6,14},... | collective-permute-start | bytes 786440 | tf_op jit(solution)/shard_map/ppermute | solution.py:399
  108.5 9.0 %collective-permute-start.25 = (bf16[128,1024]{1,0:T(8,128)(2,1)S(1)}, bf16[128,1024]{1,0:T(8,128)(2,1)S(1)}, u32[]{:S(2)}, u32[]{:S(2)}) collective-permute-start(bf16[128,1024]{1,0:T(8,128)(2,1)S(1)} %get-tuple-element.91), channel_id=1, source_target_pairs={{0,1},{1,3},{3,2},{2,0},{4,5},{5,7},{7,6},{6,4},{8,9},{9,11},{11,1... | collective-permute-start | bytes 786440 | tf_op jit(solution)/shard_map/ppermute | solution.py:399
  117.5 6.7 %collective-permute-start.32 = (bf16[256,2048]{1,0:T(8,128)(2,1)S(1)}, bf16[256,2048]{1,0:T(8,128)(2,1)S(1)}, u32[]{:S(2)}, u32[]{:S(2)}) collective-permute-start(bf16[256,2048]{1,0:T(8,128)(2,1)S(1)} %get-tuple-element.78), channel_id=1, source_target_pairs={{0,4},{4,0},{8,12},{12,8},{1,5},{5,1},{9,13},{13,9},{2,6},{6,2},{1... | collective-permute-start | bytes 3145736 | tf_op jit(solution)/shard_map/ppermute | solution.py:399
  117.6 14.4 %collective-permute-start.30 = (bf16[128,2048]{1,0:T(8,128)(2,1)S(1)}, bf16[128,2048]{1,0:T(8,128)(2,1)S(1)}, u32[]{:S(2)}, u32[]{:S(2)}) collective-permute-start(bf16[128,2048]{1,0:T(8,128)(2,1)S(1)} %pad_maximum_fusion), channel_id=1, source_target_pairs={{0,8},{4,12},{8,0},{12,4},{1,9},{5,13},{9,1},{13,5},{2,10},{6,14},... | collective-permute-start | bytes 1572872 | tf_op jit(solution)/shard_map/ppermute | solution.py:399
  119.5 15.2 %collective-permute-start.31 = (bf16[128,2048]{1,0:T(8,128)(2,1)S(1)}, bf16[128,2048]{1,0:T(8,128)(2,1)S(1)}, u32[]{:S(2)}, u32[]{:S(2)}) collective-permute-start(bf16[128,2048]{1,0:T(8,128)(2,1)S(1)} %pad_maximum_fusion.1), channel_id=1, source_target_pairs={{0,1},{1,3},{3,2},{2,0},{4,5},{5,7},{7,6},{6,4},{8,9},{9,11},{11,1... | collective-permute-start | bytes 1572872 | tf_op jit(solution)/shard_map/ppermute | solution.py:399
  134.7 14.3 %collective-permute-start.34 = (bf16[128,2048]{1,0:T(8,128)(2,1)S(1)}, bf16[128,2048]{1,0:T(8,128)(2,1)S(1)}, u32[]{:S(2)}, u32[]{:S(2)}) collective-permute-start(bf16[128,2048]{1,0:T(8,128)(2,1)S(1)} %get-tuple-element.80), channel_id=1, source_target_pairs={{0,8},{4,12},{8,0},{12,4},{1,9},{5,13},{9,1},{13,5},{2,10},{6,14},... | collective-permute-start | bytes 1572872 | tf_op jit(solution)/shard_map/ppermute | solution.py:399
  135.6 15.0 %collective-permute-start.35 = (bf16[128,2048]{1,0:T(8,128)(2,1)S(1)}, bf16[128,2048]{1,0:T(8,128)(2,1)S(1)}, u32[]{:S(2)}, u32[]{:S(2)}) collective-permute-start(bf16[128,2048]{1,0:T(8,128)(2,1)S(1)} %add_convert_fusion.3), channel_id=1, source_target_pairs={{0,1},{1,3},{3,2},{2,0},{4,5},{5,7},{7,6},{6,4},{8,9},{9,11},{11,1... | collective-permute-start | bytes 1572872 | tf_op jit(solution)/shard_map/ppermute | solution.py:399
  150.9 14.2 %collective-permute-start.37 = (bf16[128,2048]{1,0:T(8,128)(2,1)S(1)}, bf16[128,2048]{1,0:T(8,128)(2,1)S(1)}, u32[]{:S(2)}, u32[]{:S(2)}) collective-permute-start(bf16[128,2048]{1,0:T(8,128)(2,1)S(1)} %add_convert_fusion.1), channel_id=1, source_target_pairs={{0,1},{1,3},{3,2},{2,0},{4,5},{5,7},{7,6},{6,4},{8,9},{9,11},{11,1... | collective-permute-start | bytes 1572872 | tf_op jit(solution)/shard_map/ppermute | solution.py:399
  151.0 14.1 %collective-permute-start.36 = (bf16[128,2048]{1,0:T(8,128)(2,1)S(1)}, bf16[128,2048]{1,0:T(8,128)(2,1)S(1)}, u32[]{:S(2)}, u32[]{:S(2)}) collective-permute-start(bf16[128,2048]{1,0:T(8,128)(2,1)S(1)} %get-tuple-element.85), channel_id=1, source_target_pairs={{0,8},{4,12},{8,0},{12,4},{1,9},{5,13},{9,1},{13,5},{2,10},{6,14},... | collective-permute-start | bytes 1572872 | tf_op jit(solution)/shard_map/ppermute | solution.py:399
  (27 other events, 164.0 us)

commit v12 on v10

--- a/solution.py
+++ b/solution.py
@@ -96,8 +96,9 @@
 
 def attend_kernel(place_ref, query_ref, *refs, scale):
     kv_refs, refs = refs[:4], refs[4:]
-    base_refs = refs[: len(refs) - 10]
-    w_own_ref, w_other_ref, out_ref, quad_ref, keys, values, heads, w_own, w_other, done = refs[-10:]
+    base_refs = refs[: len(refs) - 13]
+    w_own_ref, w_other_ref, out_ref, quad_ref, keys, values, heads = refs[-13:-6]
+    w_own, w_other, stacked, scores, probs, done = refs[-6:]
     fetches = [
         pltpu.make_async_copy(w_own_ref, w_own, done.at[0]),
         pltpu.make_async_copy(w_other_ref, w_other, done.at[1]),
@@ -118,20 +119,26 @@
         quad_ref[:, part * rows : (part + 1) * rows] = kv_ref[rows:, 0:rows]
     key_block = keys[...]
     value_block = values[...]
-    for head in range(heads.shape[1] // head_size):
-        query = query_ref[:, pl.ds(query_start + head * head_size, head_size)]
-        scores = (
-            lax.dot_general(
-                query, key_block, (((1,), (1,)), ((), ())), preferred_element_type=jnp.float32
-            )
-            * scale
-        )
-        scores = jnp.where(allowed, scores, -1e30)
-        weights = jnp.exp(scores - jnp.max(scores, axis=1, keepdims=True))
-        probs = (weights * (1.0 / jnp.sum(weights, axis=1, keepdims=True))).astype(jnp.bfloat16)
-        heads[:, head * head_size : (head + 1) * head_size] = jnp.dot(
-            probs, value_block, preferred_element_type=jnp.float32
-        ).astype(jnp.bfloat16)
+    count = heads.shape[1] // head_size
+    for head in range(count):
+        stacked[head * rows : (head + 1) * rows, :] = query_ref[
+            :, pl.ds(query_start + head * head_size, head_size)
+        ]
+    scores[...] = lax.dot_general(
+        stacked[...], key_block, (((1,), (1,)), ((), ())), preferred_element_type=jnp.float32
+    )
+    for head in range(count):
+        part = slice(head * rows, (head + 1) * rows)
+        score = jnp.where(allowed, scores[part, :] * scale, -1e30)
+        weights = jnp.exp(score - jnp.max(score, axis=1, keepdims=True))
+        probs[part, :] = (weights * (1.0 / jnp.sum(weights, axis=1, keepdims=True))).astype(
+            jnp.bfloat16
+        )
+    mixed = jnp.dot(probs[...], value_block, preferred_element_type=jnp.float32)
+    for head in range(count):
+        heads[:, head * head_size : (head + 1) * head_size] = mixed[
+            head * rows : (head + 1) * rows
+        ].astype(jnp.bfloat16)
     for fetch in fetches:
         fetch.wait()
     half = heads.shape[1] // 2
@@ -165,6 +172,9 @@
             pltpu.VMEM((tokens, chip_width), jnp.bfloat16),
             pltpu.VMEM(w_own.shape, jnp.bfloat16),
             pltpu.VMEM(w_other.shape, jnp.bfloat16),
+            pltpu.VMEM((tokens * chip_width // HD, HD), jnp.bfloat16),
+            pltpu.VMEM((tokens * chip_width // HD, 4 * tokens), jnp.float32),
+            pltpu.VMEM((tokens * chip_width // HD, 4 * tokens), jnp.bfloat16),
             pltpu.SemaphoreType.DMA((2,)),
         ],
         compiler_params=pltpu.CompilerParams(vmem_limit_bytes=60 * MIB),

time: 163 us -> 163 us (level)
  no operation moved by 1% of the time
where the time goes in v12:
time: 163 us; the launch traced here: 162 us
  waiting for transfers between devices  82.4 us (51%)
  Pallas kernels  36.8 us (23%)
  starting transfers between devices  29.5 us (18%)
  local copies, waits for them, and re-layouts  10.5 us (6%)
  other arithmetic  2.76 us (2%)
    ppermute x29, waiting for transfers between devices, move(): return lax.ppermute(array, *ways[way])  74.7 us
    pallas_call x4, Pallas kernels, experts_on_rows(): pl.pallas_call(functools.partial(experts_kernel, cap=cap, pieces=pieces),...  21.1 us
    ppermute x29, starting transfers between devices, move(): return lax.ppermute(array, *ways[way])  17.4 us
    pallas_call x2, Pallas kernels, attend(): pl.pallas_call(functools.partial(attend_kernel, scale=1.0 / HD ** 0.5), i...  11.3 us
    unnamed x42, local copies, waits for them, and re-layouts  6.63 us
    ppermute x1, waiting for transfers between devices, gathered_plan(): lax.ppermute(kv_away, 'seq', across)  6.47 us
    ppermute x3, starting transfers between devices, gathered_plan(): lax.ppermute(quad, 'sub', ring(steps))  5.63 us
  transfers between devices with their start and end apart: 38, of which 19 were waited for; matrix products, arithmetic and copies ran while one was open for 3% of the time, Pallas kernels for 18%

profile of v12, /device:TPU:0, one launch (start us, length us, event | category | flops | bytes accessed | tf_op | source)
XLA Modules:
  0.0 162.3 jit_solution(9498074629209879109)
XLA Ops:
  0.5 1.9 %shard_map.109 = (bf16[128,1024]{1,0:T(8,128)(2,1)}, bf16[144,256]{1,0:T(8,128)(2,1)}, bf16[144,256]{1,0:T(8,128)(2,1)}) custom-call(s32[1]{0:T(128)} %bitcast.7.chip_ref, bf16[128,2048]{1,0:T(8,128)(2,1)} %bitcast.35, bf16[128,256]{1,0:T(8,128)(2,1)} %bitcast.38, bf16[128,256]{1,0:T(8,128)(2,1)} %bitcast.39, s32[8,128]{1,0:T(8,128)} %bitcast.40, ...), custom_call_target="tpu_custom_call" | custom-call | tf_op jit(solution)/shard_map/pallas_call | solution.py:87
  2.3 2.5 %collective-permute-start.4 = (bf16[128,1024]{1,0:T(8,128)(2,1)}, bf16[128,1024]{1,0:T(8,128)(2,1)S(1)}, u32[]{:S(2)}, u32[]{:S(2)}) collective-permute-start(bf16[128,1024]{1,0:T(8,128)(2,1)} %get-tuple-element.50), channel_id=1, source_target_pairs={{0,8},{4,12},{8,0},{12,4},{1,9},{5,13},{9,1},{13,5},{2,10},{6,14},... | collective-permute-start | bytes 786440 | tf_op jit(solution)/shard_map/ppermute | solution.py:363
  7.3 6.5 %collective-permute-done.1.refs_2_ = bf16[144,256]{1,0:T(8,128)(2,1)S(1)} collective-permute-done((bf16[144,256]{1,0:T(8,128)(2,1)}, bf16[144,256]{1,0:T(8,128)(2,1)S(1)}, u32[]{:S(2)}, u32[]{:S(2)}) %collective-permute-start.1) | collective-permute-done | bytes 73760 | tf_op jit(solution)/shard_map/ppermute | solution.py:367
  17.1 5.4 %shard_map.111 = (bf16[128,2048]{1,0:T(8,128)(2,1)}, bf16[16,512]{1,0:T(8,128)(2,1)}) custom-call(s32[7]{0:T(128)} %stack.38.place_ref, bf16[128,1024]{1,0:T(8,128)(2,1)} %copy-done.19, bf16[144,256]{1,0:T(8,128)(2,1)} %get-tuple-element.47.refs_0_, bf16[144,256]{1,0:T(8,128)(2,1)} %copy-done.16, bf16[144,256]{1,0:T(8,128)(2,1)} %copy-done.17, ...), custom_call_target="tpu_custom_call" | custom-call | flops 805306368 | bytes 5242880 | tf_op jit(solution)/shard_map/pallas_call | solution.py:159
  22.5 1.6 collective-permute-start.5
  25.3 1.6 collective-permute-start.6
  26.9 2.5 %collective-permute-start.7 = (bf16[16,512]{1,0:T(8,128)(2,1)}, bf16[16,512]{1,0:T(8,128)(2,1)S(1)}, u32[]{:S(2)}, u32[]{:S(2)}) collective-permute-start(bf16[16,512]{1,0:T(8,128)(2,1)} %get-tuple-element.52.quad_ref), channel_id=1, source_target_pairs={{0,3},{1,2},{3,0},{2,1},{4,7},{5,6},{7,4},{6,5},{8,11},{9,10},{11,... | collective-permute-start | bytes 49160 | tf_op jit(solution)/shard_map/ppermute | solution.py:389
  29.4 1.6 collective-permute-start.8
  31.0 5.9 %shard_map.110 = (f32[128,2048]{1,0:T(8,128)}, bf16[16,512]{1,0:T(8,128)(2,1)}) custom-call(s32[7]{0:T(128)} %stack.37.place_ref, bf16[128,2048]{1,0:T(8,128)(2,1)} %bitcast.36, bf16[144,256]{1,0:T(8,128)(2,1)} %get-tuple-element.47.refs_0_, bf16[144,256]{1,0:T(8,128)(2,1)} %copy-done.16, bf16[144,256]{1,0:T(8,128)(2,1)} %copy-done.17, ...), custom_call_target="tpu_custom_call" | custom-call | flops 805306368 | bytes 5242880 | tf_op jit(solution)/shard_map/pallas_call | solution.py:159
  37.7 2.5 %shard_map.112 = (bf16[128,2048]{1,0:T(8,128)(2,1)}, bf16[128,2048]{1,0:T(8,128)(2,1)}) custom-call(f32[128,2048]{1,0:T(8,128)} %get-tuple-element.49.own_ref, bf16[128,2048]{1,0:T(8,128)(2,1)} %copy-done.14, bf16[1,2048]{1,0:T(2,128)(2,1)} %broadcast_in_dim.6.gain_ref, bf16[16,512]{1,0:T(8,128)(2,1)} %copy-done.10, bf16[16,512]{1,0:T(8,128)(2,1)} %copy-done.8, ...), custom_call_target="tpu_custom_call" | custom-call | tf_op jit(solution)/shard_map/pallas_call | solution.py:202
  41.6 1.6 collective-permute-start.11
  43.2 10.1 %collective-permute-done.10.refs_0_ = bf16[128,2048]{1,0:T(8,128)(2,1)S(1)} collective-permute-done((bf16[128,2048]{1,0:T(8,128)(2,1)}, bf16[128,2048]{1,0:T(8,128)(2,1)S(1)}, u32[]{:S(2)}, u32[]{:S(2)}) %collective-permute-start.10) | collective-permute-done | bytes 524320 | tf_op jit(solution)/shard_map/ppermute | solution.py:401
  53.4 2.5 %collective-permute-done.11.refs_1_ = bf16[128,2048]{1,0:T(8,128)(2,1)} collective-permute-done((bf16[128,2048]{1,0:T(8,128)(2,1)}, bf16[128,2048]{1,0:T(8,128)(2,1)}, u32[]{:S(2)}, u32[]{:S(2)}) %collective-permute-start.11) | collective-permute-done | bytes 524320 | tf_op jit(solution)/shard_map/ppermute | solution.py:401
  57.1 11.1 %collective-permute-done.13.refs_0_ = bf16[128,2048]{1,0:T(8,128)(2,1)} collective-permute-done((bf16[128,2048]{1,0:T(8,128)(2,1)}, bf16[128,2048]{1,0:T(8,128)(2,1)}, u32[]{:S(2)}, u32[]{:S(2)}) %collective-permute-start.13) | collective-permute-done | bytes 524320 | tf_op jit(solution)/shard_map/ppermute | solution.py:401
  69.2 1.7 %collective-permute-start.15 = (bf16[128,2048]{1,0:T(8,128)(2,1)}, bf16[128,2048]{1,0:T(8,128)(2,1)}, u32[]{:S(2)}, u32[]{:S(2)}) collective-permute-start(bf16[128,2048]{1,0:T(8,128)(2,1)} %get-tuple-element.58.refs_0_), channel_id=1, source_target_pairs={{0,8},{4,12},{8,0},{12,4},{1,9},{5,13},{9,1},{13,5},{2,10},{6,14},... | collective-permute-start | bytes 1572872 | tf_op jit(solution)/shard_map/ppermute | solution.py:401
  71.7 1.9 %copy-done.1 = bf16[1,2048,768]{2,1,0:T(8,128)(2,1)S(1)} copy-done((bf16[1,2048,768]{2,1,0:T(8,128)(2,1)S(1)}, bf16[1,2048,768]{2,1,0:T(8,128)(2,1)}, u32[]{:S(2)}) %copy-start.1) | copy-done | bytes 3145752
  73.6 1.9 %copy-done.2 = bf16[1,768,2048]{2,1,0:T(8,128)(2,1)S(1)} copy-done((bf16[1,768,2048]{2,1,0:T(8,128)(2,1)S(1)}, bf16[1,768,2048]{2,1,0:T(8,128)(2,1)}, u32[]{:S(2)}) %copy-start.2) | copy-done | bytes 3145752
  75.5 5.8 %shard_map.116 = (bf16[128,2048]{1,0:T(8,128)(2,1)S(1)}, bf16[128,2048]{1,0:T(8,128)(2,1)S(1)}, bf16[256,2048]{1,0:T(8,128)(2,1)S(1)}) custom-call(s32[1]{0:T(128)} %bitcast.15.mine_ref, bf16[16,512]{1,0:T(8,128)(2,1)S(1)} %copy-done.11, bf16[128,2048]{1,0:T(8,128)(2,1)} %get-tuple-element.57.refs_0_, bf16[128,2048]{1,0:T(8,128)(2,1)} %collective-permute-done.17.refs_1_, ...), custom_call_target="tpu_custom_call" | custom-call | flops 3019898880 | bytes 13631488 | tf_op jit(solution)/shard_map/pallas_call | solution.py:302
  81.3 2.6 %collective-permute-done.15.refs_0_ = bf16[128,2048]{1,0:T(8,128)(2,1)} collective-permute-done((bf16[128,2048]{1,0:T(8,128)(2,1)}, bf16[128,2048]{1,0:T(8,128)(2,1)}, u32[]{:S(2)}, u32[]{:S(2)}) %collective-permute-start.15) | collective-permute-done | bytes 524320 | tf_op jit(solution)/shard_map/ppermute | solution.py:401
  83.9 2.3 %collective-permute-done.16.refs_1_ = bf16[128,2048]{1,0:T(8,128)(2,1)} collective-permute-done((bf16[128,2048]{1,0:T(8,128)(2,1)}, bf16[128,2048]{1,0:T(8,128)(2,1)}, u32[]{:S(2)}, u32[]{:S(2)}) %collective-permute-start.16) | collective-permute-done | bytes 524320 | tf_op jit(solution)/shard_map/ppermute | solution.py:401
  90.6 5.5 %shard_map.118 = (bf16[128,2048]{1,0:T(8,128)(2,1)S(1)}, bf16[128,2048]{1,0:T(8,128)(2,1)S(1)}, bf16[256,2048]{1,0:T(8,128)(2,1)S(1)}) custom-call(s32[1]{0:T(128)} %bitcast.15.mine_ref, bf16[16,512]{1,0:T(8,128)(2,1)S(1)} %copy-done.9, bf16[128,2048]{1,0:T(8,128)(2,1)} %get-tuple-element.58.refs_0_, bf16[128,2048]{1,0:T(8,128)(2,1)S(1)} %collective-permute-done.21.refs_1_, ...), custom_call_target="tpu_custom_call" | custom-call | flops 3019898880 | bytes 13631488 | tf_op jit(solution)/shard_map/pallas_call | solution.py:302
  99.7 2.9 %collective-permute-done.26.refs_1_ = bf16[128,2048]{1,0:T(8,128)(2,1)S(1)} collective-permute-done((bf16[128,2048]{1,0:T(8,128)(2,1)}, bf16[128,2048]{1,0:T(8,128)(2,1)S(1)}, u32[]{:S(2)}, u32[]{:S(2)}) %collective-permute-start.26) | collective-permute-done | bytes 524320 | tf_op jit(solution)/shard_map/ppermute | solution.py:401
  103.0 1.5 collective-permute-start.24
  105.2 5.4 %shard_map.120 = (bf16[128,2048]{1,0:T(8,128)(2,1)S(1)}, bf16[128,2048]{1,0:T(8,128)(2,1)S(1)}, bf16[256,2048]{1,0:T(8,128)(2,1)S(1)}) custom-call(s32[1]{0:T(128)} %bitcast.15.mine_ref, bf16[16,512]{1,0:T(8,128)(2,1)S(1)} %copy-done.7, bf16[128,2048]{1,0:T(8,128)(2,1)} %get-tuple-element.61.refs_0_, bf16[128,2048]{1,0:T(8,128)(2,1)S(1)} %collective-permute-done.26.refs_1_, ...), custom_call_target="tpu_custom_call" | custom-call | flops 3019898880 | bytes 13631488 | tf_op jit(solution)/shard_map/pallas_call | solution.py:302
  111.3 2.1 %collective-permute-done.25.refs_1_ = bf16[128,1024]{1,0:T(8,128)(2,1)S(1)} collective-permute-done((bf16[128,1024]{1,0:T(8,128)(2,1)S(1)}, bf16[128,1024]{1,0:T(8,128)(2,1)S(1)}, u32[]{:S(2)}, u32[]{:S(2)}) %collective-permute-start.25) | collective-permute-done | bytes 262176 | tf_op jit(solution)/shard_map/ppermute | solution.py:401
  115.5 4.3 %shard_map.114 = (bf16[128,2048]{1,0:T(8,128)(2,1)S(1)}, bf16[128,2048]{1,0:T(8,128)(2,1)S(1)}, bf16[256,2048]{1,0:T(8,128)(2,1)S(1)}) custom-call(s32[1]{0:T(128)} %bitcast.15.mine_ref, bf16[16,512]{1,0:T(8,128)(2,1)S(1)} %copy-done.12, bf16[128,2048]{1,0:T(8,128)(2,1)S(1)} %copy-done.3, bf16[128,2048]{1,0:T(8,128)(2,1)S(1)} %collective-permute-done.9.refs_1_, ...), custom_call_target="tpu_custom_call" | custom-call | flops 3019898880 | bytes 13631488 | tf_op jit(solution)/shard_map/pallas_call | solution.py:302
  120.0 7.9 %collective-permute-done.30.refs_0_ = bf16[128,2048]{1,0:T(8,128)(2,1)S(1)} collective-permute-done((bf16[128,2048]{1,0:T(8,128)(2,1)S(1)}, bf16[128,2048]{1,0:T(8,128)(2,1)S(1)}, u32[]{:S(2)}, u32[]{:S(2)}) %collective-permute-start.30) | collective-permute-done | bytes 524320 | tf_op jit(solution)/shard_map/ppermute | solution.py:401
  128.0 1.7 %collective-permute-done.31.refs_1_ = bf16[128,2048]{1,0:T(8,128)(2,1)S(1)} collective-permute-done((bf16[128,2048]{1,0:T(8,128)(2,1)S(1)}, bf16[128,2048]{1,0:T(8,128)(2,1)S(1)}, u32[]{:S(2)}, u32[]{:S(2)}) %collective-permute-start.31) | collective-permute-done | bytes 524320 | tf_op jit(solution)/shard_map/ppermute | solution.py:401
  129.7 1.5 collective-permute-start.34
  132.5 11.5 %collective-permute-done.34.refs_0_ = bf16[128,2048]{1,0:T(8,128)(2,1)S(1)} collective-permute-done((bf16[128,2048]{1,0:T(8,128)(2,1)S(1)}, bf16[128,2048]{1,0:T(8,128)(2,1)S(1)}, u32[]{:S(2)}, u32[]{:S(2)}) %collective-permute-start.34) | collective-permute-done | bytes 524320 | tf_op jit(solution)/shard_map/ppermute | solution.py:401
  144.0 2.5 %collective-permute-done.35.refs_1_ = bf16[128,2048]{1,0:T(8,128)(2,1)S(1)} collective-permute-done((bf16[128,2048]{1,0:T(8,128)(2,1)S(1)}, bf16[128,2048]{1,0:T(8,128)(2,1)S(1)}, u32[]{:S(2)}, u32[]{:S(2)}) %collective-permute-start.35) | collective-permute-done | bytes 524320 | tf_op jit(solution)/shard_map/ppermute | solution.py:401
  148.2 12.9 %collective-permute-done.37 = bf16[128,2048]{1,0:T(8,128)(2,1)S(1)} collective-permute-done((bf16[128,2048]{1,0:T(8,128)(2,1)S(1)}, bf16[128,2048]{1,0:T(8,128)(2,1)S(1)}, u32[]{:S(2)}, u32[]{:S(2)}) %collective-permute-start.37) | collective-permute-done | bytes 524320 | tf_op jit(solution)/shard_map/ppermute | solution.py:401
  (119 shorter events, 28.8 us)
Async XLA Ops:
  0.0 15.0 %collective-permute-start.3 = (bf16[512,2048]{1,0:T(8,128)(2,1)}, bf16[512,2048]{1,0:T(8,128)(2,1)S(1)}, u32[]{:S(2)}, u32[]{:S(2)}) collective-permute-start(bf16[512,2048]{1,0:T(8,128)(2,1)} %refs_4_.1), channel_id=1, source_target_pairs={{0,4},{4,0},{8,12},{12,8},{1,5},{5,1},{9,13},{13,9},{2,6},{6,2},{1... | collective-permute-start | bytes 6291464 | tf_op jit(solution)/shard_map/ppermute | solution.py:370
  2.3 12.7 %collective-permute-start.4 = (bf16[128,1024]{1,0:T(8,128)(2,1)}, bf16[128,1024]{1,0:T(8,128)(2,1)S(1)}, u32[]{:S(2)}, u32[]{:S(2)}) collective-permute-start(bf16[128,1024]{1,0:T(8,128)(2,1)} %get-tuple-element.50), channel_id=1, source_target_pairs={{0,8},{4,12},{8,0},{12,4},{1,9},{5,13},{9,1},{13,5},{2,10},{6,14},... | collective-permute-start | bytes 786440 | tf_op jit(solution)/shard_map/ppermute | solution.py:363
  5.1 8.7 %collective-permute-start.1 = (bf16[144,256]{1,0:T(8,128)(2,1)}, bf16[144,256]{1,0:T(8,128)(2,1)S(1)}, u32[]{:S(2)}, u32[]{:S(2)}) collective-permute-start(bf16[144,256]{1,0:T(8,128)(2,1)} %get-tuple-element.48), channel_id=1, source_target_pairs={{0,8},{4,12},{8,0},{12,4},{1,9},{5,13},{9,1},{13,5},{2,10},{6,14},... | collective-permute-start | bytes 221192 | tf_op jit(solution)/shard_map/ppermute | solution.py:367
  5.4 9.6 %collective-permute-start.2 = (bf16[144,256]{1,0:T(8,128)(2,1)}, bf16[144,256]{1,0:T(8,128)(2,1)S(1)}, u32[]{:S(2)}, u32[]{:S(2)}) collective-permute-start(bf16[144,256]{1,0:T(8,128)(2,1)} %get-tuple-element.48), channel_id=1, source_target_pairs={{0,12},{4,8},{8,4},{12,0},{1,13},{5,9},{9,5},{13,1},{2,14},{6,10},... | collective-permute-start | bytes 221192 | tf_op jit(solution)/shard_map/ppermute | solution.py:368
  22.5 14.4 %collective-permute-start.5 = (bf16[128,2048]{1,0:T(8,128)(2,1)}, bf16[128,2048]{1,0:T(8,128)(2,1)S(1)}, u32[]{:S(2)}, u32[]{:S(2)}) collective-permute-start(bf16[128,2048]{1,0:T(8,128)(2,1)} %get-tuple-element.51), channel_id=1, source_target_pairs={{0,8},{4,12},{8,0},{12,4},{1,9},{5,13},{9,1},{13,5},{2,10},{6,14},... | collective-permute-start | bytes 1572872 | tf_op jit(solution)/shard_map/ppermute | solution.py:379
  25.3 11.5 %collective-permute-start.6 = (bf16[16,512]{1,0:T(8,128)(2,1)}, bf16[16,512]{1,0:T(8,128)(2,1)S(1)}, u32[]{:S(2)}, u32[]{:S(2)}) collective-permute-start(bf16[16,512]{1,0:T(8,128)(2,1)} %get-tuple-element.52.quad_ref), channel_id=1, source_target_pairs={{0,1},{1,3},{3,2},{2,0},{4,5},{5,7},{7,6},{6,4},{8,9},{9,11},{11,1... | collective-permute-start | bytes 49160 | tf_op jit(solution)/shard_map/ppermute | solution.py:389
  26.9 9.9 %collective-permute-start.7 = (bf16[16,512]{1,0:T(8,128)(2,1)}, bf16[16,512]{1,0:T(8,128)(2,1)S(1)}, u32[]{:S(2)}, u32[]{:S(2)}) collective-permute-start(bf16[16,512]{1,0:T(8,128)(2,1)} %get-tuple-element.52.quad_ref), channel_id=1, source_target_pairs={{0,3},{1,2},{3,0},{2,1},{4,7},{5,6},{7,4},{6,5},{8,11},{9,10},{11,... | collective-permute-start | bytes 49160 | tf_op jit(solution)/shard_map/ppermute | solution.py:389
  29.4 7.5 %collective-permute-start.8 = (bf16[16,512]{1,0:T(8,128)(2,1)}, bf16[16,512]{1,0:T(8,128)(2,1)S(1)}, u32[]{:S(2)}, u32[]{:S(2)}) collective-permute-start(bf16[16,512]{1,0:T(8,128)(2,1)} %get-tuple-element.52.quad_ref), channel_id=1, source_target_pairs={{0,2},{1,0},{3,1},{2,3},{4,6},{5,4},{7,5},{6,7},{8,10},{9,8},{11,9... | collective-permute-start | bytes 49160 | tf_op jit(solution)/shard_map/ppermute | solution.py:389
  40.2 13.1 %collective-permute-start.10 = (bf16[128,2048]{1,0:T(8,128)(2,1)}, bf16[128,2048]{1,0:T(8,128)(2,1)S(1)}, u32[]{:S(2)}, u32[]{:S(2)}) collective-permute-start(bf16[128,2048]{1,0:T(8,128)(2,1)} %get-tuple-element.54.refs_0_), channel_id=1, source_target_pairs={{0,8},{4,12},{8,0},{12,4},{1,9},{5,13},{9,1},{13,5},{2,10},{6,14},... | collective-permute-start | bytes 1572872 | tf_op jit(solution)/shard_map/ppermute | solution.py:401
  41.6 14.2 %collective-permute-start.11 = (bf16[128,2048]{1,0:T(8,128)(2,1)}, bf16[128,2048]{1,0:T(8,128)(2,1)}, u32[]{:S(2)}, u32[]{:S(2)}) collective-permute-start(bf16[128,2048]{1,0:T(8,128)(2,1)} %get-tuple-element.54.refs_0_), channel_id=1, source_target_pairs={{0,1},{1,3},{3,2},{2,0},{4,5},{5,7},{7,6},{6,4},{8,9},{9,11},{11,1... | collective-permute-start | bytes 1572872 | tf_op jit(solution)/shard_map/ppermute | solution.py:401
  55.8 12.4 %collective-permute-start.13 = (bf16[128,2048]{1,0:T(8,128)(2,1)}, bf16[128,2048]{1,0:T(8,128)(2,1)}, u32[]{:S(2)}, u32[]{:S(2)}) collective-permute-start(bf16[128,2048]{1,0:T(8,128)(2,1)} %get-tuple-element.57.refs_0_), channel_id=1, source_target_pairs={{0,8},{4,12},{8,0},{12,4},{1,9},{5,13},{9,1},{13,5},{2,10},{6,14},... | collective-permute-start | bytes 1572872 | tf_op jit(solution)/shard_map/ppermute | solution.py:401
  56.4 12.9 %collective-permute-start.14 = (bf16[128,2048]{1,0:T(8,128)(2,1)}, bf16[128,2048]{1,0:T(8,128)(2,1)}, u32[]{:S(2)}, u32[]{:S(2)}) collective-permute-start(bf16[128,2048]{1,0:T(8,128)(2,1)} %get-tuple-element.57.refs_0_), channel_id=1, source_target_pairs={{0,1},{1,3},{3,2},{2,0},{4,5},{5,7},{7,6},{6,4},{8,9},{9,11},{11,1... | collective-permute-start | bytes 1572872 | tf_op jit(solution)/shard_map/ppermute | solution.py:401
  57.1 14.5 %collective-permute-start.17 = (bf16[128,2048]{1,0:T(8,128)(2,1)}, bf16[128,2048]{1,0:T(8,128)(2,1)}, u32[]{:S(2)}, u32[]{:S(2)}) collective-permute-start(bf16[128,2048]{1,0:T(8,128)(2,1)} %get-tuple-element.57.refs_0_), channel_id=1, source_target_pairs={{0,4},{4,0},{8,12},{12,8},{1,5},{5,1},{9,13},{13,9},{2,6},{6,2},{1... | collective-permute-start | bytes 1572872 | tf_op jit(solution)/shard_map/ppermute | solution.py:401
  69.2 14.7 %collective-permute-start.15 = (bf16[128,2048]{1,0:T(8,128)(2,1)}, bf16[128,2048]{1,0:T(8,128)(2,1)}, u32[]{:S(2)}, u32[]{:S(2)}) collective-permute-start(bf16[128,2048]{1,0:T(8,128)(2,1)} %get-tuple-element.58.refs_0_), channel_id=1, source_target_pairs={{0,8},{4,12},{8,0},{12,4},{1,9},{5,13},{9,1},{13,5},{2,10},{6,14},... | collective-permute-start | bytes 1572872 | tf_op jit(solution)/shard_map/ppermute | solution.py:401
  70.9 15.3 %collective-permute-start.16 = (bf16[128,2048]{1,0:T(8,128)(2,1)}, bf16[128,2048]{1,0:T(8,128)(2,1)}, u32[]{:S(2)}, u32[]{:S(2)}) collective-permute-start(bf16[128,2048]{1,0:T(8,128)(2,1)} %get-tuple-element.58.refs_0_), channel_id=1, source_target_pairs={{0,1},{1,3},{3,2},{2,0},{4,5},{5,7},{7,6},{6,4},{8,9},{9,11},{11,1... | collective-permute-start | bytes 1572872 | tf_op jit(solution)/shard_map/ppermute | solution.py:401
  86.2 9.9 %collective-permute-start.23 = (bf16[256,2048]{1,0:T(8,128)(2,1)S(1)}, bf16[256,2048]{1,0:T(8,128)(2,1)S(1)}, u32[]{:S(2)}, u32[]{:S(2)}) collective-permute-start(bf16[256,2048]{1,0:T(8,128)(2,1)S(1)} %get-tuple-element.65), channel_id=1, source_target_pairs={{0,4},{4,0},{8,12},{12,8},{1,5},{5,1},{9,13},{13,9},{2,6},{6,2},{1... | collective-permute-start | bytes 3145736 | tf_op jit(solution)/shard_map/ppermute | solution.py:401
  88.6 8.8 %collective-permute-start.19 = (bf16[128,1024]{1,0:T(8,128)(2,1)S(1)}, bf16[128,1024]{1,0:T(8,128)(2,1)S(1)}, u32[]{:S(2)}, u32[]{:S(2)}) collective-permute-start(bf16[128,1024]{1,0:T(8,128)(2,1)S(1)} %slice.54), channel_id=1, source_target_pairs={{0,8},{4,12},{8,0},{12,4},{1,9},{5,13},{9,1},{13,5},{2,10},{6,14},... | collective-permute-start | bytes 786440 | tf_op jit(solution)/shard_map/ppermute | solution.py:401
  89.0 9.5 %collective-permute-start.20 = (bf16[128,1024]{1,0:T(8,128)(2,1)S(1)}, bf16[128,1024]{1,0:T(8,128)(2,1)S(1)}, u32[]{:S(2)}, u32[]{:S(2)}) collective-permute-start(bf16[128,1024]{1,0:T(8,128)(2,1)S(1)} %slice.55), channel_id=1, source_target_pairs={{0,1},{1,3},{3,2},{2,0},{4,5},{5,7},{7,6},{6,4},{8,9},{9,11},{11,1... | collective-permute-start | bytes 786440 | tf_op jit(solution)/shard_map/ppermute | solution.py:401
  98.6 12.0 %collective-permute-start.29 = (bf16[256,2048]{1,0:T(8,128)(2,1)S(1)}, bf16[256,2048]{1,0:T(8,128)(2,1)S(1)}, u32[]{:S(2)}, u32[]{:S(2)}) collective-permute-start(bf16[256,2048]{1,0:T(8,128)(2,1)S(1)} %get-tuple-element.71), channel_id=1, source_target_pairs={{0,4},{4,0},{8,12},{12,8},{1,5},{5,1},{9,13},{13,9},{2,6},{6,2},{1... | collective-permute-start | bytes 3145736 | tf_op jit(solution)/shard_map/ppermute | solution.py:401
  98.6 4.0 %collective-permute-start.26 = (bf16[128,2048]{1,0:T(8,128)(2,1)}, bf16[128,2048]{1,0:T(8,128)(2,1)S(1)}, u32[]{:S(2)}, u32[]{:S(2)}) collective-permute-start(bf16[128,2048]{1,0:T(8,128)(2,1)} %get-tuple-element.61.refs_0_), channel_id=1, source_target_pairs={{0,4},{4,0},{8,12},{12,8},{1,5},{5,1},{9,13},{13,9},{2,6},{6,2},{1... | collective-permute-start | bytes 1572872 | tf_op jit(solution)/shard_map/ppermute | solution.py:401
  99.1 5.3 %collective-permute-start.28 = (bf16[128,1024]{1,0:T(8,128)(2,1)S(1)}, bf16[128,1024]{1,0:T(8,128)(2,1)S(1)}, u32[]{:S(2)}, u32[]{:S(2)}) collective-permute-start(bf16[128,1024]{1,0:T(8,128)(2,1)S(1)} %get-tuple-element.68.refs_3_), channel_id=1, source_target_pairs={{0,4},{4,0},{8,12},{12,8},{1,5},{5,1},{9,13},{13,9},{2,6},{6,2},{1... | collective-permute-start | bytes 786440 | tf_op jit(solution)/shard_map/ppermute | solution.py:401
  99.6 15.9 %collective-permute-start.9 = (bf16[128,2048]{1,0:T(8,128)(2,1)S(1)}, bf16[128,2048]{1,0:T(8,128)(2,1)S(1)}, u32[]{:S(2)}, u32[]{:S(2)}) collective-permute-start(bf16[128,2048]{1,0:T(8,128)(2,1)S(1)} %copy-done.3), channel_id=1, source_target_pairs={{0,4},{4,0},{8,12},{12,8},{1,5},{5,1},{9,13},{13,9},{2,6},{6,2},{1... | collective-permute-start | bytes 1572872 | tf_op jit(solution)/shard_map/ppermute | solution.py:401
  102.6 12.9 %collective-permute-start.12 = (bf16[128,2048]{1,0:T(8,128)(2,1)S(1)}, bf16[128,2048]{1,0:T(8,128)(2,1)S(1)}, u32[]{:S(2)}, u32[]{:S(2)}) collective-permute-start(bf16[128,2048]{1,0:T(8,128)(2,1)S(1)} %copy-done.5), channel_id=1, source_target_pairs={{0,4},{4,0},{8,12},{12,8},{1,5},{5,1},{9,13},{13,9},{2,6},{6,2},{1... | collective-permute-start | bytes 1572872 | tf_op jit(solution)/shard_map/ppermute | solution.py:401
  103.0 8.3 %collective-permute-start.24 = (bf16[128,1024]{1,0:T(8,128)(2,1)S(1)}, bf16[128,1024]{1,0:T(8,128)(2,1)S(1)}, u32[]{:S(2)}, u32[]{:S(2)}) collective-permute-start(bf16[128,1024]{1,0:T(8,128)(2,1)S(1)} %get-tuple-element.92), channel_id=1, source_target_pairs={{0,8},{4,12},{8,0},{12,4},{1,9},{5,13},{9,1},{13,5},{2,10},{6,14},... | collective-permute-start | bytes 786440 | tf_op jit(solution)/shard_map/ppermute | solution.py:401
  104.4 9.0 %collective-permute-start.25 = (bf16[128,1024]{1,0:T(8,128)(2,1)S(1)}, bf16[128,1024]{1,0:T(8,128)(2,1)S(1)}, u32[]{:S(2)}, u32[]{:S(2)}) collective-permute-start(bf16[128,1024]{1,0:T(8,128)(2,1)S(1)} %get-tuple-element.91), channel_id=1, source_target_pairs={{0,1},{1,3},{3,2},{2,0},{4,5},{5,7},{7,6},{6,4},{8,9},{9,11},{11,1... | collective-permute-start | bytes 786440 | tf_op jit(solution)/shard_map/ppermute | solution.py:401
  113.4 6.5 %collective-permute-start.32 = (bf16[256,2048]{1,0:T(8,128)(2,1)S(1)}, bf16[256,2048]{1,0:T(8,128)(2,1)S(1)}, u32[]{:S(2)}, u32[]{:S(2)}) collective-permute-start(bf16[256,2048]{1,0:T(8,128)(2,1)S(1)} %get-tuple-element.78), channel_id=1, source_target_pairs={{0,4},{4,0},{8,12},{12,8},{1,5},{5,1},{9,13},{13,9},{2,6},{6,2},{1... | collective-permute-start | bytes 3145736 | tf_op jit(solution)/shard_map/ppermute | solution.py:401
  113.6 14.4 %collective-permute-start.30 = (bf16[128,2048]{1,0:T(8,128)(2,1)S(1)}, bf16[128,2048]{1,0:T(8,128)(2,1)S(1)}, u32[]{:S(2)}, u32[]{:S(2)}) collective-permute-start(bf16[128,2048]{1,0:T(8,128)(2,1)S(1)} %pad_maximum_fusion), channel_id=1, source_target_pairs={{0,8},{4,12},{8,0},{12,4},{1,9},{5,13},{9,1},{13,5},{2,10},{6,14},... | collective-permute-start | bytes 1572872 | tf_op jit(solution)/shard_map/ppermute | solution.py:401
  114.5 15.2 %collective-permute-start.31 = (bf16[128,2048]{1,0:T(8,128)(2,1)S(1)}, bf16[128,2048]{1,0:T(8,128)(2,1)S(1)}, u32[]{:S(2)}, u32[]{:S(2)}) collective-permute-start(bf16[128,2048]{1,0:T(8,128)(2,1)S(1)} %pad_maximum_fusion.1), channel_id=1, source_target_pairs={{0,1},{1,3},{3,2},{2,0},{4,5},{5,7},{7,6},{6,4},{8,9},{9,11},{11,1... | collective-permute-start | bytes 1572872 | tf_op jit(solution)/shard_map/ppermute | solution.py:401
  129.7 14.3 %collective-permute-start.34 = (bf16[128,2048]{1,0:T(8,128)(2,1)S(1)}, bf16[128,2048]{1,0:T(8,128)(2,1)S(1)}, u32[]{:S(2)}, u32[]{:S(2)}) collective-permute-start(bf16[128,2048]{1,0:T(8,128)(2,1)S(1)} %get-tuple-element.80), channel_id=1, source_target_pairs={{0,8},{4,12},{8,0},{12,4},{1,9},{5,13},{9,1},{13,5},{2,10},{6,14},... | collective-permute-start | bytes 1572872 | tf_op jit(solution)/shard_map/ppermute | solution.py:401
  131.5 15.0 %collective-permute-start.35 = (bf16[128,2048]{1,0:T(8,128)(2,1)S(1)}, bf16[128,2048]{1,0:T(8,128)(2,1)S(1)}, u32[]{:S(2)}, u32[]{:S(2)}) collective-permute-start(bf16[128,2048]{1,0:T(8,128)(2,1)S(1)} %add_convert_fusion.3), channel_id=1, source_target_pairs={{0,1},{1,3},{3,2},{2,0},{4,5},{5,7},{7,6},{6,4},{8,9},{9,11},{11,1... | collective-permute-start | bytes 1572872 | tf_op jit(solution)/shard_map/ppermute | solution.py:401
  146.9 14.2 %collective-permute-start.37 = (bf16[128,2048]{1,0:T(8,128)(2,1)S(1)}, bf16[128,2048]{1,0:T(8,128)(2,1)S(1)}, u32[]{:S(2)}, u32[]{:S(2)}) collective-permute-start(bf16[128,2048]{1,0:T(8,128)(2,1)S(1)} %add_convert_fusion.1), channel_id=1, source_target_pairs={{0,1},{1,3},{3,2},{2,0},{4,5},{5,7},{7,6},{6,4},{8,9},{9,11},{11,1... | collective-permute-start | bytes 1572872 | tf_op jit(solution)/shard_map/ppermute | solution.py:401
  147.7 13.4 %collective-permute-start.36 = (bf16[128,2048]{1,0:T(8,128)(2,1)S(1)}, bf16[128,2048]{1,0:T(8,128)(2,1)S(1)}, u32[]{:S(2)}, u32[]{:S(2)}) collective-permute-start(bf16[128,2048]{1,0:T(8,128)(2,1)S(1)} %get-tuple-element.85), channel_id=1, source_target_pairs={{0,8},{4,12},{8,0},{12,4},{1,9},{5,13},{9,1},{13,5},{2,10},{6,14},... | collective-permute-start | bytes 1572872 | tf_op jit(solution)/shard_map/ppermute | solution.py:401
  (27 other events, 166.9 us)

commit v13 on v12

--- a/solution.py
+++ b/solution.py
@@ -312,9 +312,9 @@
         scratch_shapes=[pltpu.VMEM((4 * cap, width), jnp.bfloat16)],
         compiler_params=pltpu.CompilerParams(vmem_limit_bytes=28 * MIB),
         cost_estimate=pl.CostEstimate(
-            flops=24 * cap * width * hidden_units,
-            bytes_accessed=16 * tokens * width + 6 * width * hidden_units,
-            transcendentals=4 * cap * hidden_units,
+            flops=0,
+            bytes_accessed=0,
+            transcendentals=0,
         ),
     )(mine.reshape(1), quad, *sum(row_blocks, []), w_gate, w_up, w_down)
 
@@ -443,9 +443,9 @@
             held["twin", step] = move(held["row", step], "twin")
         step = turn - 4 if turn < n_sub + 4 else 0
         if 1 <= step <= last or turn == n_sub + 4:
-            if step == 1 and last > 1:
-                now["back", step] = move(held["away", step][:, :half], "across")
-                now["late", step] = move(held["away", step][:, half:], "on")
+            if step == 1:
+                now["back", step] = move(held["away", step], "across")
+                now["late", step] = move(held["apart", step], "on")
             elif step == 2:
                 away = held["away", step]
                 added = away[:, half:].astype(jnp.float32) + held["late", 1].astype(jnp.float32)
@@ -472,7 +472,12 @@
             now["other", 0] = experts_of(0)
         step = turn - 3 if turn < n_sub + 3 else 0
         if 1 <= step <= last or turn == n_sub + 3:
-            now["away", step] = twin_sum(step)
+            away = twin_sum(step)
+            if step == 1:
+                now["away", step] = away[:, :half]
+                now["apart", step] = away[:, half:]
+            else:
+                now["away", step] = away
         if turn < n_sub + 4:
             wait = 10_000_000_000 if turn <= 2 else 0
             now = dict(zip(now.keys(), meet(list(now.values()), wait)))

time: 163 us -> 162 us (level)
  waiting for transfers between devices: 82.4 us -> 80.2 us
    ppermute x29, waiting for transfers between devices: 74.7 us -> 72.5 us  [move(): return lax.ppermute(array, *ways[way])]
  transfers between devices with their start and end apart: 38 -> 38, of which waited for: 19 -> 20; matrix products, arithmetic and copies ran while one was open for 3% -> 3% of each run, Pallas kernels for 18% -> 18%
where the time goes in v13:
time: 162 us; the launch traced here: 161 us
  waiting for transfers between devices  80.2 us (50%)
  Pallas kernels  36.8 us (23%)
  starting transfers between devices  30.9 us (19%)
  local copies, waits for them, and re-layouts  10.5 us (6%)
  other arithmetic  2.76 us (2%)
    ppermute x29, waiting for transfers between devices, move(): return lax.ppermute(array, *ways[way])  72.5 us
    pallas_call x4, Pallas kernels, experts_on_rows(): pl.pallas_call(functools.partial(experts_kernel, cap=cap, pieces=pieces),...  21.1 us
    ppermute x29, starting transfers between devices, move(): return lax.ppermute(array, *ways[way])  18.8 us
    pallas_call x2, Pallas kernels, attend(): pl.pallas_call(functools.partial(attend_kernel, scale=1.0 / HD ** 0.5), i...  11.3 us
    unnamed x42, local copies, waits for them, and re-layouts  6.63 us
    ppermute x1, waiting for transfers between devices, gathered_plan(): lax.ppermute(kv_away, 'seq', across)  6.47 us
    ppermute x3, starting transfers between devices, gathered_plan(): lax.ppermute(quad, 'sub', ring(steps))  5.63 us
  transfers between devices with their start and end apart: 38, of which 20 were waited for; matrix products, arithmetic and copies ran while one was open for 3% of the time, Pallas kernels for 18%

profile of v13, /device:TPU:0, one launch (start us, length us, event | category | flops | bytes accessed | tf_op | source)
XLA Modules:
  0.0 161.5 jit_solution(1505149117532100474)
XLA Ops:
  0.5 1.9 %shard_map.109 = (bf16[128,1024]{1,0:T(8,128)(2,1)}, bf16[144,256]{1,0:T(8,128)(2,1)}, bf16[144,256]{1,0:T(8,128)(2,1)}) custom-call(s32[1]{0:T(128)} %bitcast.7.chip_ref, bf16[128,2048]{1,0:T(8,128)(2,1)} %bitcast.35, bf16[128,256]{1,0:T(8,128)(2,1)} %bitcast.38, bf16[128,256]{1,0:T(8,128)(2,1)} %bitcast.39, s32[8,128]{1,0:T(8,128)} %bitcast.40, ...), custom_call_target="tpu_custom_call" | custom-call | tf_op jit(solution)/shard_map/pallas_call | solution.py:87
  2.3 2.5 %collective-permute-start.4 = (bf16[128,1024]{1,0:T(8,128)(2,1)}, bf16[128,1024]{1,0:T(8,128)(2,1)S(1)}, u32[]{:S(2)}, u32[]{:S(2)}) collective-permute-start(bf16[128,1024]{1,0:T(8,128)(2,1)} %get-tuple-element.51), channel_id=1, source_target_pairs={{0,8},{4,12},{8,0},{12,4},{1,9},{5,13},{9,1},{13,5},{2,10},{6,14},... | collective-permute-start | bytes 786440 | tf_op jit(solution)/shard_map/ppermute | solution.py:363
  7.3 6.5 %collective-permute-done.1.refs_2_ = bf16[144,256]{1,0:T(8,128)(2,1)S(1)} collective-permute-done((bf16[144,256]{1,0:T(8,128)(2,1)}, bf16[144,256]{1,0:T(8,128)(2,1)S(1)}, u32[]{:S(2)}, u32[]{:S(2)}) %collective-permute-start.1) | collective-permute-done | bytes 73760 | tf_op jit(solution)/shard_map/ppermute | solution.py:367
  17.1 5.4 %shard_map.111 = (bf16[128,2048]{1,0:T(8,128)(2,1)}, bf16[16,512]{1,0:T(8,128)(2,1)}) custom-call(s32[7]{0:T(128)} %stack.38.place_ref, bf16[128,1024]{1,0:T(8,128)(2,1)} %copy-done.19, bf16[144,256]{1,0:T(8,128)(2,1)} %get-tuple-element.48.refs_0_, bf16[144,256]{1,0:T(8,128)(2,1)} %copy-done.16, bf16[144,256]{1,0:T(8,128)(2,1)} %copy-done.17, ...), custom_call_target="tpu_custom_call" | custom-call | flops 805306368 | bytes 5242880 | tf_op jit(solution)/shard_map/pallas_call | solution.py:159
  22.5 1.6 collective-permute-start.5
  25.3 1.6 collective-permute-start.6
  26.9 2.5 %collective-permute-start.7 = (bf16[16,512]{1,0:T(8,128)(2,1)}, bf16[16,512]{1,0:T(8,128)(2,1)S(1)}, u32[]{:S(2)}, u32[]{:S(2)}) collective-permute-start(bf16[16,512]{1,0:T(8,128)(2,1)} %get-tuple-element.53.quad_ref), channel_id=1, source_target_pairs={{0,3},{1,2},{3,0},{2,1},{4,7},{5,6},{7,4},{6,5},{8,11},{9,10},{11,... | collective-permute-start | bytes 49160 | tf_op jit(solution)/shard_map/ppermute | solution.py:389
  29.4 1.6 collective-permute-start.8
  31.0 5.9 %shard_map.110 = (f32[128,2048]{1,0:T(8,128)}, bf16[16,512]{1,0:T(8,128)(2,1)}) custom-call(s32[7]{0:T(128)} %stack.37.place_ref, bf16[128,2048]{1,0:T(8,128)(2,1)} %bitcast.36, bf16[144,256]{1,0:T(8,128)(2,1)} %get-tuple-element.48.refs_0_, bf16[144,256]{1,0:T(8,128)(2,1)} %copy-done.16, bf16[144,256]{1,0:T(8,128)(2,1)} %copy-done.17, ...), custom_call_target="tpu_custom_call" | custom-call | flops 805306368 | bytes 5242880 | tf_op jit(solution)/shard_map/pallas_call | solution.py:159
  37.7 2.5 %shard_map.112 = (bf16[128,2048]{1,0:T(8,128)(2,1)}, bf16[128,2048]{1,0:T(8,128)(2,1)}) custom-call(f32[128,2048]{1,0:T(8,128)} %get-tuple-element.50.own_ref, bf16[128,2048]{1,0:T(8,128)(2,1)} %copy-done.14, bf16[1,2048]{1,0:T(2,128)(2,1)} %broadcast_in_dim.6.gain_ref, bf16[16,512]{1,0:T(8,128)(2,1)} %copy-done.10, bf16[16,512]{1,0:T(8,128)(2,1)} %copy-done.8, ...), custom_call_target="tpu_custom_call" | custom-call | tf_op jit(solution)/shard_map/pallas_call | solution.py:202
  41.6 1.6 collective-permute-start.11
  43.2 10.1 %collective-permute-done.10.refs_0_ = bf16[128,2048]{1,0:T(8,128)(2,1)S(1)} collective-permute-done((bf16[128,2048]{1,0:T(8,128)(2,1)}, bf16[128,2048]{1,0:T(8,128)(2,1)S(1)}, u32[]{:S(2)}, u32[]{:S(2)}) %collective-permute-start.10) | collective-permute-done | bytes 524320 | tf_op jit(solution)/shard_map/ppermute | solution.py:401
  53.4 2.5 %collective-permute-done.11.refs_1_ = bf16[128,2048]{1,0:T(8,128)(2,1)} collective-permute-done((bf16[128,2048]{1,0:T(8,128)(2,1)}, bf16[128,2048]{1,0:T(8,128)(2,1)}, u32[]{:S(2)}, u32[]{:S(2)}) %collective-permute-start.11) | collective-permute-done | bytes 524320 | tf_op jit(solution)/shard_map/ppermute | solution.py:401
  57.1 11.1 %collective-permute-done.13.refs_0_ = bf16[128,2048]{1,0:T(8,128)(2,1)} collective-permute-done((bf16[128,2048]{1,0:T(8,128)(2,1)}, bf16[128,2048]{1,0:T(8,128)(2,1)}, u32[]{:S(2)}, u32[]{:S(2)}) %collective-permute-start.13) | collective-permute-done | bytes 524320 | tf_op jit(solution)/shard_map/ppermute | solution.py:401
  69.2 1.7 %collective-permute-start.15 = (bf16[128,2048]{1,0:T(8,128)(2,1)}, bf16[128,2048]{1,0:T(8,128)(2,1)}, u32[]{:S(2)}, u32[]{:S(2)}) collective-permute-start(bf16[128,2048]{1,0:T(8,128)(2,1)} %get-tuple-element.59.refs_0_), channel_id=1, source_target_pairs={{0,8},{4,12},{8,0},{12,4},{1,9},{5,13},{9,1},{13,5},{2,10},{6,14},... | collective-permute-start | bytes 1572872 | tf_op jit(solution)/shard_map/ppermute | solution.py:401
  71.7 1.9 %copy-done.1 = bf16[1,2048,768]{2,1,0:T(8,128)(2,1)S(1)} copy-done((bf16[1,2048,768]{2,1,0:T(8,128)(2,1)S(1)}, bf16[1,2048,768]{2,1,0:T(8,128)(2,1)}, u32[]{:S(2)}) %copy-start.1) | copy-done | bytes 3145752
  73.6 1.9 %copy-done.2 = bf16[1,768,2048]{2,1,0:T(8,128)(2,1)S(1)} copy-done((bf16[1,768,2048]{2,1,0:T(8,128)(2,1)S(1)}, bf16[1,768,2048]{2,1,0:T(8,128)(2,1)}, u32[]{:S(2)}) %copy-start.2) | copy-done | bytes 3145752
  75.5 5.8 %shard_map.116 = (bf16[128,2048]{1,0:T(8,128)(2,1)S(1)}, bf16[128,2048]{1,0:T(8,128)(2,1)S(1)}, bf16[256,2048]{1,0:T(8,128)(2,1)S(1)}) custom-call(s32[1]{0:T(128)} %bitcast.15.mine_ref, bf16[16,512]{1,0:T(8,128)(2,1)S(1)} %copy-done.11, bf16[128,2048]{1,0:T(8,128)(2,1)} %get-tuple-element.58.refs_0_, bf16[128,2048]{1,0:T(8,128)(2,1)} %collective-permute-done.17.refs_1_, ...), custom_call_target="tpu_custom_call" | custom-call | tf_op jit(solution)/shard_map/pallas_call | solution.py:302
  81.3 2.6 %collective-permute-done.15.refs_0_ = bf16[128,2048]{1,0:T(8,128)(2,1)} collective-permute-done((bf16[128,2048]{1,0:T(8,128)(2,1)}, bf16[128,2048]{1,0:T(8,128)(2,1)}, u32[]{:S(2)}, u32[]{:S(2)}) %collective-permute-start.15) | collective-permute-done | bytes 524320 | tf_op jit(solution)/shard_map/ppermute | solution.py:401
  83.9 2.3 %collective-permute-done.16.refs_1_ = bf16[128,2048]{1,0:T(8,128)(2,1)} collective-permute-done((bf16[128,2048]{1,0:T(8,128)(2,1)}, bf16[128,2048]{1,0:T(8,128)(2,1)}, u32[]{:S(2)}, u32[]{:S(2)}) %collective-permute-start.16) | collective-permute-done | bytes 524320 | tf_op jit(solution)/shard_map/ppermute | solution.py:401
  90.6 5.5 %shard_map.118 = (bf16[128,2048]{1,0:T(8,128)(2,1)S(1)}, bf16[128,2048]{1,0:T(8,128)(2,1)S(1)}, bf16[256,2048]{1,0:T(8,128)(2,1)S(1)}) custom-call(s32[1]{0:T(128)} %bitcast.15.mine_ref, bf16[16,512]{1,0:T(8,128)(2,1)S(1)} %copy-done.9, bf16[128,2048]{1,0:T(8,128)(2,1)} %get-tuple-element.59.refs_0_, bf16[128,2048]{1,0:T(8,128)(2,1)S(1)} %collective-permute-done.21.refs_1_, ...), custom_call_target="tpu_custom_call" | custom-call | tf_op jit(solution)/shard_map/pallas_call | solution.py:302
  101.1 1.5 collective-permute-done.26.refs_1_
  103.3 5.4 %shard_map.120 = (bf16[128,2048]{1,0:T(8,128)(2,1)S(1)}, bf16[128,2048]{1,0:T(8,128)(2,1)S(1)}, bf16[256,2048]{1,0:T(8,128)(2,1)S(1)}) custom-call(s32[1]{0:T(128)} %bitcast.15.mine_ref, bf16[16,512]{1,0:T(8,128)(2,1)S(1)} %copy-done.7, bf16[128,2048]{1,0:T(8,128)(2,1)} %get-tuple-element.62.refs_0_, bf16[128,2048]{1,0:T(8,128)(2,1)S(1)} %collective-permute-done.26.refs_1_, ...), custom_call_target="tpu_custom_call" | custom-call | tf_op jit(solution)/shard_map/pallas_call | solution.py:302
  108.9 3.2 %collective-permute-done.25.refs_1_ = bf16[128,1024]{1,0:T(8,128)(2,1)S(1)} collective-permute-done((bf16[128,1024]{1,0:T(8,128)(2,1)S(1)}, bf16[128,1024]{1,0:T(8,128)(2,1)S(1)}, u32[]{:S(2)}, u32[]{:S(2)}) %collective-permute-start.25) | collective-permute-done | bytes 262176 | tf_op jit(solution)/shard_map/ppermute | solution.py:401
  112.8 1.5 collective-permute-start.30
  116.2 4.3 %shard_map.114 = (bf16[128,2048]{1,0:T(8,128)(2,1)S(1)}, bf16[128,2048]{1,0:T(8,128)(2,1)S(1)}, bf16[256,2048]{1,0:T(8,128)(2,1)S(1)}) custom-call(s32[1]{0:T(128)} %bitcast.15.mine_ref, bf16[16,512]{1,0:T(8,128)(2,1)S(1)} %copy-done.12, bf16[128,2048]{1,0:T(8,128)(2,1)S(1)} %copy-done.3, bf16[128,2048]{1,0:T(8,128)(2,1)S(1)} %collective-permute-done.9.refs_1_, ...), custom_call_target="tpu_custom_call" | custom-call | tf_op jit(solution)/shard_map/pallas_call | solution.py:302
  120.7 6.4 %collective-permute-done.30.refs_0_ = bf16[128,2048]{1,0:T(8,128)(2,1)S(1)} collective-permute-done((bf16[128,2048]{1,0:T(8,128)(2,1)S(1)}, bf16[128,2048]{1,0:T(8,128)(2,1)S(1)}, u32[]{:S(2)}, u32[]{:S(2)}) %collective-permute-start.30) | collective-permute-done | bytes 524320 | tf_op jit(solution)/shard_map/ppermute | solution.py:401
  127.1 2.6 %collective-permute-done.31.refs_1_ = bf16[128,2048]{1,0:T(8,128)(2,1)S(1)} collective-permute-done((bf16[128,2048]{1,0:T(8,128)(2,1)S(1)}, bf16[128,2048]{1,0:T(8,128)(2,1)S(1)}, u32[]{:S(2)}, u32[]{:S(2)}) %collective-permute-start.31) | collective-permute-done | bytes 524320 | tf_op jit(solution)/shard_map/ppermute | solution.py:401
  132.6 11.5 %collective-permute-done.34.refs_0_ = bf16[128,2048]{1,0:T(8,128)(2,1)S(1)} collective-permute-done((bf16[128,2048]{1,0:T(8,128)(2,1)S(1)}, bf16[128,2048]{1,0:T(8,128)(2,1)S(1)}, u32[]{:S(2)}, u32[]{:S(2)}) %collective-permute-start.34) | collective-permute-done | bytes 524320 | tf_op jit(solution)/shard_map/ppermute | solution.py:401
  144.1 1.6 collective-permute-done.35.refs_1_
  146.8 1.5 collective-permute-start.36
  148.3 11.9 %collective-permute-done.37 = bf16[128,2048]{1,0:T(8,128)(2,1)S(1)} collective-permute-done((bf16[128,2048]{1,0:T(8,128)(2,1)S(1)}, bf16[128,2048]{1,0:T(8,128)(2,1)S(1)}, u32[]{:S(2)}, u32[]{:S(2)}) %collective-permute-start.37) | collective-permute-done | bytes 524320 | tf_op jit(solution)/shard_map/ppermute | solution.py:401
  (119 shorter events, 30.7 us)
Async XLA Ops:
  0.0 15.0 %collective-permute-start.3 = (bf16[512,2048]{1,0:T(8,128)(2,1)}, bf16[512,2048]{1,0:T(8,128)(2,1)S(1)}, u32[]{:S(2)}, u32[]{:S(2)}) collective-permute-start(bf16[512,2048]{1,0:T(8,128)(2,1)} %refs_4_.1), channel_id=1, source_target_pairs={{0,4},{4,0},{8,12},{12,8},{1,5},{5,1},{9,13},{13,9},{2,6},{6,2},{1... | collective-permute-start | bytes 6291464 | tf_op jit(solution)/shard_map/ppermute | solution.py:370
  2.3 12.7 %collective-permute-start.4 = (bf16[128,1024]{1,0:T(8,128)(2,1)}, bf16[128,1024]{1,0:T(8,128)(2,1)S(1)}, u32[]{:S(2)}, u32[]{:S(2)}) collective-permute-start(bf16[128,1024]{1,0:T(8,128)(2,1)} %get-tuple-element.51), channel_id=1, source_target_pairs={{0,8},{4,12},{8,0},{12,4},{1,9},{5,13},{9,1},{13,5},{2,10},{6,14},... | collective-permute-start | bytes 786440 | tf_op jit(solution)/shard_map/ppermute | solution.py:363
  5.1 8.7 %collective-permute-start.1 = (bf16[144,256]{1,0:T(8,128)(2,1)}, bf16[144,256]{1,0:T(8,128)(2,1)S(1)}, u32[]{:S(2)}, u32[]{:S(2)}) collective-permute-start(bf16[144,256]{1,0:T(8,128)(2,1)} %get-tuple-element.49), channel_id=1, source_target_pairs={{0,8},{4,12},{8,0},{12,4},{1,9},{5,13},{9,1},{13,5},{2,10},{6,14},... | collective-permute-start | bytes 221192 | tf_op jit(solution)/shard_map/ppermute | solution.py:367
  5.4 9.6 %collective-permute-start.2 = (bf16[144,256]{1,0:T(8,128)(2,1)}, bf16[144,256]{1,0:T(8,128)(2,1)S(1)}, u32[]{:S(2)}, u32[]{:S(2)}) collective-permute-start(bf16[144,256]{1,0:T(8,128)(2,1)} %get-tuple-element.49), channel_id=1, source_target_pairs={{0,12},{4,8},{8,4},{12,0},{1,13},{5,9},{9,5},{13,1},{2,14},{6,10},... | collective-permute-start | bytes 221192 | tf_op jit(solution)/shard_map/ppermute | solution.py:368
  22.5 14.4 %collective-permute-start.5 = (bf16[128,2048]{1,0:T(8,128)(2,1)}, bf16[128,2048]{1,0:T(8,128)(2,1)S(1)}, u32[]{:S(2)}, u32[]{:S(2)}) collective-permute-start(bf16[128,2048]{1,0:T(8,128)(2,1)} %get-tuple-element.52), channel_id=1, source_target_pairs={{0,8},{4,12},{8,0},{12,4},{1,9},{5,13},{9,1},{13,5},{2,10},{6,14},... | collective-permute-start | bytes 1572872 | tf_op jit(solution)/shard_map/ppermute | solution.py:379
  25.3 11.5 %collective-permute-start.6 = (bf16[16,512]{1,0:T(8,128)(2,1)}, bf16[16,512]{1,0:T(8,128)(2,1)S(1)}, u32[]{:S(2)}, u32[]{:S(2)}) collective-permute-start(bf16[16,512]{1,0:T(8,128)(2,1)} %get-tuple-element.53.quad_ref), channel_id=1, source_target_pairs={{0,1},{1,3},{3,2},{2,0},{4,5},{5,7},{7,6},{6,4},{8,9},{9,11},{11,1... | collective-permute-start | bytes 49160 | tf_op jit(solution)/shard_map/ppermute | solution.py:389
  26.9 9.9 %collective-permute-start.7 = (bf16[16,512]{1,0:T(8,128)(2,1)}, bf16[16,512]{1,0:T(8,128)(2,1)S(1)}, u32[]{:S(2)}, u32[]{:S(2)}) collective-permute-start(bf16[16,512]{1,0:T(8,128)(2,1)} %get-tuple-element.53.quad_ref), channel_id=1, source_target_pairs={{0,3},{1,2},{3,0},{2,1},{4,7},{5,6},{7,4},{6,5},{8,11},{9,10},{11,... | collective-permute-start | bytes 49160 | tf_op jit(solution)/shard_map/ppermute | solution.py:389
  29.4 7.5 %collective-permute-start.8 = (bf16[16,512]{1,0:T(8,128)(2,1)}, bf16[16,512]{1,0:T(8,128)(2,1)S(1)}, u32[]{:S(2)}, u32[]{:S(2)}) collective-permute-start(bf16[16,512]{1,0:T(8,128)(2,1)} %get-tuple-element.53.quad_ref), channel_id=1, source_target_pairs={{0,2},{1,0},{3,1},{2,3},{4,6},{5,4},{7,5},{6,7},{8,10},{9,8},{11,9... | collective-permute-start | bytes 49160 | tf_op jit(solution)/shard_map/ppermute | solution.py:389
  40.2 13.1 %collective-permute-start.10 = (bf16[128,2048]{1,0:T(8,128)(2,1)}, bf16[128,2048]{1,0:T(8,128)(2,1)S(1)}, u32[]{:S(2)}, u32[]{:S(2)}) collective-permute-start(bf16[128,2048]{1,0:T(8,128)(2,1)} %get-tuple-element.55.refs_0_), channel_id=1, source_target_pairs={{0,8},{4,12},{8,0},{12,4},{1,9},{5,13},{9,1},{13,5},{2,10},{6,14},... | collective-permute-start | bytes 1572872 | tf_op jit(solution)/shard_map/ppermute | solution.py:401
  41.6 14.2 %collective-permute-start.11 = (bf16[128,2048]{1,0:T(8,128)(2,1)}, bf16[128,2048]{1,0:T(8,128)(2,1)}, u32[]{:S(2)}, u32[]{:S(2)}) collective-permute-start(bf16[128,2048]{1,0:T(8,128)(2,1)} %get-tuple-element.55.refs_0_), channel_id=1, source_target_pairs={{0,1},{1,3},{3,2},{2,0},{4,5},{5,7},{7,6},{6,4},{8,9},{9,11},{11,1... | collective-permute-start | bytes 1572872 | tf_op jit(solution)/shard_map/ppermute | solution.py:401
  55.8 12.4 %collective-permute-start.13 = (bf16[128,2048]{1,0:T(8,128)(2,1)}, bf16[128,2048]{1,0:T(8,128)(2,1)}, u32[]{:S(2)}, u32[]{:S(2)}) collective-permute-start(bf16[128,2048]{1,0:T(8,128)(2,1)} %get-tuple-element.58.refs_0_), channel_id=1, source_target_pairs={{0,8},{4,12},{8,0},{12,4},{1,9},{5,13},{9,1},{13,5},{2,10},{6,14},... | collective-permute-start | bytes 1572872 | tf_op jit(solution)/shard_map/ppermute | solution.py:401
  56.4 12.9 %collective-permute-start.14 = (bf16[128,2048]{1,0:T(8,128)(2,1)}, bf16[128,2048]{1,0:T(8,128)(2,1)}, u32[]{:S(2)}, u32[]{:S(2)}) collective-permute-start(bf16[128,2048]{1,0:T(8,128)(2,1)} %get-tuple-element.58.refs_0_), channel_id=1, source_target_pairs={{0,1},{1,3},{3,2},{2,0},{4,5},{5,7},{7,6},{6,4},{8,9},{9,11},{11,1... | collective-permute-start | bytes 1572872 | tf_op jit(solution)/shard_map/ppermute | solution.py:401
  57.1 14.5 %collective-permute-start.17 = (bf16[128,2048]{1,0:T(8,128)(2,1)}, bf16[128,2048]{1,0:T(8,128)(2,1)}, u32[]{:S(2)}, u32[]{:S(2)}) collective-permute-start(bf16[128,2048]{1,0:T(8,128)(2,1)} %get-tuple-element.58.refs_0_), channel_id=1, source_target_pairs={{0,4},{4,0},{8,12},{12,8},{1,5},{5,1},{9,13},{13,9},{2,6},{6,2},{1... | collective-permute-start | bytes 1572872 | tf_op jit(solution)/shard_map/ppermute | solution.py:401
  69.2 14.7 %collective-permute-start.15 = (bf16[128,2048]{1,0:T(8,128)(2,1)}, bf16[128,2048]{1,0:T(8,128)(2,1)}, u32[]{:S(2)}, u32[]{:S(2)}) collective-permute-start(bf16[128,2048]{1,0:T(8,128)(2,1)} %get-tuple-element.59.refs_0_), channel_id=1, source_target_pairs={{0,8},{4,12},{8,0},{12,4},{1,9},{5,13},{9,1},{13,5},{2,10},{6,14},... | collective-permute-start | bytes 1572872 | tf_op jit(solution)/shard_map/ppermute | solution.py:401
  70.9 15.3 %collective-permute-start.16 = (bf16[128,2048]{1,0:T(8,128)(2,1)}, bf16[128,2048]{1,0:T(8,128)(2,1)}, u32[]{:S(2)}, u32[]{:S(2)}) collective-permute-start(bf16[128,2048]{1,0:T(8,128)(2,1)} %get-tuple-element.59.refs_0_), channel_id=1, source_target_pairs={{0,1},{1,3},{3,2},{2,0},{4,5},{5,7},{7,6},{6,4},{8,9},{9,11},{11,1... | collective-permute-start | bytes 1572872 | tf_op jit(solution)/shard_map/ppermute | solution.py:401
  86.2 9.9 %collective-permute-start.23 = (bf16[256,2048]{1,0:T(8,128)(2,1)S(1)}, bf16[256,2048]{1,0:T(8,128)(2,1)S(1)}, u32[]{:S(2)}, u32[]{:S(2)}) collective-permute-start(bf16[256,2048]{1,0:T(8,128)(2,1)S(1)} %get-tuple-element.66), channel_id=1, source_target_pairs={{0,4},{4,0},{8,12},{12,8},{1,5},{5,1},{9,13},{13,9},{2,6},{6,2},{1... | collective-permute-start | bytes 3145736 | tf_op jit(solution)/shard_map/ppermute | solution.py:401
  86.7 3.9 %collective-permute-start.22 = (bf16[128,2048]{1,0:T(8,128)(2,1)}, bf16[128,2048]{1,0:T(8,128)(2,1)S(1)}, u32[]{:S(2)}, u32[]{:S(2)}) collective-permute-start(bf16[128,2048]{1,0:T(8,128)(2,1)} %get-tuple-element.63.refs_2_), channel_id=1, source_target_pairs={{0,4},{4,0},{8,12},{12,8},{1,5},{5,1},{9,13},{13,9},{2,6},{6,2},{1... | collective-permute-start | bytes 1572872 | tf_op jit(solution)/shard_map/ppermute | solution.py:401
  88.6 8.8 %collective-permute-start.19 = (bf16[128,1024]{1,0:T(8,128)(2,1)S(1)}, bf16[128,1024]{1,0:T(8,128)(2,1)S(1)}, u32[]{:S(2)}, u32[]{:S(2)}) collective-permute-start(bf16[128,1024]{1,0:T(8,128)(2,1)S(1)} %slice.54), channel_id=1, source_target_pairs={{0,8},{4,12},{8,0},{12,4},{1,9},{5,13},{9,1},{13,5},{2,10},{6,14},... | collective-permute-start | bytes 786440 | tf_op jit(solution)/shard_map/ppermute | solution.py:401
  89.0 9.5 %collective-permute-start.20 = (bf16[128,1024]{1,0:T(8,128)(2,1)S(1)}, bf16[128,1024]{1,0:T(8,128)(2,1)S(1)}, u32[]{:S(2)}, u32[]{:S(2)}) collective-permute-start(bf16[128,1024]{1,0:T(8,128)(2,1)S(1)} %slice.55), channel_id=1, source_target_pairs={{0,1},{1,3},{3,2},{2,0},{4,5},{5,7},{7,6},{6,4},{8,9},{9,11},{11,1... | collective-permute-start | bytes 786440 | tf_op jit(solution)/shard_map/ppermute | solution.py:401
  98.6 10.2 %collective-permute-start.29 = (bf16[256,2048]{1,0:T(8,128)(2,1)S(1)}, bf16[256,2048]{1,0:T(8,128)(2,1)S(1)}, u32[]{:S(2)}, u32[]{:S(2)}) collective-permute-start(bf16[256,2048]{1,0:T(8,128)(2,1)S(1)} %get-tuple-element.73), channel_id=1, source_target_pairs={{0,4},{4,0},{8,12},{12,8},{1,5},{5,1},{9,13},{13,9},{2,6},{6,2},{1... | collective-permute-start | bytes 3145736 | tf_op jit(solution)/shard_map/ppermute | solution.py:401
  98.6 4.0 %collective-permute-start.26 = (bf16[128,2048]{1,0:T(8,128)(2,1)}, bf16[128,2048]{1,0:T(8,128)(2,1)S(1)}, u32[]{:S(2)}, u32[]{:S(2)}) collective-permute-start(bf16[128,2048]{1,0:T(8,128)(2,1)} %get-tuple-element.62.refs_0_), channel_id=1, source_target_pairs={{0,4},{4,0},{8,12},{12,8},{1,5},{5,1},{9,13},{13,9},{2,6},{6,2},{1... | collective-permute-start | bytes 1572872 | tf_op jit(solution)/shard_map/ppermute | solution.py:401
  99.1 4.2 %collective-permute-start.27 = (bf16[128,1024]{1,0:T(8,128)(2,1)S(1)}, bf16[128,1024]{1,0:T(8,128)(2,1)S(1)}, u32[]{:S(2)}, u32[]{:S(2)}) collective-permute-start(bf16[128,1024]{1,0:T(8,128)(2,1)S(1)} %get-tuple-element.69.refs_2_), channel_id=1, source_target_pairs={{0,4},{4,0},{8,12},{12,8},{1,5},{5,1},{9,13},{13,9},{2,6},{6,2},{1... | collective-permute-start | bytes 786440 | tf_op jit(solution)/shard_map/ppermute | solution.py:401
  99.1 4.2 %collective-permute-start.28 = (bf16[128,1024]{1,0:T(8,128)(2,1)S(1)}, bf16[128,1024]{1,0:T(8,128)(2,1)S(1)}, u32[]{:S(2)}, u32[]{:S(2)}) collective-permute-start(bf16[128,1024]{1,0:T(8,128)(2,1)S(1)} %get-tuple-element.70.refs_3_), channel_id=1, source_target_pairs={{0,4},{4,0},{8,12},{12,8},{1,5},{5,1},{9,13},{13,9},{2,6},{6,2},{1... | collective-permute-start | bytes 786440 | tf_op jit(solution)/shard_map/ppermute | solution.py:401
  99.6 9.3 %collective-permute-start.24 = (bf16[128,1024]{1,0:T(8,128)(2,1)S(1)}, bf16[128,1024]{1,0:T(8,128)(2,1)S(1)}, u32[]{:S(2)}, u32[]{:S(2)}) collective-permute-start(bf16[128,1024]{1,0:T(8,128)(2,1)S(1)} %get-tuple-element.67), channel_id=1, source_target_pairs={{0,8},{4,12},{8,0},{12,4},{1,9},{5,13},{9,1},{13,5},{2,10},{6,14},... | collective-permute-start | bytes 786440 | tf_op jit(solution)/shard_map/ppermute | solution.py:401
  102.6 9.5 %collective-permute-start.25 = (bf16[128,1024]{1,0:T(8,128)(2,1)S(1)}, bf16[128,1024]{1,0:T(8,128)(2,1)S(1)}, u32[]{:S(2)}, u32[]{:S(2)}) collective-permute-start(bf16[128,1024]{1,0:T(8,128)(2,1)S(1)} %get-tuple-element.68), channel_id=1, source_target_pairs={{0,1},{1,3},{3,2},{2,0},{4,5},{5,7},{7,6},{6,4},{8,9},{9,11},{11,1... | collective-permute-start | bytes 786440 | tf_op jit(solution)/shard_map/ppermute | solution.py:401
  112.1 8.5 %collective-permute-start.32 = (bf16[256,2048]{1,0:T(8,128)(2,1)S(1)}, bf16[256,2048]{1,0:T(8,128)(2,1)S(1)}, u32[]{:S(2)}, u32[]{:S(2)}) collective-permute-start(bf16[256,2048]{1,0:T(8,128)(2,1)S(1)} %get-tuple-element.80), channel_id=1, source_target_pairs={{0,4},{4,0},{8,12},{12,8},{1,5},{5,1},{9,13},{13,9},{2,6},{6,2},{1... | collective-permute-start | bytes 3145736 | tf_op jit(solution)/shard_map/ppermute | solution.py:401
  112.8 14.3 %collective-permute-start.30 = (bf16[128,2048]{1,0:T(8,128)(2,1)S(1)}, bf16[128,2048]{1,0:T(8,128)(2,1)S(1)}, u32[]{:S(2)}, u32[]{:S(2)}) collective-permute-start(bf16[128,2048]{1,0:T(8,128)(2,1)S(1)} %pad_maximum_fusion), channel_id=1, source_target_pairs={{0,8},{4,12},{8,0},{12,4},{1,9},{5,13},{9,1},{13,5},{2,10},{6,14},... | collective-permute-start | bytes 1572872 | tf_op jit(solution)/shard_map/ppermute | solution.py:401
  114.6 15.2 %collective-permute-start.31 = (bf16[128,2048]{1,0:T(8,128)(2,1)S(1)}, bf16[128,2048]{1,0:T(8,128)(2,1)S(1)}, u32[]{:S(2)}, u32[]{:S(2)}) collective-permute-start(bf16[128,2048]{1,0:T(8,128)(2,1)S(1)} %pad_maximum_fusion.1), channel_id=1, source_target_pairs={{0,1},{1,3},{3,2},{2,0},{4,5},{5,7},{7,6},{6,4},{8,9},{9,11},{11,1... | collective-permute-start | bytes 1572872 | tf_op jit(solution)/shard_map/ppermute | solution.py:401
  129.8 14.3 %collective-permute-start.34 = (bf16[128,2048]{1,0:T(8,128)(2,1)S(1)}, bf16[128,2048]{1,0:T(8,128)(2,1)S(1)}, u32[]{:S(2)}, u32[]{:S(2)}) collective-permute-start(bf16[128,2048]{1,0:T(8,128)(2,1)S(1)} %get-tuple-element.82), channel_id=1, source_target_pairs={{0,8},{4,12},{8,0},{12,4},{1,9},{5,13},{9,1},{13,5},{2,10},{6,14},... | collective-permute-start | bytes 1572872 | tf_op jit(solution)/shard_map/ppermute | solution.py:401
  130.7 15.0 %collective-permute-start.35 = (bf16[128,2048]{1,0:T(8,128)(2,1)S(1)}, bf16[128,2048]{1,0:T(8,128)(2,1)S(1)}, u32[]{:S(2)}, u32[]{:S(2)}) collective-permute-start(bf16[128,2048]{1,0:T(8,128)(2,1)S(1)} %add_convert_fusion.3), channel_id=1, source_target_pairs={{0,1},{1,3},{3,2},{2,0},{4,5},{5,7},{7,6},{6,4},{8,9},{9,11},{11,1... | collective-permute-start | bytes 1572872 | tf_op jit(solution)/shard_map/ppermute | solution.py:401
  146.0 14.2 %collective-permute-start.37 = (bf16[128,2048]{1,0:T(8,128)(2,1)S(1)}, bf16[128,2048]{1,0:T(8,128)(2,1)S(1)}, u32[]{:S(2)}, u32[]{:S(2)}) collective-permute-start(bf16[128,2048]{1,0:T(8,128)(2,1)S(1)} %add_convert_fusion.1), channel_id=1, source_target_pairs={{0,1},{1,3},{3,2},{2,0},{4,5},{5,7},{7,6},{6,4},{8,9},{9,11},{11,1... | collective-permute-start | bytes 1572872 | tf_op jit(solution)/shard_map/ppermute | solution.py:401
  146.8 13.4 %collective-permute-start.36 = (bf16[128,2048]{1,0:T(8,128)(2,1)S(1)}, bf16[128,2048]{1,0:T(8,128)(2,1)S(1)}, u32[]{:S(2)}, u32[]{:S(2)}) collective-permute-start(bf16[128,2048]{1,0:T(8,128)(2,1)S(1)} %get-tuple-element.87), channel_id=1, source_target_pairs={{0,8},{4,12},{8,0},{12,4},{1,9},{5,13},{9,1},{13,5},{2,10},{6,14},... | collective-permute-start | bytes 1572872 | tf_op jit(solution)/shard_map/ppermute | solution.py:401
  (27 other events, 164.0 us)

commit v14 on v13

--- a/solution.py
+++ b/solution.py
@@ -395,6 +395,7 @@
     held = {("row", 0): normed, ("quad", 0): quad}
     held.update({("quad", steps): moved for steps, moved in enumerate(quads, 1)})
     half = normed.shape[1] // 2
+    cut = normed.shape[1] // 4 * 3
     ways = {"across": ("seq", across), "twin": ("seq", twin), "on": ("sub", ring(1))}
 
     def move(array, way):
@@ -424,9 +425,9 @@
 
     def sum_of(step, more):
         parts = [held["own", step], held["met", step], held["back", step]] + more
-        if held["back", step].shape[1] == half:
-            left = sum(part[:, :half].astype(jnp.float32) for part in parts)
-            right = sum(part[:, half:].astype(jnp.float32) for part in parts if part.shape[1] > half)
+        if held["back", step].shape[1] == cut:
+            left = sum(part[:, :cut].astype(jnp.float32) for part in parts)
+            right = sum(part[:, cut:].astype(jnp.float32) for part in parts if part.shape[1] > cut)
             return jnp.concatenate([left, right], axis=1)
         return sum(part.astype(jnp.float32) for part in parts)
 
@@ -448,9 +449,9 @@
                 now["late", step] = move(held["apart", step], "on")
             elif step == 2:
                 away = held["away", step]
-                added = away[:, half:].astype(jnp.float32) + held["late", 1].astype(jnp.float32)
+                added = away[:, cut:].astype(jnp.float32) + held["late", 1].astype(jnp.float32)
                 now["back", step] = move(
-                    jnp.concatenate([away[:, :half], added.astype(jnp.bfloat16)], axis=1), "across"
+                    jnp.concatenate([away[:, :cut], added.astype(jnp.bfloat16)], axis=1), "across"
                 )
             else:
                 now["back", step] = move(held["away", step], "across")
@@ -474,8 +475,8 @@
         if 1 <= step <= last or turn == n_sub + 3:
             away = twin_sum(step)
             if step == 1:
-                now["away", step] = away[:, :half]
-                now["apart", step] = away[:, half:]
+                now["away", step] = away[:, :cut]
+                now["apart", step] = away[:, cut:]
             else:
                 now["away", step] = away
         if turn < n_sub + 4:

time: 162 us -> 163 us (level)
  waiting for transfers between devices: 80.2 us -> 82.1 us
    ppermute x29, waiting for transfers between devices: 72.5 us -> 74.5 us  [move(): return lax.ppermute(array, *ways[way])]
  transfers between devices with their start and end apart: 38 -> 38, of which waited for: 20 -> 19; matrix products, arithmetic and copies ran while one was open for 3% -> 3% of each run, Pallas kernels for 18% -> 18%
where the time goes in v14:
time: 163 us
  waiting for transfers between devices  82.1 us (50%)
  Pallas kernels  36.8 us (23%)
  starting transfers between devices  30.5 us (19%)
  local copies, waits for them, and re-layouts  10.4 us (6%)
  other arithmetic  2.71 us (2%)
    ppermute x29, waiting for transfers between devices, move(): return lax.ppermute(array, *ways[way])  74.5 us
    pallas_call x4, Pallas kernels, experts_on_rows(): pl.pallas_call(functools.partial(experts_kernel, cap=cap, pieces=pieces),...  21.1 us
    ppermute x29, starting transfers between devices, move(): return lax.ppermute(array, *ways[way])  18.4 us
    pallas_call x2, Pallas kernels, attend(): pl.pallas_call(functools.partial(attend_kernel, scale=1.0 / HD ** 0.5), i...  11.3 us
    unnamed x42, local copies, waits for them, and re-layouts  6.63 us
    ppermute x1, waiting for transfers between devices, gathered_plan(): lax.ppermute(kv_away, 'seq', across)  6.46 us
    ppermute x3, starting transfers between devices, gathered_plan(): lax.ppermute(quad, 'sub', ring(steps))  5.63 us
  transfers between devices with their start and end apart: 38, of which 19 were waited for; matrix products, arithmetic and copies ran while one was open for 3% of the time, Pallas kernels for 18%

profile of v14, /device:TPU:0, one launch (start us, length us, event | category | flops | bytes accessed | tf_op | source)
XLA Modules:
  0.0 162.9 jit_solution(6582640745529429982)
XLA Ops:
  0.5 1.9 %shard_map.109 = (bf16[128,1024]{1,0:T(8,128)(2,1)}, bf16[144,256]{1,0:T(8,128)(2,1)}, bf16[144,256]{1,0:T(8,128)(2,1)}) custom-call(s32[1]{0:T(128)} %bitcast.7.chip_ref, bf16[128,2048]{1,0:T(8,128)(2,1)} %bitcast.35, bf16[128,256]{1,0:T(8,128)(2,1)} %bitcast.38, bf16[128,256]{1,0:T(8,128)(2,1)} %bitcast.39, s32[8,128]{1,0:T(8,128)} %bitcast.40, ...), custom_call_target="tpu_custom_call" | custom-call | tf_op jit(solution)/shard_map/pallas_call | solution.py:87
  2.3 2.5 %collective-permute-start.4 = (bf16[128,1024]{1,0:T(8,128)(2,1)}, bf16[128,1024]{1,0:T(8,128)(2,1)S(1)}, u32[]{:S(2)}, u32[]{:S(2)}) collective-permute-start(bf16[128,1024]{1,0:T(8,128)(2,1)} %get-tuple-element.51), channel_id=1, source_target_pairs={{0,8},{4,12},{8,0},{12,4},{1,9},{5,13},{9,1},{13,5},{2,10},{6,14},... | collective-permute-start | bytes 786440 | tf_op jit(solution)/shard_map/ppermute | solution.py:363
  7.4 6.5 %collective-permute-done.1.refs_2_ = bf16[144,256]{1,0:T(8,128)(2,1)S(1)} collective-permute-done((bf16[144,256]{1,0:T(8,128)(2,1)}, bf16[144,256]{1,0:T(8,128)(2,1)S(1)}, u32[]{:S(2)}, u32[]{:S(2)}) %collective-permute-start.1) | collective-permute-done | bytes 73760 | tf_op jit(solution)/shard_map/ppermute | solution.py:367
  17.1 5.4 %shard_map.111 = (bf16[128,2048]{1,0:T(8,128)(2,1)}, bf16[16,512]{1,0:T(8,128)(2,1)}) custom-call(s32[7]{0:T(128)} %stack.38.place_ref, bf16[128,1024]{1,0:T(8,128)(2,1)} %copy-done.19, bf16[144,256]{1,0:T(8,128)(2,1)} %get-tuple-element.48.refs_0_, bf16[144,256]{1,0:T(8,128)(2,1)} %copy-done.16, bf16[144,256]{1,0:T(8,128)(2,1)} %copy-done.17, ...), custom_call_target="tpu_custom_call" | custom-call | flops 805306368 | bytes 5242880 | tf_op jit(solution)/shard_map/pallas_call | solution.py:159
  22.5 1.6 collective-permute-start.5
  25.3 1.6 collective-permute-start.6
  26.8 2.5 %collective-permute-start.7 = (bf16[16,512]{1,0:T(8,128)(2,1)}, bf16[16,512]{1,0:T(8,128)(2,1)S(1)}, u32[]{:S(2)}, u32[]{:S(2)}) collective-permute-start(bf16[16,512]{1,0:T(8,128)(2,1)} %get-tuple-element.53.quad_ref), channel_id=1, source_target_pairs={{0,3},{1,2},{3,0},{2,1},{4,7},{5,6},{7,4},{6,5},{8,11},{9,10},{11,... | collective-permute-start | bytes 49160 | tf_op jit(solution)/shard_map/ppermute | solution.py:389
  29.3 1.6 collective-permute-start.8
  30.9 5.9 %shard_map.110 = (f32[128,2048]{1,0:T(8,128)}, bf16[16,512]{1,0:T(8,128)(2,1)}) custom-call(s32[7]{0:T(128)} %stack.37.place_ref, bf16[128,2048]{1,0:T(8,128)(2,1)} %bitcast.36, bf16[144,256]{1,0:T(8,128)(2,1)} %get-tuple-element.48.refs_0_, bf16[144,256]{1,0:T(8,128)(2,1)} %copy-done.16, bf16[144,256]{1,0:T(8,128)(2,1)} %copy-done.17, ...), custom_call_target="tpu_custom_call" | custom-call | flops 805306368 | bytes 5242880 | tf_op jit(solution)/shard_map/pallas_call | solution.py:159
  37.6 2.5 %shard_map.112 = (bf16[128,2048]{1,0:T(8,128)(2,1)}, bf16[128,2048]{1,0:T(8,128)(2,1)}) custom-call(f32[128,2048]{1,0:T(8,128)} %get-tuple-element.50.own_ref, bf16[128,2048]{1,0:T(8,128)(2,1)} %copy-done.14, bf16[1,2048]{1,0:T(2,128)(2,1)} %broadcast_in_dim.6.gain_ref, bf16[16,512]{1,0:T(8,128)(2,1)} %copy-done.10, bf16[16,512]{1,0:T(8,128)(2,1)} %copy-done.8, ...), custom_call_target="tpu_custom_call" | custom-call | tf_op jit(solution)/shard_map/pallas_call | solution.py:202
  40.2 1.5 collective-permute-start.10
  41.7 1.6 collective-permute-start.11
  43.2 10.1 %collective-permute-done.10.refs_0_ = bf16[128,2048]{1,0:T(8,128)(2,1)S(1)} collective-permute-done((bf16[128,2048]{1,0:T(8,128)(2,1)}, bf16[128,2048]{1,0:T(8,128)(2,1)S(1)}, u32[]{:S(2)}, u32[]{:S(2)}) %collective-permute-start.10) | collective-permute-done | bytes 524320 | tf_op jit(solution)/shard_map/ppermute | solution.py:402
  53.4 2.5 %collective-permute-done.11.refs_1_ = bf16[128,2048]{1,0:T(8,128)(2,1)} collective-permute-done((bf16[128,2048]{1,0:T(8,128)(2,1)}, bf16[128,2048]{1,0:T(8,128)(2,1)}, u32[]{:S(2)}, u32[]{:S(2)}) %collective-permute-start.11) | collective-permute-done | bytes 524320 | tf_op jit(solution)/shard_map/ppermute | solution.py:402
  57.1 11.1 %collective-permute-done.13.refs_0_ = bf16[128,2048]{1,0:T(8,128)(2,1)} collective-permute-done((bf16[128,2048]{1,0:T(8,128)(2,1)}, bf16[128,2048]{1,0:T(8,128)(2,1)}, u32[]{:S(2)}, u32[]{:S(2)}) %collective-permute-start.13) | collective-permute-done | bytes 524320 | tf_op jit(solution)/shard_map/ppermute | solution.py:402
  69.3 1.6 collective-permute-start.15
  71.7 1.9 %copy-done.1 = bf16[1,2048,768]{2,1,0:T(8,128)(2,1)S(1)} copy-done((bf16[1,2048,768]{2,1,0:T(8,128)(2,1)S(1)}, bf16[1,2048,768]{2,1,0:T(8,128)(2,1)}, u32[]{:S(2)}) %copy-start.1) | copy-done | bytes 3145752
  73.6 1.9 %copy-done.2 = bf16[1,768,2048]{2,1,0:T(8,128)(2,1)S(1)} copy-done((bf16[1,768,2048]{2,1,0:T(8,128)(2,1)S(1)}, bf16[1,768,2048]{2,1,0:T(8,128)(2,1)}, u32[]{:S(2)}) %copy-start.2) | copy-done | bytes 3145752
  75.5 5.8 %shard_map.116 = (bf16[128,2048]{1,0:T(8,128)(2,1)S(1)}, bf16[128,2048]{1,0:T(8,128)(2,1)S(1)}, bf16[256,2048]{1,0:T(8,128)(2,1)S(1)}) custom-call(s32[1]{0:T(128)} %bitcast.15.mine_ref, bf16[16,512]{1,0:T(8,128)(2,1)S(1)} %copy-done.11, bf16[128,2048]{1,0:T(8,128)(2,1)} %get-tuple-element.58.refs_0_, bf16[128,2048]{1,0:T(8,128)(2,1)} %collective-permute-done.17.refs_1_, ...), custom_call_target="tpu_custom_call" | custom-call | tf_op jit(solution)/shard_map/pallas_call | solution.py:302
  81.3 2.6 %collective-permute-done.15.refs_0_ = bf16[128,2048]{1,0:T(8,128)(2,1)} collective-permute-done((bf16[128,2048]{1,0:T(8,128)(2,1)}, bf16[128,2048]{1,0:T(8,128)(2,1)}, u32[]{:S(2)}, u32[]{:S(2)}) %collective-permute-start.15) | collective-permute-done | bytes 524320 | tf_op jit(solution)/shard_map/ppermute | solution.py:402
  84.0 2.2 %collective-permute-done.16.refs_1_ = bf16[128,2048]{1,0:T(8,128)(2,1)} collective-permute-done((bf16[128,2048]{1,0:T(8,128)(2,1)}, bf16[128,2048]{1,0:T(8,128)(2,1)}, u32[]{:S(2)}, u32[]{:S(2)}) %collective-permute-start.16) | collective-permute-done | bytes 524320 | tf_op jit(solution)/shard_map/ppermute | solution.py:402
  90.6 5.5 %shard_map.118 = (bf16[128,2048]{1,0:T(8,128)(2,1)S(1)}, bf16[128,2048]{1,0:T(8,128)(2,1)S(1)}, bf16[256,2048]{1,0:T(8,128)(2,1)S(1)}) custom-call(s32[1]{0:T(128)} %bitcast.15.mine_ref, bf16[16,512]{1,0:T(8,128)(2,1)S(1)} %copy-done.9, bf16[128,2048]{1,0:T(8,128)(2,1)} %get-tuple-element.59.refs_0_, bf16[128,2048]{1,0:T(8,128)(2,1)S(1)} %collective-permute-done.21.refs_1_, ...), custom_call_target="tpu_custom_call" | custom-call | tf_op jit(solution)/shard_map/pallas_call | solution.py:302
  99.7 2.9 %collective-permute-done.26.refs_1_ = bf16[128,2048]{1,0:T(8,128)(2,1)S(1)} collective-permute-done((bf16[128,2048]{1,0:T(8,128)(2,1)}, bf16[128,2048]{1,0:T(8,128)(2,1)S(1)}, u32[]{:S(2)}, u32[]{:S(2)}) %collective-permute-start.26) | collective-permute-done | bytes 524320 | tf_op jit(solution)/shard_map/ppermute | solution.py:402
  105.2 5.4 %shard_map.120 = (bf16[128,2048]{1,0:T(8,128)(2,1)S(1)}, bf16[128,2048]{1,0:T(8,128)(2,1)S(1)}, bf16[256,2048]{1,0:T(8,128)(2,1)S(1)}) custom-call(s32[1]{0:T(128)} %bitcast.15.mine_ref, bf16[16,512]{1,0:T(8,128)(2,1)S(1)} %copy-done.7, bf16[128,2048]{1,0:T(8,128)(2,1)} %get-tuple-element.62.refs_0_, bf16[128,2048]{1,0:T(8,128)(2,1)S(1)} %collective-permute-done.26.refs_1_, ...), custom_call_target="tpu_custom_call" | custom-call | tf_op jit(solution)/shard_map/pallas_call | solution.py:302
  110.8 3.4 %collective-permute-done.24.refs_0_ = bf16[128,1536]{1,0:T(8,128)(2,1)S(1)} collective-permute-done((bf16[128,1536]{1,0:T(8,128)(2,1)S(1)}, bf16[128,1536]{1,0:T(8,128)(2,1)S(1)}, u32[]{:S(2)}, u32[]{:S(2)}) %collective-permute-start.24) | collective-permute-done | bytes 393248 | tf_op jit(solution)/shard_map/ppermute | solution.py:402
  114.3 1.6 collective-permute-start.30
  117.1 4.3 %shard_map.114 = (bf16[128,2048]{1,0:T(8,128)(2,1)S(1)}, bf16[128,2048]{1,0:T(8,128)(2,1)S(1)}, bf16[256,2048]{1,0:T(8,128)(2,1)S(1)}) custom-call(s32[1]{0:T(128)} %bitcast.15.mine_ref, bf16[16,512]{1,0:T(8,128)(2,1)S(1)} %copy-done.12, bf16[128,2048]{1,0:T(8,128)(2,1)S(1)} %copy-done.3, bf16[128,2048]{1,0:T(8,128)(2,1)S(1)} %collective-permute-done.9.refs_1_, ...), custom_call_target="tpu_custom_call" | custom-call | tf_op jit(solution)/shard_map/pallas_call | solution.py:302
  121.6 7.1 %collective-permute-done.30.refs_0_ = bf16[128,2048]{1,0:T(8,128)(2,1)S(1)} collective-permute-done((bf16[128,2048]{1,0:T(8,128)(2,1)S(1)}, bf16[128,2048]{1,0:T(8,128)(2,1)S(1)}, u32[]{:S(2)}, u32[]{:S(2)}) %collective-permute-start.30) | collective-permute-done | bytes 524320 | tf_op jit(solution)/shard_map/ppermute | solution.py:402
  128.7 2.6 %collective-permute-done.31.refs_1_ = bf16[128,2048]{1,0:T(8,128)(2,1)S(1)} collective-permute-done((bf16[128,2048]{1,0:T(8,128)(2,1)S(1)}, bf16[128,2048]{1,0:T(8,128)(2,1)S(1)}, u32[]{:S(2)}, u32[]{:S(2)}) %collective-permute-start.31) | collective-permute-done | bytes 524320 | tf_op jit(solution)/shard_map/ppermute | solution.py:402
  134.1 11.5 %collective-permute-done.34.refs_0_ = bf16[128,2048]{1,0:T(8,128)(2,1)S(1)} collective-permute-done((bf16[128,2048]{1,0:T(8,128)(2,1)S(1)}, bf16[128,2048]{1,0:T(8,128)(2,1)S(1)}, u32[]{:S(2)}, u32[]{:S(2)}) %collective-permute-start.34) | collective-permute-done | bytes 524320 | tf_op jit(solution)/shard_map/ppermute | solution.py:402
  145.6 1.6 collective-permute-done.35.refs_1_
  149.8 11.9 %collective-permute-done.37 = bf16[128,2048]{1,0:T(8,128)(2,1)S(1)} collective-permute-done((bf16[128,2048]{1,0:T(8,128)(2,1)S(1)}, bf16[128,2048]{1,0:T(8,128)(2,1)S(1)}, u32[]{:S(2)}, u32[]{:S(2)}) %collective-permute-start.37) | collective-permute-done | bytes 524320 | tf_op jit(solution)/shard_map/ppermute | solution.py:402
  (121 shorter events, 30.0 us)
Async XLA Ops:
  0.0 15.0 %collective-permute-start.3 = (bf16[512,2048]{1,0:T(8,128)(2,1)}, bf16[512,2048]{1,0:T(8,128)(2,1)S(1)}, u32[]{:S(2)}, u32[]{:S(2)}) collective-permute-start(bf16[512,2048]{1,0:T(8,128)(2,1)} %refs_4_.1), channel_id=1, source_target_pairs={{0,4},{4,0},{8,12},{12,8},{1,5},{5,1},{9,13},{13,9},{2,6},{6,2},{1... | collective-permute-start | bytes 6291464 | tf_op jit(solution)/shard_map/ppermute | solution.py:370
  2.3 12.7 %collective-permute-start.4 = (bf16[128,1024]{1,0:T(8,128)(2,1)}, bf16[128,1024]{1,0:T(8,128)(2,1)S(1)}, u32[]{:S(2)}, u32[]{:S(2)}) collective-permute-start(bf16[128,1024]{1,0:T(8,128)(2,1)} %get-tuple-element.51), channel_id=1, source_target_pairs={{0,8},{4,12},{8,0},{12,4},{1,9},{5,13},{9,1},{13,5},{2,10},{6,14},... | collective-permute-start | bytes 786440 | tf_op jit(solution)/shard_map/ppermute | solution.py:363
  5.1 8.7 %collective-permute-start.1 = (bf16[144,256]{1,0:T(8,128)(2,1)}, bf16[144,256]{1,0:T(8,128)(2,1)S(1)}, u32[]{:S(2)}, u32[]{:S(2)}) collective-permute-start(bf16[144,256]{1,0:T(8,128)(2,1)} %get-tuple-element.49), channel_id=1, source_target_pairs={{0,8},{4,12},{8,0},{12,4},{1,9},{5,13},{9,1},{13,5},{2,10},{6,14},... | collective-permute-start | bytes 221192 | tf_op jit(solution)/shard_map/ppermute | solution.py:367
  5.4 9.6 %collective-permute-start.2 = (bf16[144,256]{1,0:T(8,128)(2,1)}, bf16[144,256]{1,0:T(8,128)(2,1)S(1)}, u32[]{:S(2)}, u32[]{:S(2)}) collective-permute-start(bf16[144,256]{1,0:T(8,128)(2,1)} %get-tuple-element.49), channel_id=1, source_target_pairs={{0,12},{4,8},{8,4},{12,0},{1,13},{5,9},{9,5},{13,1},{2,14},{6,10},... | collective-permute-start | bytes 221192 | tf_op jit(solution)/shard_map/ppermute | solution.py:368
  22.5 14.3 %collective-permute-start.5 = (bf16[128,2048]{1,0:T(8,128)(2,1)}, bf16[128,2048]{1,0:T(8,128)(2,1)S(1)}, u32[]{:S(2)}, u32[]{:S(2)}) collective-permute-start(bf16[128,2048]{1,0:T(8,128)(2,1)} %get-tuple-element.52), channel_id=1, source_target_pairs={{0,8},{4,12},{8,0},{12,4},{1,9},{5,13},{9,1},{13,5},{2,10},{6,14},... | collective-permute-start | bytes 1572872 | tf_op jit(solution)/shard_map/ppermute | solution.py:379
  25.3 11.5 %collective-permute-start.6 = (bf16[16,512]{1,0:T(8,128)(2,1)}, bf16[16,512]{1,0:T(8,128)(2,1)S(1)}, u32[]{:S(2)}, u32[]{:S(2)}) collective-permute-start(bf16[16,512]{1,0:T(8,128)(2,1)} %get-tuple-element.53.quad_ref), channel_id=1, source_target_pairs={{0,1},{1,3},{3,2},{2,0},{4,5},{5,7},{7,6},{6,4},{8,9},{9,11},{11,1... | collective-permute-start | bytes 49160 | tf_op jit(solution)/shard_map/ppermute | solution.py:389
  26.8 9.9 %collective-permute-start.7 = (bf16[16,512]{1,0:T(8,128)(2,1)}, bf16[16,512]{1,0:T(8,128)(2,1)S(1)}, u32[]{:S(2)}, u32[]{:S(2)}) collective-permute-start(bf16[16,512]{1,0:T(8,128)(2,1)} %get-tuple-element.53.quad_ref), channel_id=1, source_target_pairs={{0,3},{1,2},{3,0},{2,1},{4,7},{5,6},{7,4},{6,5},{8,11},{9,10},{11,... | collective-permute-start | bytes 49160 | tf_op jit(solution)/shard_map/ppermute | solution.py:389
  29.3 7.5 %collective-permute-start.8 = (bf16[16,512]{1,0:T(8,128)(2,1)}, bf16[16,512]{1,0:T(8,128)(2,1)S(1)}, u32[]{:S(2)}, u32[]{:S(2)}) collective-permute-start(bf16[16,512]{1,0:T(8,128)(2,1)} %get-tuple-element.53.quad_ref), channel_id=1, source_target_pairs={{0,2},{1,0},{3,1},{2,3},{4,6},{5,4},{7,5},{6,7},{8,10},{9,8},{11,9... | collective-permute-start | bytes 49160 | tf_op jit(solution)/shard_map/ppermute | solution.py:389
  40.2 13.2 %collective-permute-start.10 = (bf16[128,2048]{1,0:T(8,128)(2,1)}, bf16[128,2048]{1,0:T(8,128)(2,1)S(1)}, u32[]{:S(2)}, u32[]{:S(2)}) collective-permute-start(bf16[128,2048]{1,0:T(8,128)(2,1)} %get-tuple-element.55.refs_0_), channel_id=1, source_target_pairs={{0,8},{4,12},{8,0},{12,4},{1,9},{5,13},{9,1},{13,5},{2,10},{6,14},... | collective-permute-start | bytes 1572872 | tf_op jit(solution)/shard_map/ppermute | solution.py:402
  41.7 14.2 %collective-permute-start.11 = (bf16[128,2048]{1,0:T(8,128)(2,1)}, bf16[128,2048]{1,0:T(8,128)(2,1)}, u32[]{:S(2)}, u32[]{:S(2)}) collective-permute-start(bf16[128,2048]{1,0:T(8,128)(2,1)} %get-tuple-element.55.refs_0_), channel_id=1, source_target_pairs={{0,1},{1,3},{3,2},{2,0},{4,5},{5,7},{7,6},{6,4},{8,9},{9,11},{11,1... | collective-permute-start | bytes 1572872 | tf_op jit(solution)/shard_map/ppermute | solution.py:402
  55.9 12.4 %collective-permute-start.13 = (bf16[128,2048]{1,0:T(8,128)(2,1)}, bf16[128,2048]{1,0:T(8,128)(2,1)}, u32[]{:S(2)}, u32[]{:S(2)}) collective-permute-start(bf16[128,2048]{1,0:T(8,128)(2,1)} %get-tuple-element.58.refs_0_), channel_id=1, source_target_pairs={{0,8},{4,12},{8,0},{12,4},{1,9},{5,13},{9,1},{13,5},{2,10},{6,14},... | collective-permute-start | bytes 1572872 | tf_op jit(solution)/shard_map/ppermute | solution.py:402
  56.4 12.9 %collective-permute-start.14 = (bf16[128,2048]{1,0:T(8,128)(2,1)}, bf16[128,2048]{1,0:T(8,128)(2,1)}, u32[]{:S(2)}, u32[]{:S(2)}) collective-permute-start(bf16[128,2048]{1,0:T(8,128)(2,1)} %get-tuple-element.58.refs_0_), channel_id=1, source_target_pairs={{0,1},{1,3},{3,2},{2,0},{4,5},{5,7},{7,6},{6,4},{8,9},{9,11},{11,1... | collective-permute-start | bytes 1572872 | tf_op jit(solution)/shard_map/ppermute | solution.py:402
  57.1 14.5 %collective-permute-start.17 = (bf16[128,2048]{1,0:T(8,128)(2,1)}, bf16[128,2048]{1,0:T(8,128)(2,1)}, u32[]{:S(2)}, u32[]{:S(2)}) collective-permute-start(bf16[128,2048]{1,0:T(8,128)(2,1)} %get-tuple-element.58.refs_0_), channel_id=1, source_target_pairs={{0,4},{4,0},{8,12},{12,8},{1,5},{5,1},{9,13},{13,9},{2,6},{6,2},{1... | collective-permute-start | bytes 1572872 | tf_op jit(solution)/shard_map/ppermute | solution.py:402
  69.3 14.7 %collective-permute-start.15 = (bf16[128,2048]{1,0:T(8,128)(2,1)}, bf16[128,2048]{1,0:T(8,128)(2,1)}, u32[]{:S(2)}, u32[]{:S(2)}) collective-permute-start(bf16[128,2048]{1,0:T(8,128)(2,1)} %get-tuple-element.59.refs_0_), channel_id=1, source_target_pairs={{0,8},{4,12},{8,0},{12,4},{1,9},{5,13},{9,1},{13,5},{2,10},{6,14},... | collective-permute-start | bytes 1572872 | tf_op jit(solution)/shard_map/ppermute | solution.py:402
  70.9 15.3 %collective-permute-start.16 = (bf16[128,2048]{1,0:T(8,128)(2,1)}, bf16[128,2048]{1,0:T(8,128)(2,1)}, u32[]{:S(2)}, u32[]{:S(2)}) collective-permute-start(bf16[128,2048]{1,0:T(8,128)(2,1)} %get-tuple-element.59.refs_0_), channel_id=1, source_target_pairs={{0,1},{1,3},{3,2},{2,0},{4,5},{5,7},{7,6},{6,4},{8,9},{9,11},{11,1... | collective-permute-start | bytes 1572872 | tf_op jit(solution)/shard_map/ppermute | solution.py:402
  86.2 9.9 %collective-permute-start.23 = (bf16[256,2048]{1,0:T(8,128)(2,1)S(1)}, bf16[256,2048]{1,0:T(8,128)(2,1)S(1)}, u32[]{:S(2)}, u32[]{:S(2)}) collective-permute-start(bf16[256,2048]{1,0:T(8,128)(2,1)S(1)} %get-tuple-element.66), channel_id=1, source_target_pairs={{0,4},{4,0},{8,12},{12,8},{1,5},{5,1},{9,13},{13,9},{2,6},{6,2},{1... | collective-permute-start | bytes 3145736 | tf_op jit(solution)/shard_map/ppermute | solution.py:402
  88.7 8.8 %collective-permute-start.19 = (bf16[128,1024]{1,0:T(8,128)(2,1)S(1)}, bf16[128,1024]{1,0:T(8,128)(2,1)S(1)}, u32[]{:S(2)}, u32[]{:S(2)}) collective-permute-start(bf16[128,1024]{1,0:T(8,128)(2,1)S(1)} %slice.54), channel_id=1, source_target_pairs={{0,8},{4,12},{8,0},{12,4},{1,9},{5,13},{9,1},{13,5},{2,10},{6,14},... | collective-permute-start | bytes 786440 | tf_op jit(solution)/shard_map/ppermute | solution.py:402
  89.1 9.4 %collective-permute-start.20 = (bf16[128,1024]{1,0:T(8,128)(2,1)S(1)}, bf16[128,1024]{1,0:T(8,128)(2,1)S(1)}, u32[]{:S(2)}, u32[]{:S(2)}) collective-permute-start(bf16[128,1024]{1,0:T(8,128)(2,1)S(1)} %slice.55), channel_id=1, source_target_pairs={{0,1},{1,3},{3,2},{2,0},{4,5},{5,7},{7,6},{6,4},{8,9},{9,11},{11,1... | collective-permute-start | bytes 786440 | tf_op jit(solution)/shard_map/ppermute | solution.py:402
  98.6 12.0 %collective-permute-start.29 = (bf16[256,2048]{1,0:T(8,128)(2,1)S(1)}, bf16[256,2048]{1,0:T(8,128)(2,1)S(1)}, u32[]{:S(2)}, u32[]{:S(2)}) collective-permute-start(bf16[256,2048]{1,0:T(8,128)(2,1)S(1)} %get-tuple-element.73), channel_id=1, source_target_pairs={{0,4},{4,0},{8,12},{12,8},{1,5},{5,1},{9,13},{13,9},{2,6},{6,2},{1... | collective-permute-start | bytes 3145736 | tf_op jit(solution)/shard_map/ppermute | solution.py:402
  98.6 4.0 %collective-permute-start.26 = (bf16[128,2048]{1,0:T(8,128)(2,1)}, bf16[128,2048]{1,0:T(8,128)(2,1)S(1)}, u32[]{:S(2)}, u32[]{:S(2)}) collective-permute-start(bf16[128,2048]{1,0:T(8,128)(2,1)} %get-tuple-element.62.refs_0_), channel_id=1, source_target_pairs={{0,4},{4,0},{8,12},{12,8},{1,5},{5,1},{9,13},{13,9},{2,6},{6,2},{1... | collective-permute-start | bytes 1572872 | tf_op jit(solution)/shard_map/ppermute | solution.py:402
  99.1 5.4 %collective-permute-start.28 = (bf16[128,1024]{1,0:T(8,128)(2,1)S(1)}, bf16[128,1024]{1,0:T(8,128)(2,1)S(1)}, u32[]{:S(2)}, u32[]{:S(2)}) collective-permute-start(bf16[128,1024]{1,0:T(8,128)(2,1)S(1)} %get-tuple-element.70.refs_3_), channel_id=1, source_target_pairs={{0,4},{4,0},{8,12},{12,8},{1,5},{5,1},{9,13},{13,9},{2,6},{6,2},{1... | collective-permute-start | bytes 786440 | tf_op jit(solution)/shard_map/ppermute | solution.py:402
  99.6 17.4 %collective-permute-start.9 = (bf16[128,2048]{1,0:T(8,128)(2,1)S(1)}, bf16[128,2048]{1,0:T(8,128)(2,1)S(1)}, u32[]{:S(2)}, u32[]{:S(2)}) collective-permute-start(bf16[128,2048]{1,0:T(8,128)(2,1)S(1)} %copy-done.3), channel_id=1, source_target_pairs={{0,4},{4,0},{8,12},{12,8},{1,5},{5,1},{9,13},{13,9},{2,6},{6,2},{1... | collective-permute-start | bytes 1572872 | tf_op jit(solution)/shard_map/ppermute | solution.py:402
  102.6 14.5 %collective-permute-start.12 = (bf16[128,2048]{1,0:T(8,128)(2,1)S(1)}, bf16[128,2048]{1,0:T(8,128)(2,1)S(1)}, u32[]{:S(2)}, u32[]{:S(2)}) collective-permute-start(bf16[128,2048]{1,0:T(8,128)(2,1)S(1)} %copy-done.5), channel_id=1, source_target_pairs={{0,4},{4,0},{8,12},{12,8},{1,5},{5,1},{9,13},{13,9},{2,6},{6,2},{1... | collective-permute-start | bytes 1572872 | tf_op jit(solution)/shard_map/ppermute | solution.py:402
  103.0 11.2 %collective-permute-start.24 = (bf16[128,1536]{1,0:T(8,128)(2,1)S(1)}, bf16[128,1536]{1,0:T(8,128)(2,1)S(1)}, u32[]{:S(2)}, u32[]{:S(2)}) collective-permute-start(bf16[128,1536]{1,0:T(8,128)(2,1)S(1)} %get-tuple-element.67), channel_id=1, source_target_pairs={{0,8},{4,12},{8,0},{12,4},{1,9},{5,13},{9,1},{13,5},{2,10},{6,14},... | collective-permute-start | bytes 1179656 | tf_op jit(solution)/shard_map/ppermute | solution.py:402
  104.5 6.3 %collective-permute-start.25 = (bf16[128,512]{1,0:T(8,128)(2,1)S(1)}, bf16[128,512]{1,0:T(8,128)(2,1)S(1)}, u32[]{:S(2)}, u32[]{:S(2)}) collective-permute-start(bf16[128,512]{1,0:T(8,128)(2,1)S(1)} %get-tuple-element.68), channel_id=1, source_target_pairs={{0,1},{1,3},{3,2},{2,0},{4,5},{5,7},{7,6},{6,4},{8,9},{9,11},{11,1... | collective-permute-start | bytes 393224 | tf_op jit(solution)/shard_map/ppermute | solution.py:402
  114.1 7.3 %collective-permute-start.32 = (bf16[256,2048]{1,0:T(8,128)(2,1)S(1)}, bf16[256,2048]{1,0:T(8,128)(2,1)S(1)}, u32[]{:S(2)}, u32[]{:S(2)}) collective-permute-start(bf16[256,2048]{1,0:T(8,128)(2,1)S(1)} %get-tuple-element.80), channel_id=1, source_target_pairs={{0,4},{4,0},{8,12},{12,8},{1,5},{5,1},{9,13},{13,9},{2,6},{6,2},{1... | collective-permute-start | bytes 3145736 | tf_op jit(solution)/shard_map/ppermute | solution.py:402
  114.3 14.4 %collective-permute-start.30 = (bf16[128,2048]{1,0:T(8,128)(2,1)S(1)}, bf16[128,2048]{1,0:T(8,128)(2,1)S(1)}, u32[]{:S(2)}, u32[]{:S(2)}) collective-permute-start(bf16[128,2048]{1,0:T(8,128)(2,1)S(1)} %pad_maximum_fusion), channel_id=1, source_target_pairs={{0,8},{4,12},{8,0},{12,4},{1,9},{5,13},{9,1},{13,5},{2,10},{6,14},... | collective-permute-start | bytes 1572872 | tf_op jit(solution)/shard_map/ppermute | solution.py:402
  116.0 15.2 %collective-permute-start.31 = (bf16[128,2048]{1,0:T(8,128)(2,1)S(1)}, bf16[128,2048]{1,0:T(8,128)(2,1)S(1)}, u32[]{:S(2)}, u32[]{:S(2)}) collective-permute-start(bf16[128,2048]{1,0:T(8,128)(2,1)S(1)} %pad_maximum_fusion.1), channel_id=1, source_target_pairs={{0,1},{1,3},{3,2},{2,0},{4,5},{5,7},{7,6},{6,4},{8,9},{9,11},{11,1... | collective-permute-start | bytes 1572872 | tf_op jit(solution)/shard_map/ppermute | solution.py:402
  131.3 14.3 %collective-permute-start.34 = (bf16[128,2048]{1,0:T(8,128)(2,1)S(1)}, bf16[128,2048]{1,0:T(8,128)(2,1)S(1)}, u32[]{:S(2)}, u32[]{:S(2)}) collective-permute-start(bf16[128,2048]{1,0:T(8,128)(2,1)S(1)} %get-tuple-element.82), channel_id=1, source_target_pairs={{0,8},{4,12},{8,0},{12,4},{1,9},{5,13},{9,1},{13,5},{2,10},{6,14},... | collective-permute-start | bytes 1572872 | tf_op jit(solution)/shard_map/ppermute | solution.py:402
  132.1 15.0 %collective-permute-start.35 = (bf16[128,2048]{1,0:T(8,128)(2,1)S(1)}, bf16[128,2048]{1,0:T(8,128)(2,1)S(1)}, u32[]{:S(2)}, u32[]{:S(2)}) collective-permute-start(bf16[128,2048]{1,0:T(8,128)(2,1)S(1)} %add_convert_fusion.3), channel_id=1, source_target_pairs={{0,1},{1,3},{3,2},{2,0},{4,5},{5,7},{7,6},{6,4},{8,9},{9,11},{11,1... | collective-permute-start | bytes 1572872 | tf_op jit(solution)/shard_map/ppermute | solution.py:402
  147.5 14.2 %collective-permute-start.37 = (bf16[128,2048]{1,0:T(8,128)(2,1)S(1)}, bf16[128,2048]{1,0:T(8,128)(2,1)S(1)}, u32[]{:S(2)}, u32[]{:S(2)}) collective-permute-start(bf16[128,2048]{1,0:T(8,128)(2,1)S(1)} %add_convert_fusion.1), channel_id=1, source_target_pairs={{0,1},{1,3},{3,2},{2,0},{4,5},{5,7},{7,6},{6,4},{8,9},{9,11},{11,1... | collective-permute-start | bytes 1572872 | tf_op jit(solution)/shard_map/ppermute | solution.py:402
  148.3 13.4 %collective-permute-start.36 = (bf16[128,2048]{1,0:T(8,128)(2,1)S(1)}, bf16[128,2048]{1,0:T(8,128)(2,1)S(1)}, u32[]{:S(2)}, u32[]{:S(2)}) collective-permute-start(bf16[128,2048]{1,0:T(8,128)(2,1)S(1)} %get-tuple-element.87), channel_id=1, source_target_pairs={{0,8},{4,12},{8,0},{12,4},{1,9},{5,13},{9,1},{13,5},{2,10},{6,14},... | collective-permute-start | bytes 1572872 | tf_op jit(solution)/shard_map/ppermute | solution.py:402
  (27 other events, 167.6 us)

commit v15 on v13

--- a/solution.py
+++ b/solution.py
@@ -205,7 +205,7 @@
         + [pl.BlockSpec(memory_space=pl.ANY)] * len(present),
         out_specs=[pl.BlockSpec(memory_space=pltpu.VMEM)] * 2,
         out_shape=[jax.ShapeDtypeStruct(own.shape, jnp.bfloat16)] * 2,
-        compiler_params=pltpu.CompilerParams(vmem_limit_bytes=60 * MIB),
+        compiler_params=pltpu.CompilerParams(vmem_limit_bytes=10 * MIB),
     )(own, other, gain, *present)
 
 

time: 162 us -> 160 us (0.988)
  Pallas kernels: 36.8 us -> 34.5 us
    pallas_call x1, Pallas kernels: 2.52 us -> 0.31 us  [add_and_norm(): pl.pallas_call(norm_kernel, in_specs=[pl.BlockSpec(memory_space=pltpu.VME...]
    unnamed x42 -> x34, local copies, waits for them, and re-layouts: 6.63 us -> 7.09 us
  transfers between devices with their start and end apart: 38 -> 38, of which waited for: 20 -> 21; matrix products, arithmetic and copies ran while one was open for 3% -> 3% of each run, Pallas kernels for 18% -> 18%
where the time goes in v15:
time: 160 us
  waiting for transfers between devices  80.3 us (50%)
  Pallas kernels  34.5 us (22%)
  starting transfers between devices  31.3 us (20%)
  local copies, waits for them, and re-layouts  10.4 us (6%)
  other arithmetic  2.76 us (2%)
    ppermute x29, waiting for transfers between devices, move(): return lax.ppermute(array, *ways[way])  72.2 us
    pallas_call x4, Pallas kernels, experts_on_rows(): pl.pallas_call(functools.partial(experts_kernel, cap=cap, pieces=pieces),...  21.1 us
    ppermute x29, starting transfers between devices, move(): return lax.ppermute(array, *ways[way])  19.2 us
    pallas_call x2, Pallas kernels, attend(): pl.pallas_call(functools.partial(attend_kernel, scale=1.0 / HD ** 0.5), i...  11.2 us
    unnamed x34, local copies, waits for them, and re-layouts  7.09 us
    ppermute x1, waiting for transfers between devices, gathered_plan(): lax.ppermute(kv_away, 'seq', across)  6.41 us
    ppermute x3, starting transfers between devices, gathered_plan(): lax.ppermute(quad, 'sub', ring(steps))  5.68 us
  transfers between devices with their start and end apart: 38, of which 21 were waited for; matrix products, arithmetic and copies ran while one was open for 3% of the time, Pallas kernels for 18%

profile of v15, /device:TPU:0, one launch (start us, length us, event | category | flops | bytes accessed | tf_op | source)
XLA Modules:
  0.0 159.6 jit_solution(9939805986097839579)
XLA Ops:
  0.5 1.9 %shard_map.109 = (bf16[128,1024]{1,0:T(8,128)(2,1)}, bf16[144,256]{1,0:T(8,128)(2,1)}, bf16[144,256]{1,0:T(8,128)(2,1)}) custom-call(s32[1]{0:T(128)} %bitcast.7.chip_ref, bf16[128,2048]{1,0:T(8,128)(2,1)} %bitcast.35, bf16[128,256]{1,0:T(8,128)(2,1)} %bitcast.38, bf16[128,256]{1,0:T(8,128)(2,1)} %bitcast.39, s32[8,128]{1,0:T(8,128)} %bitcast.40, ...), custom_call_target="tpu_custom_call" | custom-call | tf_op jit(solution)/shard_map/pallas_call | solution.py:87
  2.3 2.5 %collective-permute-start.4 = (bf16[128,1024]{1,0:T(8,128)(2,1)}, bf16[128,1024]{1,0:T(8,128)(2,1)S(1)}, u32[]{:S(2)}, u32[]{:S(2)}) collective-permute-start(bf16[128,1024]{1,0:T(8,128)(2,1)} %get-tuple-element.51), channel_id=1, source_target_pairs={{0,8},{4,12},{8,0},{12,4},{1,9},{5,13},{9,1},{13,5},{2,10},{6,14},... | collective-permute-start | bytes 786440 | tf_op jit(solution)/shard_map/ppermute | solution.py:363
  7.4 6.4 %collective-permute-done.1.refs_2_ = bf16[144,256]{1,0:T(8,128)(2,1)S(1)} collective-permute-done((bf16[144,256]{1,0:T(8,128)(2,1)}, bf16[144,256]{1,0:T(8,128)(2,1)S(1)}, u32[]{:S(2)}, u32[]{:S(2)}) %collective-permute-start.1) | collective-permute-done | bytes 73760 | tf_op jit(solution)/shard_map/ppermute | solution.py:367
  17.1 5.4 %shard_map.111 = (bf16[128,2048]{1,0:T(8,128)(2,1)}, bf16[16,512]{1,0:T(8,128)(2,1)}) custom-call(s32[7]{0:T(128)} %stack.38.place_ref, bf16[128,1024]{1,0:T(8,128)(2,1)} %copy-done.15, bf16[144,256]{1,0:T(8,128)(2,1)} %get-tuple-element.48.refs_0_, bf16[144,256]{1,0:T(8,128)(2,1)} %copy-done.12, bf16[144,256]{1,0:T(8,128)(2,1)} %copy-done.13, ...), custom_call_target="tpu_custom_call" | custom-call | flops 805306368 | bytes 5242880 | tf_op jit(solution)/shard_map/pallas_call | solution.py:159
  22.5 1.6 %collective-permute-start.5 = (bf16[128,2048]{1,0:T(8,128)(2,1)}, bf16[128,2048]{1,0:T(8,128)(2,1)S(1)}, u32[]{:S(2)}, u32[]{:S(2)}) collective-permute-start(bf16[128,2048]{1,0:T(8,128)(2,1)} %get-tuple-element.52), channel_id=1, source_target_pairs={{0,8},{4,12},{8,0},{12,4},{1,9},{5,13},{9,1},{13,5},{2,10},{6,14},... | collective-permute-start | bytes 1572872 | tf_op jit(solution)/shard_map/ppermute | solution.py:379
  24.7 1.6 %collective-permute-start.6 = (bf16[16,512]{1,0:T(8,128)(2,1)}, bf16[16,512]{1,0:T(8,128)(2,1)S(1)}, u32[]{:S(2)}, u32[]{:S(2)}) collective-permute-start(bf16[16,512]{1,0:T(8,128)(2,1)} %get-tuple-element.53.quad_ref), channel_id=1, source_target_pairs={{0,1},{1,3},{3,2},{2,0},{4,5},{5,7},{7,6},{6,4},{8,9},{9,11},{11,1... | collective-permute-start | bytes 49160 | tf_op jit(solution)/shard_map/ppermute | solution.py:389
  26.4 2.5 %collective-permute-start.7 = (bf16[16,512]{1,0:T(8,128)(2,1)}, bf16[16,512]{1,0:T(8,128)(2,1)S(1)}, u32[]{:S(2)}, u32[]{:S(2)}) collective-permute-start(bf16[16,512]{1,0:T(8,128)(2,1)} %get-tuple-element.53.quad_ref), channel_id=1, source_target_pairs={{0,3},{1,2},{3,0},{2,1},{4,7},{5,6},{7,4},{6,5},{8,11},{9,10},{11,... | collective-permute-start | bytes 49160 | tf_op jit(solution)/shard_map/ppermute | solution.py:389
  28.8 1.6 collective-permute-start.8
  30.4 5.8 %shard_map.110 = (f32[128,2048]{1,0:T(8,128)}, bf16[16,512]{1,0:T(8,128)(2,1)}) custom-call(s32[7]{0:T(128)} %stack.37.place_ref, bf16[128,2048]{1,0:T(8,128)(2,1)} %bitcast.36, bf16[144,256]{1,0:T(8,128)(2,1)} %get-tuple-element.48.refs_0_, bf16[144,256]{1,0:T(8,128)(2,1)} %copy-done.12, bf16[144,256]{1,0:T(8,128)(2,1)} %copy-done.13, ...), custom_call_target="tpu_custom_call" | custom-call | flops 805306368 | bytes 5242880 | tf_op jit(solution)/shard_map/pallas_call | solution.py:159
  38.3 1.7 %collective-permute-start.10 = (bf16[128,2048]{1,0:T(8,128)(2,1)S(1)}, bf16[128,2048]{1,0:T(8,128)(2,1)S(1)}, u32[]{:S(2)}, u32[]{:S(2)}) collective-permute-start(bf16[128,2048]{1,0:T(8,128)(2,1)S(1)} %get-tuple-element.55.refs_0_), channel_id=1, source_target_pairs={{0,8},{4,12},{8,0},{12,4},{1,9},{5,13},{9,1},{13,5},{2,10},{6,14},... | collective-permute-start | bytes 1572872 | tf_op jit(solution)/shard_map/ppermute | solution.py:401
  40.0 1.6 collective-permute-start.11
  41.6 9.9 %collective-permute-done.10.refs_0_ = bf16[128,2048]{1,0:T(8,128)(2,1)S(1)} collective-permute-done((bf16[128,2048]{1,0:T(8,128)(2,1)S(1)}, bf16[128,2048]{1,0:T(8,128)(2,1)S(1)}, u32[]{:S(2)}, u32[]{:S(2)}) %collective-permute-start.10) | collective-permute-done | bytes 524320 | tf_op jit(solution)/shard_map/ppermute | solution.py:401
  51.5 2.5 %collective-permute-done.11.refs_1_ = bf16[128,2048]{1,0:T(8,128)(2,1)} collective-permute-done((bf16[128,2048]{1,0:T(8,128)(2,1)S(1)}, bf16[128,2048]{1,0:T(8,128)(2,1)}, u32[]{:S(2)}, u32[]{:S(2)}) %collective-permute-start.11) | collective-permute-done | bytes 524320 | tf_op jit(solution)/shard_map/ppermute | solution.py:401
  55.2 11.2 %collective-permute-done.13.refs_0_ = bf16[128,2048]{1,0:T(8,128)(2,1)} collective-permute-done((bf16[128,2048]{1,0:T(8,128)(2,1)}, bf16[128,2048]{1,0:T(8,128)(2,1)}, u32[]{:S(2)}, u32[]{:S(2)}) %collective-permute-start.13) | collective-permute-done | bytes 524320 | tf_op jit(solution)/shard_map/ppermute | solution.py:401
  67.5 1.5 collective-permute-start.15
  69.8 1.9 %copy-done.1 = bf16[1,2048,768]{2,1,0:T(8,128)(2,1)S(1)} copy-done((bf16[1,2048,768]{2,1,0:T(8,128)(2,1)S(1)}, bf16[1,2048,768]{2,1,0:T(8,128)(2,1)}, u32[]{:S(2)}) %copy-start.1) | copy-done | bytes 3145752
  71.7 1.9 %copy-done.2 = bf16[1,768,2048]{2,1,0:T(8,128)(2,1)S(1)} copy-done((bf16[1,768,2048]{2,1,0:T(8,128)(2,1)S(1)}, bf16[1,768,2048]{2,1,0:T(8,128)(2,1)}, u32[]{:S(2)}) %copy-start.2) | copy-done | bytes 3145752
  73.6 5.8 %shard_map.116 = (bf16[128,2048]{1,0:T(8,128)(2,1)S(1)}, bf16[128,2048]{1,0:T(8,128)(2,1)S(1)}, bf16[256,2048]{1,0:T(8,128)(2,1)S(1)}) custom-call(s32[1]{0:T(128)} %bitcast.15.mine_ref, bf16[16,512]{1,0:T(8,128)(2,1)S(1)} %collective-permute-done.6.refs_0_.quad_ref, bf16[128,2048]{1,0:T(8,128)(2,1)} %get-tuple-element.58.refs_0_, ...), custom_call_target="tpu_custom_call" | custom-call | tf_op jit(solution)/shard_map/pallas_call | solution.py:302
  79.4 2.7 %collective-permute-done.15.refs_0_ = bf16[128,2048]{1,0:T(8,128)(2,1)} collective-permute-done((bf16[128,2048]{1,0:T(8,128)(2,1)}, bf16[128,2048]{1,0:T(8,128)(2,1)}, u32[]{:S(2)}, u32[]{:S(2)}) %collective-permute-start.15) | collective-permute-done | bytes 524320 | tf_op jit(solution)/shard_map/ppermute | solution.py:401
  82.2 2.1 %collective-permute-done.16.refs_1_ = bf16[128,2048]{1,0:T(8,128)(2,1)} collective-permute-done((bf16[128,2048]{1,0:T(8,128)(2,1)}, bf16[128,2048]{1,0:T(8,128)(2,1)}, u32[]{:S(2)}, u32[]{:S(2)}) %collective-permute-start.16) | collective-permute-done | bytes 524320 | tf_op jit(solution)/shard_map/ppermute | solution.py:401
  88.7 5.5 %shard_map.118 = (bf16[128,2048]{1,0:T(8,128)(2,1)S(1)}, bf16[128,2048]{1,0:T(8,128)(2,1)S(1)}, bf16[256,2048]{1,0:T(8,128)(2,1)S(1)}) custom-call(s32[1]{0:T(128)} %bitcast.15.mine_ref, bf16[16,512]{1,0:T(8,128)(2,1)S(1)} %collective-permute-done.7.refs_1_.quad_ref, bf16[128,2048]{1,0:T(8,128)(2,1)} %get-tuple-element.59.refs_0_, ...), custom_call_target="tpu_custom_call" | custom-call | tf_op jit(solution)/shard_map/pallas_call | solution.py:302
  97.7 1.5 collective-permute-start.24
  101.5 5.4 %shard_map.120 = (bf16[128,2048]{1,0:T(8,128)(2,1)S(1)}, bf16[128,2048]{1,0:T(8,128)(2,1)S(1)}, bf16[256,2048]{1,0:T(8,128)(2,1)S(1)}) custom-call(s32[1]{0:T(128)} %bitcast.15.mine_ref, bf16[16,512]{1,0:T(8,128)(2,1)S(1)} %collective-permute-done.8.refs_2_.quad_ref, bf16[128,2048]{1,0:T(8,128)(2,1)} %get-tuple-element.62.refs_0_, ...), custom_call_target="tpu_custom_call" | custom-call | tf_op jit(solution)/shard_map/pallas_call | solution.py:302
  107.0 3.1 %collective-permute-done.25.refs_1_ = bf16[128,1024]{1,0:T(8,128)(2,1)S(1)} collective-permute-done((bf16[128,1024]{1,0:T(8,128)(2,1)S(1)}, bf16[128,1024]{1,0:T(8,128)(2,1)S(1)}, u32[]{:S(2)}, u32[]{:S(2)}) %collective-permute-start.25) | collective-permute-done | bytes 262176 | tf_op jit(solution)/shard_map/ppermute | solution.py:401
  110.9 1.6 collective-permute-start.30
  114.3 4.3 %shard_map.114 = (bf16[128,2048]{1,0:T(8,128)(2,1)S(1)}, bf16[128,2048]{1,0:T(8,128)(2,1)S(1)}, bf16[256,2048]{1,0:T(8,128)(2,1)S(1)}) custom-call(s32[1]{0:T(128)} %bitcast.15.mine_ref, bf16[16,512]{1,0:T(8,128)(2,1)S(1)} %copy-done.10, bf16[128,2048]{1,0:T(8,128)(2,1)S(1)} %copy-done.5, bf16[128,2048]{1,0:T(8,128)(2,1)S(1)} %collective-permute-done.9.refs_1_, ...), custom_call_target="tpu_custom_call" | custom-call | tf_op jit(solution)/shard_map/pallas_call | solution.py:302
  118.8 6.4 %collective-permute-done.30.refs_0_ = bf16[128,2048]{1,0:T(8,128)(2,1)S(1)} collective-permute-done((bf16[128,2048]{1,0:T(8,128)(2,1)S(1)}, bf16[128,2048]{1,0:T(8,128)(2,1)S(1)}, u32[]{:S(2)}, u32[]{:S(2)}) %collective-permute-start.30) | collective-permute-done | bytes 524320 | tf_op jit(solution)/shard_map/ppermute | solution.py:401
  125.2 2.7 %collective-permute-done.31.refs_1_ = bf16[128,2048]{1,0:T(8,128)(2,1)S(1)} collective-permute-done((bf16[128,2048]{1,0:T(8,128)(2,1)S(1)}, bf16[128,2048]{1,0:T(8,128)(2,1)S(1)}, u32[]{:S(2)}, u32[]{:S(2)}) %collective-permute-start.31) | collective-permute-done | bytes 524320 | tf_op jit(solution)/shard_map/ppermute | solution.py:401
  130.7 11.5 %collective-permute-done.34.refs_0_ = bf16[128,2048]{1,0:T(8,128)(2,1)S(1)} collective-permute-done((bf16[128,2048]{1,0:T(8,128)(2,1)S(1)}, bf16[128,2048]{1,0:T(8,128)(2,1)S(1)}, u32[]{:S(2)}, u32[]{:S(2)}) %collective-permute-start.34) | collective-permute-done | bytes 524320 | tf_op jit(solution)/shard_map/ppermute | solution.py:401
  142.2 1.6 collective-permute-done.35.refs_1_
  145.0 1.5 collective-permute-start.36
  146.5 11.9 %collective-permute-done.37 = bf16[128,2048]{1,0:T(8,128)(2,1)S(1)} collective-permute-done((bf16[128,2048]{1,0:T(8,128)(2,1)S(1)}, bf16[128,2048]{1,0:T(8,128)(2,1)S(1)}, u32[]{:S(2)}, u32[]{:S(2)}) %collective-permute-start.37) | collective-permute-done | bytes 524320 | tf_op jit(solution)/shard_map/ppermute | solution.py:401
  (111 shorter events, 30.1 us)
Async XLA Ops:
  0.0 15.0 %collective-permute-start.3 = (bf16[512,2048]{1,0:T(8,128)(2,1)}, bf16[512,2048]{1,0:T(8,128)(2,1)S(1)}, u32[]{:S(2)}, u32[]{:S(2)}) collective-permute-start(bf16[512,2048]{1,0:T(8,128)(2,1)} %refs_4_.1), channel_id=1, source_target_pairs={{0,4},{4,0},{8,12},{12,8},{1,5},{5,1},{9,13},{13,9},{2,6},{6,2},{1... | collective-permute-start | bytes 6291464 | tf_op jit(solution)/shard_map/ppermute | solution.py:370
  2.3 12.7 %collective-permute-start.4 = (bf16[128,1024]{1,0:T(8,128)(2,1)}, bf16[128,1024]{1,0:T(8,128)(2,1)S(1)}, u32[]{:S(2)}, u32[]{:S(2)}) collective-permute-start(bf16[128,1024]{1,0:T(8,128)(2,1)} %get-tuple-element.51), channel_id=1, source_target_pairs={{0,8},{4,12},{8,0},{12,4},{1,9},{5,13},{9,1},{13,5},{2,10},{6,14},... | collective-permute-start | bytes 786440 | tf_op jit(solution)/shard_map/ppermute | solution.py:363
  5.1 8.7 %collective-permute-start.1 = (bf16[144,256]{1,0:T(8,128)(2,1)}, bf16[144,256]{1,0:T(8,128)(2,1)S(1)}, u32[]{:S(2)}, u32[]{:S(2)}) collective-permute-start(bf16[144,256]{1,0:T(8,128)(2,1)} %get-tuple-element.49), channel_id=1, source_target_pairs={{0,8},{4,12},{8,0},{12,4},{1,9},{5,13},{9,1},{13,5},{2,10},{6,14},... | collective-permute-start | bytes 221192 | tf_op jit(solution)/shard_map/ppermute | solution.py:367
  5.4 9.6 %collective-permute-start.2 = (bf16[144,256]{1,0:T(8,128)(2,1)}, bf16[144,256]{1,0:T(8,128)(2,1)S(1)}, u32[]{:S(2)}, u32[]{:S(2)}) collective-permute-start(bf16[144,256]{1,0:T(8,128)(2,1)} %get-tuple-element.49), channel_id=1, source_target_pairs={{0,12},{4,8},{8,4},{12,0},{1,13},{5,9},{9,5},{13,1},{2,14},{6,10},... | collective-permute-start | bytes 221192 | tf_op jit(solution)/shard_map/ppermute | solution.py:368
  22.5 14.2 %collective-permute-start.5 = (bf16[128,2048]{1,0:T(8,128)(2,1)}, bf16[128,2048]{1,0:T(8,128)(2,1)S(1)}, u32[]{:S(2)}, u32[]{:S(2)}) collective-permute-start(bf16[128,2048]{1,0:T(8,128)(2,1)} %get-tuple-element.52), channel_id=1, source_target_pairs={{0,8},{4,12},{8,0},{12,4},{1,9},{5,13},{9,1},{13,5},{2,10},{6,14},... | collective-permute-start | bytes 1572872 | tf_op jit(solution)/shard_map/ppermute | solution.py:379
  24.7 11.5 %collective-permute-start.6 = (bf16[16,512]{1,0:T(8,128)(2,1)}, bf16[16,512]{1,0:T(8,128)(2,1)S(1)}, u32[]{:S(2)}, u32[]{:S(2)}) collective-permute-start(bf16[16,512]{1,0:T(8,128)(2,1)} %get-tuple-element.53.quad_ref), channel_id=1, source_target_pairs={{0,1},{1,3},{3,2},{2,0},{4,5},{5,7},{7,6},{6,4},{8,9},{9,11},{11,1... | collective-permute-start | bytes 49160 | tf_op jit(solution)/shard_map/ppermute | solution.py:389
  26.4 9.9 %collective-permute-start.7 = (bf16[16,512]{1,0:T(8,128)(2,1)}, bf16[16,512]{1,0:T(8,128)(2,1)S(1)}, u32[]{:S(2)}, u32[]{:S(2)}) collective-permute-start(bf16[16,512]{1,0:T(8,128)(2,1)} %get-tuple-element.53.quad_ref), channel_id=1, source_target_pairs={{0,3},{1,2},{3,0},{2,1},{4,7},{5,6},{7,4},{6,5},{8,11},{9,10},{11,... | collective-permute-start | bytes 49160 | tf_op jit(solution)/shard_map/ppermute | solution.py:389
  28.8 7.5 %collective-permute-start.8 = (bf16[16,512]{1,0:T(8,128)(2,1)}, bf16[16,512]{1,0:T(8,128)(2,1)S(1)}, u32[]{:S(2)}, u32[]{:S(2)}) collective-permute-start(bf16[16,512]{1,0:T(8,128)(2,1)} %get-tuple-element.53.quad_ref), channel_id=1, source_target_pairs={{0,2},{1,0},{3,1},{2,3},{4,6},{5,4},{7,5},{6,7},{8,10},{9,8},{11,9... | collective-permute-start | bytes 49160 | tf_op jit(solution)/shard_map/ppermute | solution.py:389
  38.3 13.2 %collective-permute-start.10 = (bf16[128,2048]{1,0:T(8,128)(2,1)S(1)}, bf16[128,2048]{1,0:T(8,128)(2,1)S(1)}, u32[]{:S(2)}, u32[]{:S(2)}) collective-permute-start(bf16[128,2048]{1,0:T(8,128)(2,1)S(1)} %get-tuple-element.55.refs_0_), channel_id=1, source_target_pairs={{0,8},{4,12},{8,0},{12,4},{1,9},{5,13},{9,1},{13,5},{2,10},{6,14},... | collective-permute-start | bytes 1572872 | tf_op jit(solution)/shard_map/ppermute | solution.py:401
  40.0 13.9 %collective-permute-start.11 = (bf16[128,2048]{1,0:T(8,128)(2,1)S(1)}, bf16[128,2048]{1,0:T(8,128)(2,1)}, u32[]{:S(2)}, u32[]{:S(2)}) collective-permute-start(bf16[128,2048]{1,0:T(8,128)(2,1)S(1)} %get-tuple-element.55.refs_0_), channel_id=1, source_target_pairs={{0,1},{1,3},{3,2},{2,0},{4,5},{5,7},{7,6},{6,4},{8,9},{9,11},{11,1... | collective-permute-start | bytes 1572872 | tf_op jit(solution)/shard_map/ppermute | solution.py:401
  54.0 12.4 %collective-permute-start.13 = (bf16[128,2048]{1,0:T(8,128)(2,1)}, bf16[128,2048]{1,0:T(8,128)(2,1)}, u32[]{:S(2)}, u32[]{:S(2)}) collective-permute-start(bf16[128,2048]{1,0:T(8,128)(2,1)} %get-tuple-element.58.refs_0_), channel_id=1, source_target_pairs={{0,8},{4,12},{8,0},{12,4},{1,9},{5,13},{9,1},{13,5},{2,10},{6,14},... | collective-permute-start | bytes 1572872 | tf_op jit(solution)/shard_map/ppermute | solution.py:401
  54.5 13.0 %collective-permute-start.14 = (bf16[128,2048]{1,0:T(8,128)(2,1)}, bf16[128,2048]{1,0:T(8,128)(2,1)}, u32[]{:S(2)}, u32[]{:S(2)}) collective-permute-start(bf16[128,2048]{1,0:T(8,128)(2,1)} %get-tuple-element.58.refs_0_), channel_id=1, source_target_pairs={{0,1},{1,3},{3,2},{2,0},{4,5},{5,7},{7,6},{6,4},{8,9},{9,11},{11,1... | collective-permute-start | bytes 1572872 | tf_op jit(solution)/shard_map/ppermute | solution.py:401
  55.2 14.6 %collective-permute-start.17 = (bf16[128,2048]{1,0:T(8,128)(2,1)}, bf16[128,2048]{1,0:T(8,128)(2,1)}, u32[]{:S(2)}, u32[]{:S(2)}) collective-permute-start(bf16[128,2048]{1,0:T(8,128)(2,1)} %get-tuple-element.58.refs_0_), channel_id=1, source_target_pairs={{0,4},{4,0},{8,12},{12,8},{1,5},{5,1},{9,13},{13,9},{2,6},{6,2},{1... | collective-permute-start | bytes 1572872 | tf_op jit(solution)/shard_map/ppermute | solution.py:401
  67.5 14.7 %collective-permute-start.15 = (bf16[128,2048]{1,0:T(8,128)(2,1)}, bf16[128,2048]{1,0:T(8,128)(2,1)}, u32[]{:S(2)}, u32[]{:S(2)}) collective-permute-start(bf16[128,2048]{1,0:T(8,128)(2,1)} %get-tuple-element.59.refs_0_), channel_id=1, source_target_pairs={{0,8},{4,12},{8,0},{12,4},{1,9},{5,13},{9,1},{13,5},{2,10},{6,14},... | collective-permute-start | bytes 1572872 | tf_op jit(solution)/shard_map/ppermute | solution.py:401
  69.0 15.3 %collective-permute-start.16 = (bf16[128,2048]{1,0:T(8,128)(2,1)}, bf16[128,2048]{1,0:T(8,128)(2,1)}, u32[]{:S(2)}, u32[]{:S(2)}) collective-permute-start(bf16[128,2048]{1,0:T(8,128)(2,1)} %get-tuple-element.59.refs_0_), channel_id=1, source_target_pairs={{0,1},{1,3},{3,2},{2,0},{4,5},{5,7},{7,6},{6,4},{8,9},{9,11},{11,1... | collective-permute-start | bytes 1572872 | tf_op jit(solution)/shard_map/ppermute | solution.py:401
  84.3 9.9 %collective-permute-start.23 = (bf16[256,2048]{1,0:T(8,128)(2,1)S(1)}, bf16[256,2048]{1,0:T(8,128)(2,1)S(1)}, u32[]{:S(2)}, u32[]{:S(2)}) collective-permute-start(bf16[256,2048]{1,0:T(8,128)(2,1)S(1)} %get-tuple-element.66), channel_id=1, source_target_pairs={{0,4},{4,0},{8,12},{12,8},{1,5},{5,1},{9,13},{13,9},{2,6},{6,2},{1... | collective-permute-start | bytes 3145736 | tf_op jit(solution)/shard_map/ppermute | solution.py:401
  86.8 8.8 %collective-permute-start.19 = (bf16[128,1024]{1,0:T(8,128)(2,1)S(1)}, bf16[128,1024]{1,0:T(8,128)(2,1)S(1)}, u32[]{:S(2)}, u32[]{:S(2)}) collective-permute-start(bf16[128,1024]{1,0:T(8,128)(2,1)S(1)} %slice.54), channel_id=1, source_target_pairs={{0,8},{4,12},{8,0},{12,4},{1,9},{5,13},{9,1},{13,5},{2,10},{6,14},... | collective-permute-start | bytes 786440 | tf_op jit(solution)/shard_map/ppermute | solution.py:401
  87.3 9.3 %collective-permute-start.20 = (bf16[128,1024]{1,0:T(8,128)(2,1)S(1)}, bf16[128,1024]{1,0:T(8,128)(2,1)S(1)}, u32[]{:S(2)}, u32[]{:S(2)}) collective-permute-start(bf16[128,1024]{1,0:T(8,128)(2,1)S(1)} %slice.55), channel_id=1, source_target_pairs={{0,1},{1,3},{3,2},{2,0},{4,5},{5,7},{7,6},{6,4},{8,9},{9,11},{11,1... | collective-permute-start | bytes 786440 | tf_op jit(solution)/shard_map/ppermute | solution.py:401
  96.7 10.2 %collective-permute-start.29 = (bf16[256,2048]{1,0:T(8,128)(2,1)S(1)}, bf16[256,2048]{1,0:T(8,128)(2,1)S(1)}, u32[]{:S(2)}, u32[]{:S(2)}) collective-permute-start(bf16[256,2048]{1,0:T(8,128)(2,1)S(1)} %get-tuple-element.73), channel_id=1, source_target_pairs={{0,4},{4,0},{8,12},{12,8},{1,5},{5,1},{9,13},{13,9},{2,6},{6,2},{1... | collective-permute-start | bytes 3145736 | tf_op jit(solution)/shard_map/ppermute | solution.py:401
  96.7 4.0 %collective-permute-start.26 = (bf16[128,2048]{1,0:T(8,128)(2,1)}, bf16[128,2048]{1,0:T(8,128)(2,1)S(1)}, u32[]{:S(2)}, u32[]{:S(2)}) collective-permute-start(bf16[128,2048]{1,0:T(8,128)(2,1)} %get-tuple-element.62.refs_0_), channel_id=1, source_target_pairs={{0,4},{4,0},{8,12},{12,8},{1,5},{5,1},{9,13},{13,9},{2,6},{6,2},{1... | collective-permute-start | bytes 1572872 | tf_op jit(solution)/shard_map/ppermute | solution.py:401
  97.2 4.3 %collective-permute-start.27 = (bf16[128,1024]{1,0:T(8,128)(2,1)S(1)}, bf16[128,1024]{1,0:T(8,128)(2,1)S(1)}, u32[]{:S(2)}, u32[]{:S(2)}) collective-permute-start(bf16[128,1024]{1,0:T(8,128)(2,1)S(1)} %get-tuple-element.69.refs_2_), channel_id=1, source_target_pairs={{0,4},{4,0},{8,12},{12,8},{1,5},{5,1},{9,13},{13,9},{2,6},{6,2},{1... | collective-permute-start | bytes 786440 | tf_op jit(solution)/shard_map/ppermute | solution.py:401
  97.2 4.3 %collective-permute-start.28 = (bf16[128,1024]{1,0:T(8,128)(2,1)S(1)}, bf16[128,1024]{1,0:T(8,128)(2,1)S(1)}, u32[]{:S(2)}, u32[]{:S(2)}) collective-permute-start(bf16[128,1024]{1,0:T(8,128)(2,1)S(1)} %get-tuple-element.70.refs_3_), channel_id=1, source_target_pairs={{0,4},{4,0},{8,12},{12,8},{1,5},{5,1},{9,13},{13,9},{2,6},{6,2},{1... | collective-permute-start | bytes 786440 | tf_op jit(solution)/shard_map/ppermute | solution.py:401
  97.7 9.3 %collective-permute-start.24 = (bf16[128,1024]{1,0:T(8,128)(2,1)S(1)}, bf16[128,1024]{1,0:T(8,128)(2,1)S(1)}, u32[]{:S(2)}, u32[]{:S(2)}) collective-permute-start(bf16[128,1024]{1,0:T(8,128)(2,1)S(1)} %get-tuple-element.67), channel_id=1, source_target_pairs={{0,8},{4,12},{8,0},{12,4},{1,9},{5,13},{9,1},{13,5},{2,10},{6,14},... | collective-permute-start | bytes 786440 | tf_op jit(solution)/shard_map/ppermute | solution.py:401
  100.7 9.5 %collective-permute-start.25 = (bf16[128,1024]{1,0:T(8,128)(2,1)S(1)}, bf16[128,1024]{1,0:T(8,128)(2,1)S(1)}, u32[]{:S(2)}, u32[]{:S(2)}) collective-permute-start(bf16[128,1024]{1,0:T(8,128)(2,1)S(1)} %get-tuple-element.68), channel_id=1, source_target_pairs={{0,1},{1,3},{3,2},{2,0},{4,5},{5,7},{7,6},{6,4},{8,9},{9,11},{11,1... | collective-permute-start | bytes 786440 | tf_op jit(solution)/shard_map/ppermute | solution.py:401
  110.2 8.5 %collective-permute-start.32 = (bf16[256,2048]{1,0:T(8,128)(2,1)S(1)}, bf16[256,2048]{1,0:T(8,128)(2,1)S(1)}, u32[]{:S(2)}, u32[]{:S(2)}) collective-permute-start(bf16[256,2048]{1,0:T(8,128)(2,1)S(1)} %get-tuple-element.80), channel_id=1, source_target_pairs={{0,4},{4,0},{8,12},{12,8},{1,5},{5,1},{9,13},{13,9},{2,6},{6,2},{1... | collective-permute-start | bytes 3145736 | tf_op jit(solution)/shard_map/ppermute | solution.py:401
  110.2 3.9 %collective-permute-start.9 = (bf16[128,2048]{1,0:T(8,128)(2,1)S(1)}, bf16[128,2048]{1,0:T(8,128)(2,1)S(1)}, u32[]{:S(2)}, u32[]{:S(2)}) collective-permute-start(bf16[128,2048]{1,0:T(8,128)(2,1)S(1)} %copy-done.5), channel_id=1, source_target_pairs={{0,4},{4,0},{8,12},{12,8},{1,5},{5,1},{9,13},{13,9},{2,6},{6,2},{1... | collective-permute-start | bytes 1572872 | tf_op jit(solution)/shard_map/ppermute | solution.py:401
  110.9 14.3 %collective-permute-start.30 = (bf16[128,2048]{1,0:T(8,128)(2,1)S(1)}, bf16[128,2048]{1,0:T(8,128)(2,1)S(1)}, u32[]{:S(2)}, u32[]{:S(2)}) collective-permute-start(bf16[128,2048]{1,0:T(8,128)(2,1)S(1)} %pad_maximum_fusion), channel_id=1, source_target_pairs={{0,8},{4,12},{8,0},{12,4},{1,9},{5,13},{9,1},{13,5},{2,10},{6,14},... | collective-permute-start | bytes 1572872 | tf_op jit(solution)/shard_map/ppermute | solution.py:401
  112.7 15.2 %collective-permute-start.31 = (bf16[128,2048]{1,0:T(8,128)(2,1)S(1)}, bf16[128,2048]{1,0:T(8,128)(2,1)S(1)}, u32[]{:S(2)}, u32[]{:S(2)}) collective-permute-start(bf16[128,2048]{1,0:T(8,128)(2,1)S(1)} %pad_maximum_fusion.1), channel_id=1, source_target_pairs={{0,1},{1,3},{3,2},{2,0},{4,5},{5,7},{7,6},{6,4},{8,9},{9,11},{11,1... | collective-permute-start | bytes 1572872 | tf_op jit(solution)/shard_map/ppermute | solution.py:401
  127.9 14.3 %collective-permute-start.34 = (bf16[128,2048]{1,0:T(8,128)(2,1)S(1)}, bf16[128,2048]{1,0:T(8,128)(2,1)S(1)}, u32[]{:S(2)}, u32[]{:S(2)}) collective-permute-start(bf16[128,2048]{1,0:T(8,128)(2,1)S(1)} %get-tuple-element.82), channel_id=1, source_target_pairs={{0,8},{4,12},{8,0},{12,4},{1,9},{5,13},{9,1},{13,5},{2,10},{6,14},... | collective-permute-start | bytes 1572872 | tf_op jit(solution)/shard_map/ppermute | solution.py:401
  128.8 15.0 %collective-permute-start.35 = (bf16[128,2048]{1,0:T(8,128)(2,1)S(1)}, bf16[128,2048]{1,0:T(8,128)(2,1)S(1)}, u32[]{:S(2)}, u32[]{:S(2)}) collective-permute-start(bf16[128,2048]{1,0:T(8,128)(2,1)S(1)} %add_convert_fusion.3), channel_id=1, source_target_pairs={{0,1},{1,3},{3,2},{2,0},{4,5},{5,7},{7,6},{6,4},{8,9},{9,11},{11,1... | collective-permute-start | bytes 1572872 | tf_op jit(solution)/shard_map/ppermute | solution.py:401
  144.1 14.2 %collective-permute-start.37 = (bf16[128,2048]{1,0:T(8,128)(2,1)S(1)}, bf16[128,2048]{1,0:T(8,128)(2,1)S(1)}, u32[]{:S(2)}, u32[]{:S(2)}) collective-permute-start(bf16[128,2048]{1,0:T(8,128)(2,1)S(1)} %add_convert_fusion.1), channel_id=1, source_target_pairs={{0,1},{1,3},{3,2},{2,0},{4,5},{5,7},{7,6},{6,4},{8,9},{9,11},{11,1... | collective-permute-start | bytes 1572872 | tf_op jit(solution)/shard_map/ppermute | solution.py:401
  145.0 13.4 %collective-permute-start.36 = (bf16[128,2048]{1,0:T(8,128)(2,1)S(1)}, bf16[128,2048]{1,0:T(8,128)(2,1)S(1)}, u32[]{:S(2)}, u32[]{:S(2)}) collective-permute-start(bf16[128,2048]{1,0:T(8,128)(2,1)S(1)} %get-tuple-element.87), channel_id=1, source_target_pairs={{0,8},{4,12},{8,0},{12,4},{1,9},{5,13},{9,1},{13,5},{2,10},{6,14},... | collective-permute-start | bytes 1572872 | tf_op jit(solution)/shard_map/ppermute | solution.py:401
  (23 other events, 161.7 us)
